TPU v7x, 32 devices: a whole 2x2x4 slice. The times are simulated.
32 devices in a mesh: grp: 2 (over x), row: 16 (over z, y, core).
Axes of the slice: x: 2, y: 2, z: 4, core: 2. Of those that a mesh axis runs over, the one named last changes fastest.
Arguments:
- features: float32 [8, 32768], P(None, ('grp', 'row')), parts along dimension 1, may hold values from -6 to 6
- lengthscale: float32 [8], replicated, may hold values from 1 to 3
- noise: float32 [32768], P(('grp', 'row')), parts along dimension 0, may hold values from 0.1 to 1
- rhs: float32 [8, 32768], P(None, ('grp', 'row')), parts along dimension 1, may hold values from -15 to 15, as said below
Outputs:
- solution: float32 [8, 32768], P(None, ('grp', 'row')), parts along dimension 1
- residual: float32 [8, 32768], P(None, ('grp', 'row')), parts along dimension 1
There are 2 independent parts, one for each index of `grp`. A program takes and returns all parts, laid end to end along the dimension named above; an argument that names none is the same for every part. Nothing has to cross between parts.
Inputs may be any that keep to these rules, and one draw needn't show every extreme that they name: `rhs`: real values of order one.
All inputs are finite; a program needn't handle non-finite values.
Results may differ from a plain program's by a relative error of at most 0.00013.
Values sent between devices are 32-bit elements; how exact they have to be, the bound alone decides.
No kernel may reach another device: no remote copies, remote signals or barrier semaphores. Data moves between devices by JAX's collectives and lax.ppermute only.
A program may use at most 64 MiB of HBM per device.

v0:
```python
import math

import jax
import jax.numpy as jnp
from jax import lax
from jax.sharding import PartitionSpec as P

ITERS = 2


def shifted(value, axis, by):
    length = lax.axis_size(axis)
    return lax.ppermute(value, axis, [(i, (i + by) % length) for i in range(length)])


def block_term(mine, mine_sq, pts, dirs):
    pts_sq = jnp.sum(pts * pts, axis=0)
    cross = lax.dot_general(
        mine,
        pts,
        (((0,), (0,)), ((), ())),
        precision=lax.Precision.HIGHEST,
        preferred_element_type=jnp.float32,
    )
    weight = jnp.exp(-0.5 * (mine_sq[:, None] + pts_sq[None, :] - 2.0 * cross))
    return lax.dot_general(
        dirs,
        weight,
        (((1,), (1,)), ((), ())),
        precision=lax.Precision.HIGHEST,
        preferred_element_type=jnp.float32,
    )


def blocked_term(mine, mine_sq, pts, dirs):
    return block_term(mine, mine_sq, pts, dirs)


def pair_terms(left_pts, right_pts, left_dirs, right_dirs):
    left_sq = jnp.sum(left_pts * left_pts, axis=0)
    right_sq = jnp.sum(right_pts * right_pts, axis=0)
    cross = lax.dot_general(
        left_pts,
        right_pts,
        (((0,), (0,)), ((), ())),
        precision=lax.Precision.HIGHEST,
        preferred_element_type=jnp.float32,
    )
    weight = jnp.exp(-0.5 * (left_sq[:, None] + right_sq[None, :] - 2.0 * cross))
    to_left = lax.dot_general(
        right_dirs,
        weight,
        (((1,), (1,)), ((), ())),
        precision=lax.Precision.HIGHEST,
        preferred_element_type=jnp.float32,
    )
    to_right = lax.dot_general(
        left_dirs,
        weight,
        (((1,), (0,)), ((), ())),
        precision=lax.Precision.HIGHEST,
        preferred_element_type=jnp.float32,
    )
    return (to_left, to_right)


def shards(features, lengthscale, noise, rhs):
    scaled = features / lengthscale[:, None]
    scaled_sq = jnp.sum(scaled * scaled, axis=0)
    npoints = features.shape[1]
    nfeat = features.shape[0]
    nrhs = rhs.shape[0]
    devs = lax.axis_size("row")
    amplitude = 1.0 / math.sqrt(npoints * devs)
    solution = jnp.zeros_like(rhs)
    residual = rhs
    direc = rhs
    norm_now = lax.psum(jnp.sum(rhs * rhs, axis=1), "row")
    for step in range(ITERS):
        half_pts = npoints // 2
        lower = lax.axis_index("row") < devs // 2
        own_total = blocked_term(scaled, scaled_sq, scaled, direc)
        packed = jnp.concatenate([scaled, direc, jnp.zeros(direc.shape, jnp.float32)], axis=0)

        def cycle_step(turn, carry):
            moving, own_acc = carry
            moving = shifted(moving, "row", 1)
            to_own, to_visit = pair_terms(
                scaled, moving[:nfeat], direc, moving[nfeat : nfeat + nrhs]
            )
            collected = moving[nfeat + nrhs :] + to_visit
            moving = jnp.concatenate([moving[: nfeat + nrhs], collected], axis=0)
            return (moving, own_acc + to_own)

        packed, own_total = lax.fori_loop(0, devs // 2 - 1, cycle_step, (packed, own_total))
        packed = shifted(packed, "row", 1)
        visit_pts = packed[:nfeat]
        visit_dirs = packed[nfeat : nfeat + nrhs]
        visit_acc = packed[nfeat + nrhs :]
        left_pts = jnp.where(lower, scaled, visit_pts)
        left_dirs = jnp.where(lower, direc, visit_dirs)
        right_pts = jnp.where(lower, visit_pts[:, :half_pts], scaled[:, half_pts:])
        right_dirs = jnp.where(lower, visit_dirs[:, :half_pts], direc[:, half_pts:])
        to_left, to_right = pair_terms(left_pts, right_pts, left_dirs, right_dirs)
        zero_half = jnp.zeros((nrhs, npoints - half_pts), jnp.float32)
        own_total = own_total + jnp.where(
            lower, to_left, jnp.concatenate([zero_half, to_right], axis=1)
        )
        visit_acc = visit_acc + jnp.where(
            lower, jnp.concatenate([to_right, zero_half], axis=1), to_left
        )
        returned = shifted(visit_acc, "row", devs // 2)
        total = own_total + returned
        image = amplitude * total + noise[None, :] * direc
        local_curv = jnp.sum(direc * image, axis=1)
        curv = lax.psum(local_curv, "row")
        alpha = norm_now / curv
        solution = solution + alpha[:, None] * direc
        residual = residual - alpha[:, None] * image
        if step + 1 < ITERS:
            norm_next = lax.psum(jnp.sum(residual * residual, axis=1), "row")
            direc = residual + (norm_next / norm_now)[:, None] * direc
            norm_now = norm_next
    return (solution, residual)


def solution(mesh):
    in_specs = (P(None, ("grp", "row")), P(), P(("grp", "row")), P(None, ("grp", "row")))
    out_specs = (P(None, ("grp", "row")), P(None, ("grp", "row")))
    return jax.shard_map(shards, mesh=mesh, in_specs=in_specs, out_specs=out_specs, check_vma=False)
```

profile of v0, /device:TPU:0, one launch (start us, length us, event | category | flops | bytes accessed | tf_op | source)
XLA Modules:
  0.0 395.5 jit_solution(17791008789617114264)
XLA Ops:
  1.5 3.5 fusion.67
  7.0 4.5 %fusion.50 = f32[8,1024]{1,0:T(8,128)S(1)} fusion(f32[8,1024]{1,0:T(8,128)S(1)} %copy-done.1, f32[1024,1024]{1,0:T(8,128)S(1)} %fusion.67, f32[1024]{0:T(1024)S(1)} %get-tuple-element.277), kind=kOutput, calls=%fused_computation.61 | convolution fusion | flops 104857600 | bytes 4263936 | tf_op jit(solution)/shard_map/dot_general | solution.py:26
  11.4 127.6 %while.28 = (s32[]{:T(128)}, f32[24,1024]{1,0:T(8,128)S(1)}, f32[8,1024]{1,0:T(8,128)S(1)}, f32[1024]{0:T(1024)S(1)}, f32[8,1024]{1,0:T(8,128)S(1)}, /*index=5*/f32[8,1024]{1,0:T(8,128)S(1)}, s32[]{:T(128)}) while((s32[]{:T(128)}, f32[24,1024]{1,0:T(8,128)S(1)}, f32[8,1024]{1,0:T(8,128)S(1)}, f32[1024]{0:T(1024)S(1)}, ...), condition=%wide.region_5.6_spmd, body=%wide.region_3.5_spmd.sunk | while | flops 310434816 | bytes 13619317 | solution.py:95
  12.5 7.3 %collective-permute-done = f32[24,1024]{1,0:T(8,128)S(1)} collective-permute-done((f32[24,1024]{1,0:T(8,128)S(1)}, f32[24,1024]{1,0:T(8,128)S(1)}, u32[]{:S(2)}, u32[]{:S(2)}) %collective-permute-start) | collective-permute-done | bytes 98336 | tf_op jit(solution)/shard_map/while/body/eval_jaxpr/ppermute | solution.py:13
  19.8 3.5 fusion.96
  23.3 3.2 slice_add_fusion.6
  26.5 4.5 %fusion.97 = f32[8,1024]{1,0:T(8,128)S(1)} fusion(f32[8,1024]{1,0:T(8,128)S(1)} %get-tuple-element.262, f32[1024,1024]{1,0:T(8,128)S(1)} %fusion.96, f32[1024]{0:T(1024)S(1)} %multiply_reduce_fusion.13, f32[1024]{0:T(1024)S(1)} %get-tuple-element.270, f32[24,1024]{1,0:T(8,128)S(1)} %collective-permute-done), kind=kOutput, calls=%fused_computation.13.clone.1 | convolution fusion | flops 104865792 | bytes 4300800 | tf_op jit(solution)/shard_map/while/body/eval_jaxpr/dot_general | solution.py:50
  31.0 6.8 %collective-permute-done = f32[24,1024]{1,0:T(8,128)S(1)} collective-permute-done((f32[24,1024]{1,0:T(8,128)S(1)}, f32[24,1024]{1,0:T(8,128)S(1)}, u32[]{:S(2)}, u32[]{:S(2)}) %collective-permute-start) | collective-permute-done | bytes 98336 | tf_op jit(solution)/shard_map/while/body/eval_jaxpr/ppermute | solution.py:13
  37.8 3.5 fusion.96
  41.4 3.2 slice_add_fusion.6
  44.5 4.5 %fusion.97 = f32[8,1024]{1,0:T(8,128)S(1)} fusion(f32[8,1024]{1,0:T(8,128)S(1)} %get-tuple-element.262, f32[1024,1024]{1,0:T(8,128)S(1)} %fusion.96, f32[1024]{0:T(1024)S(1)} %multiply_reduce_fusion.13, f32[1024]{0:T(1024)S(1)} %get-tuple-element.270, f32[24,1024]{1,0:T(8,128)S(1)} %collective-permute-done), kind=kOutput, calls=%fused_computation.13.clone.1 | convolution fusion | flops 104865792 | bytes 4300800 | tf_op jit(solution)/shard_map/while/body/eval_jaxpr/dot_general | solution.py:50
  49.0 6.8 %collective-permute-done = f32[24,1024]{1,0:T(8,128)S(1)} collective-permute-done((f32[24,1024]{1,0:T(8,128)S(1)}, f32[24,1024]{1,0:T(8,128)S(1)}, u32[]{:S(2)}, u32[]{:S(2)}) %collective-permute-start) | collective-permute-done | bytes 98336 | tf_op jit(solution)/shard_map/while/body/eval_jaxpr/ppermute | solution.py:13
  55.8 3.5 fusion.96
  59.4 3.2 slice_add_fusion.6
  62.5 4.5 %fusion.97 = f32[8,1024]{1,0:T(8,128)S(1)} fusion(f32[8,1024]{1,0:T(8,128)S(1)} %get-tuple-element.262, f32[1024,1024]{1,0:T(8,128)S(1)} %fusion.96, f32[1024]{0:T(1024)S(1)} %multiply_reduce_fusion.13, f32[1024]{0:T(1024)S(1)} %get-tuple-element.270, f32[24,1024]{1,0:T(8,128)S(1)} %collective-permute-done), kind=kOutput, calls=%fused_computation.13.clone.1 | convolution fusion | flops 104865792 | bytes 4300800 | tf_op jit(solution)/shard_map/while/body/eval_jaxpr/dot_general | solution.py:50
  67.0 6.8 %collective-permute-done = f32[24,1024]{1,0:T(8,128)S(1)} collective-permute-done((f32[24,1024]{1,0:T(8,128)S(1)}, f32[24,1024]{1,0:T(8,128)S(1)}, u32[]{:S(2)}, u32[]{:S(2)}) %collective-permute-start) | collective-permute-done | bytes 98336 | tf_op jit(solution)/shard_map/while/body/eval_jaxpr/ppermute | solution.py:13
  73.8 3.5 fusion.96
  77.4 3.2 slice_add_fusion.6
  80.5 4.5 %fusion.97 = f32[8,1024]{1,0:T(8,128)S(1)} fusion(f32[8,1024]{1,0:T(8,128)S(1)} %get-tuple-element.262, f32[1024,1024]{1,0:T(8,128)S(1)} %fusion.96, f32[1024]{0:T(1024)S(1)} %multiply_reduce_fusion.13, f32[1024]{0:T(1024)S(1)} %get-tuple-element.270, f32[24,1024]{1,0:T(8,128)S(1)} %collective-permute-done), kind=kOutput, calls=%fused_computation.13.clone.1 | convolution fusion | flops 104865792 | bytes 4300800 | tf_op jit(solution)/shard_map/while/body/eval_jaxpr/dot_general | solution.py:50
  85.0 6.8 %collective-permute-done = f32[24,1024]{1,0:T(8,128)S(1)} collective-permute-done((f32[24,1024]{1,0:T(8,128)S(1)}, f32[24,1024]{1,0:T(8,128)S(1)}, u32[]{:S(2)}, u32[]{:S(2)}) %collective-permute-start) | collective-permute-done | bytes 98336 | tf_op jit(solution)/shard_map/while/body/eval_jaxpr/ppermute | solution.py:13
  91.8 3.5 fusion.96
  95.4 3.2 slice_add_fusion.6
  98.6 4.5 %fusion.97 = f32[8,1024]{1,0:T(8,128)S(1)} fusion(f32[8,1024]{1,0:T(8,128)S(1)} %get-tuple-element.262, f32[1024,1024]{1,0:T(8,128)S(1)} %fusion.96, f32[1024]{0:T(1024)S(1)} %multiply_reduce_fusion.13, f32[1024]{0:T(1024)S(1)} %get-tuple-element.270, f32[24,1024]{1,0:T(8,128)S(1)} %collective-permute-done), kind=kOutput, calls=%fused_computation.13.clone.1 | convolution fusion | flops 104865792 | bytes 4300800 | tf_op jit(solution)/shard_map/while/body/eval_jaxpr/dot_general | solution.py:50
  103.1 6.8 %collective-permute-done = f32[24,1024]{1,0:T(8,128)S(1)} collective-permute-done((f32[24,1024]{1,0:T(8,128)S(1)}, f32[24,1024]{1,0:T(8,128)S(1)}, u32[]{:S(2)}, u32[]{:S(2)}) %collective-permute-start) | collective-permute-done | bytes 98336 | tf_op jit(solution)/shard_map/while/body/eval_jaxpr/ppermute | solution.py:13
  109.8 3.5 fusion.96
  113.4 3.2 slice_add_fusion.6
  116.6 4.5 %fusion.97 = f32[8,1024]{1,0:T(8,128)S(1)} fusion(f32[8,1024]{1,0:T(8,128)S(1)} %get-tuple-element.262, f32[1024,1024]{1,0:T(8,128)S(1)} %fusion.96, f32[1024]{0:T(1024)S(1)} %multiply_reduce_fusion.13, f32[1024]{0:T(1024)S(1)} %get-tuple-element.270, f32[24,1024]{1,0:T(8,128)S(1)} %collective-permute-done), kind=kOutput, calls=%fused_computation.13.clone.1 | convolution fusion | flops 104865792 | bytes 4300800 | tf_op jit(solution)/shard_map/while/body/eval_jaxpr/dot_general | solution.py:50
  121.1 6.8 %collective-permute-done = f32[24,1024]{1,0:T(8,128)S(1)} collective-permute-done((f32[24,1024]{1,0:T(8,128)S(1)}, f32[24,1024]{1,0:T(8,128)S(1)}, u32[]{:S(2)}, u32[]{:S(2)}) %collective-permute-start) | collective-permute-done | bytes 98336 | tf_op jit(solution)/shard_map/while/body/eval_jaxpr/ppermute | solution.py:13
  127.8 3.5 fusion.96
  131.4 3.2 slice_add_fusion.6
  134.6 4.5 %fusion.97 = f32[8,1024]{1,0:T(8,128)S(1)} fusion(f32[8,1024]{1,0:T(8,128)S(1)} %get-tuple-element.262, f32[1024,1024]{1,0:T(8,128)S(1)} %fusion.96, f32[1024]{0:T(1024)S(1)} %multiply_reduce_fusion.13, f32[1024]{0:T(1024)S(1)} %get-tuple-element.270, f32[24,1024]{1,0:T(8,128)S(1)} %collective-permute-done), kind=kOutput, calls=%fused_computation.13.clone.1 | convolution fusion | flops 104865792 | bytes 4300800 | tf_op jit(solution)/shard_map/while/body/eval_jaxpr/dot_general | solution.py:50
  139.3 6.7 %collective-permute-done.2 = f32[24,1024]{1,0:T(8,128)S(1)} collective-permute-done((f32[24,1024]{1,0:T(8,128)S(1)}, f32[24,1024]{1,0:T(8,128)S(1)}, u32[]{:S(2)}, u32[]{:S(2)}) %collective-permute-start.2) | collective-permute-done | bytes 98336 | tf_op jit(solution)/shard_map/ppermute | solution.py:13
  151.1 4.8 %collective-permute-done.3 = f32[8,1024]{1,0:T(8,128)S(1)} collective-permute-done((f32[8,1024]{1,0:T(8,128)S(1)}, f32[8,1024]{1,0:T(8,128)S(1)}, u32[]{:S(2)}, u32[]{:S(2)}) %collective-permute-start.3) | collective-permute-done | bytes 32800 | tf_op jit(solution)/shard_map/ppermute | solution.py:13
  156.1 29.5 %all-reduce.4 = (f32[8]{0:T(128)S(1)}, f32[8]{0:T(128)S(1)}) all-reduce(f32[8]{0:T(128)S(1)} %get-tuple-element.141, f32[8]{0:T(128)S(1)} %get-tuple-element.140), channel_id=1, replica_groups=mesh['grp'=2,'row'=16] {'row'}, use_global_device_ids=true, to_apply=%region_1.0 | all-reduce | flops 16 | bytes 128 | tf_op jit(solution)/shard_map/psum | solution.py:78
  185.8 29.5 %psum.30 = f32[8]{0:T(128)S(1)} all-reduce(f32[8]{0:T(128)S(1)} %multiply_reduce_fusion.4), channel_id=1, replica_groups=mesh['grp'=2,'row'=16] {'row'}, use_global_device_ids=true, to_apply=%region_11.12 | all-reduce | flops 8 | bytes 64 | tf_op jit(solution)/shard_map/psum | solution.py:121
  215.4 6.2 %fusion.40 = f32[8,1024]{1,0:T(8,128)S(1)} fusion(f32[8,1024]{1,0:T(8,128)S(1)} %multiply_add_fusion.2, f32[1024,1024]{1,0:T(8,128)} %copy-done, f32[1024]{0:T(1024)S(1)} %get-tuple-element.311), kind=kOutput, calls=%fused_computation.49 | convolution fusion | flops 104857600 | bytes 4263936 | tf_op jit(solution)/shard_map/dot_general | solution.py:26
  221.7 126.3 %while.29 = (s32[]{:T(128)}, f32[24,1024]{1,0:T(8,128)S(1)}, f32[8,1024]{1,0:T(8,128)S(1)}, f32[1024]{0:T(1024)S(1)}, f32[8,1024]{1,0:T(8,128)S(1)}, /*index=5*/f32[8,1024]{1,0:T(8,128)S(1)}, s32[]{:T(128)}) while((s32[]{:T(128)}, f32[24,1024]{1,0:T(8,128)S(1)}, f32[8,1024]{1,0:T(8,128)S(1)}, f32[1024]{0:T(1024)S(1)}, ...), condition=%wide.region_14.15_spmd, body=%wide.region_12.14_spmd.sunk | while | flops 310434816 | bytes 13619317 | solution.py:95
  222.0 6.7 %collective-permute-done.1 = f32[24,1024]{1,0:T(8,128)S(1)} collective-permute-done((f32[24,1024]{1,0:T(8,128)S(1)}, f32[24,1024]{1,0:T(8,128)S(1)}, u32[]{:S(2)}, u32[]{:S(2)}) %collective-permute-start.1) | collective-permute-done | bytes 98336 | tf_op jit(solution)/shard_map/while/body/eval_jaxpr/ppermute | solution.py:13
  228.7 3.5 fusion.102
  232.3 3.2 slice_add_fusion.7
  235.4 4.5 %fusion.103 = f32[8,1024]{1,0:T(8,128)S(1)} fusion(f32[8,1024]{1,0:T(8,128)S(1)} %get-tuple-element.283, f32[1024,1024]{1,0:T(8,128)S(1)} %fusion.102, f32[1024]{0:T(1024)S(1)} %multiply_reduce_fusion.14, f32[1024]{0:T(1024)S(1)} %get-tuple-element.291, f32[24,1024]{1,0:T(8,128)S(1)} %collective-permute-done.1), kind=kOutput, calls=%fused_computation.37.clone.1 | convolution fusion | flops 104865792 | bytes 4300800 | tf_op jit(solution)/shard_map/while/body/eval_jaxpr/dot_general | solution.py:50
  239.9 6.8 %collective-permute-done.1 = f32[24,1024]{1,0:T(8,128)S(1)} collective-permute-done((f32[24,1024]{1,0:T(8,128)S(1)}, f32[24,1024]{1,0:T(8,128)S(1)}, u32[]{:S(2)}, u32[]{:S(2)}) %collective-permute-start.1) | collective-permute-done | bytes 98336 | tf_op jit(solution)/shard_map/while/body/eval_jaxpr/ppermute | solution.py:13
  246.7 3.5 fusion.102
  250.3 3.2 slice_add_fusion.7
  253.4 4.5 %fusion.103 = f32[8,1024]{1,0:T(8,128)S(1)} fusion(f32[8,1024]{1,0:T(8,128)S(1)} %get-tuple-element.283, f32[1024,1024]{1,0:T(8,128)S(1)} %fusion.102, f32[1024]{0:T(1024)S(1)} %multiply_reduce_fusion.14, f32[1024]{0:T(1024)S(1)} %get-tuple-element.291, f32[24,1024]{1,0:T(8,128)S(1)} %collective-permute-done.1), kind=kOutput, calls=%fused_computation.37.clone.1 | convolution fusion | flops 104865792 | bytes 4300800 | tf_op jit(solution)/shard_map/while/body/eval_jaxpr/dot_general | solution.py:50
  257.9 6.8 %collective-permute-done.1 = f32[24,1024]{1,0:T(8,128)S(1)} collective-permute-done((f32[24,1024]{1,0:T(8,128)S(1)}, f32[24,1024]{1,0:T(8,128)S(1)}, u32[]{:S(2)}, u32[]{:S(2)}) %collective-permute-start.1) | collective-permute-done | bytes 98336 | tf_op jit(solution)/shard_map/while/body/eval_jaxpr/ppermute | solution.py:13
  264.7 3.5 fusion.102
  271.5 4.5 %fusion.103 = f32[8,1024]{1,0:T(8,128)S(1)} fusion(f32[8,1024]{1,0:T(8,128)S(1)} %get-tuple-element.283, f32[1024,1024]{1,0:T(8,128)S(1)} %fusion.102, f32[1024]{0:T(1024)S(1)} %multiply_reduce_fusion.14, f32[1024]{0:T(1024)S(1)} %get-tuple-element.291, f32[24,1024]{1,0:T(8,128)S(1)} %collective-permute-done.1), kind=kOutput, calls=%fused_computation.37.clone.1 | convolution fusion | flops 104865792 | bytes 4300800 | tf_op jit(solution)/shard_map/while/body/eval_jaxpr/dot_general | solution.py:50
  276.0 6.8 %collective-permute-done.1 = f32[24,1024]{1,0:T(8,128)S(1)} collective-permute-done((f32[24,1024]{1,0:T(8,128)S(1)}, f32[24,1024]{1,0:T(8,128)S(1)}, u32[]{:S(2)}, u32[]{:S(2)}) %collective-permute-start.1) | collective-permute-done | bytes 98336 | tf_op jit(solution)/shard_map/while/body/eval_jaxpr/ppermute | solution.py:13
  282.7 3.5 fusion.102
  289.5 4.5 %fusion.103 = f32[8,1024]{1,0:T(8,128)S(1)} fusion(f32[8,1024]{1,0:T(8,128)S(1)} %get-tuple-element.283, f32[1024,1024]{1,0:T(8,128)S(1)} %fusion.102, f32[1024]{0:T(1024)S(1)} %multiply_reduce_fusion.14, f32[1024]{0:T(1024)S(1)} %get-tuple-element.291, f32[24,1024]{1,0:T(8,128)S(1)} %collective-permute-done.1), kind=kOutput, calls=%fused_computation.37.clone.1 | convolution fusion | flops 104865792 | bytes 4300800 | tf_op jit(solution)/shard_map/while/body/eval_jaxpr/dot_general | solution.py:50
  293.9 6.8 %collective-permute-done.1 = f32[24,1024]{1,0:T(8,128)S(1)} collective-permute-done((f32[24,1024]{1,0:T(8,128)S(1)}, f32[24,1024]{1,0:T(8,128)S(1)}, u32[]{:S(2)}, u32[]{:S(2)}) %collective-permute-start.1) | collective-permute-done | bytes 98336 | tf_op jit(solution)/shard_map/while/body/eval_jaxpr/ppermute | solution.py:13
  300.7 3.5 fusion.102
  307.5 4.5 %fusion.103 = f32[8,1024]{1,0:T(8,128)S(1)} fusion(f32[8,1024]{1,0:T(8,128)S(1)} %get-tuple-element.283, f32[1024,1024]{1,0:T(8,128)S(1)} %fusion.102, f32[1024]{0:T(1024)S(1)} %multiply_reduce_fusion.14, f32[1024]{0:T(1024)S(1)} %get-tuple-element.291, f32[24,1024]{1,0:T(8,128)S(1)} %collective-permute-done.1), kind=kOutput, calls=%fused_computation.37.clone.1 | convolution fusion | flops 104865792 | bytes 4300800 | tf_op jit(solution)/shard_map/while/body/eval_jaxpr/dot_general | solution.py:50
  312.0 6.8 %collective-permute-done.1 = f32[24,1024]{1,0:T(8,128)S(1)} collective-permute-done((f32[24,1024]{1,0:T(8,128)S(1)}, f32[24,1024]{1,0:T(8,128)S(1)}, u32[]{:S(2)}, u32[]{:S(2)}) %collective-permute-start.1) | collective-permute-done | bytes 98336 | tf_op jit(solution)/shard_map/while/body/eval_jaxpr/ppermute | solution.py:13
  318.7 3.5 fusion.102
  325.5 4.5 %fusion.103 = f32[8,1024]{1,0:T(8,128)S(1)} fusion(f32[8,1024]{1,0:T(8,128)S(1)} %get-tuple-element.283, f32[1024,1024]{1,0:T(8,128)S(1)} %fusion.102, f32[1024]{0:T(1024)S(1)} %multiply_reduce_fusion.14, f32[1024]{0:T(1024)S(1)} %get-tuple-element.291, f32[24,1024]{1,0:T(8,128)S(1)} %collective-permute-done.1), kind=kOutput, calls=%fused_computation.37.clone.1 | convolution fusion | flops 104865792 | bytes 4300800 | tf_op jit(solution)/shard_map/while/body/eval_jaxpr/dot_general | solution.py:50
  330.0 6.8 %collective-permute-done.1 = f32[24,1024]{1,0:T(8,128)S(1)} collective-permute-done((f32[24,1024]{1,0:T(8,128)S(1)}, f32[24,1024]{1,0:T(8,128)S(1)}, u32[]{:S(2)}, u32[]{:S(2)}) %collective-permute-start.1) | collective-permute-done | bytes 98336 | tf_op jit(solution)/shard_map/while/body/eval_jaxpr/ppermute | solution.py:13
  336.7 3.5 fusion.102
  340.3 3.2 slice_add_fusion.7
  343.5 4.5 %fusion.103 = f32[8,1024]{1,0:T(8,128)S(1)} fusion(f32[8,1024]{1,0:T(8,128)S(1)} %get-tuple-element.283, f32[1024,1024]{1,0:T(8,128)S(1)} %fusion.102, f32[1024]{0:T(1024)S(1)} %multiply_reduce_fusion.14, f32[1024]{0:T(1024)S(1)} %get-tuple-element.291, f32[24,1024]{1,0:T(8,128)S(1)} %collective-permute-done.1), kind=kOutput, calls=%fused_computation.37.clone.1 | convolution fusion | flops 104865792 | bytes 4300800 | tf_op jit(solution)/shard_map/while/body/eval_jaxpr/dot_general | solution.py:50
  348.2 6.7 %collective-permute-done.4 = f32[24,1024]{1,0:T(8,128)S(1)} collective-permute-done((f32[24,1024]{1,0:T(8,128)S(1)}, f32[24,1024]{1,0:T(8,128)S(1)}, u32[]{:S(2)}, u32[]{:S(2)}) %collective-permute-start.4) | collective-permute-done | bytes 98336 | tf_op jit(solution)/shard_map/ppermute | solution.py:13
  360.1 4.8 %collective-permute-done.5 = f32[8,1024]{1,0:T(8,128)S(1)} collective-permute-done((f32[8,1024]{1,0:T(8,128)S(1)}, f32[8,1024]{1,0:T(8,128)S(1)}, u32[]{:S(2)}, u32[]{:S(2)}) %collective-permute-start.5) | collective-permute-done | bytes 32800 | tf_op jit(solution)/shard_map/ppermute | solution.py:13
  365.0 29.5 %psum.31 = f32[8]{0:T(128)S(1)} all-reduce(f32[8]{0:T(128)S(1)} %get-tuple-element.168), channel_id=1, replica_groups=mesh['grp'=2,'row'=16] {'row'}, use_global_device_ids=true, to_apply=%region_18.19 | all-reduce | flops 8 | bytes 64 | tf_op jit(solution)/shard_map/psum | solution.py:116
  (93 shorter events, 28.5 us)
Async XLA Ops:
  0.6 4.5 %copy-start.1 = (f32[8,1024]{1,0:T(8,128)S(1)}, f32[8,1024]{1,0:T(8,128)}, u32[]{:S(2)}) copy-start(f32[8,1024]{1,0:T(8,128)} %param.11) | copy-start | bytes 98308
  5.0 1.9 copy-start
  12.0 7.8 %collective-permute-start = (f32[24,1024]{1,0:T(8,128)S(1)}, f32[24,1024]{1,0:T(8,128)S(1)}, u32[]{:S(2)}, u32[]{:S(2)}) collective-permute-start(f32[24,1024]{1,0:T(8,128)S(1)} %get-tuple-element.261), channel_id=1, source_target_pairs={{0,1},{1,2},{2,3},{3,4},{4,5},{5,6},{6,7},{7,8},{8,9},{9,10},{10,1... | collective-permute-start | bytes 294920 | tf_op jit(solution)/shard_map/while/body/eval_jaxpr/ppermute | solution.py:13
  31.0 6.8 %collective-permute-start = (f32[24,1024]{1,0:T(8,128)S(1)}, f32[24,1024]{1,0:T(8,128)S(1)}, u32[]{:S(2)}, u32[]{:S(2)}) collective-permute-start(f32[24,1024]{1,0:T(8,128)S(1)} %get-tuple-element.261), channel_id=1, source_target_pairs={{0,1},{1,2},{2,3},{3,4},{4,5},{5,6},{6,7},{7,8},{8,9},{9,10},{10,1... | collective-permute-start | bytes 294920 | tf_op jit(solution)/shard_map/while/body/eval_jaxpr/ppermute | solution.py:13
  49.0 6.8 %collective-permute-start = (f32[24,1024]{1,0:T(8,128)S(1)}, f32[24,1024]{1,0:T(8,128)S(1)}, u32[]{:S(2)}, u32[]{:S(2)}) collective-permute-start(f32[24,1024]{1,0:T(8,128)S(1)} %get-tuple-element.261), channel_id=1, source_target_pairs={{0,1},{1,2},{2,3},{3,4},{4,5},{5,6},{6,7},{7,8},{8,9},{9,10},{10,1... | collective-permute-start | bytes 294920 | tf_op jit(solution)/shard_map/while/body/eval_jaxpr/ppermute | solution.py:13
  67.0 6.8 %collective-permute-start = (f32[24,1024]{1,0:T(8,128)S(1)}, f32[24,1024]{1,0:T(8,128)S(1)}, u32[]{:S(2)}, u32[]{:S(2)}) collective-permute-start(f32[24,1024]{1,0:T(8,128)S(1)} %get-tuple-element.261), channel_id=1, source_target_pairs={{0,1},{1,2},{2,3},{3,4},{4,5},{5,6},{6,7},{7,8},{8,9},{9,10},{10,1... | collective-permute-start | bytes 294920 | tf_op jit(solution)/shard_map/while/body/eval_jaxpr/ppermute | solution.py:13
  85.0 6.8 %collective-permute-start = (f32[24,1024]{1,0:T(8,128)S(1)}, f32[24,1024]{1,0:T(8,128)S(1)}, u32[]{:S(2)}, u32[]{:S(2)}) collective-permute-start(f32[24,1024]{1,0:T(8,128)S(1)} %get-tuple-element.261), channel_id=1, source_target_pairs={{0,1},{1,2},{2,3},{3,4},{4,5},{5,6},{6,7},{7,8},{8,9},{9,10},{10,1... | collective-permute-start | bytes 294920 | tf_op jit(solution)/shard_map/while/body/eval_jaxpr/ppermute | solution.py:13
  103.1 6.8 %collective-permute-start = (f32[24,1024]{1,0:T(8,128)S(1)}, f32[24,1024]{1,0:T(8,128)S(1)}, u32[]{:S(2)}, u32[]{:S(2)}) collective-permute-start(f32[24,1024]{1,0:T(8,128)S(1)} %get-tuple-element.261), channel_id=1, source_target_pairs={{0,1},{1,2},{2,3},{3,4},{4,5},{5,6},{6,7},{7,8},{8,9},{9,10},{10,1... | collective-permute-start | bytes 294920 | tf_op jit(solution)/shard_map/while/body/eval_jaxpr/ppermute | solution.py:13
  121.1 6.8 %collective-permute-start = (f32[24,1024]{1,0:T(8,128)S(1)}, f32[24,1024]{1,0:T(8,128)S(1)}, u32[]{:S(2)}, u32[]{:S(2)}) collective-permute-start(f32[24,1024]{1,0:T(8,128)S(1)} %get-tuple-element.261), channel_id=1, source_target_pairs={{0,1},{1,2},{2,3},{3,4},{4,5},{5,6},{6,7},{7,8},{8,9},{9,10},{10,1... | collective-permute-start | bytes 294920 | tf_op jit(solution)/shard_map/while/body/eval_jaxpr/ppermute | solution.py:13
  139.1 16.9 %copy-start.2 = (f32[1024]{0:T(1024)S(1)}, f32[1024]{0:T(1024)}, u32[]{:S(2)}) copy-start(f32[1024]{0:T(1024)} %param.10) | copy-start | bytes 12292
  139.1 6.9 %collective-permute-start.2 = (f32[24,1024]{1,0:T(8,128)S(1)}, f32[24,1024]{1,0:T(8,128)S(1)}, u32[]{:S(2)}, u32[]{:S(2)}) collective-permute-start(f32[24,1024]{1,0:T(8,128)S(1)} %get-tuple-element.137), channel_id=1, source_target_pairs={{0,1},{1,2},{2,3},{3,4},{4,5},{5,6},{6,7},{7,8},{8,9},{9,10},{10,1... | collective-permute-start | bytes 294920 | tf_op jit(solution)/shard_map/ppermute | solution.py:13
  151.1 4.8 %collective-permute-start.3 = (f32[8,1024]{1,0:T(8,128)S(1)}, f32[8,1024]{1,0:T(8,128)S(1)}, u32[]{:S(2)}, u32[]{:S(2)}) collective-permute-start(f32[8,1024]{1,0:T(8,128)S(1)} %get-tuple-element.175), channel_id=1, source_target_pairs={{0,8},{1,9},{2,10},{3,11},{4,12},{5,13},{6,14},{7,15},{8,0},{9,1},... | collective-permute-start | bytes 98312 | tf_op jit(solution)/shard_map/ppermute | solution.py:13
  221.9 6.8 %collective-permute-start.1 = (f32[24,1024]{1,0:T(8,128)S(1)}, f32[24,1024]{1,0:T(8,128)S(1)}, u32[]{:S(2)}, u32[]{:S(2)}) collective-permute-start(f32[24,1024]{1,0:T(8,128)S(1)} %get-tuple-element.282), channel_id=1, source_target_pairs={{0,1},{1,2},{2,3},{3,4},{4,5},{5,6},{6,7},{7,8},{8,9},{9,10},{10,1... | collective-permute-start | bytes 294920 | tf_op jit(solution)/shard_map/while/body/eval_jaxpr/ppermute | solution.py:13
  239.9 6.8 %collective-permute-start.1 = (f32[24,1024]{1,0:T(8,128)S(1)}, f32[24,1024]{1,0:T(8,128)S(1)}, u32[]{:S(2)}, u32[]{:S(2)}) collective-permute-start(f32[24,1024]{1,0:T(8,128)S(1)} %get-tuple-element.282), channel_id=1, source_target_pairs={{0,1},{1,2},{2,3},{3,4},{4,5},{5,6},{6,7},{7,8},{8,9},{9,10},{10,1... | collective-permute-start | bytes 294920 | tf_op jit(solution)/shard_map/while/body/eval_jaxpr/ppermute | solution.py:13
  257.9 6.8 %collective-permute-start.1 = (f32[24,1024]{1,0:T(8,128)S(1)}, f32[24,1024]{1,0:T(8,128)S(1)}, u32[]{:S(2)}, u32[]{:S(2)}) collective-permute-start(f32[24,1024]{1,0:T(8,128)S(1)} %get-tuple-element.282), channel_id=1, source_target_pairs={{0,1},{1,2},{2,3},{3,4},{4,5},{5,6},{6,7},{7,8},{8,9},{9,10},{10,1... | collective-permute-start | bytes 294920 | tf_op jit(solution)/shard_map/while/body/eval_jaxpr/ppermute | solution.py:13
  275.9 6.8 %collective-permute-start.1 = (f32[24,1024]{1,0:T(8,128)S(1)}, f32[24,1024]{1,0:T(8,128)S(1)}, u32[]{:S(2)}, u32[]{:S(2)}) collective-permute-start(f32[24,1024]{1,0:T(8,128)S(1)} %get-tuple-element.282), channel_id=1, source_target_pairs={{0,1},{1,2},{2,3},{3,4},{4,5},{5,6},{6,7},{7,8},{8,9},{9,10},{10,1... | collective-permute-start | bytes 294920 | tf_op jit(solution)/shard_map/while/body/eval_jaxpr/ppermute | solution.py:13
  293.9 6.8 %collective-permute-start.1 = (f32[24,1024]{1,0:T(8,128)S(1)}, f32[24,1024]{1,0:T(8,128)S(1)}, u32[]{:S(2)}, u32[]{:S(2)}) collective-permute-start(f32[24,1024]{1,0:T(8,128)S(1)} %get-tuple-element.282), channel_id=1, source_target_pairs={{0,1},{1,2},{2,3},{3,4},{4,5},{5,6},{6,7},{7,8},{8,9},{9,10},{10,1... | collective-permute-start | bytes 294920 | tf_op jit(solution)/shard_map/while/body/eval_jaxpr/ppermute | solution.py:13
  312.0 6.8 %collective-permute-start.1 = (f32[24,1024]{1,0:T(8,128)S(1)}, f32[24,1024]{1,0:T(8,128)S(1)}, u32[]{:S(2)}, u32[]{:S(2)}) collective-permute-start(f32[24,1024]{1,0:T(8,128)S(1)} %get-tuple-element.282), channel_id=1, source_target_pairs={{0,1},{1,2},{2,3},{3,4},{4,5},{5,6},{6,7},{7,8},{8,9},{9,10},{10,1... | collective-permute-start | bytes 294920 | tf_op jit(solution)/shard_map/while/body/eval_jaxpr/ppermute | solution.py:13
  330.0 6.8 %collective-permute-start.1 = (f32[24,1024]{1,0:T(8,128)S(1)}, f32[24,1024]{1,0:T(8,128)S(1)}, u32[]{:S(2)}, u32[]{:S(2)}) collective-permute-start(f32[24,1024]{1,0:T(8,128)S(1)} %get-tuple-element.282), channel_id=1, source_target_pairs={{0,1},{1,2},{2,3},{3,4},{4,5},{5,6},{6,7},{7,8},{8,9},{9,10},{10,1... | collective-permute-start | bytes 294920 | tf_op jit(solution)/shard_map/while/body/eval_jaxpr/ppermute | solution.py:13
  348.0 7.0 %collective-permute-start.4 = (f32[24,1024]{1,0:T(8,128)S(1)}, f32[24,1024]{1,0:T(8,128)S(1)}, u32[]{:S(2)}, u32[]{:S(2)}) collective-permute-start(f32[24,1024]{1,0:T(8,128)S(1)} %get-tuple-element.139), channel_id=1, source_target_pairs={{0,1},{1,2},{2,3},{3,4},{4,5},{5,6},{6,7},{7,8},{8,9},{9,10},{10,1... | collective-permute-start | bytes 294920 | tf_op jit(solution)/shard_map/ppermute | solution.py:13
  360.1 4.8 %collective-permute-start.5 = (f32[8,1024]{1,0:T(8,128)S(1)}, f32[8,1024]{1,0:T(8,128)S(1)}, u32[]{:S(2)}, u32[]{:S(2)}) collective-permute-start(f32[8,1024]{1,0:T(8,128)S(1)} %get-tuple-element.177), channel_id=1, source_target_pairs={{0,8},{1,9},{2,10},{3,11},{4,12},{5,13},{6,14},{7,15},{8,0},{9,1},... | collective-permute-start | bytes 98312 | tf_op jit(solution)/shard_map/ppermute | solution.py:13
where the time goes:
time: 401 us; the launch traced here: 396 us
  matrix products  181 us (45%)
  waiting for transfers between devices  118 us (29%)
  blocking collectives  88.5 us (22%)
    ppermute x18, waiting for transfers between devices, shifted(): lax.ppermute(value, axis, [(i, (i + by) % length) for i in range(length)])  118 us
    dot_general x16, matrix products, pair_terms(): lax.dot_general(right_dirs, weight, (((1,), (1,)), ((), ())), precision=l...  66.5 us
    dot_general x16, matrix products, pair_terms(): lax.dot_general(left_pts, right_pts, (((0,), (0,)), ((), ())), precision=...  53.7 us
    dot_general x16, matrix products, pair_terms(): lax.dot_general(left_dirs, weight, (((1,), (0,)), ((), ())), precision=la...  46.6 us
    psum x1, blocking collectives, shards(): norm_now = lax.psum(jnp.sum(rhs * rhs, axis=1), 'row')  29.5 us
    psum x1, blocking collectives, shards(): norm_next = lax.psum(jnp.sum(residual * residual, axis=1), 'row')  29.5 us
    psum x1, blocking collectives, shards(): curv = lax.psum(local_curv, 'row')  29.5 us
    dot_general x2, matrix products, block_term(): lax.dot_general(dirs, weight, (((1,), (1,)), ((), ())), precision=lax.Pre...  10.7 us
  transfers between devices with their start and end apart: 18, of which 18 were waited for; matrix products, arithmetic and copies ran while one was open for 0% of the time, Pallas kernels for 0%

commit v1 on v0

v1 whole, which is shorter than its diff:
```python
import functools
import math

import jax
import jax.numpy as jnp
from jax import lax
from jax.experimental import pallas as pl
from jax.experimental.pallas import tpu as pltpu
from jax.sharding import PartitionSpec as P

ITERS = 2
LOG2E = math.log2(math.e)
DEPTH = 64
TILE = 256
F32 = jnp.float32
BF16 = jnp.bfloat16


def shifted(value, by):
    length = lax.axis_size("row")
    return lax.ppermute(value, "row", [(i, (i + by) % length) for i in range(length)])


def gathered(value):
    return [value] + [shifted(value, by) for by in range(1, lax.axis_size("row"))]


def pieces(value, count):
    parts = []
    for _ in range(count):
        part = value.astype(BF16).astype(F32)
        parts.append(part)
        value = value - part
    return parts


def exponent_rows(points, factor, visiting):
    big, mid, low = pieces(points * factor, 3)
    half_sq = jnp.sum(points * points, axis=0, keepdims=True) * (-0.5 * LOG2E)
    sq_parts = pieces(half_sq, 3)
    row = lax.broadcasted_iota(jnp.int32, points.shape, 0)
    first = 0 if visiting else 3
    tail = jnp.where((row >= 3 - first) & (row < 6 - first), 1.0, 0.0)
    for k, part in enumerate(sq_parts):
        tail = jnp.where(row == first + k, part, tail)
    order = [big, big, big, mid, mid, low] if visiting else [big, mid, low, big, mid, big]
    return jnp.concatenate(order + [tail, jnp.zeros_like(tail)], axis=0)


def operator_loop(yt_ref, own_ref, dirs_ref, acc_ref):
    width = own_ref.shape[1]
    acc_ref[...] = jnp.zeros_like(acc_ref)

    def step(t, carry):
        rows = pl.ds(pl.multiple_of(t * TILE, TILE), TILE)
        lhs = yt_ref[rows, :]
        dirs = dirs_ref[t]
        for c in range(width // TILE):
            cols = slice(c * TILE, (c + 1) * TILE)
            expo = jnp.dot(lhs, own_ref[:, cols], preferred_element_type=F32)
            weight = jnp.exp2(expo)
            high = weight.astype(BF16)
            low = (weight - high.astype(F32)).astype(BF16)
            acc_ref[:, cols] += jnp.dot(
                dirs, high, preferred_element_type=F32
            ) + jnp.dot(dirs, low, preferred_element_type=F32)
        return carry

    lax.fori_loop(0, dirs_ref.shape[0], step, 0)


def put_dirs(dirs_ref, block, value):
    both = jnp.concatenate(pieces(value, 2), axis=0).astype(BF16)
    per = value.shape[1] // TILE
    for k in range(per):
        dirs_ref[block * per + k] = both[:, k * TILE : (k + 1) * TILE]


def prepare_points(scale_ref, blocks, nfeat, yt_ref, own_ref):
    width = blocks[0].shape[1]
    for b, ref in enumerate(blocks):
        points = ref[0:nfeat, :] / scale_ref[...]
        rows = exponent_rows(points, LOG2E, True)
        yt_ref[b * width : (b + 1) * width, :] = rows.T.astype(BF16)
        if b == 0:
            own_ref[...] = exponent_rows(points, 1.0, False).astype(BF16)


def first_kernel(nfeat, amplitude, scale_ref, noise_ref, *refs):
    *blocks, image_ref, yt_ref, own_ref, dirs_ref, acc_ref = refs
    prepare_points(scale_ref, blocks, nfeat, yt_ref, own_ref)
    for b, ref in enumerate(blocks):
        put_dirs(dirs_ref, b, ref[nfeat:, :])
    operator_loop(yt_ref, own_ref, dirs_ref, acc_ref)
    nrhs = image_ref.shape[0]
    total = acc_ref[0:nrhs, :] + acc_ref[nrhs:, :]
    image_ref[...] = amplitude * total + noise_ref[...] * blocks[0][nfeat:, :]


def second_kernel(nfeat, amplitude, count, scale_ref, noise_ref, *refs):
    blocks = refs[:count]
    images = refs[count : 2 * count]
    outs = refs[2 * count :]
    sol_ref, res_ref, dir_ref, image_ref, norm_ref, curv_ref = outs[:6]
    yt_ref, own_ref, dirs_ref, acc_ref = outs[6:]
    prepare_points(scale_ref, blocks, nfeat, yt_ref, own_ref)
    norm = sum(jnp.sum(b[nfeat:, :] * b[nfeat:, :], axis=1, keepdims=True) for b in blocks)
    curv = sum(
        jnp.sum(b[nfeat:, :] * m[...], axis=1, keepdims=True) for b, m in zip(blocks, images)
    )
    alpha = norm / curv
    norm_next = 0.0
    for b, m in zip(blocks, images):
        left = b[nfeat:, :] - alpha * m[...]
        norm_next += jnp.sum(left * left, axis=1, keepdims=True)
    beta = norm_next / norm
    for k, (b, m) in enumerate(zip(blocks, images)):
        direc = (b[nfeat:, :] - alpha * m[...]) + beta * b[nfeat:, :]
        put_dirs(dirs_ref, k, direc)
    rhs = blocks[0][nfeat:, :]
    residual = rhs - alpha * images[0][...]
    direc = residual + beta * rhs
    sol_ref[...] = alpha * rhs
    res_ref[...] = residual
    dir_ref[...] = direc
    operator_loop(yt_ref, own_ref, dirs_ref, acc_ref)
    nrhs = image_ref.shape[0]
    total = acc_ref[0:nrhs, :] + acc_ref[nrhs:, :]
    image = amplitude * total + noise_ref[...] * direc
    image_ref[...] = image
    norm_ref[...] = jnp.broadcast_to(norm_next, norm_ref.shape)
    curv_ref[...] = jnp.broadcast_to(
        jnp.sum(direc * image, axis=1, keepdims=True), curv_ref.shape
    )


def last_kernel(sol_ref, res_ref, dir_ref, image_ref, norm_ref, *refs):
    *curvs, out_sol, out_res = refs
    alpha = norm_ref[:, 0:1] / sum(c[:, 0:1] for c in curvs)
    out_sol[...] = sol_ref[...] + alpha * dir_ref[...]
    out_res[...] = res_ref[...] - alpha * image_ref[...]


def shards(features, lengthscale, noise, rhs):
    nfeat, width = features.shape
    nrhs = rhs.shape[0]
    count = lax.axis_size("row")
    amplitude = 1.0 / math.sqrt(width * count)
    scale = lengthscale[:, None]
    noise = noise[None, :]
    blocks = gathered(jnp.concatenate([features, rhs], axis=0))
    field = jax.ShapeDtypeStruct((nrhs, width), F32)
    small = jax.ShapeDtypeStruct((nrhs, 128), F32)
    scratch = [
        pltpu.VMEM((count * width, DEPTH), BF16),
        pltpu.VMEM((DEPTH, width), BF16),
        pltpu.VMEM((count * width // TILE, 2 * nrhs, TILE), BF16),
        pltpu.VMEM((2 * nrhs, width), F32),
    ]
    entries = count * width * width
    params = pltpu.CompilerParams(
        vmem_limit_bytes=min(16 * 1024 * 1024 + 512 * count * width, 60 * 1024 * 1024)
    )
    cost = pl.CostEstimate(
        flops=2 * entries * (DEPTH + 4 * nrhs),
        bytes_accessed=4 * count * (nfeat + nrhs) * width,
        transcendentals=entries,
    )
    image = pl.pallas_call(
        functools.partial(first_kernel, nfeat, amplitude),
        out_shape=field,
        scratch_shapes=scratch,
        compiler_params=params,
        cost_estimate=cost,
        name="first_operator",
    )(scale, noise, *blocks)
    images = gathered(image)
    sol, res, direc, image, norm, curv = pl.pallas_call(
        functools.partial(second_kernel, nfeat, amplitude, count),
        out_shape=(field, field, field, field, small, small),
        scratch_shapes=scratch,
        compiler_params=params,
        cost_estimate=cost,
        name="second_operator",
    )(scale, noise, *blocks, *images)
    curvs = gathered(curv)
    return pl.pallas_call(
        last_kernel, out_shape=(field, field), name="last_update"
    )(sol, res, direc, image, norm, *curvs)


def solution(mesh):
    in_specs = (P(None, ("grp", "row")), P(), P(("grp", "row")), P(None, ("grp", "row")))
    out_specs = (P(None, ("grp", "row")), P(None, ("grp", "row")))
    return jax.shard_map(shards, mesh=mesh, in_specs=in_specs, out_specs=out_specs, check_vma=False)
```

time: 401 us -> 164 us (0.41); the launches traced: 396 us -> 164 us
  matrix products: 181 us -> 0 us
  waiting for transfers between devices: 118 us -> 24 us
  blocking collectives: 88.5 us -> 0 us
  Pallas kernels: 0 us -> 77 us
  starting transfers between devices: 1.02 us -> 58.3 us
    dot_general x51 -> x0, matrix products: 181 us -> none  [the longest x16 66.5 us: pair_terms(): lax.dot_general(right_dirs, weight, (((1,), (1,)), ((), ())), precision=l...]
    ppermute x18 -> x45, waiting for transfers between devices: 118 us -> 24 us  [shifted(): lax.ppermute(value, 'row', [(i, (i + by) % length) for i in range(length)])]
    psum x3 -> x0, blocking collectives: 88.5 us -> none  [the longest x1 29.5 us: shards(): norm_now = lax.psum(jnp.sum(rhs * rhs, axis=1), 'row')]
    pallas_call x0 -> x3, Pallas kernels: none -> 77 us  [the longest x1 38.3 us: shards(): pl.pallas_call(functools.partial(second_kernel, nfeat, amplitude, count),...]
    ppermute x18 -> x45, starting transfers between devices: 1.02 us -> 58.3 us  [shifted(): lax.ppermute(value, 'row', [(i, (i + by) % length) for i in range(length)])]
  transfers between devices with their start and end apart: 18 -> 45, of which waited for: 18 -> 13; matrix products, arithmetic and copies ran while one was open for 0% -> 0% of each run, Pallas kernels for 0% -> 0%
where the time goes in v1:
time: 164 us
  Pallas kernels  77 us (47%)
  starting transfers between devices  58.3 us (36%)
  waiting for transfers between devices  24 us (15%)
  local copies, waits for them, and re-layouts  3.79 us (2%)
    ppermute x45, starting transfers between devices, shifted(): lax.ppermute(value, 'row', [(i, (i + by) % length) for i in range(length)])  58.3 us
    pallas_call x1, Pallas kernels, shards(): pl.pallas_call(functools.partial(second_kernel, nfeat, amplitude, count),...  38.3 us
    pallas_call x1, Pallas kernels, shards(): pl.pallas_call(functools.partial(first_kernel, nfeat, amplitude), out_sha...  37.1 us
    ppermute x45, waiting for transfers between devices, shifted(): lax.ppermute(value, 'row', [(i, (i + by) % length) for i in range(length)])  24 us
    unnamed x49, local copies, waits for them, and re-layouts  3.71 us
  transfers between devices with their start and end apart: 45, of which 13 were waited for; matrix products, arithmetic and copies ran while one was open for 0% of the time, Pallas kernels for 0%

profile of v1, /device:TPU:0, one launch (start us, length us, event | category | flops | bytes accessed | tf_op | source)
XLA Modules:
  0.0 163.9 jit_solution(9363736797115872584)
XLA Ops:
  0.6 0.8 constant_dynamic-update-slice_fusion.1
  1.4 0.0 copy-start.6
  1.4 5.5 %collective-permute-start.14 = (f32[16,1024]{1,0:T(8,128)S(1)}, f32[16,1024]{1,0:T(8,128)S(1)}, u32[]{:S(2)}, u32[]{:S(2)}) collective-permute-start(f32[16,1024]{1,0:T(8,128)S(1)} %constant_dynamic-update-slice_fusion.refs_0_), channel_id=1, source_target_pairs={{0,15},{1,0},{2,1},{3,2},{4,3},{5,4},{6,5},{7,6},{8,7},{9,8},{10,9... | collective-permute-start | bytes 196616 | tf_op jit(solution)/shard_map/ppermute | solution.py:21
  6.9 0.6 collective-permute-start.13
  7.6 0.2 collective-permute-start.12
  7.8 0.4 collective-permute-start.11
  8.2 0.1 collective-permute-start.10
  8.3 1.0 collective-permute-done.14.refs_15_
  9.3 3.4 %collective-permute-start.9 = (f32[16,1024]{1,0:T(8,128)S(1)}, f32[16,1024]{1,0:T(8,128)S(1)}, u32[]{:S(2)}, u32[]{:S(2)}) collective-permute-start(f32[16,1024]{1,0:T(8,128)S(1)} %constant_dynamic-update-slice_fusion.refs_0_), channel_id=1, source_target_pairs={{0,10},{1,11},{2,12},{3,13},{4,14},{5,15},{6,0},{7,1},{8,2},{9,3},... | collective-permute-start | bytes 196616 | tf_op jit(solution)/shard_map/ppermute | solution.py:21
  12.7 0.0 collective-permute-done.13.refs_14_
  12.7 1.6 collective-permute-start.7
  14.3 0.0 collective-permute-done.11.refs_12_
  14.3 1.1 collective-permute-start.6
  15.4 0.0 collective-permute-done.10.refs_11_
  15.4 4.4 %collective-permute-start.5 = (f32[16,1024]{1,0:T(8,128)S(1)}, f32[16,1024]{1,0:T(8,128)S(1)}, u32[]{:S(2)}, u32[]{:S(2)}) collective-permute-start(f32[16,1024]{1,0:T(8,128)S(1)} %constant_dynamic-update-slice_fusion.refs_0_), channel_id=1, source_target_pairs={{0,6},{1,7},{2,8},{3,9},{4,10},{5,11},{6,12},{7,13},{8,14},{9,15},... | collective-permute-start | bytes 196616 | tf_op jit(solution)/shard_map/ppermute | solution.py:21
  19.8 2.1 %collective-permute-start.4 = (f32[16,1024]{1,0:T(8,128)S(1)}, f32[16,1024]{1,0:T(8,128)S(1)}, u32[]{:S(2)}, u32[]{:S(2)}) collective-permute-start(f32[16,1024]{1,0:T(8,128)S(1)} %constant_dynamic-update-slice_fusion.refs_0_), channel_id=1, source_target_pairs={{0,5},{1,6},{2,7},{3,8},{4,9},{5,10},{6,11},{7,12},{8,13},{9,14},{... | collective-permute-start | bytes 196616 | tf_op jit(solution)/shard_map/ppermute | solution.py:21
  21.9 4.2 %collective-permute-start.3 = (f32[16,1024]{1,0:T(8,128)S(1)}, f32[16,1024]{1,0:T(8,128)S(1)}, u32[]{:S(2)}, u32[]{:S(2)}) collective-permute-start(f32[16,1024]{1,0:T(8,128)S(1)} %constant_dynamic-update-slice_fusion.refs_0_), channel_id=1, source_target_pairs={{0,4},{1,5},{2,6},{3,7},{4,8},{5,9},{6,10},{7,11},{8,12},{9,13},{1... | collective-permute-start | bytes 196616 | tf_op jit(solution)/shard_map/ppermute | solution.py:21
  26.1 2.2 %collective-permute-done.7.refs_8_ = f32[16,1024]{1,0:T(8,128)S(1)} collective-permute-done((f32[16,1024]{1,0:T(8,128)S(1)}, f32[16,1024]{1,0:T(8,128)S(1)}, u32[]{:S(2)}, u32[]{:S(2)}) %collective-permute-start.7) | collective-permute-done | bytes 65568 | tf_op jit(solution)/shard_map/ppermute | solution.py:21
  28.3 1.6 collective-permute-done.6.refs_7_
  29.9 0.1 copy.7.scale_ref
  30.0 3.8 %collective-permute-done.2.refs_3_ = f32[16,1024]{1,0:T(8,128)S(1)} collective-permute-done((f32[16,1024]{1,0:T(8,128)S(1)}, f32[16,1024]{1,0:T(8,128)S(1)}, u32[]{:S(2)}, u32[]{:S(2)}) %collective-permute-start.2) | collective-permute-done | bytes 65568 | tf_op jit(solution)/shard_map/ppermute | solution.py:21
  33.8 3.5 %collective-permute-done.1.refs_2_ = f32[16,1024]{1,0:T(8,128)S(1)} collective-permute-done((f32[16,1024]{1,0:T(8,128)S(1)}, f32[16,1024]{1,0:T(8,128)S(1)}, u32[]{:S(2)}, u32[]{:S(2)}) %collective-permute-start.1) | collective-permute-done | bytes 65568 | tf_op jit(solution)/shard_map/ppermute | solution.py:21
  37.3 37.1 %first_operator.1.refs_16_ = f32[8,1024]{1,0:T(8,128)S(1)} custom-call(f32[8,1]{1,0:T(8,128)S(1)} %copy.7.scale_ref, f32[1,1024]{1,0:T(1,128)S(1)} %bitcast.2, f32[16,1024]{1,0:T(8,128)S(1)} %constant_dynamic-update-slice_fusion.refs_0_, f32[16,1024]{1,0:T(8,128)S(1)} %collective-permute-done.refs_1_, f32[16,1024]{1,0:T(8,128)S(1)} %collective-permute-done.1.refs_2_, ...), custom_call_target="tpu_custom_call" | custom-call | flops 3221225472 | bytes 1048576 | tf_op jit(solution)/shard_map/first_operator/pallas_call | solution.py:169
  74.4 0.1 collective-permute-start.29
  74.5 1.2 collective-permute-start.28
  75.7 0.2 collective-permute-start.27
  75.9 0.1 collective-permute-start.26
  76.0 2.9 %collective-permute-start.25 = (f32[8,1024]{1,0:T(8,128)S(1)}, f32[8,1024]{1,0:T(8,128)S(1)}, u32[]{:S(2)}, u32[]{:S(2)}) collective-permute-start(f32[8,1024]{1,0:T(8,128)S(1)} %first_operator.1.refs_16_), channel_id=1, source_target_pairs={{0,11},{1,12},{2,13},{3,14},{4,15},{5,0},{6,1},{7,2},{8,3},{9,4},{... | collective-permute-start | bytes 98312 | tf_op jit(solution)/shard_map/ppermute | solution.py:21
  78.9 2.2 %collective-permute-start.24 = (f32[8,1024]{1,0:T(8,128)S(1)}, f32[8,1024]{1,0:T(8,128)S(1)}, u32[]{:S(2)}, u32[]{:S(2)}) collective-permute-start(f32[8,1024]{1,0:T(8,128)S(1)} %first_operator.1.refs_16_), channel_id=1, source_target_pairs={{0,10},{1,11},{2,12},{3,13},{4,14},{5,15},{6,0},{7,1},{8,2},{9,3},... | collective-permute-start | bytes 98312 | tf_op jit(solution)/shard_map/ppermute | solution.py:21
  81.2 1.8 %collective-permute-start.22 = (f32[8,1024]{1,0:T(8,128)S(1)}, f32[8,1024]{1,0:T(8,128)S(1)}, u32[]{:S(2)}, u32[]{:S(2)}) collective-permute-start(f32[8,1024]{1,0:T(8,128)S(1)} %first_operator.1.refs_16_), channel_id=1, source_target_pairs={{0,8},{1,9},{2,10},{3,11},{4,12},{5,13},{6,14},{7,15},{8,0},{9,1},... | collective-permute-start | bytes 98312 | tf_op jit(solution)/shard_map/ppermute | solution.py:21
  83.0 0.9 collective-permute-start.21
  83.9 2.2 %collective-permute-start.20 = (f32[8,1024]{1,0:T(8,128)S(1)}, f32[8,1024]{1,0:T(8,128)S(1)}, u32[]{:S(2)}, u32[]{:S(2)}) collective-permute-start(f32[8,1024]{1,0:T(8,128)S(1)} %first_operator.1.refs_16_), channel_id=1, source_target_pairs={{0,6},{1,7},{2,8},{3,9},{4,10},{5,11},{6,12},{7,13},{8,14},{9,15},... | collective-permute-start | bytes 98312 | tf_op jit(solution)/shard_map/ppermute | solution.py:21
  86.1 0.5 collective-permute-start.19
  86.6 2.1 %collective-permute-start.18 = (f32[8,1024]{1,0:T(8,128)S(1)}, f32[8,1024]{1,0:T(8,128)S(1)}, u32[]{:S(2)}, u32[]{:S(2)}) collective-permute-start(f32[8,1024]{1,0:T(8,128)S(1)} %first_operator.1.refs_16_), channel_id=1, source_target_pairs={{0,4},{1,5},{2,6},{3,7},{4,8},{5,9},{6,10},{7,11},{8,12},{9,13},{1... | collective-permute-start | bytes 98312 | tf_op jit(solution)/shard_map/ppermute | solution.py:21
  88.7 2.1 %collective-permute-start.17 = (f32[8,1024]{1,0:T(8,128)S(1)}, f32[8,1024]{1,0:T(8,128)S(1)}, u32[]{:S(2)}, u32[]{:S(2)}) collective-permute-start(f32[8,1024]{1,0:T(8,128)S(1)} %first_operator.1.refs_16_), channel_id=1, source_target_pairs={{0,3},{1,4},{2,5},{3,6},{4,7},{5,8},{6,9},{7,10},{8,11},{9,12},{10... | collective-permute-start | bytes 98312 | tf_op jit(solution)/shard_map/ppermute | solution.py:21
  90.8 0.7 collective-permute-start.16
  91.5 0.5 collective-permute-done.19.refs_21_
  92.0 0.5 collective-permute-done.18.refs_20_
  92.5 1.7 %collective-permute-done.17.refs_19_ = f32[8,1024]{1,0:T(8,128)S(1)} collective-permute-done((f32[8,1024]{1,0:T(8,128)S(1)}, f32[8,1024]{1,0:T(8,128)S(1)}, u32[]{:S(2)}, u32[]{:S(2)}) %collective-permute-start.17) | collective-permute-done | bytes 32800 | tf_op jit(solution)/shard_map/ppermute | solution.py:21
  94.2 3.5 %collective-permute-done.16.refs_18_ = f32[8,1024]{1,0:T(8,128)S(1)} collective-permute-done((f32[8,1024]{1,0:T(8,128)S(1)}, f32[8,1024]{1,0:T(8,128)S(1)}, u32[]{:S(2)}, u32[]{:S(2)}) %collective-permute-start.16) | collective-permute-done | bytes 32800 | tf_op jit(solution)/shard_map/ppermute | solution.py:21
  97.6 0.1 collective-permute-done.15.refs_17_
  97.8 38.3 %second_operator.1 = (f32[8,1024]{1,0:T(8,128)S(1)}, f32[8,1024]{1,0:T(8,128)S(1)}, f32[8,1024]{1,0:T(8,128)S(1)}, f32[8,1024]{1,0:T(8,128)S(1)}, f32[8,128]{1,0:T(8,128)S(1)}, /*index=5*/f32[8,128]{1,0:T(8,128)S(1)}) custom-call(f32[8,1]{1,0:T(8,128)S(1)} %copy.7.scale_ref, f32[1,1024]{1,0:T(1,128)S(1)} %bitcast.3, ...), custom_call_target="tpu_custom_call" | custom-call | flops 3221225472 | bytes 1048576 | tf_op jit(solution)/shard_map/second_operator/pallas_call | solution.py:178
  136.0 0.6 copy-done
  136.6 0.6 copy-done.1
  137.2 0.6 copy-done.2
  137.8 0.6 copy-done.3
  138.5 1.1 collective-permute-start.43
  139.6 0.4 collective-permute-start.42
  139.9 0.8 collective-permute-start.41
  140.8 0.9 collective-permute-start.40
  141.7 2.6 %collective-permute-start.39 = (f32[8,128]{1,0:T(8,128)S(1)}, f32[8,128]{1,0:T(8,128)S(1)}, u32[]{:S(2)}, u32[]{:S(2)}) collective-permute-start(f32[8,128]{1,0:T(8,128)S(1)} %get-tuple-element.13.refs_0_), channel_id=1, source_target_pairs={{0,10},{1,11},{2,12},{3,13},{4,14},{5,15},{6,0},{7,1},{8,2},{9,3},... | collective-permute-start | bytes 12296 | tf_op jit(solution)/shard_map/ppermute | solution.py:21
  144.3 0.5 collective-permute-start.38
  144.8 1.3 collective-permute-start.37
  146.1 2.1 %collective-permute-start.36 = (f32[8,128]{1,0:T(8,128)S(1)}, f32[8,128]{1,0:T(8,128)S(1)}, u32[]{:S(2)}, u32[]{:S(2)}) collective-permute-start(f32[8,128]{1,0:T(8,128)S(1)} %get-tuple-element.13.refs_0_), channel_id=1, source_target_pairs={{0,7},{1,8},{2,9},{3,10},{4,11},{5,12},{6,13},{7,14},{8,15},{9,0},... | collective-permute-start | bytes 12296 | tf_op jit(solution)/shard_map/ppermute | solution.py:21
  148.2 1.9 %collective-permute-start.35 = (f32[8,128]{1,0:T(8,128)S(1)}, f32[8,128]{1,0:T(8,128)S(1)}, u32[]{:S(2)}, u32[]{:S(2)}) collective-permute-start(f32[8,128]{1,0:T(8,128)S(1)} %get-tuple-element.13.refs_0_), channel_id=1, source_target_pairs={{0,6},{1,7},{2,8},{3,9},{4,10},{5,11},{6,12},{7,13},{8,14},{9,15},... | collective-permute-start | bytes 12296 | tf_op jit(solution)/shard_map/ppermute | solution.py:21
  150.2 0.4 collective-permute-start.34
  150.6 2.0 %collective-permute-start.33 = (f32[8,128]{1,0:T(8,128)S(1)}, f32[8,128]{1,0:T(8,128)S(1)}, u32[]{:S(2)}, u32[]{:S(2)}) collective-permute-start(f32[8,128]{1,0:T(8,128)S(1)} %get-tuple-element.13.refs_0_), channel_id=1, source_target_pairs={{0,4},{1,5},{2,6},{3,7},{4,8},{5,9},{6,10},{7,11},{8,12},{9,13},{1... | collective-permute-start | bytes 12296 | tf_op jit(solution)/shard_map/ppermute | solution.py:21
  152.6 2.1 %collective-permute-start.32 = (f32[8,128]{1,0:T(8,128)S(1)}, f32[8,128]{1,0:T(8,128)S(1)}, u32[]{:S(2)}, u32[]{:S(2)}) collective-permute-start(f32[8,128]{1,0:T(8,128)S(1)} %get-tuple-element.13.refs_0_), channel_id=1, source_target_pairs={{0,3},{1,4},{2,5},{3,6},{4,7},{5,8},{6,9},{7,10},{8,11},{9,12},{10... | collective-permute-start | bytes 12296 | tf_op jit(solution)/shard_map/ppermute | solution.py:21
  154.7 1.3 collective-permute-start.31
  156.1 1.4 collective-permute-done.32.refs_3_
  157.5 3.5 %collective-permute-done.31.refs_2_ = f32[8,128]{1,0:T(8,128)S(1)} collective-permute-done((f32[8,128]{1,0:T(8,128)S(1)}, f32[8,128]{1,0:T(8,128)S(1)}, u32[]{:S(2)}, u32[]{:S(2)}) %collective-permute-start.31) | collective-permute-done | bytes 4128 | tf_op jit(solution)/shard_map/ppermute | solution.py:21
  161.0 0.7 collective-permute-done.30.refs_1_
  161.9 0.4 copy-done.22
  162.3 1.6 last_update.1
  (80 shorter events, 0.2 us)
Async XLA Ops:
  0.6 0.8 copy-start.7
  1.4 28.5 %copy-start.23 = (f32[8]{0:T(128)S(1)}, f32[8]{0:T(128)}, u32[]{:S(2)}) copy-start(f32[8]{0:T(128)} %param.5) | copy-start | bytes 100
  1.4 35.9 %copy-start.6 = (f32[1024]{0:T(1024)S(1)}, f32[1024]{0:T(1024)}, u32[]{:S(2)}) copy-start(f32[1024]{0:T(1024)} %param.6) | copy-start | bytes 12292
  1.4 7.9 %collective-permute-start.14 = (f32[16,1024]{1,0:T(8,128)S(1)}, f32[16,1024]{1,0:T(8,128)S(1)}, u32[]{:S(2)}, u32[]{:S(2)}) collective-permute-start(f32[16,1024]{1,0:T(8,128)S(1)} %constant_dynamic-update-slice_fusion.refs_0_), channel_id=1, source_target_pairs={{0,15},{1,0},{2,1},{3,2},{4,3},{5,4},{6,5},{7,6},{8,7},{9,8},{10,9... | collective-permute-start | bytes 196616 | tf_op jit(solution)/shard_map/ppermute | solution.py:21
  6.9 5.7 %collective-permute-start.13 = (f32[16,1024]{1,0:T(8,128)S(1)}, f32[16,1024]{1,0:T(8,128)S(1)}, u32[]{:S(2)}, u32[]{:S(2)}) collective-permute-start(f32[16,1024]{1,0:T(8,128)S(1)} %constant_dynamic-update-slice_fusion.refs_0_), channel_id=1, source_target_pairs={{0,14},{1,15},{2,0},{3,1},{4,2},{5,3},{6,4},{7,5},{8,6},{9,7},{10,... | collective-permute-start | bytes 196616 | tf_op jit(solution)/shard_map/ppermute | solution.py:21
  7.6 5.1 %collective-permute-start.12 = (f32[16,1024]{1,0:T(8,128)S(1)}, f32[16,1024]{1,0:T(8,128)S(1)}, u32[]{:S(2)}, u32[]{:S(2)}) collective-permute-start(f32[16,1024]{1,0:T(8,128)S(1)} %constant_dynamic-update-slice_fusion.refs_0_), channel_id=1, source_target_pairs={{0,13},{1,14},{2,15},{3,0},{4,1},{5,2},{6,3},{7,4},{8,5},{9,6},{10... | collective-permute-start | bytes 196616 | tf_op jit(solution)/shard_map/ppermute | solution.py:21
  7.8 6.5 %collective-permute-start.11 = (f32[16,1024]{1,0:T(8,128)S(1)}, f32[16,1024]{1,0:T(8,128)S(1)}, u32[]{:S(2)}, u32[]{:S(2)}) collective-permute-start(f32[16,1024]{1,0:T(8,128)S(1)} %constant_dynamic-update-slice_fusion.refs_0_), channel_id=1, source_target_pairs={{0,12},{1,13},{2,14},{3,15},{4,0},{5,1},{6,2},{7,3},{8,4},{9,5},{1... | collective-permute-start | bytes 196616 | tf_op jit(solution)/shard_map/ppermute | solution.py:21
  8.2 7.2 %collective-permute-start.10 = (f32[16,1024]{1,0:T(8,128)S(1)}, f32[16,1024]{1,0:T(8,128)S(1)}, u32[]{:S(2)}, u32[]{:S(2)}) collective-permute-start(f32[16,1024]{1,0:T(8,128)S(1)} %constant_dynamic-update-slice_fusion.refs_0_), channel_id=1, source_target_pairs={{0,11},{1,12},{2,13},{3,14},{4,15},{5,0},{6,1},{7,2},{8,3},{9,4},{... | collective-permute-start | bytes 196616 | tf_op jit(solution)/shard_map/ppermute | solution.py:21
  9.3 10.5 %collective-permute-start.9 = (f32[16,1024]{1,0:T(8,128)S(1)}, f32[16,1024]{1,0:T(8,128)S(1)}, u32[]{:S(2)}, u32[]{:S(2)}) collective-permute-start(f32[16,1024]{1,0:T(8,128)S(1)} %constant_dynamic-update-slice_fusion.refs_0_), channel_id=1, source_target_pairs={{0,10},{1,11},{2,12},{3,13},{4,14},{5,15},{6,0},{7,1},{8,2},{9,3},... | collective-permute-start | bytes 196616 | tf_op jit(solution)/shard_map/ppermute | solution.py:21
  12.7 9.3 %collective-permute-start.8 = (f32[16,1024]{1,0:T(8,128)S(1)}, f32[16,1024]{1,0:T(8,128)S(1)}, u32[]{:S(2)}, u32[]{:S(2)}) collective-permute-start(f32[16,1024]{1,0:T(8,128)S(1)} %constant_dynamic-update-slice_fusion.refs_0_), channel_id=1, source_target_pairs={{0,9},{1,10},{2,11},{3,12},{4,13},{5,14},{6,15},{7,0},{8,1},{9,2},... | collective-permute-start | bytes 196616 | tf_op jit(solution)/shard_map/ppermute | solution.py:21
  12.7 15.6 %collective-permute-start.7 = (f32[16,1024]{1,0:T(8,128)S(1)}, f32[16,1024]{1,0:T(8,128)S(1)}, u32[]{:S(2)}, u32[]{:S(2)}) collective-permute-start(f32[16,1024]{1,0:T(8,128)S(1)} %constant_dynamic-update-slice_fusion.refs_0_), channel_id=1, source_target_pairs={{0,8},{1,9},{2,10},{3,11},{4,12},{5,13},{6,14},{7,15},{8,0},{9,1},... | collective-permute-start | bytes 196616 | tf_op jit(solution)/shard_map/ppermute | solution.py:21
  14.3 15.6 %collective-permute-start.6 = (f32[16,1024]{1,0:T(8,128)S(1)}, f32[16,1024]{1,0:T(8,128)S(1)}, u32[]{:S(2)}, u32[]{:S(2)}) collective-permute-start(f32[16,1024]{1,0:T(8,128)S(1)} %constant_dynamic-update-slice_fusion.refs_0_), channel_id=1, source_target_pairs={{0,7},{1,8},{2,9},{3,10},{4,11},{5,12},{6,13},{7,14},{8,15},{9,0},... | collective-permute-start | bytes 196616 | tf_op jit(solution)/shard_map/ppermute | solution.py:21
  15.4 14.5 %collective-permute-start.5 = (f32[16,1024]{1,0:T(8,128)S(1)}, f32[16,1024]{1,0:T(8,128)S(1)}, u32[]{:S(2)}, u32[]{:S(2)}) collective-permute-start(f32[16,1024]{1,0:T(8,128)S(1)} %constant_dynamic-update-slice_fusion.refs_0_), channel_id=1, source_target_pairs={{0,6},{1,7},{2,8},{3,9},{4,10},{5,11},{6,12},{7,13},{8,14},{9,15},... | collective-permute-start | bytes 196616 | tf_op jit(solution)/shard_map/ppermute | solution.py:21
  19.8 10.2 %collective-permute-start.4 = (f32[16,1024]{1,0:T(8,128)S(1)}, f32[16,1024]{1,0:T(8,128)S(1)}, u32[]{:S(2)}, u32[]{:S(2)}) collective-permute-start(f32[16,1024]{1,0:T(8,128)S(1)} %constant_dynamic-update-slice_fusion.refs_0_), channel_id=1, source_target_pairs={{0,5},{1,6},{2,7},{3,8},{4,9},{5,10},{6,11},{7,12},{8,13},{9,14},{... | collective-permute-start | bytes 196616 | tf_op jit(solution)/shard_map/ppermute | solution.py:21
  21.9 8.1 %collective-permute-start.3 = (f32[16,1024]{1,0:T(8,128)S(1)}, f32[16,1024]{1,0:T(8,128)S(1)}, u32[]{:S(2)}, u32[]{:S(2)}) collective-permute-start(f32[16,1024]{1,0:T(8,128)S(1)} %constant_dynamic-update-slice_fusion.refs_0_), channel_id=1, source_target_pairs={{0,4},{1,5},{2,6},{3,7},{4,8},{5,9},{6,10},{7,11},{8,12},{9,13},{1... | collective-permute-start | bytes 196616 | tf_op jit(solution)/shard_map/ppermute | solution.py:21
  28.3 5.5 %collective-permute-start.2 = (f32[16,1024]{1,0:T(8,128)S(1)}, f32[16,1024]{1,0:T(8,128)S(1)}, u32[]{:S(2)}, u32[]{:S(2)}) collective-permute-start(f32[16,1024]{1,0:T(8,128)S(1)} %constant_dynamic-update-slice_fusion.refs_0_), channel_id=1, source_target_pairs={{0,3},{1,4},{2,5},{3,6},{4,7},{5,8},{6,9},{7,10},{8,11},{9,12},{10... | collective-permute-start | bytes 196616 | tf_op jit(solution)/shard_map/ppermute | solution.py:21
  29.9 7.4 %collective-permute-start.1 = (f32[16,1024]{1,0:T(8,128)S(1)}, f32[16,1024]{1,0:T(8,128)S(1)}, u32[]{:S(2)}, u32[]{:S(2)}) collective-permute-start(f32[16,1024]{1,0:T(8,128)S(1)} %constant_dynamic-update-slice_fusion.refs_0_), channel_id=1, source_target_pairs={{0,2},{1,3},{2,4},{3,5},{4,6},{5,7},{6,8},{7,9},{8,10},{9,11},{10,... | collective-permute-start | bytes 196616 | tf_op jit(solution)/shard_map/ppermute | solution.py:21
  29.9 7.4 %collective-permute-start = (f32[16,1024]{1,0:T(8,128)S(1)}, f32[16,1024]{1,0:T(8,128)S(1)}, u32[]{:S(2)}, u32[]{:S(2)}) collective-permute-start(f32[16,1024]{1,0:T(8,128)S(1)} %constant_dynamic-update-slice_fusion.refs_0_), channel_id=1, source_target_pairs={{0,1},{1,2},{2,3},{3,4},{4,5},{5,6},{6,7},{7,8},{8,9},{9,10},{10,1... | collective-permute-start | bytes 196616 | tf_op jit(solution)/shard_map/ppermute | solution.py:21
  74.4 4.5 %collective-permute-start.29 = (f32[8,1024]{1,0:T(8,128)S(1)}, f32[8,1024]{1,0:T(8,128)S(1)}, u32[]{:S(2)}, u32[]{:S(2)}) collective-permute-start(f32[8,1024]{1,0:T(8,128)S(1)} %first_operator.1.refs_16_), channel_id=1, source_target_pairs={{0,15},{1,0},{2,1},{3,2},{4,3},{5,4},{6,5},{7,6},{8,7},{9,8},{10,9... | collective-permute-start | bytes 98312 | tf_op jit(solution)/shard_map/ppermute | solution.py:21
  74.5 6.7 %collective-permute-start.28 = (f32[8,1024]{1,0:T(8,128)S(1)}, f32[8,1024]{1,0:T(8,128)S(1)}, u32[]{:S(2)}, u32[]{:S(2)}) collective-permute-start(f32[8,1024]{1,0:T(8,128)S(1)} %first_operator.1.refs_16_), channel_id=1, source_target_pairs={{0,14},{1,15},{2,0},{3,1},{4,2},{5,3},{6,4},{7,5},{8,6},{9,7},{10,... | collective-permute-start | bytes 98312 | tf_op jit(solution)/shard_map/ppermute | solution.py:21
  75.7 5.5 %collective-permute-start.27 = (f32[8,1024]{1,0:T(8,128)S(1)}, f32[8,1024]{1,0:T(8,128)S(1)}, u32[]{:S(2)}, u32[]{:S(2)}) collective-permute-start(f32[8,1024]{1,0:T(8,128)S(1)} %first_operator.1.refs_16_), channel_id=1, source_target_pairs={{0,13},{1,14},{2,15},{3,0},{4,1},{5,2},{6,3},{7,4},{8,5},{9,6},{10... | collective-permute-start | bytes 98312 | tf_op jit(solution)/shard_map/ppermute | solution.py:21
  75.9 7.0 %collective-permute-start.26 = (f32[8,1024]{1,0:T(8,128)S(1)}, f32[8,1024]{1,0:T(8,128)S(1)}, u32[]{:S(2)}, u32[]{:S(2)}) collective-permute-start(f32[8,1024]{1,0:T(8,128)S(1)} %first_operator.1.refs_16_), channel_id=1, source_target_pairs={{0,12},{1,13},{2,14},{3,15},{4,0},{5,1},{6,2},{7,3},{8,4},{9,5},{1... | collective-permute-start | bytes 98312 | tf_op jit(solution)/shard_map/ppermute | solution.py:21
  76.0 7.9 %collective-permute-start.25 = (f32[8,1024]{1,0:T(8,128)S(1)}, f32[8,1024]{1,0:T(8,128)S(1)}, u32[]{:S(2)}, u32[]{:S(2)}) collective-permute-start(f32[8,1024]{1,0:T(8,128)S(1)} %first_operator.1.refs_16_), channel_id=1, source_target_pairs={{0,11},{1,12},{2,13},{3,14},{4,15},{5,0},{6,1},{7,2},{8,3},{9,4},{... | collective-permute-start | bytes 98312 | tf_op jit(solution)/shard_map/ppermute | solution.py:21
  78.9 7.2 %collective-permute-start.24 = (f32[8,1024]{1,0:T(8,128)S(1)}, f32[8,1024]{1,0:T(8,128)S(1)}, u32[]{:S(2)}, u32[]{:S(2)}) collective-permute-start(f32[8,1024]{1,0:T(8,128)S(1)} %first_operator.1.refs_16_), channel_id=1, source_target_pairs={{0,10},{1,11},{2,12},{3,13},{4,14},{5,15},{6,0},{7,1},{8,2},{9,3},... | collective-permute-start | bytes 98312 | tf_op jit(solution)/shard_map/ppermute | solution.py:21
  81.2 5.5 %collective-permute-start.23 = (f32[8,1024]{1,0:T(8,128)S(1)}, f32[8,1024]{1,0:T(8,128)S(1)}, u32[]{:S(2)}, u32[]{:S(2)}) collective-permute-start(f32[8,1024]{1,0:T(8,128)S(1)} %first_operator.1.refs_16_), channel_id=1, source_target_pairs={{0,9},{1,10},{2,11},{3,12},{4,13},{5,14},{6,15},{7,0},{8,1},{9,2},... | collective-permute-start | bytes 98312 | tf_op jit(solution)/shard_map/ppermute | solution.py:21
  81.2 7.5 %collective-permute-start.22 = (f32[8,1024]{1,0:T(8,128)S(1)}, f32[8,1024]{1,0:T(8,128)S(1)}, u32[]{:S(2)}, u32[]{:S(2)}) collective-permute-start(f32[8,1024]{1,0:T(8,128)S(1)} %first_operator.1.refs_16_), channel_id=1, source_target_pairs={{0,8},{1,9},{2,10},{3,11},{4,12},{5,13},{6,14},{7,15},{8,0},{9,1},... | collective-permute-start | bytes 98312 | tf_op jit(solution)/shard_map/ppermute | solution.py:21
  83.0 7.8 %collective-permute-start.21 = (f32[8,1024]{1,0:T(8,128)S(1)}, f32[8,1024]{1,0:T(8,128)S(1)}, u32[]{:S(2)}, u32[]{:S(2)}) collective-permute-start(f32[8,1024]{1,0:T(8,128)S(1)} %first_operator.1.refs_16_), channel_id=1, source_target_pairs={{0,7},{1,8},{2,9},{3,10},{4,11},{5,12},{6,13},{7,14},{8,15},{9,0},... | collective-permute-start | bytes 98312 | tf_op jit(solution)/shard_map/ppermute | solution.py:21
  83.9 7.6 %collective-permute-start.20 = (f32[8,1024]{1,0:T(8,128)S(1)}, f32[8,1024]{1,0:T(8,128)S(1)}, u32[]{:S(2)}, u32[]{:S(2)}) collective-permute-start(f32[8,1024]{1,0:T(8,128)S(1)} %first_operator.1.refs_16_), channel_id=1, source_target_pairs={{0,6},{1,7},{2,8},{3,9},{4,10},{5,11},{6,12},{7,13},{8,14},{9,15},... | collective-permute-start | bytes 98312 | tf_op jit(solution)/shard_map/ppermute | solution.py:21
  86.1 5.8 %collective-permute-start.19 = (f32[8,1024]{1,0:T(8,128)S(1)}, f32[8,1024]{1,0:T(8,128)S(1)}, u32[]{:S(2)}, u32[]{:S(2)}) collective-permute-start(f32[8,1024]{1,0:T(8,128)S(1)} %first_operator.1.refs_16_), channel_id=1, source_target_pairs={{0,5},{1,6},{2,7},{3,8},{4,9},{5,10},{6,11},{7,12},{8,13},{9,14},{... | collective-permute-start | bytes 98312 | tf_op jit(solution)/shard_map/ppermute | solution.py:21
  86.6 5.9 %collective-permute-start.18 = (f32[8,1024]{1,0:T(8,128)S(1)}, f32[8,1024]{1,0:T(8,128)S(1)}, u32[]{:S(2)}, u32[]{:S(2)}) collective-permute-start(f32[8,1024]{1,0:T(8,128)S(1)} %first_operator.1.refs_16_), channel_id=1, source_target_pairs={{0,4},{1,5},{2,6},{3,7},{4,8},{5,9},{6,10},{7,11},{8,12},{9,13},{1... | collective-permute-start | bytes 98312 | tf_op jit(solution)/shard_map/ppermute | solution.py:21
  88.7 5.4 %collective-permute-start.17 = (f32[8,1024]{1,0:T(8,128)S(1)}, f32[8,1024]{1,0:T(8,128)S(1)}, u32[]{:S(2)}, u32[]{:S(2)}) collective-permute-start(f32[8,1024]{1,0:T(8,128)S(1)} %first_operator.1.refs_16_), channel_id=1, source_target_pairs={{0,3},{1,4},{2,5},{3,6},{4,7},{5,8},{6,9},{7,10},{8,11},{9,12},{10... | collective-permute-start | bytes 98312 | tf_op jit(solution)/shard_map/ppermute | solution.py:21
  90.8 6.8 %collective-permute-start.16 = (f32[8,1024]{1,0:T(8,128)S(1)}, f32[8,1024]{1,0:T(8,128)S(1)}, u32[]{:S(2)}, u32[]{:S(2)}) collective-permute-start(f32[8,1024]{1,0:T(8,128)S(1)} %first_operator.1.refs_16_), channel_id=1, source_target_pairs={{0,2},{1,3},{2,4},{3,5},{4,6},{5,7},{6,8},{7,9},{8,10},{9,11},{10,... | collective-permute-start | bytes 98312 | tf_op jit(solution)/shard_map/ppermute | solution.py:21
  91.5 6.3 %collective-permute-start.15 = (f32[8,1024]{1,0:T(8,128)S(1)}, f32[8,1024]{1,0:T(8,128)S(1)}, u32[]{:S(2)}, u32[]{:S(2)}) collective-permute-start(f32[8,1024]{1,0:T(8,128)S(1)} %first_operator.1.refs_16_), channel_id=1, source_target_pairs={{0,1},{1,2},{2,3},{3,4},{4,5},{5,6},{6,7},{7,8},{8,9},{9,10},{10,1... | collective-permute-start | bytes 98312 | tf_op jit(solution)/shard_map/ppermute | solution.py:21
  138.4 23.3 %copy-start.4 = (f32[8,128]{1,0:T(8,128)}, f32[8,128]{1,0:T(8,128)S(1)}, u32[]{:S(2)}) copy-start(f32[8,128]{1,0:T(8,128)S(1)} %get-tuple-element.12.norm_ref) | copy-start | bytes 12292
  138.4 23.3 %copy-start.5 = (f32[8,128]{1,0:T(8,128)}, f32[8,128]{1,0:T(8,128)S(1)}, u32[]{:S(2)}) copy-start(f32[8,128]{1,0:T(8,128)S(1)} %get-tuple-element.13.refs_0_) | copy-start | bytes 12292
  138.4 3.2 %collective-permute-start.44 = (f32[8,128]{1,0:T(8,128)S(1)}, f32[8,128]{1,0:T(8,128)S(1)}, u32[]{:S(2)}, u32[]{:S(2)}) collective-permute-start(f32[8,128]{1,0:T(8,128)S(1)} %get-tuple-element.13.refs_0_), channel_id=1, source_target_pairs={{0,15},{1,0},{2,1},{3,2},{4,3},{5,4},{6,5},{7,6},{8,7},{9,8},{10,9... | collective-permute-start | bytes 12296 | tf_op jit(solution)/shard_map/ppermute | solution.py:21
  138.5 5.8 %collective-permute-start.43 = (f32[8,128]{1,0:T(8,128)S(1)}, f32[8,128]{1,0:T(8,128)S(1)}, u32[]{:S(2)}, u32[]{:S(2)}) collective-permute-start(f32[8,128]{1,0:T(8,128)S(1)} %get-tuple-element.13.refs_0_), channel_id=1, source_target_pairs={{0,14},{1,15},{2,0},{3,1},{4,2},{5,3},{6,4},{7,5},{8,6},{9,7},{10,... | collective-permute-start | bytes 12296 | tf_op jit(solution)/shard_map/ppermute | solution.py:21
  139.6 5.2 %collective-permute-start.42 = (f32[8,128]{1,0:T(8,128)S(1)}, f32[8,128]{1,0:T(8,128)S(1)}, u32[]{:S(2)}, u32[]{:S(2)}) collective-permute-start(f32[8,128]{1,0:T(8,128)S(1)} %get-tuple-element.13.refs_0_), channel_id=1, source_target_pairs={{0,13},{1,14},{2,15},{3,0},{4,1},{5,2},{6,3},{7,4},{8,5},{9,6},{10... | collective-permute-start | bytes 12296 | tf_op jit(solution)/shard_map/ppermute | solution.py:21
  139.9 6.2 %collective-permute-start.41 = (f32[8,128]{1,0:T(8,128)S(1)}, f32[8,128]{1,0:T(8,128)S(1)}, u32[]{:S(2)}, u32[]{:S(2)}) collective-permute-start(f32[8,128]{1,0:T(8,128)S(1)} %get-tuple-element.13.refs_0_), channel_id=1, source_target_pairs={{0,12},{1,13},{2,14},{3,15},{4,0},{5,1},{6,2},{7,3},{8,4},{9,5},{1... | collective-permute-start | bytes 12296 | tf_op jit(solution)/shard_map/ppermute | solution.py:21
  140.8 7.5 %collective-permute-start.40 = (f32[8,128]{1,0:T(8,128)S(1)}, f32[8,128]{1,0:T(8,128)S(1)}, u32[]{:S(2)}, u32[]{:S(2)}) collective-permute-start(f32[8,128]{1,0:T(8,128)S(1)} %get-tuple-element.13.refs_0_), channel_id=1, source_target_pairs={{0,11},{1,12},{2,13},{3,14},{4,15},{5,0},{6,1},{7,2},{8,3},{9,4},{... | collective-permute-start | bytes 12296 | tf_op jit(solution)/shard_map/ppermute | solution.py:21
  141.7 20.1 %copy-start.8 = (f32[8,128]{1,0:T(8,128)}, f32[8,128]{1,0:T(8,128)S(1)}, u32[]{:S(2)}) copy-start(f32[8,128]{1,0:T(8,128)S(1)} %collective-permute-done.44.refs_15_) | copy-start | bytes 12292
  141.7 8.5 %collective-permute-start.39 = (f32[8,128]{1,0:T(8,128)S(1)}, f32[8,128]{1,0:T(8,128)S(1)}, u32[]{:S(2)}, u32[]{:S(2)}) collective-permute-start(f32[8,128]{1,0:T(8,128)S(1)} %get-tuple-element.13.refs_0_), channel_id=1, source_target_pairs={{0,10},{1,11},{2,12},{3,13},{4,14},{5,15},{6,0},{7,1},{8,2},{9,3},... | collective-permute-start | bytes 12296 | tf_op jit(solution)/shard_map/ppermute | solution.py:21
  144.3 17.5 %copy-start.9 = (f32[8,128]{1,0:T(8,128)}, f32[8,128]{1,0:T(8,128)S(1)}, u32[]{:S(2)}) copy-start(f32[8,128]{1,0:T(8,128)S(1)} %collective-permute-done.43.refs_14_) | copy-start | bytes 12292
  144.3 6.3 %collective-permute-start.38 = (f32[8,128]{1,0:T(8,128)S(1)}, f32[8,128]{1,0:T(8,128)S(1)}, u32[]{:S(2)}, u32[]{:S(2)}) collective-permute-start(f32[8,128]{1,0:T(8,128)S(1)} %get-tuple-element.13.refs_0_), channel_id=1, source_target_pairs={{0,9},{1,10},{2,11},{3,12},{4,13},{5,14},{6,15},{7,0},{8,1},{9,2},... | collective-permute-start | bytes 12296 | tf_op jit(solution)/shard_map/ppermute | solution.py:21
  144.8 17.0 %copy-start.10 = (f32[8,128]{1,0:T(8,128)}, f32[8,128]{1,0:T(8,128)S(1)}, u32[]{:S(2)}) copy-start(f32[8,128]{1,0:T(8,128)S(1)} %collective-permute-done.42.refs_13_) | copy-start | bytes 12292
  144.8 7.8 %collective-permute-start.37 = (f32[8,128]{1,0:T(8,128)S(1)}, f32[8,128]{1,0:T(8,128)S(1)}, u32[]{:S(2)}, u32[]{:S(2)}) collective-permute-start(f32[8,128]{1,0:T(8,128)S(1)} %get-tuple-element.13.refs_0_), channel_id=1, source_target_pairs={{0,8},{1,9},{2,10},{3,11},{4,12},{5,13},{6,14},{7,15},{8,0},{9,1},... | collective-permute-start | bytes 12296 | tf_op jit(solution)/shard_map/ppermute | solution.py:21
  146.1 15.7 %copy-start.11 = (f32[8,128]{1,0:T(8,128)}, f32[8,128]{1,0:T(8,128)S(1)}, u32[]{:S(2)}) copy-start(f32[8,128]{1,0:T(8,128)S(1)} %collective-permute-done.41.refs_12_) | copy-start | bytes 12292
  146.1 8.6 %collective-permute-start.36 = (f32[8,128]{1,0:T(8,128)S(1)}, f32[8,128]{1,0:T(8,128)S(1)}, u32[]{:S(2)}, u32[]{:S(2)}) collective-permute-start(f32[8,128]{1,0:T(8,128)S(1)} %get-tuple-element.13.refs_0_), channel_id=1, source_target_pairs={{0,7},{1,8},{2,9},{3,10},{4,11},{5,12},{6,13},{7,14},{8,15},{9,0},... | collective-permute-start | bytes 12296 | tf_op jit(solution)/shard_map/ppermute | solution.py:21
  148.2 13.6 %copy-start.12 = (f32[8,128]{1,0:T(8,128)}, f32[8,128]{1,0:T(8,128)S(1)}, u32[]{:S(2)}) copy-start(f32[8,128]{1,0:T(8,128)S(1)} %collective-permute-done.40.refs_11_) | copy-start | bytes 12292
  148.2 7.8 %collective-permute-start.35 = (f32[8,128]{1,0:T(8,128)S(1)}, f32[8,128]{1,0:T(8,128)S(1)}, u32[]{:S(2)}, u32[]{:S(2)}) collective-permute-start(f32[8,128]{1,0:T(8,128)S(1)} %get-tuple-element.13.refs_0_), channel_id=1, source_target_pairs={{0,6},{1,7},{2,8},{3,9},{4,10},{5,11},{6,12},{7,13},{8,14},{9,15},... | collective-permute-start | bytes 12296 | tf_op jit(solution)/shard_map/ppermute | solution.py:21
  150.2 11.6 %copy-start.13 = (f32[8,128]{1,0:T(8,128)}, f32[8,128]{1,0:T(8,128)S(1)}, u32[]{:S(2)}) copy-start(f32[8,128]{1,0:T(8,128)S(1)} %collective-permute-done.39.refs_10_) | copy-start | bytes 12292
  150.2 5.9 %collective-permute-start.34 = (f32[8,128]{1,0:T(8,128)S(1)}, f32[8,128]{1,0:T(8,128)S(1)}, u32[]{:S(2)}, u32[]{:S(2)}) collective-permute-start(f32[8,128]{1,0:T(8,128)S(1)} %get-tuple-element.13.refs_0_), channel_id=1, source_target_pairs={{0,5},{1,6},{2,7},{3,8},{4,9},{5,10},{6,11},{7,12},{8,13},{9,14},{... | collective-permute-start | bytes 12296 | tf_op jit(solution)/shard_map/ppermute | solution.py:21
  150.6 11.2 %copy-start.14 = (f32[8,128]{1,0:T(8,128)}, f32[8,128]{1,0:T(8,128)S(1)}, u32[]{:S(2)}) copy-start(f32[8,128]{1,0:T(8,128)S(1)} %collective-permute-done.38.refs_9_) | copy-start | bytes 12292
  150.6 5.5 %collective-permute-start.33 = (f32[8,128]{1,0:T(8,128)S(1)}, f32[8,128]{1,0:T(8,128)S(1)}, u32[]{:S(2)}, u32[]{:S(2)}) collective-permute-start(f32[8,128]{1,0:T(8,128)S(1)} %get-tuple-element.13.refs_0_), channel_id=1, source_target_pairs={{0,4},{1,5},{2,6},{3,7},{4,8},{5,9},{6,10},{7,11},{8,12},{9,13},{1... | collective-permute-start | bytes 12296 | tf_op jit(solution)/shard_map/ppermute | solution.py:21
  152.6 9.2 %copy-start.15 = (f32[8,128]{1,0:T(8,128)}, f32[8,128]{1,0:T(8,128)S(1)}, u32[]{:S(2)}) copy-start(f32[8,128]{1,0:T(8,128)S(1)} %collective-permute-done.37.refs_8_) | copy-start | bytes 12292
  152.6 4.9 %collective-permute-start.32 = (f32[8,128]{1,0:T(8,128)S(1)}, f32[8,128]{1,0:T(8,128)S(1)}, u32[]{:S(2)}, u32[]{:S(2)}) collective-permute-start(f32[8,128]{1,0:T(8,128)S(1)} %get-tuple-element.13.refs_0_), channel_id=1, source_target_pairs={{0,3},{1,4},{2,5},{3,6},{4,7},{5,8},{6,9},{7,10},{8,11},{9,12},{10... | collective-permute-start | bytes 12296 | tf_op jit(solution)/shard_map/ppermute | solution.py:21
  154.7 7.1 %copy-start.16 = (f32[8,128]{1,0:T(8,128)}, f32[8,128]{1,0:T(8,128)S(1)}, u32[]{:S(2)}) copy-start(f32[8,128]{1,0:T(8,128)S(1)} %collective-permute-done.36.refs_7_) | copy-start | bytes 12292
  154.7 6.3 %collective-permute-start.31 = (f32[8,128]{1,0:T(8,128)S(1)}, f32[8,128]{1,0:T(8,128)S(1)}, u32[]{:S(2)}, u32[]{:S(2)}) collective-permute-start(f32[8,128]{1,0:T(8,128)S(1)} %get-tuple-element.13.refs_0_), channel_id=1, source_target_pairs={{0,2},{1,3},{2,4},{3,5},{4,6},{5,7},{6,8},{7,9},{8,10},{9,11},{10,... | collective-permute-start | bytes 12296 | tf_op jit(solution)/shard_map/ppermute | solution.py:21
  156.0 5.8 %copy-start.17 = (f32[8,128]{1,0:T(8,128)}, f32[8,128]{1,0:T(8,128)S(1)}, u32[]{:S(2)}) copy-start(f32[8,128]{1,0:T(8,128)S(1)} %collective-permute-done.35.refs_6_) | copy-start | bytes 12292
  156.0 5.7 %collective-permute-start.30 = (f32[8,128]{1,0:T(8,128)S(1)}, f32[8,128]{1,0:T(8,128)S(1)}, u32[]{:S(2)}, u32[]{:S(2)}) collective-permute-start(f32[8,128]{1,0:T(8,128)S(1)} %get-tuple-element.13.refs_0_), channel_id=1, source_target_pairs={{0,1},{1,2},{2,3},{3,4},{4,5},{5,6},{6,7},{7,8},{8,9},{9,10},{10,1... | collective-permute-start | bytes 12296 | tf_op jit(solution)/shard_map/ppermute | solution.py:21
  156.0 5.8 %copy-start.18 = (f32[8,128]{1,0:T(8,128)}, f32[8,128]{1,0:T(8,128)S(1)}, u32[]{:S(2)}) copy-start(f32[8,128]{1,0:T(8,128)S(1)} %collective-permute-done.34.refs_5_) | copy-start | bytes 12292
  156.1 5.8 %copy-start.19 = (f32[8,128]{1,0:T(8,128)}, f32[8,128]{1,0:T(8,128)S(1)}, u32[]{:S(2)}) copy-start(f32[8,128]{1,0:T(8,128)S(1)} %collective-permute-done.33.refs_4_) | copy-start | bytes 12292
  157.5 4.4 %copy-start.20 = (f32[8,128]{1,0:T(8,128)}, f32[8,128]{1,0:T(8,128)S(1)}, u32[]{:S(2)}) copy-start(f32[8,128]{1,0:T(8,128)S(1)} %collective-permute-done.32.refs_3_) | copy-start | bytes 12292
  161.0 0.9 copy-start.21
  (5 other events, 3.0 us)

commit v2 on v1

v2 whole, which is shorter than its diff:
```python
import functools
import math

import jax
import jax.numpy as jnp
from jax import lax
from jax.experimental import pallas as pl
from jax.experimental.pallas import tpu as pltpu
from jax.sharding import PartitionSpec as P

LOG2E = math.log2(math.e)
DEPTH = 64
TILE = 256
F32 = jnp.float32
BF16 = jnp.bfloat16


def pieces(value, count):
    parts = []
    for _ in range(count):
        part = value.astype(BF16).astype(F32)
        parts.append(part)
        value = value - part
    return parts


def exponent_rows(points, factor, visiting):
    big, mid, low = pieces(points * factor, 3)
    half_sq = jnp.sum(points * points, axis=0, keepdims=True) * (-0.5 * LOG2E)
    sq_parts = pieces(half_sq, 3)
    row = lax.broadcasted_iota(jnp.int32, points.shape, 0)
    first = 0 if visiting else 3
    tail = jnp.where((row >= 3 - first) & (row < 6 - first), 1.0, 0.0)
    for k, part in enumerate(sq_parts):
        tail = jnp.where(row == first + k, part, tail)
    order = [big, big, big, mid, mid, low] if visiting else [big, mid, low, big, mid, big]
    return jnp.concatenate(order + [tail, jnp.zeros_like(tail)], axis=0)


def stacked(value):
    return jnp.concatenate(pieces(value, 2), axis=0).astype(BF16)


def prepare_points(scale_ref, mine_ref, all_ref, nfeat, rows_ref, own_ref):
    own = exponent_rows(mine_ref[0:nfeat, :] / scale_ref[...], 1.0, False)
    own_ref[...] = own.T.astype(BF16)

    def block(b, carry):
        points = all_ref[b, 0:nfeat, :] / scale_ref[...]
        rows_ref[b] = exponent_rows(points, LOG2E, True).astype(BF16)
        return carry

    lax.fori_loop(0, all_ref.shape[0], block, 0)


def operator_loop(rows_ref, own_ref, dirs_ref, acc_ref):
    count, _, width = rows_ref.shape
    acc_ref[...] = jnp.zeros_like(acc_ref)
    chunks = width // TILE

    def step(t, carry):
        b = t // chunks
        at = pl.ds(pl.multiple_of((t % chunks) * TILE, TILE), TILE)
        own = own_ref[at, :]
        total = acc_ref[at, :]
        for c in range(chunks):
            cols = slice(c * TILE, (c + 1) * TILE)
            expo = jnp.dot(own, rows_ref[b, :, cols], preferred_element_type=F32)
            weight = jnp.exp2(expo)
            high = weight.astype(BF16)
            low = (weight - high.astype(F32)).astype(BF16)
            dirs = dirs_ref[b, :, cols]
            for piece in (high, low):
                total = total + lax.dot_general(
                    piece, dirs, (((1,), (1,)), ((), ())), preferred_element_type=F32
                )
        acc_ref[at, :] = total
        return carry

    lax.fori_loop(0, count * chunks, step, 0)


def collected(acc_ref, nrhs):
    total = acc_ref[...].T
    return total[0:nrhs, :] + total[nrhs:, :]


def first_kernel(
    nfeat, amplitude, scale_ref, noise_ref, mine_ref, all_ref,
    image_ref, rows_ref, own_ref, dirs_ref, acc_ref,
):
    prepare_points(scale_ref, mine_ref, all_ref, nfeat, rows_ref, own_ref)

    def block(b, carry):
        dirs_ref[b] = stacked(all_ref[b, nfeat:, :])
        return carry

    lax.fori_loop(0, all_ref.shape[0], block, 0)
    operator_loop(rows_ref, own_ref, dirs_ref, acc_ref)
    total = collected(acc_ref, image_ref.shape[0])
    image_ref[...] = amplitude * total + noise_ref[...] * mine_ref[nfeat:, :]


def second_kernel(
    nfeat, amplitude, scale_ref, noise_ref, mine_ref, all_ref, image0_ref, images_ref,
    sol_ref, res_ref, dir_ref, image_ref, norm_ref, curv_ref,
    rows_ref, own_ref, dirs_ref, acc_ref,
):
    prepare_points(scale_ref, mine_ref, all_ref, nfeat, rows_ref, own_ref)
    count = all_ref.shape[0]
    nrhs = image_ref.shape[0]
    nothing = jnp.zeros((nrhs, image_ref.shape[1]), F32)

    def sums(b, carry):
        rhs = all_ref[b, nfeat:, :]
        return carry[0] + rhs * rhs, carry[1] + rhs * images_ref[b]

    norm, curv = lax.fori_loop(0, count, sums, (nothing, nothing))
    norm = jnp.sum(norm, axis=1, keepdims=True)
    alpha = norm / jnp.sum(curv, axis=1, keepdims=True)

    def next_sum(b, carry):
        left = all_ref[b, nfeat:, :] - alpha * images_ref[b]
        return carry + left * left

    norm_next = jnp.sum(lax.fori_loop(0, count, next_sum, nothing), axis=1, keepdims=True)
    beta = norm_next / norm

    def block(b, carry):
        rhs = all_ref[b, nfeat:, :]
        dirs_ref[b] = stacked((rhs - alpha * images_ref[b]) + beta * rhs)
        return carry

    lax.fori_loop(0, count, block, 0)
    rhs = mine_ref[nfeat:, :]
    residual = rhs - alpha * image0_ref[...]
    direc = residual + beta * rhs
    sol_ref[...] = alpha * rhs
    res_ref[...] = residual
    dir_ref[...] = direc
    operator_loop(rows_ref, own_ref, dirs_ref, acc_ref)
    image = amplitude * collected(acc_ref, nrhs) + noise_ref[...] * direc
    image_ref[...] = image
    norm_ref[...] = jnp.broadcast_to(norm_next, norm_ref.shape)
    curv_ref[...] = jnp.broadcast_to(
        jnp.sum(direc * image, axis=1, keepdims=True), curv_ref.shape
    )


def last_kernel(sol_ref, res_ref, dir_ref, image_ref, norm_ref, curvs_ref, out_sol, out_res):
    curv = jnp.sum(curvs_ref[...], axis=0)[:, 0:1]
    alpha = norm_ref[:, 0:1] / curv
    out_sol[...] = sol_ref[...] + alpha * dir_ref[...]
    out_res[...] = res_ref[...] - alpha * image_ref[...]


def shards(features, lengthscale, noise, rhs):
    nfeat, width = features.shape
    nrhs = rhs.shape[0]
    count = lax.axis_size("row")
    amplitude = 1.0 / math.sqrt(width * count)
    scale = lengthscale[:, None]
    noise = noise[None, :]
    mine = jnp.concatenate([features, rhs], axis=0)
    everything = lax.all_gather(mine, "row")
    field = jax.ShapeDtypeStruct((nrhs, width), F32)
    small = jax.ShapeDtypeStruct((nrhs, 128), F32)
    scratch = [
        pltpu.VMEM((count, DEPTH, width), BF16),
        pltpu.VMEM((width, DEPTH), BF16),
        pltpu.VMEM((count, 2 * nrhs, width), BF16),
        pltpu.VMEM((width, 2 * nrhs), F32),
    ]
    entries = count * width * width
    params = pltpu.CompilerParams(
        vmem_limit_bytes=min(16 * 1024 * 1024 + 512 * count * width, 60 * 1024 * 1024)
    )
    cost = pl.CostEstimate(
        flops=2 * entries * (DEPTH + 4 * nrhs),
        bytes_accessed=4 * count * (nfeat + nrhs) * width,
        transcendentals=entries,
    )
    image = pl.pallas_call(
        functools.partial(first_kernel, nfeat, amplitude),
        out_shape=field,
        scratch_shapes=scratch,
        compiler_params=params,
        cost_estimate=cost,
        name="first_operator",
    )(scale, noise, mine, everything)
    images = lax.all_gather(image, "row")
    sol, res, direc, image, norm, curv = pl.pallas_call(
        functools.partial(second_kernel, nfeat, amplitude),
        out_shape=(field, field, field, field, small, small),
        scratch_shapes=scratch,
        compiler_params=params,
        cost_estimate=cost,
        name="second_operator",
    )(scale, noise, mine, everything, image, images)
    curvs = lax.all_gather(curv, "row")
    return pl.pallas_call(
        last_kernel, out_shape=(field, field), name="last_update"
    )(sol, res, direc, image, norm, curvs)


def solution(mesh):
    in_specs = (P(None, ("grp", "row")), P(), P(("grp", "row")), P(None, ("grp", "row")))
    out_specs = (P(None, ("grp", "row")), P(None, ("grp", "row")))
    return jax.shard_map(shards, mesh=mesh, in_specs=in_specs, out_specs=out_specs, check_vma=False)
```

time: 164 us -> 225 us (1.37)
  starting transfers between devices: 58.3 us -> 0.04 us
  Pallas kernels: 77 us -> 124 us
  blocking collectives: 0 us -> 39.7 us
  waiting for transfers between devices: 24 us -> 41.5 us
  between operations: 0.88 us -> 14.1 us
    ppermute x45 -> x0, starting transfers between devices: 58.3 us -> none  [shifted(): lax.ppermute(value, 'row', [(i, (i + by) % length) for i in range(length)])]
    all_gather x0 -> x1, waiting for transfers between devices: none -> 41.5 us  [shards(): everything = lax.all_gather(mine, 'row')]
    all_gather x0 -> x2, blocking collectives: none -> 39.7 us  [the longest x1 20.8 us: shards(): images = lax.all_gather(image, 'row')]
    ppermute x45 -> x0, waiting for transfers between devices: 24 us -> none  [shifted(): lax.ppermute(value, 'row', [(i, (i + by) % length) for i in range(length)])]
    pallas_call x1, Pallas kernels: 37.1 us -> 61 us  [shards(): pl.pallas_call(functools.partial(first_kernel, nfeat, amplitude), out_sha...]
    pallas_call x1, Pallas kernels: 38.3 us -> 61.7 us  [shards(): pl.pallas_call(functools.partial(second_kernel, nfeat, amplitude), out_sh...]
    unnamed x49 -> x23, local copies, waits for them, and re-layouts: 3.71 us -> 5.34 us
  transfers between devices with their start and end apart: 45 -> 1, of which waited for: 13 -> 1; matrix products, arithmetic and copies ran while one was open for 0% -> 0% of each run, Pallas kernels for 0% -> 0%
where the time goes in v2:
time: 225 us
  Pallas kernels  124 us (55%)
  waiting for transfers between devices  41.5 us (18%)
  blocking collectives  39.7 us (18%)
  between operations  14.1 us (6%)
  local copies, waits for them, and re-layouts  5.42 us (2%)
    pallas_call x1, Pallas kernels, shards(): pl.pallas_call(functools.partial(second_kernel, nfeat, amplitude), out_sh...  61.7 us
    pallas_call x1, Pallas kernels, shards(): pl.pallas_call(functools.partial(first_kernel, nfeat, amplitude), out_sha...  61 us
    all_gather x1, waiting for transfers between devices, shards(): everything = lax.all_gather(mine, 'row')  41.5 us
    all_gather x1, blocking collectives, shards(): images = lax.all_gather(image, 'row')  20.8 us
    all_gather x1, blocking collectives, shards(): curvs = lax.all_gather(curv, 'row')  19 us
    unnamed x23, local copies, waits for them, and re-layouts  5.34 us
  transfers between devices with their start and end apart: 1, of which 1 were waited for; matrix products, arithmetic and copies ran while one was open for 0% of the time, Pallas kernels for 0%

profile of v2, /device:TPU:0, one launch (start us, length us, event | category | flops | bytes accessed | tf_op | source)
XLA Modules:
  0.0 225.1 jit_solution(10661254521661930694)
XLA Ops:
  7.2 0.0 copy-start.9
  7.2 0.0 all-gather.5.cloned.1.call-start
  7.2 0.8 constant_dynamic-update-slice_fusion.1
  8.0 0.0 copy-done.9
  8.0 0.0 copy-start
  8.0 0.6 copy-done
  8.6 0.0 all-gather.5.cloned.1.call-update
  8.6 0.0 copy-start.10
  8.6 0.6 copy-done.10
  9.3 0.0 copy-start.8
  9.3 0.1 copy.7.scale_ref
  9.4 41.5 %all-gather.5.cloned.1.call-done = f32[256,1024]{1,0:T(8,128)} async-done(((f32[16,1024]{1,0:T(8,128)}), f32[256,1024]{1,0:T(8,128)}) %all-gather.5.cloned.1.call-update) | async-done | bytes 1048592 | tf_op jit(solution)/shard_map/all_gather | solution.py:165
  50.8 0.0 copy-done.8
  50.8 0.0 copy-start.1
  50.8 0.8 copy-done.1
  51.7 0.0 copy-start.7
  51.7 1.2 copy-done.7
  52.9 61.0 %first_operator.1.image0_ref = f32[8,1024]{1,0:T(8,128)S(1)} custom-call(f32[8,1]{1,0:T(8,128)S(1)} %copy.7.scale_ref, f32[1,1024]{1,0:T(1,128)S(1)} %bitcast.8, f32[16,1024]{1,0:T(8,128)S(1)} %copy-done.1, f32[16,16,1024]{2,1,0:T(8,128)S(1)} %bitcast.6), custom_call_target="tpu_custom_call" | custom-call | flops 3221225472 | bytes 1048576 | tf_op jit(solution)/shard_map/first_operator/pallas_call | solution.py:183
  113.9 20.8 %all-gather.1 = f32[128,1024]{1,0:T(8,128)S(1)} all-gather(f32[8,1024]{1,0:T(8,128)S(1)} %first_operator.1.image0_ref), channel_id=3, replica_groups=mesh['grp'=2,'row'=16] {'row'}, dimensions={0}, use_global_device_ids=true | all-gather | bytes 557056 | tf_op jit(solution)/shard_map/all_gather | solution.py:191
  134.7 61.7 %second_operator.1 = (f32[8,1024]{1,0:T(8,128)S(1)}, f32[8,1024]{1,0:T(8,128)S(1)}, f32[8,1024]{1,0:T(8,128)S(1)}, f32[8,1024]{1,0:T(8,128)S(1)}, f32[8,128]{1,0:T(8,128)S(1)}, /*index=5*/f32[8,128]{1,0:T(8,128)S(1)}) custom-call(f32[8,1]{1,0:T(8,128)S(1)} %copy.7.scale_ref, f32[1,1024]{1,0:T(1,128)S(1)} %bitcast.9, f32[16,1024]{1,0:T(8,128)S(1)} %copy-done.1, ...), custom_call_target="tpu_custom_call" | custom-call | flops 3221225472 | bytes 1048576 | tf_op jit(solution)/shard_map/second_operator/pallas_call | solution.py:192
  196.4 0.0 copy-start.4
  196.4 0.6 copy-done.4
  197.0 0.0 copy-start.5
  197.0 0.6 copy-done.5
  197.6 0.0 copy-start.2
  197.6 0.0 copy-start.3
  197.6 0.0 copy-start.6
  197.6 19.0 %all-gather.2 = f32[128,128]{1,0:T(8,128)} all-gather(f32[8,128]{1,0:T(8,128)S(1)} %get-tuple-element.13), channel_id=4, replica_groups=mesh['grp'=2,'row'=16] {'row'}, dimensions={0}, use_global_device_ids=true | all-gather | bytes 69632 | tf_op jit(solution)/shard_map/all_gather | solution.py:200
  216.6 0.0 copy-done.2
  216.6 0.0 copy-done.3
  216.6 0.0 copy-done.6
  216.6 1.6 last_update.1
  (1 shorter events, 0.0 us)
Async XLA Ops:
  7.2 0.8 copy-start.9
  7.2 43.7 %all-gather.5.cloned.1.call-start = ((), (), s32[]{:S(2)}) async-start(), calls=%async_computation | async-start | bytes 1114112 | tf_op jit(solution)/shard_map/all_gather | solution.py:165
  8.0 0.6 copy-start
  8.6 0.7 copy-start.10
  9.3 41.6 %copy-start.8 = (f32[1024]{0:T(1024)S(1)}, f32[1024]{0:T(1024)}, u32[]{:S(2)}) copy-start(f32[1024]{0:T(1024)} %param.6) | copy-start | bytes 12292
  50.8 0.8 copy-start.1
  51.7 1.2 copy-start.7
  196.4 0.6 copy-start.4
  197.0 0.6 copy-start.5
  197.6 19.0 %copy-start.2 = (f32[8,1024]{1,0:T(8,128)}, f32[8,1024]{1,0:T(8,128)S(1)}, u32[]{:S(2)}) copy-start(f32[8,1024]{1,0:T(8,128)S(1)} %get-tuple-element.8.sol_ref) | copy-start | bytes 98308
  197.6 19.0 %copy-start.3 = (f32[8,1024]{1,0:T(8,128)}, f32[8,1024]{1,0:T(8,128)S(1)}, u32[]{:S(2)}) copy-start(f32[8,1024]{1,0:T(8,128)S(1)} %get-tuple-element.9.res_ref) | copy-start | bytes 98308
  197.6 19.0 %copy-start.6 = (f32[8,128]{1,0:T(8,128)}, f32[8,128]{1,0:T(8,128)S(1)}, u32[]{:S(2)}) copy-start(f32[8,128]{1,0:T(8,128)S(1)} %get-tuple-element.12.norm_ref) | copy-start | bytes 12292
Sparse Core Ops, SparseCore 0:
  10.2 40.6 all-gather.4

commit v3 on v1

v3 whole, which is shorter than its diff:
```python
import functools
import math

import jax
import jax.numpy as jnp
from jax import lax
from jax.experimental import pallas as pl
from jax.experimental.pallas import tpu as pltpu
from jax.sharding import PartitionSpec as P

LOG2E = math.log2(math.e)
DEPTH = 64
TILE = 256
F32 = jnp.float32
BF16 = jnp.bfloat16


def pieces(value, count):
    parts = []
    for _ in range(count):
        part = value.astype(BF16).astype(F32)
        parts.append(part)
        value = value - part
    return parts


def exponent_rows(points, factor, visiting):
    big, mid, low = pieces(points * factor, 3)
    half_sq = jnp.sum(points * points, axis=0, keepdims=True) * (-0.5 * LOG2E)
    sq_parts = pieces(half_sq, 3)
    row = lax.broadcasted_iota(jnp.int32, points.shape, 0)
    first = 0 if visiting else 3
    tail = jnp.where((row >= 3 - first) & (row < 6 - first), 1.0, 0.0)
    for k, part in enumerate(sq_parts):
        tail = jnp.where(row == first + k, part, tail)
    order = [big, big, big, mid, mid, low] if visiting else [big, mid, low, big, mid, big]
    return jnp.concatenate(order + [tail, jnp.zeros_like(tail)], axis=0)


def stacked(value):
    return jnp.concatenate(pieces(value, 2), axis=0).astype(BF16)


def shifted(value, stride, size, by):
    length = lax.axis_size("row")
    pairs = []
    for i in range(length):
        digit = (i // stride) % size
        pairs.append((i, i + ((digit - by) % size - digit) * stride))
    return lax.ppermute(value, "row", pairs)


def gathered(value):
    length = lax.axis_size("row")
    chips = length // 2
    near = 1
    while near * near * 4 <= chips:
        near *= 2
    far = chips // near
    value = value[None]
    stacks = [value] + [shifted(value, 2 * near, far, by) for by in range(1, far)]
    group = jnp.concatenate(stacks, axis=0)
    groups = [group] + [shifted(group, 2, near, by) for by in range(1, near)]
    return stacks, groups[1:] + [shifted(g, 1, 2, 1) for g in groups]


def prepare_points(scale_ref, blocks, nfeat, yt_ref, own_ref):
    width = own_ref.shape[1]
    own_ref[...] = exponent_rows(blocks[0][0, 0:nfeat, :] / scale_ref[...], 1.0, False).astype(BF16)
    base = 0
    for ref in blocks:

        def block(b, carry, ref=ref, base=base):
            rows = exponent_rows(ref[b, 0:nfeat, :] / scale_ref[...], LOG2E, True)
            yt_ref[base + b] = rows.T.astype(BF16)
            return carry

        lax.fori_loop(0, ref.shape[0], block, 0)
        base += ref.shape[0]


def operator_loop(yt_ref, own_ref, dirs_ref, acc_ref):
    count, _, width = dirs_ref.shape
    chunks = width // TILE
    acc_ref[...] = jnp.zeros_like(acc_ref)

    def step(b, carry):
        for c in range(chunks):
            cols = slice(c * TILE, (c + 1) * TILE)
            expo = jnp.dot(yt_ref[b], own_ref[:, cols], preferred_element_type=F32)
            weight = jnp.exp2(expo)
            high = weight.astype(BF16)
            low = (weight - high.astype(F32)).astype(BF16)
            dirs = dirs_ref[b]
            acc_ref[:, cols] += jnp.dot(
                dirs, high, preferred_element_type=F32
            ) + jnp.dot(dirs, low, preferred_element_type=F32)
        return carry

    lax.fori_loop(0, count, step, 0)


def each(stacks, function, carry):
    base = 0
    for refs in zip(*stacks):

        def block(b, carry, refs=refs, base=base):
            return function(base + b, carry, *[r[b] for r in refs])

        carry = lax.fori_loop(0, refs[0].shape[0], block, carry)
        base += refs[0].shape[0]
    return carry


def total_of(acc_ref, nrhs):
    return acc_ref[0:nrhs, :] + acc_ref[nrhs:, :]


def first_kernel(nfeat, amplitude, scale_ref, noise_ref, *refs):
    *blocks, image_ref, yt_ref, own_ref, dirs_ref, acc_ref = refs
    prepare_points(scale_ref, blocks, nfeat, yt_ref, own_ref)

    def block(b, carry, value):
        dirs_ref[b] = stacked(value[nfeat:, :])
        return carry

    each([blocks], block, 0)
    operator_loop(yt_ref, own_ref, dirs_ref, acc_ref)
    total = total_of(acc_ref, image_ref.shape[0])
    image_ref[...] = amplitude * total + noise_ref[...] * blocks[0][0, nfeat:, :]


def second_kernel(nfeat, amplitude, count, scale_ref, noise_ref, *refs):
    blocks = refs[:count]
    images = refs[count : 2 * count]
    outs = refs[2 * count :]
    sol_ref, res_ref, dir_ref, image_ref, norm_ref, curv_ref = outs[:6]
    yt_ref, own_ref, dirs_ref, acc_ref = outs[6:]
    prepare_points(scale_ref, blocks, nfeat, yt_ref, own_ref)
    nrhs = image_ref.shape[0]
    nothing = jnp.zeros(image_ref.shape, F32)

    def sums(b, carry, value, image):
        rhs = value[nfeat:, :]
        return carry[0] + rhs * rhs, carry[1] + rhs * image

    norm, curv = each([blocks, images], sums, (nothing, nothing))
    norm = jnp.sum(norm, axis=1, keepdims=True)
    alpha = norm / jnp.sum(curv, axis=1, keepdims=True)

    def next_sum(b, carry, value, image):
        left = value[nfeat:, :] - alpha * image
        return carry + left * left

    norm_next = jnp.sum(each([blocks, images], next_sum, nothing), axis=1, keepdims=True)
    beta = norm_next / norm

    def block(b, carry, value, image):
        rhs = value[nfeat:, :]
        dirs_ref[b] = stacked((rhs - alpha * image) + beta * rhs)
        return carry

    each([blocks, images], block, 0)
    rhs = blocks[0][0, nfeat:, :]
    residual = rhs - alpha * images[0][0]
    direc = residual + beta * rhs
    sol_ref[...] = alpha * rhs
    res_ref[...] = residual
    dir_ref[...] = direc
    operator_loop(yt_ref, own_ref, dirs_ref, acc_ref)
    image = amplitude * total_of(acc_ref, nrhs) + noise_ref[...] * direc
    image_ref[...] = image
    norm_ref[...] = jnp.broadcast_to(norm_next, norm_ref.shape)
    curv_ref[...] = jnp.broadcast_to(
        jnp.sum(direc * image, axis=1, keepdims=True), curv_ref.shape
    )


def last_kernel(sol_ref, res_ref, dir_ref, image_ref, norm_ref, *refs):
    *curvs, out_sol, out_res = refs
    curv = sum(jnp.sum(c[...], axis=0) for c in curvs)[:, 0:1]
    alpha = norm_ref[:, 0:1] / curv
    out_sol[...] = sol_ref[...] + alpha * dir_ref[...]
    out_res[...] = res_ref[...] - alpha * image_ref[...]


def shards(features, lengthscale, noise, rhs):
    nfeat, width = features.shape
    nrhs = rhs.shape[0]
    count = lax.axis_size("row")
    amplitude = 1.0 / math.sqrt(width * count)
    scale = lengthscale[:, None]
    noise = noise[None, :]
    mine = jnp.concatenate([features, rhs], axis=0)
    blocks = [x for part in gathered(mine) for x in part]
    field = jax.ShapeDtypeStruct((nrhs, width), F32)
    small = jax.ShapeDtypeStruct((nrhs, 128), F32)
    scratch = [
        pltpu.VMEM((count, width, DEPTH), BF16),
        pltpu.VMEM((DEPTH, width), BF16),
        pltpu.VMEM((count, 2 * nrhs, width), BF16),
        pltpu.VMEM((2 * nrhs, width), F32),
    ]
    entries = count * width * width
    params = pltpu.CompilerParams(
        vmem_limit_bytes=min(16 * 1024 * 1024 + 512 * count * width, 60 * 1024 * 1024)
    )
    cost = pl.CostEstimate(
        flops=2 * entries * (DEPTH + 4 * nrhs),
        bytes_accessed=4 * count * (nfeat + nrhs) * width,
        transcendentals=entries,
    )
    image = pl.pallas_call(
        functools.partial(first_kernel, nfeat, amplitude),
        out_shape=field,
        scratch_shapes=scratch,
        compiler_params=params,
        cost_estimate=cost,
        name="first_operator",
    )(scale, noise, *blocks)
    images = [x for part in gathered(image) for x in part]
    sol, res, direc, image, norm, curv = pl.pallas_call(
        functools.partial(second_kernel, nfeat, amplitude, len(blocks)),
        out_shape=(field, field, field, field, small, small),
        scratch_shapes=scratch,
        compiler_params=params,
        cost_estimate=cost,
        name="second_operator",
    )(scale, noise, *blocks, *images)
    curvs = [x for part in gathered(curv) for x in part]
    return pl.pallas_call(
        last_kernel, out_shape=(field, field), name="last_update"
    )(sol, res, direc, image, norm, *curvs)


def solution(mesh):
    in_specs = (P(None, ("grp", "row")), P(), P(("grp", "row")), P(None, ("grp", "row")))
    out_specs = (P(None, ("grp", "row")), P(None, ("grp", "row")))
    return jax.shard_map(shards, mesh=mesh, in_specs=in_specs, out_specs=out_specs, check_vma=False)
```

time: 164 us -> 107 us (0.65)
  starting transfers between devices: 58.3 us -> 20.1 us
  Pallas kernels: 77 us -> 55.9 us
    ppermute x45 -> x18, starting transfers between devices: 58.3 us -> 20.1 us  [shifted(): return lax.ppermute(value, 'row', pairs)]
    pallas_call x1, Pallas kernels: 38.3 us -> 27.5 us  [shards(): pl.pallas_call(functools.partial(second_kernel, nfeat, amplitude, len(blo...]
    pallas_call x1, Pallas kernels: 37.1 us -> 26.9 us  [shards(): pl.pallas_call(functools.partial(first_kernel, nfeat, amplitude), out_sha...]
    ppermute x45 -> x18, waiting for transfers between devices: 24 us -> 25.2 us  [shifted(): return lax.ppermute(value, 'row', pairs)]
    unnamed x49 -> x28, local copies, waits for them, and re-layouts: 3.71 us -> 3.63 us
  transfers between devices with their start and end apart: 45 -> 18, of which waited for: 13 -> 14; matrix products, arithmetic and copies ran while one was open for 0% -> 0% of each run, Pallas kernels for 0% -> 0%
where the time goes in v3:
time: 107 us; the launch traced here: 106 us
  Pallas kernels  55.9 us (52%)
  waiting for transfers between devices  25.2 us (24%)
  starting transfers between devices  20.1 us (19%)
  local copies, waits for them, and re-layouts  3.71 us (3%)
    pallas_call x1, Pallas kernels, shards(): pl.pallas_call(functools.partial(second_kernel, nfeat, amplitude, len(blo...  27.5 us
    pallas_call x1, Pallas kernels, shards(): pl.pallas_call(functools.partial(first_kernel, nfeat, amplitude), out_sha...  26.9 us
    ppermute x18, waiting for transfers between devices, shifted(): return lax.ppermute(value, 'row', pairs)  25.2 us
    ppermute x18, starting transfers between devices, shifted(): return lax.ppermute(value, 'row', pairs)  20.1 us
    unnamed x28, local copies, waits for them, and re-layouts  3.63 us
  transfers between devices with their start and end apart: 18, of which 14 were waited for; matrix products, arithmetic and copies ran while one was open for 0% of the time, Pallas kernels for 0%

profile of v3, /device:TPU:0, one launch (start us, length us, event | category | flops | bytes accessed | tf_op | source)
XLA Modules:
  0.0 106.4 jit_solution(17725055949870332705)
XLA Ops:
  0.6 0.8 maximum_bitcast_fusion.refs_0_
  1.4 3.0 %collective-permute-start.2 = (f32[1,16,1024]{2,1,0:T(8,128)S(1)}, f32[1,16,1024]{2,1,0:T(8,128)S(1)}, u32[]{:S(2)}, u32[]{:S(2)}) collective-permute-start(f32[1,16,1024]{2,1,0:T(8,128)S(1)} %maximum_bitcast_fusion.refs_0_), channel_id=1, source_target_pairs={{0,4},{1,5},{2,6},{3,7},{4,8},{5,9},{6,10},{7,11},{8,12},{9,13},{1... | collective-permute-start | bytes 196616 | tf_op jit(solution)/shard_map/ppermute | solution.py:50
  4.4 2.6 %collective-permute-start.1 = (f32[1,16,1024]{2,1,0:T(8,128)S(1)}, f32[1,16,1024]{2,1,0:T(8,128)S(1)}, u32[]{:S(2)}, u32[]{:S(2)}) collective-permute-start(f32[1,16,1024]{2,1,0:T(8,128)S(1)} %maximum_bitcast_fusion.refs_0_), channel_id=1, source_target_pairs={{0,8},{1,9},{2,10},{3,11},{4,12},{5,13},{6,14},{7,15},{8,0},{9,1},... | collective-permute-start | bytes 196616 | tf_op jit(solution)/shard_map/ppermute | solution.py:50
  7.0 1.3 %collective-permute-start = (f32[1,16,1024]{2,1,0:T(8,128)S(1)}, f32[1,16,1024]{2,1,0:T(8,128)S(1)}, u32[]{:S(2)}, u32[]{:S(2)}) collective-permute-start(f32[1,16,1024]{2,1,0:T(8,128)S(1)} %maximum_bitcast_fusion.refs_0_), channel_id=1, source_target_pairs={{0,12},{1,13},{2,14},{3,15},{4,0},{5,1},{6,2},{7,3},{8,4},{9,5},{1... | collective-permute-start | bytes 196616 | tf_op jit(solution)/shard_map/ppermute | solution.py:50
  8.4 0.6 collective-permute-done.2.refs_3_
  9.0 2.5 %collective-permute-done.1.refs_2_ = f32[1,16,1024]{2,1,0:T(8,128)S(1)} collective-permute-done((f32[1,16,1024]{2,1,0:T(8,128)S(1)}, f32[1,16,1024]{2,1,0:T(8,128)S(1)}, u32[]{:S(2)}, u32[]{:S(2)}) %collective-permute-start.1) | collective-permute-done | bytes 65568 | tf_op jit(solution)/shard_map/ppermute | solution.py:50
  11.5 0.2 collective-permute-done.refs_1_
  11.7 0.0 copy-start.13
  11.8 0.0 copy-start.6
  11.8 1.6 %collective-permute-start.3 = (f32[4,16,1024]{2,1,0:T(8,128)S(1)}, f32[4,16,1024]{2,1,0:T(8,128)S(1)}, u32[]{:S(2)}, u32[]{:S(2)}) collective-permute-start(f32[4,16,1024]{2,1,0:T(8,128)S(1)} %pad_maximum_fusion), channel_id=1, source_target_pairs={{0,2},{1,3},{2,0},{3,1},{4,6},{5,7},{6,4},{7,5},{8,10},{9,11},{10,... | collective-permute-start | bytes 786440 | tf_op jit(solution)/shard_map/ppermute | solution.py:50
  13.4 0.0 collective-permute-start.4
  13.4 6.2 %collective-permute-done.3.refs_4_ = f32[4,16,1024]{2,1,0:T(8,128)S(1)} collective-permute-done((f32[4,16,1024]{2,1,0:T(8,128)S(1)}, f32[4,16,1024]{2,1,0:T(8,128)S(1)}, u32[]{:S(2)}, u32[]{:S(2)}) %collective-permute-start.3) | collective-permute-done | bytes 262176 | tf_op jit(solution)/shard_map/ppermute | solution.py:50
  19.6 0.0 collective-permute-start.5
  19.6 0.0 copy-done.13
  19.6 0.1 copy.7.scale_ref
  19.7 0.0 collective-permute-done.4.refs_5_
  19.7 1.4 %collective-permute-done.5.refs_6_ = f32[4,16,1024]{2,1,0:T(8,128)S(1)} collective-permute-done((f32[4,16,1024]{2,1,0:T(8,128)S(1)}, f32[4,16,1024]{2,1,0:T(8,128)S(1)}, u32[]{:S(2)}, u32[]{:S(2)}) %collective-permute-start.5) | collective-permute-done | bytes 262176 | tf_op jit(solution)/shard_map/ppermute | solution.py:50
  21.2 0.0 copy-done.6
  21.2 26.9 %first_operator.1 = f32[8,1024]{1,0:T(8,128)S(1)} custom-call(f32[8,1]{1,0:T(8,128)S(1)} %copy.7.scale_ref, f32[1,1024]{1,0:T(1,128)S(1)} %bitcast.16, f32[1,16,1024]{2,1,0:T(8,128)S(1)} %maximum_bitcast_fusion.refs_0_, f32[1,16,1024]{2,1,0:T(8,128)S(1)} %collective-permute-done.refs_1_, f32[1,16,1024]{2,1,0:T(8,128)S(1)} %collective-permute-done.1.refs_2_, ...), custom_call_target="tpu_custom_call" | custom-call | flops 3221225472 | bytes 1048576 | tf_op jit(solution)/shard_map/first_operator/pallas_call | solution.py:213
  48.0 2.0 %collective-permute-start.8 = (f32[1,8,1024]{2,1,0:T(8,128)S(1)}, f32[1,8,1024]{2,1,0:T(8,128)S(1)}, u32[]{:S(2)}, u32[]{:S(2)}) collective-permute-start(f32[1,8,1024]{2,1,0:T(8,128)S(1)} %bitcast.6), channel_id=1, source_target_pairs={{0,4},{1,5},{2,6},{3,7},{4,8},{5,9},{6,10},{7,11},{8,12},{9,13},{1... | collective-permute-start | bytes 98312 | tf_op jit(solution)/shard_map/ppermute | solution.py:50
  50.0 0.3 collective-permute-start.7
  50.3 2.2 %collective-permute-start.6 = (f32[1,8,1024]{2,1,0:T(8,128)S(1)}, f32[1,8,1024]{2,1,0:T(8,128)S(1)}, u32[]{:S(2)}, u32[]{:S(2)}) collective-permute-start(f32[1,8,1024]{2,1,0:T(8,128)S(1)} %bitcast.8), channel_id=1, source_target_pairs={{0,12},{1,13},{2,14},{3,15},{4,0},{5,1},{6,2},{7,3},{8,4},{9,5},{1... | collective-permute-start | bytes 98312 | tf_op jit(solution)/shard_map/ppermute | solution.py:50
  52.5 1.5 %collective-permute-done.8.refs_10_ = f32[1,8,1024]{2,1,0:T(8,128)S(1)} collective-permute-done((f32[1,8,1024]{2,1,0:T(8,128)S(1)}, f32[1,8,1024]{2,1,0:T(8,128)S(1)}, u32[]{:S(2)}, u32[]{:S(2)}) %collective-permute-start.8) | collective-permute-done | bytes 32800 | tf_op jit(solution)/shard_map/ppermute | solution.py:50
  53.9 1.3 %collective-permute-done.7.refs_9_ = f32[1,8,1024]{2,1,0:T(8,128)S(1)} collective-permute-done((f32[1,8,1024]{2,1,0:T(8,128)S(1)}, f32[1,8,1024]{2,1,0:T(8,128)S(1)}, u32[]{:S(2)}, u32[]{:S(2)}) %collective-permute-start.7) | collective-permute-done | bytes 32800 | tf_op jit(solution)/shard_map/ppermute | solution.py:50
  55.2 0.0 collective-permute-done.6.refs_8_
  55.2 1.2 %collective-permute-start.9 = (f32[4,8,1024]{2,1,0:T(8,128)S(1)}, f32[4,8,1024]{2,1,0:T(8,128)S(1)}, u32[]{:S(2)}, u32[]{:S(2)}) collective-permute-start(f32[4,8,1024]{2,1,0:T(8,128)S(1)} %pad_maximum_fusion.1), channel_id=1, source_target_pairs={{0,2},{1,3},{2,0},{3,1},{4,6},{5,7},{6,4},{7,5},{8,10},{9,11},{10,... | collective-permute-start | bytes 393224 | tf_op jit(solution)/shard_map/ppermute | solution.py:50
  56.4 0.0 collective-permute-start.10
  56.4 3.8 %collective-permute-done.9.refs_11_ = f32[4,8,1024]{2,1,0:T(8,128)S(1)} collective-permute-done((f32[4,8,1024]{2,1,0:T(8,128)S(1)}, f32[4,8,1024]{2,1,0:T(8,128)S(1)}, u32[]{:S(2)}, u32[]{:S(2)}) %collective-permute-start.9) | collective-permute-done | bytes 131104 | tf_op jit(solution)/shard_map/ppermute | solution.py:50
  60.3 0.0 collective-permute-start.11
  60.3 0.0 collective-permute-done.10.refs_12_
  60.3 1.3 %collective-permute-done.11.refs_13_ = f32[4,8,1024]{2,1,0:T(8,128)S(1)} collective-permute-done((f32[4,8,1024]{2,1,0:T(8,128)S(1)}, f32[4,8,1024]{2,1,0:T(8,128)S(1)}, u32[]{:S(2)}, u32[]{:S(2)}) %collective-permute-start.11) | collective-permute-done | bytes 131104 | tf_op jit(solution)/shard_map/ppermute | solution.py:50
  61.6 27.5 %second_operator.1 = (f32[8,1024]{1,0:T(8,128)S(1)}, f32[8,1024]{1,0:T(8,128)S(1)}, f32[8,1024]{1,0:T(8,128)S(1)}, f32[8,1024]{1,0:T(8,128)S(1)}, f32[8,128]{1,0:T(8,128)S(1)}, /*index=5*/f32[8,128]{1,0:T(8,128)S(1)}) custom-call(f32[8,1]{1,0:T(8,128)S(1)} %copy.7.scale_ref, f32[1,1024]{1,0:T(1,128)S(1)} %bitcast.17, ...), custom_call_target="tpu_custom_call" | custom-call | flops 3221225472 | bytes 1048576 | tf_op jit(solution)/shard_map/second_operator/pallas_call | solution.py:222
  89.1 0.6 copy-done
  89.7 0.6 copy-done.1
  90.3 0.0 copy-start.2
  90.3 0.6 copy-done.2
  91.0 0.0 copy-start.3
  91.0 0.6 copy-done.3
  91.6 0.0 copy-start.4
  91.6 0.0 copy-start.5
  91.6 1.1 %collective-permute-start.14 = (f32[1,8,128]{2,1,0:T(8,128)S(1)}, f32[1,8,128]{2,1,0:T(8,128)S(1)}, u32[]{:S(2)}, u32[]{:S(2)}) collective-permute-start(f32[1,8,128]{2,1,0:T(8,128)S(1)} %bitcast.11), channel_id=1, source_target_pairs={{0,4},{1,5},{2,6},{3,7},{4,8},{5,9},{6,10},{7,11},{8,12},{9,13},{1... | collective-permute-start | bytes 12296 | tf_op jit(solution)/shard_map/ppermute | solution.py:50
  92.7 2.4 %collective-permute-start.13 = (f32[1,8,128]{2,1,0:T(8,128)S(1)}, f32[1,8,128]{2,1,0:T(8,128)S(1)}, u32[]{:S(2)}, u32[]{:S(2)}) collective-permute-start(f32[1,8,128]{2,1,0:T(8,128)S(1)} %bitcast.12), channel_id=1, source_target_pairs={{0,8},{1,9},{2,10},{3,11},{4,12},{5,13},{6,14},{7,15},{8,0},{9,1},... | collective-permute-start | bytes 12296 | tf_op jit(solution)/shard_map/ppermute | solution.py:50
  95.1 1.0 collective-permute-start.12
  96.1 0.8 collective-permute-done.14.refs_3_
  97.0 0.0 copy-start.10
  97.0 0.2 collective-permute-done.13.refs_2_
  97.2 0.0 copy-start.11
  97.2 1.5 %collective-permute-done.12.refs_1_ = f32[1,8,128]{2,1,0:T(8,128)S(1)} collective-permute-done((f32[1,8,128]{2,1,0:T(8,128)S(1)}, f32[1,8,128]{2,1,0:T(8,128)S(1)}, u32[]{:S(2)}, u32[]{:S(2)}) %collective-permute-start.12) | collective-permute-done | bytes 4128 | tf_op jit(solution)/shard_map/ppermute | solution.py:50
  98.7 0.0 copy-done.4
  98.7 0.0 copy-done.5
  98.7 0.0 copy-done.10
  98.7 0.0 copy-done.11
  98.7 0.5 copy-done.12
  99.3 1.2 %collective-permute-start.15 = (f32[4,8,128]{2,1,0:T(8,128)S(1)}, f32[4,8,128]{2,1,0:T(8,128)S(1)}, u32[]{:S(2)}, u32[]{:S(2)}) collective-permute-start(f32[4,8,128]{2,1,0:T(8,128)S(1)} %pad_maximum_fusion.2), channel_id=1, source_target_pairs={{0,2},{1,3},{2,0},{3,1},{4,6},{5,7},{6,4},{7,5},{8,10},{9,11},{10,... | collective-permute-start | bytes 49160 | tf_op jit(solution)/shard_map/ppermute | solution.py:50
  100.5 0.0 collective-permute-start.16
  100.5 2.5 %collective-permute-done.15.refs_4_ = f32[4,8,128]{2,1,0:T(8,128)S(1)} collective-permute-done((f32[4,8,128]{2,1,0:T(8,128)S(1)}, f32[4,8,128]{2,1,0:T(8,128)S(1)}, u32[]{:S(2)}, u32[]{:S(2)}) %collective-permute-start.15) | collective-permute-done | bytes 16416 | tf_op jit(solution)/shard_map/ppermute | solution.py:50
  103.0 0.0 collective-permute-start.17
  103.0 0.0 collective-permute-done.16.refs_5_
  103.0 0.0 copy-start.8
  103.0 1.2 %collective-permute-done.17.refs_6_ = f32[4,8,128]{2,1,0:T(8,128)S(1)} collective-permute-done((f32[4,8,128]{2,1,0:T(8,128)S(1)}, f32[4,8,128]{2,1,0:T(8,128)S(1)}, u32[]{:S(2)}, u32[]{:S(2)}) %collective-permute-start.17) | collective-permute-done | bytes 16416 | tf_op jit(solution)/shard_map/ppermute | solution.py:50
  104.2 0.0 copy-done.7
  104.2 0.0 copy-done.8
  104.2 0.6 copy-done.9
  104.8 1.6 %last_update.1 = (f32[8,1024]{1,0:T(8,128)}, f32[8,1024]{1,0:T(8,128)}) custom-call(f32[8,1024]{1,0:T(8,128)} %copy-done, f32[8,1024]{1,0:T(8,128)} %copy-done.1, f32[8,1024]{1,0:T(8,128)} %copy-done.2, f32[8,1024]{1,0:T(8,128)} %copy-done.3, f32[8,128]{1,0:T(8,128)} %copy-done.5, f32[1,8,128]{2,1,0:T(8,128)} %bitcast.15, f32[1,8,128]{2,1,0:T(8,128)} %copy-done.12, ...), custom_call_target="tpu_custom_call" | custom-call | tf_op jit(solution)/shard_map/last_update/pallas_call | solution.py:231
  (8 shorter events, 0.0 us)
Async XLA Ops:
  1.4 7.6 %collective-permute-start.2 = (f32[1,16,1024]{2,1,0:T(8,128)S(1)}, f32[1,16,1024]{2,1,0:T(8,128)S(1)}, u32[]{:S(2)}, u32[]{:S(2)}) collective-permute-start(f32[1,16,1024]{2,1,0:T(8,128)S(1)} %maximum_bitcast_fusion.refs_0_), channel_id=1, source_target_pairs={{0,4},{1,5},{2,6},{3,7},{4,8},{5,9},{6,10},{7,11},{8,12},{9,13},{1... | collective-permute-start | bytes 196616 | tf_op jit(solution)/shard_map/ppermute | solution.py:50
  4.4 7.1 %collective-permute-start.1 = (f32[1,16,1024]{2,1,0:T(8,128)S(1)}, f32[1,16,1024]{2,1,0:T(8,128)S(1)}, u32[]{:S(2)}, u32[]{:S(2)}) collective-permute-start(f32[1,16,1024]{2,1,0:T(8,128)S(1)} %maximum_bitcast_fusion.refs_0_), channel_id=1, source_target_pairs={{0,8},{1,9},{2,10},{3,11},{4,12},{5,13},{6,14},{7,15},{8,0},{9,1},... | collective-permute-start | bytes 196616 | tf_op jit(solution)/shard_map/ppermute | solution.py:50
  7.0 4.7 %collective-permute-start = (f32[1,16,1024]{2,1,0:T(8,128)S(1)}, f32[1,16,1024]{2,1,0:T(8,128)S(1)}, u32[]{:S(2)}, u32[]{:S(2)}) collective-permute-start(f32[1,16,1024]{2,1,0:T(8,128)S(1)} %maximum_bitcast_fusion.refs_0_), channel_id=1, source_target_pairs={{0,12},{1,13},{2,14},{3,15},{4,0},{5,1},{6,2},{7,3},{8,4},{9,5},{1... | collective-permute-start | bytes 196616 | tf_op jit(solution)/shard_map/ppermute | solution.py:50
  11.7 7.9 %copy-start.13 = (f32[8]{0:T(128)S(1)}, f32[8]{0:T(128)}, u32[]{:S(2)}) copy-start(f32[8]{0:T(128)} %param.5) | copy-start | bytes 100
  11.8 9.4 %copy-start.6 = (f32[1024]{0:T(1024)S(1)}, f32[1024]{0:T(1024)}, u32[]{:S(2)}) copy-start(f32[1024]{0:T(1024)} %param.6) | copy-start | bytes 12292
  11.8 7.9 %collective-permute-start.3 = (f32[4,16,1024]{2,1,0:T(8,128)S(1)}, f32[4,16,1024]{2,1,0:T(8,128)S(1)}, u32[]{:S(2)}, u32[]{:S(2)}) collective-permute-start(f32[4,16,1024]{2,1,0:T(8,128)S(1)} %pad_maximum_fusion), channel_id=1, source_target_pairs={{0,2},{1,3},{2,0},{3,1},{4,6},{5,7},{6,4},{7,5},{8,10},{9,11},{10,... | collective-permute-start | bytes 786440 | tf_op jit(solution)/shard_map/ppermute | solution.py:50
  13.4 6.3 %collective-permute-start.4 = (f32[4,16,1024]{2,1,0:T(8,128)S(1)}, f32[4,16,1024]{2,1,0:T(8,128)S(1)}, u32[]{:S(2)}, u32[]{:S(2)}) collective-permute-start(f32[4,16,1024]{2,1,0:T(8,128)S(1)} %pad_maximum_fusion), channel_id=1, source_target_pairs={{0,1},{1,0},{2,3},{3,2},{4,5},{5,4},{6,7},{7,6},{8,9},{9,8},{10,11... | collective-permute-start | bytes 786440 | tf_op jit(solution)/shard_map/ppermute | solution.py:50
  19.6 1.5 %collective-permute-start.5 = (f32[4,16,1024]{2,1,0:T(8,128)S(1)}, f32[4,16,1024]{2,1,0:T(8,128)S(1)}, u32[]{:S(2)}, u32[]{:S(2)}) collective-permute-start(f32[4,16,1024]{2,1,0:T(8,128)S(1)} %collective-permute-done.3.refs_4_), channel_id=1, source_target_pairs={{0,1},{1,0},{2,3},{3,2},{4,5},{5,4},{6,7},{7,6},{8,9},{9,8},{10,11... | collective-permute-start | bytes 786440 | tf_op jit(solution)/shard_map/ppermute | solution.py:50
  48.0 5.9 %collective-permute-start.8 = (f32[1,8,1024]{2,1,0:T(8,128)S(1)}, f32[1,8,1024]{2,1,0:T(8,128)S(1)}, u32[]{:S(2)}, u32[]{:S(2)}) collective-permute-start(f32[1,8,1024]{2,1,0:T(8,128)S(1)} %bitcast.6), channel_id=1, source_target_pairs={{0,4},{1,5},{2,6},{3,7},{4,8},{5,9},{6,10},{7,11},{8,12},{9,13},{1... | collective-permute-start | bytes 98312 | tf_op jit(solution)/shard_map/ppermute | solution.py:50
  50.0 5.2 %collective-permute-start.7 = (f32[1,8,1024]{2,1,0:T(8,128)S(1)}, f32[1,8,1024]{2,1,0:T(8,128)S(1)}, u32[]{:S(2)}, u32[]{:S(2)}) collective-permute-start(f32[1,8,1024]{2,1,0:T(8,128)S(1)} %bitcast.7), channel_id=1, source_target_pairs={{0,8},{1,9},{2,10},{3,11},{4,12},{5,13},{6,14},{7,15},{8,0},{9,1},... | collective-permute-start | bytes 98312 | tf_op jit(solution)/shard_map/ppermute | solution.py:50
  50.3 4.9 %collective-permute-start.6 = (f32[1,8,1024]{2,1,0:T(8,128)S(1)}, f32[1,8,1024]{2,1,0:T(8,128)S(1)}, u32[]{:S(2)}, u32[]{:S(2)}) collective-permute-start(f32[1,8,1024]{2,1,0:T(8,128)S(1)} %bitcast.8), channel_id=1, source_target_pairs={{0,12},{1,13},{2,14},{3,15},{4,0},{5,1},{6,2},{7,3},{8,4},{9,5},{1... | collective-permute-start | bytes 98312 | tf_op jit(solution)/shard_map/ppermute | solution.py:50
  55.2 5.1 %collective-permute-start.9 = (f32[4,8,1024]{2,1,0:T(8,128)S(1)}, f32[4,8,1024]{2,1,0:T(8,128)S(1)}, u32[]{:S(2)}, u32[]{:S(2)}) collective-permute-start(f32[4,8,1024]{2,1,0:T(8,128)S(1)} %pad_maximum_fusion.1), channel_id=1, source_target_pairs={{0,2},{1,3},{2,0},{3,1},{4,6},{5,7},{6,4},{7,5},{8,10},{9,11},{10,... | collective-permute-start | bytes 393224 | tf_op jit(solution)/shard_map/ppermute | solution.py:50
  56.4 3.9 %collective-permute-start.10 = (f32[4,8,1024]{2,1,0:T(8,128)S(1)}, f32[4,8,1024]{2,1,0:T(8,128)S(1)}, u32[]{:S(2)}, u32[]{:S(2)}) collective-permute-start(f32[4,8,1024]{2,1,0:T(8,128)S(1)} %pad_maximum_fusion.1), channel_id=1, source_target_pairs={{0,1},{1,0},{2,3},{3,2},{4,5},{5,4},{6,7},{7,6},{8,9},{9,8},{10,11... | collective-permute-start | bytes 393224 | tf_op jit(solution)/shard_map/ppermute | solution.py:50
  60.3 1.3 %collective-permute-start.11 = (f32[4,8,1024]{2,1,0:T(8,128)S(1)}, f32[4,8,1024]{2,1,0:T(8,128)S(1)}, u32[]{:S(2)}, u32[]{:S(2)}) collective-permute-start(f32[4,8,1024]{2,1,0:T(8,128)S(1)} %collective-permute-done.9.refs_11_), channel_id=1, source_target_pairs={{0,1},{1,0},{2,3},{3,2},{4,5},{5,4},{6,7},{7,6},{8,9},{9,8},{10,11... | collective-permute-start | bytes 393224 | tf_op jit(solution)/shard_map/ppermute | solution.py:50
  89.1 0.6 copy-start
  89.7 0.6 copy-start.1
  90.3 0.6 copy-start.2
  91.0 0.6 copy-start.3
  91.6 7.1 %copy-start.4 = (f32[8,128]{1,0:T(8,128)}, f32[8,128]{1,0:T(8,128)S(1)}, u32[]{:S(2)}) copy-start(f32[8,128]{1,0:T(8,128)S(1)} %get-tuple-element.13) | copy-start | bytes 12292
  91.6 7.1 %copy-start.5 = (f32[8,128]{1,0:T(8,128)}, f32[8,128]{1,0:T(8,128)S(1)}, u32[]{:S(2)}) copy-start(f32[8,128]{1,0:T(8,128)S(1)} %get-tuple-element.12.norm_ref) | copy-start | bytes 12292
  91.6 5.4 %collective-permute-start.14 = (f32[1,8,128]{2,1,0:T(8,128)S(1)}, f32[1,8,128]{2,1,0:T(8,128)S(1)}, u32[]{:S(2)}, u32[]{:S(2)}) collective-permute-start(f32[1,8,128]{2,1,0:T(8,128)S(1)} %bitcast.11), channel_id=1, source_target_pairs={{0,4},{1,5},{2,6},{3,7},{4,8},{5,9},{6,10},{7,11},{8,12},{9,13},{1... | collective-permute-start | bytes 12296 | tf_op jit(solution)/shard_map/ppermute | solution.py:50
  92.7 4.5 %collective-permute-start.13 = (f32[1,8,128]{2,1,0:T(8,128)S(1)}, f32[1,8,128]{2,1,0:T(8,128)S(1)}, u32[]{:S(2)}, u32[]{:S(2)}) collective-permute-start(f32[1,8,128]{2,1,0:T(8,128)S(1)} %bitcast.12), channel_id=1, source_target_pairs={{0,8},{1,9},{2,10},{3,11},{4,12},{5,13},{6,14},{7,15},{8,0},{9,1},... | collective-permute-start | bytes 12296 | tf_op jit(solution)/shard_map/ppermute | solution.py:50
  95.1 3.6 %collective-permute-start.12 = (f32[1,8,128]{2,1,0:T(8,128)S(1)}, f32[1,8,128]{2,1,0:T(8,128)S(1)}, u32[]{:S(2)}, u32[]{:S(2)}) collective-permute-start(f32[1,8,128]{2,1,0:T(8,128)S(1)} %bitcast.13), channel_id=1, source_target_pairs={{0,12},{1,13},{2,14},{3,15},{4,0},{5,1},{6,2},{7,3},{8,4},{9,5},{1... | collective-permute-start | bytes 12296 | tf_op jit(solution)/shard_map/ppermute | solution.py:50
  97.0 1.7 %copy-start.10 = (f32[1,8,128]{2,1,0:T(8,128)}, f32[1,8,128]{2,1,0:T(8,128)S(1)}, u32[]{:S(2)}) copy-start(f32[1,8,128]{2,1,0:T(8,128)S(1)} %collective-permute-done.14.refs_3_) | copy-start | bytes 12292
  97.2 1.5 %copy-start.11 = (f32[1,8,128]{2,1,0:T(8,128)}, f32[1,8,128]{2,1,0:T(8,128)S(1)}, u32[]{:S(2)}) copy-start(f32[1,8,128]{2,1,0:T(8,128)S(1)} %collective-permute-done.13.refs_2_) | copy-start | bytes 12292
  98.7 0.6 copy-start.12
  99.3 3.7 %collective-permute-start.15 = (f32[4,8,128]{2,1,0:T(8,128)S(1)}, f32[4,8,128]{2,1,0:T(8,128)S(1)}, u32[]{:S(2)}, u32[]{:S(2)}) collective-permute-start(f32[4,8,128]{2,1,0:T(8,128)S(1)} %pad_maximum_fusion.2), channel_id=1, source_target_pairs={{0,2},{1,3},{2,0},{3,1},{4,6},{5,7},{6,4},{7,5},{8,10},{9,11},{10,... | collective-permute-start | bytes 49160 | tf_op jit(solution)/shard_map/ppermute | solution.py:50
  100.5 2.5 %collective-permute-start.16 = (f32[4,8,128]{2,1,0:T(8,128)S(1)}, f32[4,8,128]{2,1,0:T(8,128)S(1)}, u32[]{:S(2)}, u32[]{:S(2)}) collective-permute-start(f32[4,8,128]{2,1,0:T(8,128)S(1)} %pad_maximum_fusion.2), channel_id=1, source_target_pairs={{0,1},{1,0},{2,3},{3,2},{4,5},{5,4},{6,7},{7,6},{8,9},{9,8},{10,11... | collective-permute-start | bytes 49160 | tf_op jit(solution)/shard_map/ppermute | solution.py:50
  103.0 1.2 %copy-start.7 = (f32[4,8,128]{2,1,0:T(8,128)}, f32[4,8,128]{2,1,0:T(8,128)S(1)}, u32[]{:S(2)}) copy-start(f32[4,8,128]{2,1,0:T(8,128)S(1)} %collective-permute-done.15.refs_4_) | copy-start | bytes 49156
  103.0 1.2 %collective-permute-start.17 = (f32[4,8,128]{2,1,0:T(8,128)S(1)}, f32[4,8,128]{2,1,0:T(8,128)S(1)}, u32[]{:S(2)}, u32[]{:S(2)}) collective-permute-start(f32[4,8,128]{2,1,0:T(8,128)S(1)} %collective-permute-done.15.refs_4_), channel_id=1, source_target_pairs={{0,1},{1,0},{2,3},{3,2},{4,5},{5,4},{6,7},{7,6},{8,9},{9,8},{10,11... | collective-permute-start | bytes 49160 | tf_op jit(solution)/shard_map/ppermute | solution.py:50
  103.0 1.2 %copy-start.8 = (f32[4,8,128]{2,1,0:T(8,128)}, f32[4,8,128]{2,1,0:T(8,128)S(1)}, u32[]{:S(2)}) copy-start(f32[4,8,128]{2,1,0:T(8,128)S(1)} %collective-permute-done.16.refs_5_) | copy-start | bytes 49156
  104.2 0.6 copy-start.9

commit v4 on v3

v4 whole, which is shorter than its diff:
```python
import functools
import math

import jax
import jax.numpy as jnp
from jax import lax
from jax.experimental import pallas as pl
from jax.experimental.pallas import tpu as pltpu
from jax.sharding import PartitionSpec as P

LOG2E = math.log2(math.e)
DEPTH = 64
TILE = 256
F32 = jnp.float32
BF16 = jnp.bfloat16


def pieces(value, count):
    parts = []
    for _ in range(count):
        part = value.astype(BF16).astype(F32)
        parts.append(part)
        value = value - part
    return parts


def exponent_rows(points, factor, visiting):
    big, mid, low = pieces(points * factor, 3)
    half_sq = jnp.sum(points * points, axis=0, keepdims=True) * (-0.5 * LOG2E)
    sq_parts = pieces(half_sq, 3)
    row = lax.broadcasted_iota(jnp.int32, points.shape, 0)
    first = 0 if visiting else 3
    tail = jnp.where((row >= 3 - first) & (row < 6 - first), 1.0, 0.0)
    for k, part in enumerate(sq_parts):
        tail = jnp.where(row == first + k, part, tail)
    order = [big, big, big, mid, mid, low] if visiting else [big, mid, low, big, mid, big]
    return jnp.concatenate(order + [tail, jnp.zeros_like(tail)], axis=0)


def stacked(value):
    return jnp.concatenate(pieces(value, 2), axis=0).astype(BF16)


def shifted(value, stride, size, by):
    length = lax.axis_size("row")
    pairs = []
    for i in range(length):
        digit = (i // stride) % size
        pairs.append((i, i + ((digit - by) % size - digit) * stride))
    return lax.ppermute(value, "row", pairs)


def digits():
    chips = lax.axis_size("row") // 2
    near = 1
    while near * near * 4 <= chips:
        near *= 2
    return chips // near, near


def gathered(value):
    far, near = digits()
    own = value[None]
    line = [shifted(own, 2 * near, far, by) for by in range(1, far)]
    group = jnp.concatenate([own] + line, axis=0)
    beside = [shifted(group, 2, near, by) for by in range(1, near)]
    across = [shifted(g, 1, 2, 1) for g in [group] + beside]
    return [own], line, beside + across[:1], across[1:]


def summed(value):
    far, near = digits()
    value = sum([shifted(value, 2 * near, far, by) for by in range(1, far)], value)
    quad = [shifted(value, 1, 2, 1)]
    for by in range(1, near):
        beside = shifted(value, 2, near, by)
        quad += [beside, shifted(beside, 1, 2, 1)]
    return sum(quad, value)


def tables():
    far, near = digits()
    place = lax.axis_index("row")
    core = place % 2
    side = (place // 2 % near) // (near // 2)
    picks = jnp.arange(far // 2, dtype=jnp.int32) * 2
    first, second, last_first, last_second = [], [], [], []
    for k in range(near - 1):
        base = k * far
        shift = k + 1
        if 2 * shift == near:
            first.append(base + picks + side)
            second.append(base + picks + 1 - side)
        else:
            whole = base + jnp.arange(far, dtype=jnp.int32)
            (first if 2 * shift < near else second).append(whole)
    base = (near - 1) * far
    first.append(base + picks + core)
    second.append(base + picks + 1 - core)
    for k in range(near - 1):
        last_first.append(k * far + picks + core)
        last_second.append(k * far + picks + 1 - core)
    return [jnp.concatenate(t) for t in (first, second, last_first, last_second)]


def add_block(yt_ref, at, own_ref, dirs, acc_ref):
    for c in range(own_ref.shape[1] // TILE):
        cols = slice(c * TILE, (c + 1) * TILE)
        expo = jnp.dot(yt_ref[at], own_ref[:, cols], preferred_element_type=F32)
        weight = jnp.exp2(expo)
        high = weight.astype(BF16)
        low = (weight - high.astype(F32)).astype(BF16)
        acc_ref[:, cols] += jnp.dot(
            dirs, high, preferred_element_type=F32
        ) + jnp.dot(dirs, low, preferred_element_type=F32)


def folded(acc_ref):
    nrhs = acc_ref.shape[0] // 2
    return acc_ref[0:nrhs, :] + acc_ref[nrhs:, :]


def each(stacks, function):
    base = 0
    for ref in stacks:

        def block(b, carry, ref=ref, base=base):
            function(base + b, ref[b])
            return carry

        if ref.shape[0] == 1:
            block(0, 0)
        else:
            lax.fori_loop(0, ref.shape[0], block, 0)
        base += ref.shape[0]


def over_points(nfeat, nstacks, first, amplitude, *refs):
    scale_ref, *refs = refs
    own_ref = refs.pop(0) if not first else None
    sofar_ref = refs.pop(0) if not first else None
    noise_ref, mine_ref = (refs.pop(0), refs.pop(0)) if amplitude else (None, None)
    stacks = refs[:nstacks]
    refs = refs[nstacks:]
    if first:
        own_ref = refs.pop(0)
        own_ref[...] = exponent_rows(
            stacks[0][0, 0:nfeat, :] / scale_ref[...], 1.0, False
        ).astype(BF16)
    yt_ref, out_ref, dirs_ref, acc_ref = refs

    def prepare(b, value):
        rows = exponent_rows(value[0:nfeat, :] / scale_ref[...], LOG2E, True)
        yt_ref[b] = rows.T.astype(BF16)
        dirs_ref[b] = stacked(value[nfeat:, :])

    each(stacks, prepare)
    acc_ref[...] = jnp.zeros_like(acc_ref)

    def step(b, carry):
        add_block(yt_ref, b, own_ref, dirs_ref[b], acc_ref)
        return carry

    lax.fori_loop(0, yt_ref.shape[0], step, 0)
    total = folded(acc_ref)
    if not first:
        total = total + sofar_ref[...]
    if amplitude:
        total = amplitude * total + noise_ref[...] * mine_ref[0, nfeat:, :]
    out_ref[...] = total


def over_images(nstacks, table, sofar, form, amplitude, *refs):
    refs = list(refs)
    table_ref = refs.pop(0) if table else None
    sofar_ref = refs.pop(0) if sofar else None
    if form:
        once_ref, noise_ref, mine_ref = refs.pop(0), refs.pop(0), refs.pop(0)
    own_ref, yt_ref, *refs = refs
    stacks = refs[:nstacks]
    out_ref, *refs = refs[nstacks:]
    form_ref = refs.pop(0) if form else None
    dirs_ref, acc_ref = refs

    def prepare(b, value):
        dirs_ref[b] = stacked(value)

    each(stacks, prepare)
    acc_ref[...] = jnp.zeros_like(acc_ref)

    def step(s, carry):
        b = table_ref[s] if table else s
        add_block(yt_ref, b, own_ref, dirs_ref[b], acc_ref)
        return carry

    lax.fori_loop(0, table_ref.shape[0] if table else yt_ref.shape[0], step, 0)
    total = folded(acc_ref)
    if sofar:
        total = total + sofar_ref[...]
    if form:
        mine = mine_ref[0]
        twice = once_ref[...] + 2.0 * total
        inner = mine * (amplitude * twice + noise_ref[...] * mine)
        form_ref[...] = jnp.broadcast_to(
            jnp.sum(inner, axis=1, keepdims=True), form_ref.shape
        )
        total = total + once_ref[...]
    out_ref[...] = total


def scalars_kernel(nfeat, count, *refs):
    blocks = refs[:count]
    images = refs[count : 2 * count]
    out_ref = refs[2 * count]
    nothing = jnp.zeros((images[0].shape[1], images[0].shape[2]), F32)

    def walk(function, carry):
        for b_ref, m_ref in zip(blocks, images):

            def block(k, carry, b_ref=b_ref, m_ref=m_ref):
                return function(carry, b_ref[k, nfeat:, :], m_ref[k])

            carry = lax.fori_loop(0, b_ref.shape[0], block, carry)
        return carry

    def total(value):
        return jnp.sum(value, axis=1, keepdims=True)

    norm, curv, square = walk(
        lambda c, r, w: (c[0] + r * r, c[1] + r * w, c[2] + w * w), (nothing,) * 3
    )
    norm, curv, square = total(norm), total(curv), total(square)
    alpha = norm / curv

    def left(carry, r, w):
        rest = r - alpha * w
        return carry + rest * rest

    norm_next = total(walk(left, nothing))
    gain = 1.0 + norm_next / norm
    part = gain * (gain * curv - 2.0 * alpha * square)
    for k, value in enumerate((alpha, gain, norm_next, part)):
        out_ref[k] = jnp.broadcast_to(value, out_ref.shape[1:])


def last_kernel(
    nfeat, amplitude, scalars_ref, form_ref, total_ref, noise_ref, mine_ref, image_ref,
    sol_ref, res_ref,
):
    alpha, gain, norm_next, part = [scalars_ref[k][:, 0:1] for k in range(4)]
    alpha_next = norm_next / (part + alpha * alpha * form_ref[:, 0:1])
    rhs = mine_ref[0, nfeat:, :]
    image = image_ref[0]
    twice = amplitude * total_ref[...] + noise_ref[...] * image
    sol_ref[...] = alpha * rhs + alpha_next * (gain * rhs - alpha * image)
    res_ref[...] = (rhs - alpha * image) - alpha_next * (gain * image - alpha * twice)


def shards(features, lengthscale, noise, rhs):
    nfeat, width = features.shape
    nrhs = rhs.shape[0]
    amplitude = 1.0 / math.sqrt(width * lax.axis_size("row"))
    scale = lengthscale[:, None]
    noise = noise[None, :]
    field = jax.ShapeDtypeStruct((nrhs, width), F32)
    small = jax.ShapeDtypeStruct((nrhs, 128), F32)
    smem = pl.BlockSpec(memory_space=pltpu.SMEM)
    vmem = pl.BlockSpec(memory_space=pltpu.VMEM)

    def call(kernel, blocks, work, out_shape, operands, name, table=False):
        entries = work * width * width
        return pl.pallas_call(
            kernel,
            out_shape=out_shape,
            in_specs=[smem if table and k == 0 else vmem for k in range(len(operands))],
            scratch_shapes=[
                pltpu.VMEM((blocks, 2 * nrhs, width), BF16),
                pltpu.VMEM((2 * nrhs, width), F32),
            ],
            compiler_params=pltpu.CompilerParams(
                vmem_limit_bytes=min(16 * 1024 * 1024 + blocks * 1024 * width, 60 * 1024 * 1024)
            ),
            cost_estimate=pl.CostEstimate(
                flops=2 * entries * 4 * TILE, bytes_accessed=1024 * width, transcendentals=entries
            ),
            name=name,
        )(*operands)

    def amount(stacks):
        return sum(s.shape[0] for s in stacks)

    def points_shape(stacks):
        return jax.ShapeDtypeStruct((amount(stacks), width, DEPTH), BF16)

    groups = gathered(jnp.concatenate([features, rhs], axis=0))
    mine = groups[0][0]
    own_shape = jax.ShapeDtypeStruct((DEPTH, width), BF16)
    own, points, total = call(
        functools.partial(over_points, nfeat, 1, True, None),
        1, 1, (own_shape, points_shape(groups[0]), field), (scale, mine), "own_block",
    )
    prepared = [points]
    for k, stacks in enumerate(groups[1:]):
        final = k == 2
        points, total = call(
            functools.partial(over_points, nfeat, len(stacks), False, amplitude if final else None),
            amount(stacks), amount(stacks), (points_shape(stacks), field),
            (scale, own, total) + ((noise, mine) if final else ()) + tuple(stacks),
            "blocks_%d" % k,
        )
        prepared.append(points)
    images = gathered(total)
    image = images[0][0]

    def again(group, out, name, sofar=(), table=None, form=()):
        stacks = images[group]
        listed = () if table is None else (table,)
        work = amount(stacks) if table is None else table.shape[0]
        return call(
            functools.partial(
                over_images, len(stacks), table is not None, bool(sofar), bool(form), amplitude
            ),
            amount(stacks), work, out,
            listed + tuple(sofar) + tuple(form) + (own, prepared[group]) + tuple(stacks),
            name, table is not None,
        )

    first, second, last_first, last_second = tables()
    once = again(0, field, "own_again")
    once = again(1, field, "line_again", sofar=(once,))
    half = again(2, field, "beside_half", table=first)
    total, form = again(
        3, (field, small), "across_half", sofar=(half,), table=last_first,
        form=(once, noise, image),
    )
    form = summed(form)
    total = again(2, field, "beside_rest", sofar=(total,), table=second)
    total = again(3, field, "across_rest", sofar=(total,), table=last_second)
    flat = [s for g in groups for s in g]
    flat_images = [s for g in images for s in g]
    scalars = pl.pallas_call(
        functools.partial(scalars_kernel, nfeat, len(flat)),
        out_shape=jax.ShapeDtypeStruct((4, nrhs, 128), F32),
        name="scalars",
    )(*flat, *flat_images)
    return pl.pallas_call(
        functools.partial(last_kernel, nfeat, amplitude),
        out_shape=(field, field),
        name="last_update",
    )(scalars, form, total, noise, mine, image)


def solution(mesh):
    in_specs = (P(None, ("grp", "row")), P(), P(("grp", "row")), P(None, ("grp", "row")))
    out_specs = (P(None, ("grp", "row")), P(None, ("grp", "row")))
    return jax.shard_map(shards, mesh=mesh, in_specs=in_specs, out_specs=out_specs, check_vma=False)
```

time: 107 us -> 89.9 us (0.84)
  waiting for transfers between devices: 25.2 us -> 11.5 us
  starting transfers between devices: 20.1 us -> 17.1 us
  local copies, waits for them, and re-layouts: 3.71 us -> 1.43 us
  Pallas kernels: 55.9 us -> 57.1 us
    ppermute x18, waiting for transfers between devices: 25.2 us -> 11.5 us  [shifted(): return lax.ppermute(value, 'row', pairs)]
    ppermute x18, starting transfers between devices: 20.1 us -> 17.1 us  [shifted(): return lax.ppermute(value, 'row', pairs)]
    unnamed x28 -> x32, local copies, waits for them, and re-layouts: 3.63 us -> 0.7 us
    pallas_call x3 -> x12, Pallas kernels: 55.9 us -> 57.1 us  [the longest x10 53 us: call(): pl.pallas_call(kernel, out_shape=out_shape, in_specs=[smem if table and k...]
  transfers between devices with their start and end apart: 18 -> 18, of which waited for: 14 -> 7; matrix products, arithmetic and copies ran while one was open for 0% -> 1% of each run, Pallas kernels for 0% -> 50%
where the time goes in v4:
time: 89.9 us; the launch traced here: 89.7 us
  Pallas kernels  57.1 us (64%)
  starting transfers between devices  17.1 us (19%)
  waiting for transfers between devices  11.5 us (13%)
  other arithmetic  1.59 us (2%)
  local copies, waits for them, and re-layouts  1.43 us (2%)
    pallas_call x10, Pallas kernels, call(): pl.pallas_call(kernel, out_shape=out_shape, in_specs=[smem if table and k...  53 us
    ppermute x18, starting transfers between devices, shifted(): return lax.ppermute(value, 'row', pairs)  17.1 us
    ppermute x18, waiting for transfers between devices, shifted(): return lax.ppermute(value, 'row', pairs)  11.5 us
    pallas_call x1, Pallas kernels, shards(): pl.pallas_call(functools.partial(scalars_kernel, nfeat, len(flat)), out_s...  2.49 us
  transfers between devices with their start and end apart: 18, of which 7 were waited for; matrix products, arithmetic and copies ran while one was open for 1% of the time, Pallas kernels for 50%

profile of v4, /device:TPU:0, one launch (start us, length us, event | category | flops | bytes accessed | tf_op | source)
XLA Modules:
  0.0 89.7 jit_solution(13689891619437532597)
XLA Ops:
  0.6 0.8 maximum_bitcast_fusion.refs_1_.refs_4_.refs_0_.mine_ref
  1.4 5.1 %collective-permute-start = (f32[1,16,1024]{2,1,0:T(8,128)S(1)}, f32[1,16,1024]{2,1,0:T(8,128)S(1)}, u32[]{:S(2)}, u32[]{:S(2)}) collective-permute-start(f32[1,16,1024]{2,1,0:T(8,128)S(1)} %maximum_bitcast_fusion.refs_1_.refs_4_.refs_0_.mine_ref), channel_id=1, source_target_pairs={{0,12},{1,13},{2,14},{3,15},{4,0},{5,1},{6,2},{7,3},{8,4},{9,5},{1... | collective-permute-start | bytes 196616 | tf_op jit(solution)/shard_map/ppermute | solution.py:50
  6.5 0.0 collective-permute-start.1
  6.5 1.0 %collective-permute-start.2 = (f32[1,16,1024]{2,1,0:T(8,128)S(1)}, f32[1,16,1024]{2,1,0:T(8,128)S(1)}, u32[]{:S(2)}, u32[]{:S(2)}) collective-permute-start(f32[1,16,1024]{2,1,0:T(8,128)S(1)} %maximum_bitcast_fusion.refs_1_.refs_4_.refs_0_.mine_ref), channel_id=1, source_target_pairs={{0,4},{1,5},{2,6},{3,7},{4,8},{5,9},{6,10},{7,11},{8,12},{9,13},{1... | collective-permute-start | bytes 196616 | tf_op jit(solution)/shard_map/ppermute | solution.py:50
  7.5 0.7 copy.9.refs_0_
  8.3 1.6 %own_block.1 = (bf16[64,1024]{1,0:T(8,128)(2,1)S(1)}, bf16[1,1024,64]{2,1,0:T(8,128)(2,1)S(1)}, f32[8,1024]{1,0:T(8,128)S(1)}) custom-call(f32[8,1]{1,0:T(8,128)S(1)} %copy.9.refs_0_, f32[1,16,1024]{2,1,0:T(8,128)S(1)} %maximum_bitcast_fusion.refs_1_.refs_4_.refs_0_.mine_ref), custom_call_target="tpu_custom_call" | custom-call | flops 2147483648 | bytes 1048576 | tf_op jit(solution)/shard_map/own_block/pallas_call | solution.py:272
  9.9 0.1 pad_add_fusion.refs_0_
  10.0 0.0 collective-permute-done.refs_3_.refs_1_
  10.0 3.0 %collective-permute-done.1.refs_4_.refs_2_ = f32[1,16,1024]{2,1,0:T(8,128)S(1)} collective-permute-done((f32[1,16,1024]{2,1,0:T(8,128)S(1)}, f32[1,16,1024]{2,1,0:T(8,128)S(1)}, u32[]{:S(2)}, u32[]{:S(2)}) %collective-permute-start.1) | collective-permute-done | bytes 65568 | tf_op jit(solution)/shard_map/ppermute | solution.py:50
  13.0 0.0 collective-permute-done.2.refs_5_.refs_3_
  13.0 1.6 %collective-permute-start.3 = (f32[4,16,1024]{2,1,0:T(8,128)S(1)}, f32[4,16,1024]{2,1,0:T(8,128)S(1)}, u32[]{:S(2)}, u32[]{:S(2)}) collective-permute-start(f32[4,16,1024]{2,1,0:T(8,128)S(1)} %pad_maximum_fusion), channel_id=1, source_target_pairs={{0,2},{1,3},{2,0},{3,1},{4,6},{5,7},{6,4},{7,5},{8,10},{9,11},{10,... | collective-permute-start | bytes 786440 | tf_op jit(solution)/shard_map/ppermute | solution.py:50
  14.6 0.0 collective-permute-start.4
  14.6 4.8 %blocks_0.1 = (bf16[3,1024,64]{2,1,0:T(8,128)(2,1)S(1)}, f32[8,1024]{1,0:T(8,128)S(1)}) custom-call(f32[8,1]{1,0:T(8,128)S(1)} %copy.9.refs_0_, bf16[64,1024]{1,0:T(8,128)(2,1)S(1)} %get-tuple-element.13.refs_1_.refs_0_.refs_5_.refs_2_, f32[8,1024]{1,0:T(8,128)S(1)} %get-tuple-element.14.refs_2_, f32[1,16,1024]{2,1,0:T(8,128)S(1)} %collective-permute-done.refs_3_.refs_1_, ...), custom_call_target="tpu_custom_call" | custom-call | flops 6442450944 | bytes 1048576 | tf_op jit(solution)/shard_map/blocks_0/pallas_call | solution.py:272
  19.4 0.0 copy-done.5
  19.4 1.7 %collective-permute-done.3.refs_3_.refs_4_ = f32[4,16,1024]{2,1,0:T(8,128)S(1)} collective-permute-done((f32[4,16,1024]{2,1,0:T(8,128)S(1)}, f32[4,16,1024]{2,1,0:T(8,128)S(1)}, u32[]{:S(2)}, u32[]{:S(2)}) %collective-permute-start.3) | collective-permute-done | bytes 262176 | tf_op jit(solution)/shard_map/ppermute | solution.py:50
  21.1 0.0 collective-permute-start.5
  21.1 0.0 collective-permute-done.4.refs_4_.refs_5_
  21.1 0.0 copy-start.3
  21.1 0.0 copy-start.15
  21.1 13.6 %blocks_1.1 = (bf16[8,1024,64]{2,1,0:T(8,128)(2,1)S(1)}, f32[8,1024]{1,0:T(8,128)S(1)}) custom-call(f32[8,1]{1,0:T(8,128)S(1)} %copy.9.refs_0_, bf16[64,1024]{1,0:T(8,128)(2,1)S(1)} %get-tuple-element.13.refs_1_.refs_0_.refs_5_.refs_2_, f32[8,1024]{1,0:T(8,128)S(1)} %get-tuple-element.15.refs_2_, f32[4,16,1024]{2,1,0:T(8,128)S(1)} %collective-permute-done.3.refs_3_.refs_4_, ...), custom_call_target="tpu_custom_call" | custom-call | flops 17179869184 | bytes 1048576 | tf_op jit(solution)/shard_map/blocks_1/pallas_call | solution.py:272
  34.7 0.0 copy-done.2
  34.8 0.0 collective-permute-done.5.refs_5_.refs_6_
  34.8 0.0 copy-start.4
  34.8 0.0 copy-done
  34.8 0.0 copy-done.15
  34.8 6.8 %blocks_2.1 = (bf16[4,1024,64]{2,1,0:T(8,128)(2,1)S(1)}, f32[8,1024]{1,0:T(8,128)S(1)}) custom-call(f32[8,1]{1,0:T(8,128)S(1)} %copy.9.refs_0_, bf16[64,1024]{1,0:T(8,128)(2,1)S(1)} %get-tuple-element.13.refs_1_.refs_0_.refs_5_.refs_2_, f32[8,1024]{1,0:T(8,128)S(1)} %get-tuple-element.16.refs_2_, f32[1,1024]{1,0:T(1,128)S(1)} %bitcast.14, ...), custom_call_target="tpu_custom_call" | custom-call | flops 8589934592 | bytes 1048576 | tf_op jit(solution)/shard_map/blocks_2/pallas_call | solution.py:272
  41.6 0.8 collective-permute-start.6
  42.5 0.7 collective-permute-start.7
  43.2 1.9 %collective-permute-start.8 = (f32[1,8,1024]{2,1,0:T(8,128)S(1)}, f32[1,8,1024]{2,1,0:T(8,128)S(1)}, u32[]{:S(2)}, u32[]{:S(2)}) collective-permute-start(f32[1,8,1024]{2,1,0:T(8,128)S(1)} %bitcast.7), channel_id=1, source_target_pairs={{0,4},{1,5},{2,6},{3,7},{4,8},{5,9},{6,10},{7,11},{8,12},{9,13},{1... | collective-permute-start | bytes 98312 | tf_op jit(solution)/shard_map/ppermute | solution.py:50
  45.1 1.5 %own_again.1.refs_0_ = f32[8,1024]{1,0:T(8,128)S(1)} custom-call(bf16[64,1024]{1,0:T(8,128)(2,1)S(1)} %get-tuple-element.13.refs_1_.refs_0_.refs_5_.refs_2_, bf16[1,1024,64]{2,1,0:T(8,128)(2,1)S(1)} %get-tuple-element.19.refs_1_, f32[1,8,1024]{2,1,0:T(8,128)S(1)} %bitcast.8), custom_call_target="tpu_custom_call" | custom-call | flops 2147483648 | bytes 1048576 | tf_op jit(solution)/shard_map/own_again/pallas_call | solution.py:272
  46.6 0.0 collective-permute-done.6.refs_8_.refs_3_
  46.6 0.9 %collective-permute-done.7.refs_9_.refs_4_ = f32[1,8,1024]{2,1,0:T(8,128)S(1)} collective-permute-done((f32[1,8,1024]{2,1,0:T(8,128)S(1)}, f32[1,8,1024]{2,1,0:T(8,128)S(1)}, u32[]{:S(2)}, u32[]{:S(2)}) %collective-permute-start.7) | collective-permute-done | bytes 32800 | tf_op jit(solution)/shard_map/ppermute | solution.py:50
  47.5 1.3 %collective-permute-done.8.refs_10_.refs_5_ = f32[1,8,1024]{2,1,0:T(8,128)S(1)} collective-permute-done((f32[1,8,1024]{2,1,0:T(8,128)S(1)}, f32[1,8,1024]{2,1,0:T(8,128)S(1)}, u32[]{:S(2)}, u32[]{:S(2)}) %collective-permute-start.8) | collective-permute-done | bytes 32800 | tf_op jit(solution)/shard_map/ppermute | solution.py:50
  48.9 0.1 collective-permute-start.10
  49.0 1.6 %collective-permute-start.9 = (f32[4,8,1024]{2,1,0:T(8,128)S(1)}, f32[4,8,1024]{2,1,0:T(8,128)S(1)}, u32[]{:S(2)}, u32[]{:S(2)}) collective-permute-start(f32[4,8,1024]{2,1,0:T(8,128)S(1)} %pad_maximum_fusion.1), channel_id=1, source_target_pairs={{0,2},{1,3},{2,0},{3,1},{4,6},{5,7},{6,4},{7,5},{8,10},{9,11},{10,... | collective-permute-start | bytes 393224 | tf_op jit(solution)/shard_map/ppermute | solution.py:50
  50.6 4.5 %line_again.1.refs_2_ = f32[8,1024]{1,0:T(8,128)S(1)} custom-call(f32[8,1024]{1,0:T(8,128)S(1)} %own_again.1.refs_0_, bf16[64,1024]{1,0:T(8,128)(2,1)S(1)} %get-tuple-element.13.refs_1_.refs_0_.refs_5_.refs_2_, bf16[3,1024,64]{2,1,0:T(8,128)(2,1)S(1)} %get-tuple-element.20.refs_2_, f32[1,8,1024]{2,1,0:T(8,128)S(1)} %collective-permute-done.6.refs_8_.refs_3_, ...), custom_call_target="tpu_custom_call" | custom-call | flops 6442450944 | bytes 1048576 | tf_op jit(solution)/shard_map/line_again/pallas_call | solution.py:272
  55.0 0.0 copy-done.11
  55.0 0.0 copy-done.12
  55.1 0.0 collective-permute-done.9.refs_11_.refs_3_.refs_4_
  55.1 0.2 collective-permute-start.11
  55.3 0.0 collective-permute-done.10.refs_12_.refs_4_.refs_5_
  55.3 6.5 %beside_half.1.refs_1_ = f32[8,1024]{1,0:T(8,128)S(1)} custom-call(s32[4]{0:T(128)S(1)} %pad_add_fusion.refs_0_, bf16[64,1024]{1,0:T(8,128)(2,1)S(1)} %get-tuple-element.13.refs_1_.refs_0_.refs_5_.refs_2_, bf16[8,1024,64]{2,1,0:T(8,128)(2,1)S(1)} %get-tuple-element.18.refs_2_.refs_3_, f32[4,8,1024]{2,1,0:T(8,128)S(1)} %collective-permute-done.9.refs_11_.refs_3_.refs_4_, ...), custom_call_target="tpu_custom_call" | custom-call | flops 8589934592 | bytes 1048576 | tf_op jit(solution)/shard_map/beside_half/pallas_call | solution.py:272
  61.9 0.0 collective-permute-done.11.refs_13_.refs_7_.refs_4_
  61.9 3.6 %across_half.1 = (f32[8,1024]{1,0:T(8,128)S(1)}, f32[8,128]{1,0:T(8,128)S(1)}) custom-call(s32[2]{0:T(128)S(1)} %fusion.2.refs_0_, f32[8,1024]{1,0:T(8,128)S(1)} %beside_half.1.refs_1_, f32[8,1024]{1,0:T(8,128)S(1)} %line_again.1.refs_2_, f32[1,1024]{1,0:T(1,128)S(1)} %bitcast.15, f32[1,8,1024]{2,1,0:T(8,128)S(1)} %bitcast.10, ...), custom_call_target="tpu_custom_call" | custom-call | flops 4294967296 | bytes 1048576 | tf_op jit(solution)/shard_map/across_half/pallas_call | solution.py:272
  65.5 1.1 %collective-permute-start.12 = (f32[8,128]{1,0:T(8,128)S(1)}, f32[8,128]{1,0:T(8,128)S(1)}, u32[]{:S(2)}, u32[]{:S(2)}) collective-permute-start(f32[8,128]{1,0:T(8,128)S(1)} %get-tuple-element.22), channel_id=1, source_target_pairs={{0,12},{1,13},{2,14},{3,15},{4,0},{5,1},{6,2},{7,3},{8,4},{9,5},{1... | collective-permute-start | bytes 12296 | tf_op jit(solution)/shard_map/ppermute | solution.py:50
  66.7 0.5 collective-permute-start.13
  67.1 0.8 collective-permute-start.14
  67.9 0.1 pad_add_fusion.1.refs_0_
  68.0 1.1 %collective-permute-done.12 = f32[8,128]{1,0:T(8,128)S(1)} collective-permute-done((f32[8,128]{1,0:T(8,128)S(1)}, f32[8,128]{1,0:T(8,128)S(1)}, u32[]{:S(2)}, u32[]{:S(2)}) %collective-permute-start.12) | collective-permute-done | bytes 4128 | tf_op jit(solution)/shard_map/ppermute | solution.py:50
  69.1 2.0 %collective-permute-done.13 = f32[8,128]{1,0:T(8,128)S(1)} collective-permute-done((f32[8,128]{1,0:T(8,128)S(1)}, f32[8,128]{1,0:T(8,128)S(1)}, u32[]{:S(2)}, u32[]{:S(2)}) %collective-permute-start.13) | collective-permute-done | bytes 4128 | tf_op jit(solution)/shard_map/ppermute | solution.py:50
  71.2 1.4 %collective-permute-done.14 = f32[8,128]{1,0:T(8,128)S(1)} collective-permute-done((f32[8,128]{1,0:T(8,128)S(1)}, f32[8,128]{1,0:T(8,128)S(1)}, u32[]{:S(2)}, u32[]{:S(2)}) %collective-permute-start.14) | collective-permute-done | bytes 4128 | tf_op jit(solution)/shard_map/ppermute | solution.py:50
  72.6 1.1 %collective-permute-start.16 = (f32[8,128]{1,0:T(8,128)S(1)}, f32[8,128]{1,0:T(8,128)S(1)}, u32[]{:S(2)}, u32[]{:S(2)}) collective-permute-start(f32[8,128]{1,0:T(8,128)S(1)} %add_add_fusion.1), channel_id=1, source_target_pairs={{0,2},{1,3},{2,0},{3,1},{4,6},{5,7},{6,4},{7,5},{8,10},{9,11},{10,... | collective-permute-start | bytes 12296 | tf_op jit(solution)/shard_map/ppermute | solution.py:50
  73.7 6.5 %beside_rest.1.refs_1_ = f32[8,1024]{1,0:T(8,128)S(1)} custom-call(s32[4]{0:T(128)S(1)} %pad_add_fusion.1.refs_0_, f32[8,1024]{1,0:T(8,128)S(1)} %get-tuple-element.23.refs_1_, bf16[64,1024]{1,0:T(8,128)(2,1)S(1)} %get-tuple-element.13.refs_1_.refs_0_.refs_5_.refs_2_, bf16[8,1024,64]{2,1,0:T(8,128)(2,1)S(1)} %get-tuple-element.18.refs_2_.refs_3_, ...), custom_call_target="tpu_custom_call" | custom-call | flops 8589934592 | bytes 1048576 | tf_op jit(solution)/shard_map/beside_rest/pallas_call | solution.py:272
  80.2 0.0 collective-permute-start.15
  80.3 0.0 collective-permute-done.16
  80.3 0.5 collective-permute-start.17
  80.8 3.5 %across_rest.1.total_ref = f32[8,1024]{1,0:T(8,128)S(1)} custom-call(s32[2]{0:T(128)S(1)} %fusion.4.refs_0_, f32[8,1024]{1,0:T(8,128)S(1)} %beside_rest.1.refs_1_, bf16[64,1024]{1,0:T(8,128)(2,1)S(1)} %get-tuple-element.13.refs_1_.refs_0_.refs_5_.refs_2_, bf16[4,1024,64]{2,1,0:T(8,128)(2,1)S(1)} %get-tuple-element.21.refs_6_.refs_3_, ...), custom_call_target="tpu_custom_call" | custom-call | flops 4294967296 | bytes 1048576 | tf_op jit(solution)/shard_map/across_rest/pallas_call | solution.py:272
  84.3 0.0 copy-start.14
  84.3 0.6 copy-done.14
  84.9 2.5 %scalars.1.scalars_ref = f32[4,8,128]{2,1,0:T(8,128)} custom-call(f32[1,16,1024]{2,1,0:T(8,128)} %copy-done, f32[1,16,1024]{2,1,0:T(8,128)} %copy-done.5, f32[1,16,1024]{2,1,0:T(8,128)} %copy-done.6, f32[1,16,1024]{2,1,0:T(8,128)} %copy-done.7, f32[4,16,1024]{2,1,0:T(8,128)} %copy-done.2, f32[4,16,1024]{2,1,0:T(8,128)} %copy-done.3, ...), custom_call_target="tpu_custom_call" | custom-call | tf_op jit(solution)/shard_map/scalars/pallas_call | solution.py:341
  87.4 0.0 collective-permute-done.15
  87.4 0.0 collective-permute-done.17
  87.4 0.6 add_add_fusion.form_ref
  88.0 1.6 %last_update.1 = (f32[8,1024]{1,0:T(8,128)}, f32[8,1024]{1,0:T(8,128)}) custom-call(f32[4,8,128]{2,1,0:T(8,128)} %scalars.1.scalars_ref, f32[8,128]{1,0:T(8,128)} %add_add_fusion.form_ref, f32[8,1024]{1,0:T(8,128)} %copy-done.14, f32[1,1024]{1,0:T(1,128)} %bitcast.13, f32[1,16,1024]{2,1,0:T(8,128)} %copy-done, f32[1,8,1024]{2,1,0:T(8,128)} %bitcast.12), custom_call_target="tpu_custom_call" | custom-call | tf_op jit(solution)/shard_map/last_update/pallas_call | solution.py:346
  (28 shorter events, 0.1 us)
Async XLA Ops:
  1.4 33.4 %copy-start = (f32[1,16,1024]{2,1,0:T(8,128)}, f32[1,16,1024]{2,1,0:T(8,128)S(1)}, u32[]{:S(2)}) copy-start(f32[1,16,1024]{2,1,0:T(8,128)S(1)} %maximum_bitcast_fusion.refs_1_.refs_4_.refs_0_.mine_ref) | copy-start | bytes 196612
  1.4 8.6 %collective-permute-start = (f32[1,16,1024]{2,1,0:T(8,128)S(1)}, f32[1,16,1024]{2,1,0:T(8,128)S(1)}, u32[]{:S(2)}, u32[]{:S(2)}) collective-permute-start(f32[1,16,1024]{2,1,0:T(8,128)S(1)} %maximum_bitcast_fusion.refs_1_.refs_4_.refs_0_.mine_ref), channel_id=1, source_target_pairs={{0,12},{1,13},{2,14},{3,15},{4,0},{5,1},{6,2},{7,3},{8,4},{9,5},{1... | collective-permute-start | bytes 196616 | tf_op jit(solution)/shard_map/ppermute | solution.py:50
  6.5 6.5 %collective-permute-start.1 = (f32[1,16,1024]{2,1,0:T(8,128)S(1)}, f32[1,16,1024]{2,1,0:T(8,128)S(1)}, u32[]{:S(2)}, u32[]{:S(2)}) collective-permute-start(f32[1,16,1024]{2,1,0:T(8,128)S(1)} %maximum_bitcast_fusion.refs_1_.refs_4_.refs_0_.mine_ref), channel_id=1, source_target_pairs={{0,8},{1,9},{2,10},{3,11},{4,12},{5,13},{6,14},{7,15},{8,0},{9,1},... | collective-permute-start | bytes 196616 | tf_op jit(solution)/shard_map/ppermute | solution.py:50
  6.5 6.5 %collective-permute-start.2 = (f32[1,16,1024]{2,1,0:T(8,128)S(1)}, f32[1,16,1024]{2,1,0:T(8,128)S(1)}, u32[]{:S(2)}, u32[]{:S(2)}) collective-permute-start(f32[1,16,1024]{2,1,0:T(8,128)S(1)} %maximum_bitcast_fusion.refs_1_.refs_4_.refs_0_.mine_ref), channel_id=1, source_target_pairs={{0,4},{1,5},{2,6},{3,7},{4,8},{5,9},{6,10},{7,11},{8,12},{9,13},{1... | collective-permute-start | bytes 196616 | tf_op jit(solution)/shard_map/ppermute | solution.py:50
  10.0 9.4 %copy-start.5 = (f32[1,16,1024]{2,1,0:T(8,128)}, f32[1,16,1024]{2,1,0:T(8,128)S(1)}, u32[]{:S(2)}) copy-start(f32[1,16,1024]{2,1,0:T(8,128)S(1)} %collective-permute-done.refs_3_.refs_1_) | copy-start | bytes 196612
  13.0 6.4 %copy-start.6 = (f32[1,16,1024]{2,1,0:T(8,128)}, f32[1,16,1024]{2,1,0:T(8,128)S(1)}, u32[]{:S(2)}) copy-start(f32[1,16,1024]{2,1,0:T(8,128)S(1)} %collective-permute-done.1.refs_4_.refs_2_) | copy-start | bytes 196612
  13.0 6.4 %copy-start.7 = (f32[1,16,1024]{2,1,0:T(8,128)}, f32[1,16,1024]{2,1,0:T(8,128)S(1)}, u32[]{:S(2)}) copy-start(f32[1,16,1024]{2,1,0:T(8,128)S(1)} %collective-permute-done.2.refs_5_.refs_3_) | copy-start | bytes 196612
  13.0 8.1 %collective-permute-start.3 = (f32[4,16,1024]{2,1,0:T(8,128)S(1)}, f32[4,16,1024]{2,1,0:T(8,128)S(1)}, u32[]{:S(2)}, u32[]{:S(2)}) collective-permute-start(f32[4,16,1024]{2,1,0:T(8,128)S(1)} %pad_maximum_fusion), channel_id=1, source_target_pairs={{0,2},{1,3},{2,0},{3,1},{4,6},{5,7},{6,4},{7,5},{8,10},{9,11},{10,... | collective-permute-start | bytes 786440 | tf_op jit(solution)/shard_map/ppermute | solution.py:50
  14.6 6.5 %collective-permute-start.4 = (f32[4,16,1024]{2,1,0:T(8,128)S(1)}, f32[4,16,1024]{2,1,0:T(8,128)S(1)}, u32[]{:S(2)}, u32[]{:S(2)}) collective-permute-start(f32[4,16,1024]{2,1,0:T(8,128)S(1)} %pad_maximum_fusion), channel_id=1, source_target_pairs={{0,1},{1,0},{2,3},{3,2},{4,5},{5,4},{6,7},{7,6},{8,9},{9,8},{10,11... | collective-permute-start | bytes 786440 | tf_op jit(solution)/shard_map/ppermute | solution.py:50
  21.1 13.6 %copy-start.2 = (f32[4,16,1024]{2,1,0:T(8,128)}, f32[4,16,1024]{2,1,0:T(8,128)S(1)}, u32[]{:S(2)}) copy-start(f32[4,16,1024]{2,1,0:T(8,128)S(1)} %collective-permute-done.3.refs_3_.refs_4_) | copy-start | bytes 786436
  21.1 13.6 %collective-permute-start.5 = (f32[4,16,1024]{2,1,0:T(8,128)S(1)}, f32[4,16,1024]{2,1,0:T(8,128)S(1)}, u32[]{:S(2)}, u32[]{:S(2)}) collective-permute-start(f32[4,16,1024]{2,1,0:T(8,128)S(1)} %collective-permute-done.3.refs_3_.refs_4_), channel_id=1, source_target_pairs={{0,1},{1,0},{2,3},{3,2},{4,5},{5,4},{6,7},{7,6},{8,9},{9,8},{10,11... | collective-permute-start | bytes 786440 | tf_op jit(solution)/shard_map/ppermute | solution.py:50
  21.1 13.6 %copy-start.3 = (f32[4,16,1024]{2,1,0:T(8,128)}, f32[4,16,1024]{2,1,0:T(8,128)S(1)}, u32[]{:S(2)}) copy-start(f32[4,16,1024]{2,1,0:T(8,128)S(1)} %collective-permute-done.4.refs_4_.refs_5_) | copy-start | bytes 786436
  21.1 13.7 %copy-start.15 = (f32[1024]{0:T(1024)S(1)}, f32[1024]{0:T(1024)}, u32[]{:S(2)}) copy-start(f32[1024]{0:T(1024)} %param.6) | copy-start | bytes 12292
  34.8 6.8 %copy-start.4 = (f32[4,16,1024]{2,1,0:T(8,128)}, f32[4,16,1024]{2,1,0:T(8,128)S(1)}, u32[]{:S(2)}) copy-start(f32[4,16,1024]{2,1,0:T(8,128)S(1)} %collective-permute-done.5.refs_5_.refs_6_) | copy-start | bytes 786436
  41.6 20.3 %copy-start.1 = (f32[8,1024]{1,0:T(8,128)}, f32[8,1024]{1,0:T(8,128)S(1)}, u32[]{:S(2)}) copy-start(f32[8,1024]{1,0:T(8,128)S(1)} %get-tuple-element.17) | copy-start | bytes 98308
  41.6 5.0 %collective-permute-start.6 = (f32[1,8,1024]{2,1,0:T(8,128)S(1)}, f32[1,8,1024]{2,1,0:T(8,128)S(1)}, u32[]{:S(2)}, u32[]{:S(2)}) collective-permute-start(f32[1,8,1024]{2,1,0:T(8,128)S(1)} %bitcast.5), channel_id=1, source_target_pairs={{0,12},{1,13},{2,14},{3,15},{4,0},{5,1},{6,2},{7,3},{8,4},{9,5},{1... | collective-permute-start | bytes 98312 | tf_op jit(solution)/shard_map/ppermute | solution.py:50
  42.5 5.1 %collective-permute-start.7 = (f32[1,8,1024]{2,1,0:T(8,128)S(1)}, f32[1,8,1024]{2,1,0:T(8,128)S(1)}, u32[]{:S(2)}, u32[]{:S(2)}) collective-permute-start(f32[1,8,1024]{2,1,0:T(8,128)S(1)} %bitcast.6), channel_id=1, source_target_pairs={{0,8},{1,9},{2,10},{3,11},{4,12},{5,13},{6,14},{7,15},{8,0},{9,1},... | collective-permute-start | bytes 98312 | tf_op jit(solution)/shard_map/ppermute | solution.py:50
  43.2 5.7 %collective-permute-start.8 = (f32[1,8,1024]{2,1,0:T(8,128)S(1)}, f32[1,8,1024]{2,1,0:T(8,128)S(1)}, u32[]{:S(2)}, u32[]{:S(2)}) collective-permute-start(f32[1,8,1024]{2,1,0:T(8,128)S(1)} %bitcast.7), channel_id=1, source_target_pairs={{0,4},{1,5},{2,6},{3,7},{4,8},{5,9},{6,10},{7,11},{8,12},{9,13},{1... | collective-permute-start | bytes 98312 | tf_op jit(solution)/shard_map/ppermute | solution.py:50
  46.6 8.4 %copy-start.11 = (f32[1,8,1024]{2,1,0:T(8,128)}, f32[1,8,1024]{2,1,0:T(8,128)S(1)}, u32[]{:S(2)}) copy-start(f32[1,8,1024]{2,1,0:T(8,128)S(1)} %collective-permute-done.6.refs_8_.refs_3_) | copy-start | bytes 98308
  47.5 7.5 %copy-start.12 = (f32[1,8,1024]{2,1,0:T(8,128)}, f32[1,8,1024]{2,1,0:T(8,128)S(1)}, u32[]{:S(2)}) copy-start(f32[1,8,1024]{2,1,0:T(8,128)S(1)} %collective-permute-done.7.refs_9_.refs_4_) | copy-start | bytes 98308
  48.9 6.2 %copy-start.13 = (f32[1,8,1024]{2,1,0:T(8,128)}, f32[1,8,1024]{2,1,0:T(8,128)S(1)}, u32[]{:S(2)}) copy-start(f32[1,8,1024]{2,1,0:T(8,128)S(1)} %collective-permute-done.8.refs_10_.refs_5_) | copy-start | bytes 98308
  48.9 6.4 %collective-permute-start.10 = (f32[4,8,1024]{2,1,0:T(8,128)S(1)}, f32[4,8,1024]{2,1,0:T(8,128)S(1)}, u32[]{:S(2)}, u32[]{:S(2)}) collective-permute-start(f32[4,8,1024]{2,1,0:T(8,128)S(1)} %pad_maximum_fusion.1), channel_id=1, source_target_pairs={{0,1},{1,0},{2,3},{3,2},{4,5},{5,4},{6,7},{7,6},{8,9},{9,8},{10,11... | collective-permute-start | bytes 393224 | tf_op jit(solution)/shard_map/ppermute | solution.py:50
  49.0 6.1 %collective-permute-start.9 = (f32[4,8,1024]{2,1,0:T(8,128)S(1)}, f32[4,8,1024]{2,1,0:T(8,128)S(1)}, u32[]{:S(2)}, u32[]{:S(2)}) collective-permute-start(f32[4,8,1024]{2,1,0:T(8,128)S(1)} %pad_maximum_fusion.1), channel_id=1, source_target_pairs={{0,2},{1,3},{2,0},{3,1},{4,6},{5,7},{6,4},{7,5},{8,10},{9,11},{10,... | collective-permute-start | bytes 393224 | tf_op jit(solution)/shard_map/ppermute | solution.py:50
  55.1 18.6 %copy-start.9 = (f32[4,8,1024]{2,1,0:T(8,128)}, f32[4,8,1024]{2,1,0:T(8,128)S(1)}, u32[]{:S(2)}) copy-start(f32[4,8,1024]{2,1,0:T(8,128)S(1)} %collective-permute-done.9.refs_11_.refs_3_.refs_4_) | copy-start | bytes 393220
  55.1 6.8 %collective-permute-start.11 = (f32[4,8,1024]{2,1,0:T(8,128)S(1)}, f32[4,8,1024]{2,1,0:T(8,128)S(1)}, u32[]{:S(2)}, u32[]{:S(2)}) collective-permute-start(f32[4,8,1024]{2,1,0:T(8,128)S(1)} %collective-permute-done.9.refs_11_.refs_3_.refs_4_), channel_id=1, source_target_pairs={{0,1},{1,0},{2,3},{3,2},{4,5},{5,4},{6,7},{7,6},{8,9},{9,8},{10,11... | collective-permute-start | bytes 393224 | tf_op jit(solution)/shard_map/ppermute | solution.py:50
  55.3 18.4 %copy-start.8 = (f32[4,8,1024]{2,1,0:T(8,128)}, f32[4,8,1024]{2,1,0:T(8,128)S(1)}, u32[]{:S(2)}) copy-start(f32[4,8,1024]{2,1,0:T(8,128)S(1)} %collective-permute-done.10.refs_12_.refs_4_.refs_5_) | copy-start | bytes 393220
  61.9 18.9 %copy-start.10 = (f32[4,8,1024]{2,1,0:T(8,128)}, f32[4,8,1024]{2,1,0:T(8,128)S(1)}, u32[]{:S(2)}) copy-start(f32[4,8,1024]{2,1,0:T(8,128)S(1)} %collective-permute-done.11.refs_13_.refs_7_.refs_4_) | copy-start | bytes 393220
  65.5 3.6 %collective-permute-start.12 = (f32[8,128]{1,0:T(8,128)S(1)}, f32[8,128]{1,0:T(8,128)S(1)}, u32[]{:S(2)}, u32[]{:S(2)}) collective-permute-start(f32[8,128]{1,0:T(8,128)S(1)} %get-tuple-element.22), channel_id=1, source_target_pairs={{0,12},{1,13},{2,14},{3,15},{4,0},{5,1},{6,2},{7,3},{8,4},{9,5},{1... | collective-permute-start | bytes 12296 | tf_op jit(solution)/shard_map/ppermute | solution.py:50
  66.7 4.5 %collective-permute-start.13 = (f32[8,128]{1,0:T(8,128)S(1)}, f32[8,128]{1,0:T(8,128)S(1)}, u32[]{:S(2)}, u32[]{:S(2)}) collective-permute-start(f32[8,128]{1,0:T(8,128)S(1)} %get-tuple-element.22), channel_id=1, source_target_pairs={{0,8},{1,9},{2,10},{3,11},{4,12},{5,13},{6,14},{7,15},{8,0},{9,1},... | collective-permute-start | bytes 12296 | tf_op jit(solution)/shard_map/ppermute | solution.py:50
  67.1 5.4 %collective-permute-start.14 = (f32[8,128]{1,0:T(8,128)S(1)}, f32[8,128]{1,0:T(8,128)S(1)}, u32[]{:S(2)}, u32[]{:S(2)}) collective-permute-start(f32[8,128]{1,0:T(8,128)S(1)} %get-tuple-element.22), channel_id=1, source_target_pairs={{0,4},{1,5},{2,6},{3,7},{4,8},{5,9},{6,10},{7,11},{8,12},{9,13},{1... | collective-permute-start | bytes 12296 | tf_op jit(solution)/shard_map/ppermute | solution.py:50
  72.6 7.7 %collective-permute-start.16 = (f32[8,128]{1,0:T(8,128)S(1)}, f32[8,128]{1,0:T(8,128)S(1)}, u32[]{:S(2)}, u32[]{:S(2)}) collective-permute-start(f32[8,128]{1,0:T(8,128)S(1)} %add_add_fusion.1), channel_id=1, source_target_pairs={{0,2},{1,3},{2,0},{3,1},{4,6},{5,7},{6,4},{7,5},{8,10},{9,11},{10,... | collective-permute-start | bytes 12296 | tf_op jit(solution)/shard_map/ppermute | solution.py:50
  80.2 7.2 %collective-permute-start.15 = (f32[8,128]{1,0:T(8,128)S(1)}, f32[8,128]{1,0:T(8,128)S(1)}, u32[]{:S(2)}, u32[]{:S(2)}) collective-permute-start(f32[8,128]{1,0:T(8,128)S(1)} %add_add_fusion.1), channel_id=1, source_target_pairs={{0,1},{1,0},{2,3},{3,2},{4,5},{5,4},{6,7},{7,6},{8,9},{9,8},{10,11... | collective-permute-start | bytes 12296 | tf_op jit(solution)/shard_map/ppermute | solution.py:50
  80.3 7.2 %collective-permute-start.17 = (f32[8,128]{1,0:T(8,128)S(1)}, f32[8,128]{1,0:T(8,128)S(1)}, u32[]{:S(2)}, u32[]{:S(2)}) collective-permute-start(f32[8,128]{1,0:T(8,128)S(1)} %collective-permute-done.16), channel_id=1, source_target_pairs={{0,1},{1,0},{2,3},{3,2},{4,5},{5,4},{6,7},{7,6},{8,9},{9,8},{10,11... | collective-permute-start | bytes 12296 | tf_op jit(solution)/shard_map/ppermute | solution.py:50
  84.3 0.6 copy-start.14

commit v5 on v4

--- a/solution.py
+++ b/solution.py
@@ -13,6 +13,9 @@
 TILE = 256
 F32 = jnp.float32
 BF16 = jnp.bfloat16
+F8 = jnp.float8_e4m3fn
+LOW_SCALE = 2.0**16
+TOP = 256.0
 
 
 def pieces(value, count):
@@ -41,6 +44,16 @@
     return jnp.concatenate(pieces(value, 2), axis=0).astype(BF16)
 
 
+def small_stacked(value):
+    top = jnp.maximum(jnp.max(jnp.abs(value), axis=1, keepdims=True), 1e-30)
+    part = value * (TOP / top)
+    first = part.astype(F8).astype(F32)
+    second = part - first
+    pad = jnp.zeros_like(value)
+    both = jnp.concatenate([first, second, pad, pad], axis=0).astype(F8)
+    return both, jnp.broadcast_to(top * (1.0 / (TOP * LOW_SCALE)), (value.shape[0], 128))
+
+
 def shifted(value, stride, size, by):
     length = lax.axis_size("row")
     pairs = []
@@ -68,14 +81,23 @@
     return [own], line, beside + across[:1], across[1:]
 
 
-def summed(value):
+def along_line(value):
     far, near = digits()
-    value = sum([shifted(value, 2 * near, far, by) for by in range(1, far)], value)
+    return [shifted(value, 2 * near, far, by) for by in range(1, far)]
+
+
+def over_quad(value):
+    _, near = digits()
+    length = lax.axis_size("row")
     quad = [shifted(value, 1, 2, 1)]
     for by in range(1, near):
-        beside = shifted(value, 2, near, by)
-        quad += [beside, shifted(beside, 1, 2, 1)]
-    return sum(quad, value)
+        quad.append(shifted(value, 2, near, by))
+        pairs = []
+        for i in range(length):
+            digit = (i // 2) % near
+            pairs.append((i, (i + ((digit - by) % near - digit) * 2) ^ 1))
+        quad.append(lax.ppermute(value, "row", pairs))
+    return quad
 
 
 def tables():
@@ -103,21 +125,27 @@
     return [jnp.concatenate(t) for t in (first, second, last_first, last_second)]
 
 
-def add_block(yt_ref, at, own_ref, dirs, acc_ref):
+def put_dirs(refs, at, value):
+    dirs_ref, small_ref, factor_ref = refs
+    dirs_ref[at] = stacked(value)
+    small_ref[at], factor_ref[at] = small_stacked(value)
+
+
+def add_block(yt_ref, at, own_ref, dir_refs, b, acc_ref):
+    dirs_ref, small_ref, factor_ref = dir_refs
+    nrhs = acc_ref.shape[0]
+    factor = factor_ref[b][:, 0:1]
     for c in range(own_ref.shape[1] // TILE):
         cols = slice(c * TILE, (c + 1) * TILE)
         expo = jnp.dot(yt_ref[at], own_ref[:, cols], preferred_element_type=F32)
         weight = jnp.exp2(expo)
         high = weight.astype(BF16)
-        low = (weight - high.astype(F32)).astype(BF16)
-        acc_ref[:, cols] += jnp.dot(
-            dirs, high, preferred_element_type=F32
-        ) + jnp.dot(dirs, low, preferred_element_type=F32)
-
-
-def folded(acc_ref):
-    nrhs = acc_ref.shape[0] // 2
-    return acc_ref[0:nrhs, :] + acc_ref[nrhs:, :]
+        low = ((weight - high.astype(F32)) * LOW_SCALE).astype(F8)
+        big = jnp.dot(dirs_ref[b], high, preferred_element_type=F32)
+        rest = jnp.dot(small_ref[b], low, preferred_element_type=F32)
+        acc_ref[:, cols] += (big[:nrhs] + big[nrhs:]) + factor * (
+            rest[:nrhs] + rest[nrhs : 2 * nrhs]
+        )
 
 
 def each(stacks, function):
@@ -147,22 +175,22 @@
         own_ref[...] = exponent_rows(
             stacks[0][0, 0:nfeat, :] / scale_ref[...], 1.0, False
         ).astype(BF16)
-    yt_ref, out_ref, dirs_ref, acc_ref = refs
+    yt_ref, out_ref, *dir_refs, acc_ref = refs
 
     def prepare(b, value):
         rows = exponent_rows(value[0:nfeat, :] / scale_ref[...], LOG2E, True)
         yt_ref[b] = rows.T.astype(BF16)
-        dirs_ref[b] = stacked(value[nfeat:, :])
+        put_dirs(dir_refs, b, value[nfeat:, :])
 
     each(stacks, prepare)
     acc_ref[...] = jnp.zeros_like(acc_ref)
 
     def step(b, carry):
-        add_block(yt_ref, b, own_ref, dirs_ref[b], acc_ref)
+        add_block(yt_ref, b, own_ref, dir_refs, b, acc_ref)
         return carry
 
     lax.fori_loop(0, yt_ref.shape[0], step, 0)
-    total = folded(acc_ref)
+    total = acc_ref[...]
     if not first:
         total = total + sofar_ref[...]
     if amplitude:
@@ -180,21 +208,21 @@
     stacks = refs[:nstacks]
     out_ref, *refs = refs[nstacks:]
     form_ref = refs.pop(0) if form else None
-    dirs_ref, acc_ref = refs
+    *dir_refs, acc_ref = refs
 
     def prepare(b, value):
-        dirs_ref[b] = stacked(value)
+        put_dirs(dir_refs, b, value)
 
     each(stacks, prepare)
     acc_ref[...] = jnp.zeros_like(acc_ref)
 
     def step(s, carry):
         b = table_ref[s] if table else s
-        add_block(yt_ref, b, own_ref, dirs_ref[b], acc_ref)
+        add_block(yt_ref, b, own_ref, dir_refs, b, acc_ref)
         return carry
 
     lax.fori_loop(0, table_ref.shape[0] if table else yt_ref.shape[0], step, 0)
-    total = folded(acc_ref)
+    total = acc_ref[...]
     if sofar:
         total = total + sofar_ref[...]
     if form:
@@ -275,7 +303,9 @@
             in_specs=[smem if table and k == 0 else vmem for k in range(len(operands))],
             scratch_shapes=[
                 pltpu.VMEM((blocks, 2 * nrhs, width), BF16),
-                pltpu.VMEM((2 * nrhs, width), F32),
+                pltpu.VMEM((blocks, 4 * nrhs, width), F8),
+                pltpu.VMEM((blocks, nrhs, 128), F32),
+                pltpu.VMEM((nrhs, width), F32),
             ],
             compiler_params=pltpu.CompilerParams(
                 vmem_limit_bytes=min(16 * 1024 * 1024 + blocks * 1024 * width, 60 * 1024 * 1024)
@@ -333,9 +363,14 @@
         3, (field, small), "across_half", sofar=(half,), table=last_first,
         form=(once, noise, image),
     )
-    form = summed(form)
+    parts = along_line(form)
     total = again(2, field, "beside_rest", sofar=(total,), table=second)
+    *parts, total = lax.optimization_barrier((*parts, total))
+    form = sum(parts, form)
+    parts = over_quad(form)
     total = again(3, field, "across_rest", sofar=(total,), table=last_second)
+    *parts, total = lax.optimization_barrier((*parts, total))
+    form = sum(parts, form)
     flat = [s for g in groups for s in g]
     flat_images = [s for g in images for s in g]
     scalars = pl.pallas_call(

time: 89.9 us -> 103 us (1.15)
  Pallas kernels: 57.1 us -> 76.4 us
  waiting for transfers between devices: 11.5 us -> 4.31 us
    pallas_call x10, Pallas kernels: 53 us -> 72.3 us  [call(): pl.pallas_call(kernel, out_shape=out_shape, in_specs=[smem if table and k...]
    ppermute x18 -> x17, waiting for transfers between devices: 11.5 us -> 4.3 us  [shifted(): return lax.ppermute(value, 'row', pairs)]
    ppermute x18 -> x17, starting transfers between devices: 17.1 us -> 17.7 us  [shifted(): return lax.ppermute(value, 'row', pairs)]
  transfers between devices with their start and end apart: 18 -> 18, of which waited for: 7 -> 4; matrix products, arithmetic and copies ran while one was open for 1% -> 1% of each run, Pallas kernels for 50% -> 59%
where the time goes in v5:
time: 103 us
  Pallas kernels  76.4 us (74%)
  starting transfers between devices  18 us (17%)
  waiting for transfers between devices  4.31 us (4%)
  other arithmetic  1.6 us (2%)
  local copies, waits for them, and re-layouts  1.41 us (1%)
    pallas_call x10, Pallas kernels, call(): pl.pallas_call(kernel, out_shape=out_shape, in_specs=[smem if table and k...  72.3 us
    ppermute x17, starting transfers between devices, shifted(): return lax.ppermute(value, 'row', pairs)  17.7 us
    ppermute x17, waiting for transfers between devices, shifted(): return lax.ppermute(value, 'row', pairs)  4.3 us
    pallas_call x1, Pallas kernels, shards(): pl.pallas_call(functools.partial(scalars_kernel, nfeat, len(flat)), out_s...  2.5 us
  transfers between devices with their start and end apart: 18, of which 4 were waited for; matrix products, arithmetic and copies ran while one was open for 1% of the time, Pallas kernels for 59%

profile of v5, /device:TPU:0, one launch (start us, length us, event | category | flops | bytes accessed | tf_op | source)
XLA Modules:
  0.0 102.7 jit_solution(15530386361736389476)
XLA Ops:
  0.6 0.8 maximum_bitcast_fusion.refs_1_.refs_4_.refs_0_.mine_ref
  1.4 5.1 %collective-permute-start = (f32[1,16,1024]{2,1,0:T(8,128)S(1)}, f32[1,16,1024]{2,1,0:T(8,128)S(1)}, u32[]{:S(2)}, u32[]{:S(2)}) collective-permute-start(f32[1,16,1024]{2,1,0:T(8,128)S(1)} %maximum_bitcast_fusion.refs_1_.refs_4_.refs_0_.mine_ref), channel_id=1, source_target_pairs={{0,12},{1,13},{2,14},{3,15},{4,0},{5,1},{6,2},{7,3},{8,4},{9,5},{1... | collective-permute-start | bytes 196616 | tf_op jit(solution)/shard_map/ppermute | solution.py:63
  6.5 0.0 collective-permute-start.1
  6.5 1.0 collective-permute-start.2
  7.5 0.7 copy.9.refs_0_
  8.3 2.1 %own_block.1 = (bf16[64,1024]{1,0:T(8,128)(2,1)S(1)}, bf16[1,1024,64]{2,1,0:T(8,128)(2,1)S(1)}, f32[8,1024]{1,0:T(8,128)S(1)}) custom-call(f32[8,1]{1,0:T(8,128)S(1)} %copy.9.refs_0_, f32[1,16,1024]{2,1,0:T(8,128)S(1)} %maximum_bitcast_fusion.refs_1_.refs_4_.refs_0_.mine_ref), custom_call_target="tpu_custom_call" | custom-call | flops 2147483648 | bytes 1048576 | tf_op jit(solution)/shard_map/own_block/pallas_call | solution.py:300
  10.4 0.1 pad_add_fusion.refs_0_
  10.5 0.1 pad_add_fusion.1.refs_0_
  10.6 0.0 collective-permute-done.refs_3_.refs_1_
  10.6 2.4 %collective-permute-done.1.refs_4_.refs_2_ = f32[1,16,1024]{2,1,0:T(8,128)S(1)} collective-permute-done((f32[1,16,1024]{2,1,0:T(8,128)S(1)}, f32[1,16,1024]{2,1,0:T(8,128)S(1)}, u32[]{:S(2)}, u32[]{:S(2)}) %collective-permute-start.1) | collective-permute-done | bytes 65568 | tf_op jit(solution)/shard_map/ppermute | solution.py:63
  13.0 0.0 collective-permute-done.2.refs_5_.refs_3_
  13.0 1.6 %collective-permute-start.3 = (f32[4,16,1024]{2,1,0:T(8,128)S(1)}, f32[4,16,1024]{2,1,0:T(8,128)S(1)}, u32[]{:S(2)}, u32[]{:S(2)}) collective-permute-start(f32[4,16,1024]{2,1,0:T(8,128)S(1)} %pad_maximum_fusion), channel_id=1, source_target_pairs={{0,2},{1,3},{2,0},{3,1},{4,6},{5,7},{6,4},{7,5},{8,10},{9,11},{10,... | collective-permute-start | bytes 786440 | tf_op jit(solution)/shard_map/ppermute | solution.py:63
  14.6 0.0 collective-permute-start.4
  14.6 6.4 %blocks_0.1 = (bf16[3,1024,64]{2,1,0:T(8,128)(2,1)S(1)}, f32[8,1024]{1,0:T(8,128)S(1)}) custom-call(f32[8,1]{1,0:T(8,128)S(1)} %copy.9.refs_0_, bf16[64,1024]{1,0:T(8,128)(2,1)S(1)} %get-tuple-element.21.refs_1_.refs_0_.refs_5_.refs_2_, f32[8,1024]{1,0:T(8,128)S(1)} %get-tuple-element.22.refs_2_, f32[1,16,1024]{2,1,0:T(8,128)S(1)} %collective-permute-done.refs_3_.refs_1_, ...), custom_call_target="tpu_custom_call" | custom-call | flops 6442450944 | bytes 1048576 | tf_op jit(solution)/shard_map/blocks_0/pallas_call | solution.py:300
  21.0 0.0 copy-done.5
  21.0 0.0 copy-done.6
  21.0 0.0 copy-done.7
  21.0 0.1 collective-permute-done.3.refs_3_.refs_4_
  21.1 0.5 collective-permute-start.5
  21.6 0.0 collective-permute-done.4.refs_4_.refs_5_
  21.6 18.0 %blocks_1.1 = (bf16[8,1024,64]{2,1,0:T(8,128)(2,1)S(1)}, f32[8,1024]{1,0:T(8,128)S(1)}) custom-call(f32[8,1]{1,0:T(8,128)S(1)} %copy.9.refs_0_, bf16[64,1024]{1,0:T(8,128)(2,1)S(1)} %get-tuple-element.21.refs_1_.refs_0_.refs_5_.refs_2_, f32[8,1024]{1,0:T(8,128)S(1)} %get-tuple-element.23.refs_2_, f32[4,16,1024]{2,1,0:T(8,128)S(1)} %collective-permute-done.3.refs_3_.refs_4_, ...), custom_call_target="tpu_custom_call" | custom-call | flops 17179869184 | bytes 1048576 | tf_op jit(solution)/shard_map/blocks_1/pallas_call | solution.py:300
  39.7 0.0 copy-done.2
  39.7 0.0 copy-done.3
  39.7 0.0 collective-permute-done.5.refs_5_.refs_6_
  39.7 0.0 copy-start.4
  39.7 0.0 copy-done
  39.7 0.0 copy-done.16
  39.7 9.0 %blocks_2.1 = (bf16[4,1024,64]{2,1,0:T(8,128)(2,1)S(1)}, f32[8,1024]{1,0:T(8,128)S(1)}) custom-call(f32[8,1]{1,0:T(8,128)S(1)} %copy.9.refs_0_, bf16[64,1024]{1,0:T(8,128)(2,1)S(1)} %get-tuple-element.21.refs_1_.refs_0_.refs_5_.refs_2_, f32[8,1024]{1,0:T(8,128)S(1)} %get-tuple-element.24.refs_2_, f32[1,1024]{1,0:T(1,128)S(1)} %bitcast.14, ...), custom_call_target="tpu_custom_call" | custom-call | flops 8589934592 | bytes 1048576 | tf_op jit(solution)/shard_map/blocks_2/pallas_call | solution.py:300
  48.8 0.0 copy-done.4
  48.8 1.9 %collective-permute-start.6 = (f32[1,8,1024]{2,1,0:T(8,128)S(1)}, f32[1,8,1024]{2,1,0:T(8,128)S(1)}, u32[]{:S(2)}, u32[]{:S(2)}) collective-permute-start(f32[1,8,1024]{2,1,0:T(8,128)S(1)} %bitcast.5), channel_id=1, source_target_pairs={{0,12},{1,13},{2,14},{3,15},{4,0},{5,1},{6,2},{7,3},{8,4},{9,5},{1... | collective-permute-start | bytes 98312 | tf_op jit(solution)/shard_map/ppermute | solution.py:63
  50.7 0.0 collective-permute-start.7
  50.7 1.9 %collective-permute-start.8 = (f32[1,8,1024]{2,1,0:T(8,128)S(1)}, f32[1,8,1024]{2,1,0:T(8,128)S(1)}, u32[]{:S(2)}, u32[]{:S(2)}) collective-permute-start(f32[1,8,1024]{2,1,0:T(8,128)S(1)} %bitcast.7), channel_id=1, source_target_pairs={{0,4},{1,5},{2,6},{3,7},{4,8},{5,9},{6,10},{7,11},{8,12},{9,13},{1... | collective-permute-start | bytes 98312 | tf_op jit(solution)/shard_map/ppermute | solution.py:63
  52.6 2.0 %own_again.1.refs_0_ = f32[8,1024]{1,0:T(8,128)S(1)} custom-call(bf16[64,1024]{1,0:T(8,128)(2,1)S(1)} %get-tuple-element.21.refs_1_.refs_0_.refs_5_.refs_2_, bf16[1,1024,64]{2,1,0:T(8,128)(2,1)S(1)} %get-tuple-element.27.refs_1_, f32[1,8,1024]{2,1,0:T(8,128)S(1)} %bitcast.8), custom_call_target="tpu_custom_call" | custom-call | flops 2147483648 | bytes 1048576 | tf_op jit(solution)/shard_map/own_again/pallas_call | solution.py:300
  54.6 0.0 collective-permute-done.6.refs_8_.refs_3_
  54.6 0.0 copy-start.12
  54.7 1.2 %collective-permute-done.7.refs_9_.refs_4_ = f32[1,8,1024]{2,1,0:T(8,128)S(1)} collective-permute-done((f32[1,8,1024]{2,1,0:T(8,128)S(1)}, f32[1,8,1024]{2,1,0:T(8,128)S(1)}, u32[]{:S(2)}, u32[]{:S(2)}) %collective-permute-start.7) | collective-permute-done | bytes 32800 | tf_op jit(solution)/shard_map/ppermute | solution.py:63
  55.8 0.6 collective-permute-done.8.refs_10_.refs_5_
  56.5 0.1 collective-permute-start.10
  56.6 0.7 collective-permute-start.9
  57.3 6.1 %line_again.1.refs_2_ = f32[8,1024]{1,0:T(8,128)S(1)} custom-call(f32[8,1024]{1,0:T(8,128)S(1)} %own_again.1.refs_0_, bf16[64,1024]{1,0:T(8,128)(2,1)S(1)} %get-tuple-element.21.refs_1_.refs_0_.refs_5_.refs_2_, bf16[3,1024,64]{2,1,0:T(8,128)(2,1)S(1)} %get-tuple-element.28.refs_2_, f32[1,8,1024]{2,1,0:T(8,128)S(1)} %collective-permute-done.6.refs_8_.refs_3_, ...), custom_call_target="tpu_custom_call" | custom-call | flops 6442450944 | bytes 1048576 | tf_op jit(solution)/shard_map/line_again/pallas_call | solution.py:300
  63.4 0.0 collective-permute-done.9.refs_11_.refs_3_.refs_4_
  63.5 0.2 collective-permute-start.11
  63.7 0.0 collective-permute-done.10.refs_12_.refs_4_.refs_5_
  63.7 9.3 %beside_half.1.refs_1_ = f32[8,1024]{1,0:T(8,128)S(1)} custom-call(s32[4]{0:T(128)S(1)} %pad_add_fusion.refs_0_, bf16[64,1024]{1,0:T(8,128)(2,1)S(1)} %get-tuple-element.21.refs_1_.refs_0_.refs_5_.refs_2_, bf16[8,1024,64]{2,1,0:T(8,128)(2,1)S(1)} %get-tuple-element.26.refs_2_.refs_3_, f32[4,8,1024]{2,1,0:T(8,128)S(1)} %collective-permute-done.9.refs_11_.refs_3_.refs_4_, ...), custom_call_target="tpu_custom_call" | custom-call | flops 8589934592 | bytes 1048576 | tf_op jit(solution)/shard_map/beside_half/pallas_call | solution.py:300
  73.0 0.0 collective-permute-done.11.refs_13_.refs_7_.refs_4_
  73.0 5.0 %across_half.1 = (f32[8,1024]{1,0:T(8,128)S(1)}, f32[8,128]{1,0:T(8,128)S(1)}) custom-call(s32[2]{0:T(128)S(1)} %fusion.2.refs_0_, f32[8,1024]{1,0:T(8,128)S(1)} %beside_half.1.refs_1_, f32[8,1024]{1,0:T(8,128)S(1)} %line_again.1.refs_2_, f32[1,1024]{1,0:T(1,128)S(1)} %bitcast.15, f32[1,8,1024]{2,1,0:T(8,128)S(1)} %bitcast.10, ...), custom_call_target="tpu_custom_call" | custom-call | flops 4294967296 | bytes 1048576 | tf_op jit(solution)/shard_map/across_half/pallas_call | solution.py:300
  78.1 1.3 %collective-permute-start.12 = (f32[8,128]{1,0:T(8,128)S(1)}, f32[8,128]{1,0:T(8,128)S(1)}, u32[]{:S(2)}, u32[]{:S(2)}) collective-permute-start(f32[8,128]{1,0:T(8,128)S(1)} %get-tuple-element.30), channel_id=1, source_target_pairs={{0,12},{1,13},{2,14},{3,15},{4,0},{5,1},{6,2},{7,3},{8,4},{9,5},{1... | collective-permute-start | bytes 12296 | tf_op jit(solution)/shard_map/ppermute | solution.py:63
  79.3 0.3 collective-permute-start.13
  79.7 1.4 %collective-permute-start.14 = (f32[8,128]{1,0:T(8,128)S(1)}, f32[8,128]{1,0:T(8,128)S(1)}, u32[]{:S(2)}, u32[]{:S(2)}) collective-permute-start(f32[8,128]{1,0:T(8,128)S(1)} %get-tuple-element.30), channel_id=1, source_target_pairs={{0,4},{1,5},{2,6},{3,7},{4,8},{5,9},{6,10},{7,11},{8,12},{9,13},{1... | collective-permute-start | bytes 12296 | tf_op jit(solution)/shard_map/ppermute | solution.py:63
  81.1 9.3 %beside_rest.1.refs_1_ = f32[8,1024]{1,0:T(8,128)S(1)} custom-call(s32[4]{0:T(128)S(1)} %pad_add_fusion.1.refs_0_, f32[8,1024]{1,0:T(8,128)S(1)} %get-tuple-element.31.refs_1_, bf16[64,1024]{1,0:T(8,128)(2,1)S(1)} %get-tuple-element.21.refs_1_.refs_0_.refs_5_.refs_2_, bf16[8,1024,64]{2,1,0:T(8,128)(2,1)S(1)} %get-tuple-element.26.refs_2_.refs_3_, ...), custom_call_target="tpu_custom_call" | custom-call | flops 8589934592 | bytes 1048576 | tf_op jit(solution)/shard_map/beside_rest/pallas_call | solution.py:300
  90.4 2.5 %scalars.1.scalars_ref = f32[4,8,128]{2,1,0:T(8,128)} custom-call(f32[1,16,1024]{2,1,0:T(8,128)} %copy-done, f32[1,16,1024]{2,1,0:T(8,128)} %copy-done.5, f32[1,16,1024]{2,1,0:T(8,128)} %copy-done.6, f32[1,16,1024]{2,1,0:T(8,128)} %copy-done.7, f32[4,16,1024]{2,1,0:T(8,128)} %copy-done.2, f32[4,16,1024]{2,1,0:T(8,128)} %copy-done.3, ...), custom_call_target="tpu_custom_call" | custom-call | tf_op jit(solution)/shard_map/scalars/pallas_call | solution.py:376
  92.9 0.0 collective-permute-done.12
  92.9 0.0 collective-permute-done.13
  92.9 0.0 collective-permute-done.14
  93.0 0.1 collective-permute-start.15
  93.0 1.6 %collective-permute-start.16 = (f32[8,128]{1,0:T(8,128)S(1)}, f32[8,128]{1,0:T(8,128)S(1)}, u32[]{:S(2)}, u32[]{:S(2)}) collective-permute-start(f32[8,128]{1,0:T(8,128)S(1)} %add_add_fusion.1), channel_id=1, source_target_pairs={{0,2},{1,3},{2,0},{3,1},{4,6},{5,7},{6,4},{7,5},{8,10},{9,11},{10,... | collective-permute-start | bytes 12296 | tf_op jit(solution)/shard_map/ppermute | solution.py:63
  94.6 0.3 collective-permute-start.17
  94.9 4.9 %across_rest.1.total_ref = f32[8,1024]{1,0:T(8,128)S(1)} custom-call(s32[2]{0:T(128)S(1)} %fusion.3.refs_0_, f32[8,1024]{1,0:T(8,128)S(1)} %beside_rest.1.refs_1_, bf16[64,1024]{1,0:T(8,128)(2,1)S(1)} %get-tuple-element.21.refs_1_.refs_0_.refs_5_.refs_2_, bf16[4,1024,64]{2,1,0:T(8,128)(2,1)S(1)} %get-tuple-element.29.refs_6_.refs_3_, f32[4,8,1024]{2,1,0:T(8,128)S(1)} %copy-done.9), custom_call_target="tpu_custom_call" | custom-call | flops 4294967296 | bytes 1048576 | tf_op jit(solution)/shard_map/across_rest/pallas_call | solution.py:300
  99.8 0.6 copy-done.15
  100.4 0.0 collective-permute-done.15
  100.4 0.0 collective-permute-done.16
  100.5 0.0 collective-permute-done.17
  100.5 0.6 add_add_fusion.form_ref
  101.1 1.6 %last_update.1 = (f32[8,1024]{1,0:T(8,128)}, f32[8,1024]{1,0:T(8,128)}) custom-call(f32[4,8,128]{2,1,0:T(8,128)} %scalars.1.scalars_ref, f32[8,128]{1,0:T(8,128)} %add_add_fusion.form_ref, f32[8,1024]{1,0:T(8,128)} %copy-done.15, f32[1,1024]{1,0:T(1,128)} %bitcast.13, f32[1,16,1024]{2,1,0:T(8,128)} %copy-done, f32[1,8,1024]{2,1,0:T(8,128)} %bitcast.12), custom_call_target="tpu_custom_call" | custom-call | tf_op jit(solution)/shard_map/last_update/pallas_call | solution.py:381
  (30 shorter events, 0.1 us)
Async XLA Ops:
  1.4 38.3 %copy-start = (f32[1,16,1024]{2,1,0:T(8,128)}, f32[1,16,1024]{2,1,0:T(8,128)S(1)}, u32[]{:S(2)}) copy-start(f32[1,16,1024]{2,1,0:T(8,128)S(1)} %maximum_bitcast_fusion.refs_1_.refs_4_.refs_0_.mine_ref) | copy-start | bytes 196612
  1.4 9.2 %collective-permute-start = (f32[1,16,1024]{2,1,0:T(8,128)S(1)}, f32[1,16,1024]{2,1,0:T(8,128)S(1)}, u32[]{:S(2)}, u32[]{:S(2)}) collective-permute-start(f32[1,16,1024]{2,1,0:T(8,128)S(1)} %maximum_bitcast_fusion.refs_1_.refs_4_.refs_0_.mine_ref), channel_id=1, source_target_pairs={{0,12},{1,13},{2,14},{3,15},{4,0},{5,1},{6,2},{7,3},{8,4},{9,5},{1... | collective-permute-start | bytes 196616 | tf_op jit(solution)/shard_map/ppermute | solution.py:63
  6.5 6.5 %collective-permute-start.1 = (f32[1,16,1024]{2,1,0:T(8,128)S(1)}, f32[1,16,1024]{2,1,0:T(8,128)S(1)}, u32[]{:S(2)}, u32[]{:S(2)}) collective-permute-start(f32[1,16,1024]{2,1,0:T(8,128)S(1)} %maximum_bitcast_fusion.refs_1_.refs_4_.refs_0_.mine_ref), channel_id=1, source_target_pairs={{0,8},{1,9},{2,10},{3,11},{4,12},{5,13},{6,14},{7,15},{8,0},{9,1},... | collective-permute-start | bytes 196616 | tf_op jit(solution)/shard_map/ppermute | solution.py:63
  6.5 6.5 %collective-permute-start.2 = (f32[1,16,1024]{2,1,0:T(8,128)S(1)}, f32[1,16,1024]{2,1,0:T(8,128)S(1)}, u32[]{:S(2)}, u32[]{:S(2)}) collective-permute-start(f32[1,16,1024]{2,1,0:T(8,128)S(1)} %maximum_bitcast_fusion.refs_1_.refs_4_.refs_0_.mine_ref), channel_id=1, source_target_pairs={{0,4},{1,5},{2,6},{3,7},{4,8},{5,9},{6,10},{7,11},{8,12},{9,13},{1... | collective-permute-start | bytes 196616 | tf_op jit(solution)/shard_map/ppermute | solution.py:63
  10.6 10.4 %copy-start.5 = (f32[1,16,1024]{2,1,0:T(8,128)}, f32[1,16,1024]{2,1,0:T(8,128)S(1)}, u32[]{:S(2)}) copy-start(f32[1,16,1024]{2,1,0:T(8,128)S(1)} %collective-permute-done.refs_3_.refs_1_) | copy-start | bytes 196612
  13.0 8.0 %copy-start.6 = (f32[1,16,1024]{2,1,0:T(8,128)}, f32[1,16,1024]{2,1,0:T(8,128)S(1)}, u32[]{:S(2)}) copy-start(f32[1,16,1024]{2,1,0:T(8,128)S(1)} %collective-permute-done.1.refs_4_.refs_2_) | copy-start | bytes 196612
  13.0 8.0 %copy-start.7 = (f32[1,16,1024]{2,1,0:T(8,128)}, f32[1,16,1024]{2,1,0:T(8,128)S(1)}, u32[]{:S(2)}) copy-start(f32[1,16,1024]{2,1,0:T(8,128)S(1)} %collective-permute-done.2.refs_5_.refs_3_) | copy-start | bytes 196612
  13.0 8.1 %collective-permute-start.3 = (f32[4,16,1024]{2,1,0:T(8,128)S(1)}, f32[4,16,1024]{2,1,0:T(8,128)S(1)}, u32[]{:S(2)}, u32[]{:S(2)}) collective-permute-start(f32[4,16,1024]{2,1,0:T(8,128)S(1)} %pad_maximum_fusion), channel_id=1, source_target_pairs={{0,2},{1,3},{2,0},{3,1},{4,6},{5,7},{6,4},{7,5},{8,10},{9,11},{10,... | collective-permute-start | bytes 786440 | tf_op jit(solution)/shard_map/ppermute | solution.py:63
  14.6 7.0 %collective-permute-start.4 = (f32[4,16,1024]{2,1,0:T(8,128)S(1)}, f32[4,16,1024]{2,1,0:T(8,128)S(1)}, u32[]{:S(2)}, u32[]{:S(2)}) collective-permute-start(f32[4,16,1024]{2,1,0:T(8,128)S(1)} %pad_maximum_fusion), channel_id=1, source_target_pairs={{0,1},{1,0},{2,3},{3,2},{4,5},{5,4},{6,7},{7,6},{8,9},{9,8},{10,11... | collective-permute-start | bytes 786440 | tf_op jit(solution)/shard_map/ppermute | solution.py:63
  21.1 18.6 %copy-start.2 = (f32[4,16,1024]{2,1,0:T(8,128)}, f32[4,16,1024]{2,1,0:T(8,128)S(1)}, u32[]{:S(2)}) copy-start(f32[4,16,1024]{2,1,0:T(8,128)S(1)} %collective-permute-done.3.refs_3_.refs_4_) | copy-start | bytes 786436
  21.1 18.6 %collective-permute-start.5 = (f32[4,16,1024]{2,1,0:T(8,128)S(1)}, f32[4,16,1024]{2,1,0:T(8,128)S(1)}, u32[]{:S(2)}, u32[]{:S(2)}) collective-permute-start(f32[4,16,1024]{2,1,0:T(8,128)S(1)} %collective-permute-done.3.refs_3_.refs_4_), channel_id=1, source_target_pairs={{0,1},{1,0},{2,3},{3,2},{4,5},{5,4},{6,7},{7,6},{8,9},{9,8},{10,11... | collective-permute-start | bytes 786440 | tf_op jit(solution)/shard_map/ppermute | solution.py:63
  21.6 18.1 %copy-start.3 = (f32[4,16,1024]{2,1,0:T(8,128)}, f32[4,16,1024]{2,1,0:T(8,128)S(1)}, u32[]{:S(2)}) copy-start(f32[4,16,1024]{2,1,0:T(8,128)S(1)} %collective-permute-done.4.refs_4_.refs_5_) | copy-start | bytes 786436
  21.6 18.1 %copy-start.16 = (f32[1024]{0:T(1024)S(1)}, f32[1024]{0:T(1024)}, u32[]{:S(2)}) copy-start(f32[1024]{0:T(1024)} %param.6) | copy-start | bytes 12292
  39.7 9.1 %copy-start.4 = (f32[4,16,1024]{2,1,0:T(8,128)}, f32[4,16,1024]{2,1,0:T(8,128)S(1)}, u32[]{:S(2)}) copy-start(f32[4,16,1024]{2,1,0:T(8,128)S(1)} %collective-permute-done.5.refs_5_.refs_6_) | copy-start | bytes 786436
  48.8 24.3 %copy-start.1 = (f32[8,1024]{1,0:T(8,128)}, f32[8,1024]{1,0:T(8,128)S(1)}, u32[]{:S(2)}) copy-start(f32[8,1024]{1,0:T(8,128)S(1)} %get-tuple-element.25) | copy-start | bytes 98308
  48.8 5.8 %collective-permute-start.6 = (f32[1,8,1024]{2,1,0:T(8,128)S(1)}, f32[1,8,1024]{2,1,0:T(8,128)S(1)}, u32[]{:S(2)}, u32[]{:S(2)}) collective-permute-start(f32[1,8,1024]{2,1,0:T(8,128)S(1)} %bitcast.5), channel_id=1, source_target_pairs={{0,12},{1,13},{2,14},{3,15},{4,0},{5,1},{6,2},{7,3},{8,4},{9,5},{1... | collective-permute-start | bytes 98312 | tf_op jit(solution)/shard_map/ppermute | solution.py:63
  50.7 5.1 %collective-permute-start.7 = (f32[1,8,1024]{2,1,0:T(8,128)S(1)}, f32[1,8,1024]{2,1,0:T(8,128)S(1)}, u32[]{:S(2)}, u32[]{:S(2)}) collective-permute-start(f32[1,8,1024]{2,1,0:T(8,128)S(1)} %bitcast.6), channel_id=1, source_target_pairs={{0,8},{1,9},{2,10},{3,11},{4,12},{5,13},{6,14},{7,15},{8,0},{9,1},... | collective-permute-start | bytes 98312 | tf_op jit(solution)/shard_map/ppermute | solution.py:63
  50.7 5.7 %collective-permute-start.8 = (f32[1,8,1024]{2,1,0:T(8,128)S(1)}, f32[1,8,1024]{2,1,0:T(8,128)S(1)}, u32[]{:S(2)}, u32[]{:S(2)}) collective-permute-start(f32[1,8,1024]{2,1,0:T(8,128)S(1)} %bitcast.7), channel_id=1, source_target_pairs={{0,4},{1,5},{2,6},{3,7},{4,8},{5,9},{6,10},{7,11},{8,12},{9,13},{1... | collective-permute-start | bytes 98312 | tf_op jit(solution)/shard_map/ppermute | solution.py:63
  54.6 8.8 %copy-start.12 = (f32[1,8,1024]{2,1,0:T(8,128)}, f32[1,8,1024]{2,1,0:T(8,128)S(1)}, u32[]{:S(2)}) copy-start(f32[1,8,1024]{2,1,0:T(8,128)S(1)} %collective-permute-done.6.refs_8_.refs_3_) | copy-start | bytes 98308
  55.8 7.6 %copy-start.13 = (f32[1,8,1024]{2,1,0:T(8,128)}, f32[1,8,1024]{2,1,0:T(8,128)S(1)}, u32[]{:S(2)}) copy-start(f32[1,8,1024]{2,1,0:T(8,128)S(1)} %collective-permute-done.7.refs_9_.refs_4_) | copy-start | bytes 98308
  56.5 7.0 %copy-start.14 = (f32[1,8,1024]{2,1,0:T(8,128)}, f32[1,8,1024]{2,1,0:T(8,128)S(1)}, u32[]{:S(2)}) copy-start(f32[1,8,1024]{2,1,0:T(8,128)S(1)} %collective-permute-done.8.refs_10_.refs_5_) | copy-start | bytes 98308
  56.5 7.2 %collective-permute-start.10 = (f32[4,8,1024]{2,1,0:T(8,128)S(1)}, f32[4,8,1024]{2,1,0:T(8,128)S(1)}, u32[]{:S(2)}, u32[]{:S(2)}) collective-permute-start(f32[4,8,1024]{2,1,0:T(8,128)S(1)} %pad_maximum_fusion.1), channel_id=1, source_target_pairs={{0,1},{1,0},{2,3},{3,2},{4,5},{5,4},{6,7},{7,6},{8,9},{9,8},{10,11... | collective-permute-start | bytes 393224 | tf_op jit(solution)/shard_map/ppermute | solution.py:63
  56.6 6.9 %collective-permute-start.9 = (f32[4,8,1024]{2,1,0:T(8,128)S(1)}, f32[4,8,1024]{2,1,0:T(8,128)S(1)}, u32[]{:S(2)}, u32[]{:S(2)}) collective-permute-start(f32[4,8,1024]{2,1,0:T(8,128)S(1)} %pad_maximum_fusion.1), channel_id=1, source_target_pairs={{0,2},{1,3},{2,0},{3,1},{4,6},{5,7},{6,4},{7,5},{8,10},{9,11},{10,... | collective-permute-start | bytes 393224 | tf_op jit(solution)/shard_map/ppermute | solution.py:63
  63.4 17.6 %copy-start.11 = (f32[4,8,1024]{2,1,0:T(8,128)}, f32[4,8,1024]{2,1,0:T(8,128)S(1)}, u32[]{:S(2)}) copy-start(f32[4,8,1024]{2,1,0:T(8,128)S(1)} %collective-permute-done.9.refs_11_.refs_3_.refs_4_) | copy-start | bytes 393220
  63.5 9.6 %collective-permute-start.11 = (f32[4,8,1024]{2,1,0:T(8,128)S(1)}, f32[4,8,1024]{2,1,0:T(8,128)S(1)}, u32[]{:S(2)}, u32[]{:S(2)}) collective-permute-start(f32[4,8,1024]{2,1,0:T(8,128)S(1)} %collective-permute-done.9.refs_11_.refs_3_.refs_4_), channel_id=1, source_target_pairs={{0,1},{1,0},{2,3},{3,2},{4,5},{5,4},{6,7},{7,6},{8,9},{9,8},{10,11... | collective-permute-start | bytes 393224 | tf_op jit(solution)/shard_map/ppermute | solution.py:63
  63.7 17.4 %copy-start.10 = (f32[4,8,1024]{2,1,0:T(8,128)}, f32[4,8,1024]{2,1,0:T(8,128)S(1)}, u32[]{:S(2)}) copy-start(f32[4,8,1024]{2,1,0:T(8,128)S(1)} %collective-permute-done.10.refs_12_.refs_4_.refs_5_) | copy-start | bytes 393220
  73.0 5.0 %copy-start.8 = (f32[4,8,1024]{2,1,0:T(8,128)}, f32[4,8,1024]{2,1,0:T(8,128)S(1)}, u32[]{:S(2)}) copy-start(f32[4,8,1024]{2,1,0:T(8,128)S(1)} %collective-permute-done.11.refs_13_.refs_7_.refs_4_) | copy-start | bytes 393220
  78.1 14.8 %collective-permute-start.12 = (f32[8,128]{1,0:T(8,128)S(1)}, f32[8,128]{1,0:T(8,128)S(1)}, u32[]{:S(2)}, u32[]{:S(2)}) collective-permute-start(f32[8,128]{1,0:T(8,128)S(1)} %get-tuple-element.30), channel_id=1, source_target_pairs={{0,12},{1,13},{2,14},{3,15},{4,0},{5,1},{6,2},{7,3},{8,4},{9,5},{1... | collective-permute-start | bytes 12296 | tf_op jit(solution)/shard_map/ppermute | solution.py:63
  79.3 13.6 %collective-permute-start.13 = (f32[8,128]{1,0:T(8,128)S(1)}, f32[8,128]{1,0:T(8,128)S(1)}, u32[]{:S(2)}, u32[]{:S(2)}) collective-permute-start(f32[8,128]{1,0:T(8,128)S(1)} %get-tuple-element.30), channel_id=1, source_target_pairs={{0,8},{1,9},{2,10},{3,11},{4,12},{5,13},{6,14},{7,15},{8,0},{9,1},... | collective-permute-start | bytes 12296 | tf_op jit(solution)/shard_map/ppermute | solution.py:63
  79.7 13.3 %collective-permute-start.14 = (f32[8,128]{1,0:T(8,128)S(1)}, f32[8,128]{1,0:T(8,128)S(1)}, u32[]{:S(2)}, u32[]{:S(2)}) collective-permute-start(f32[8,128]{1,0:T(8,128)S(1)} %get-tuple-element.30), channel_id=1, source_target_pairs={{0,4},{1,5},{2,6},{3,7},{4,8},{5,9},{6,10},{7,11},{8,12},{9,13},{1... | collective-permute-start | bytes 12296 | tf_op jit(solution)/shard_map/ppermute | solution.py:63
  81.1 13.8 %copy-start.9 = (f32[4,8,1024]{2,1,0:T(8,128)S(1)}, f32[4,8,1024]{2,1,0:T(8,128)}, u32[]{:S(2)}) copy-start(f32[4,8,1024]{2,1,0:T(8,128)} %copy-done.8) | copy-start | bytes 393220
  93.0 7.5 %collective-permute-start.15 = (f32[8,128]{1,0:T(8,128)S(1)}, f32[8,128]{1,0:T(8,128)S(1)}, u32[]{:S(2)}, u32[]{:S(2)}) collective-permute-start(f32[8,128]{1,0:T(8,128)S(1)} %add_add_fusion.1), channel_id=1, source_target_pairs={{0,1},{1,0},{2,3},{3,2},{4,5},{5,4},{6,7},{7,6},{8,9},{9,8},{10,11... | collective-permute-start | bytes 12296 | tf_op jit(solution)/shard_map/ppermute | solution.py:63
  93.0 7.4 %collective-permute-start.16 = (f32[8,128]{1,0:T(8,128)S(1)}, f32[8,128]{1,0:T(8,128)S(1)}, u32[]{:S(2)}, u32[]{:S(2)}) collective-permute-start(f32[8,128]{1,0:T(8,128)S(1)} %add_add_fusion.1), channel_id=1, source_target_pairs={{0,2},{1,3},{2,0},{3,1},{4,6},{5,7},{6,4},{7,5},{8,10},{9,11},{10,... | collective-permute-start | bytes 12296 | tf_op jit(solution)/shard_map/ppermute | solution.py:63
  94.6 5.8 %collective-permute-start.17 = (f32[8,128]{1,0:T(8,128)S(1)}, f32[8,128]{1,0:T(8,128)S(1)}, u32[]{:S(2)}, u32[]{:S(2)}) collective-permute-start(f32[8,128]{1,0:T(8,128)S(1)} %add_add_fusion.1), channel_id=1, source_target_pairs={{0,3},{1,2},{2,1},{3,0},{4,7},{5,6},{6,5},{7,4},{8,11},{9,10},{10,... | collective-permute-start | bytes 12296 | tf_op jit(solution)/shard_map/ppermute | solution.py:99
  99.8 0.6 copy-start.15

commit v6 on v4

--- a/solution.py
+++ b/solution.py
@@ -11,6 +11,7 @@
 LOG2E = math.log2(math.e)
 DEPTH = 64
 TILE = 256
+STRIP = 128
 F32 = jnp.float32
 BF16 = jnp.bfloat16
 
@@ -37,8 +38,18 @@
     return jnp.concatenate(order + [tail, jnp.zeros_like(tail)], axis=0)
 
 
-def stacked(value):
-    return jnp.concatenate(pieces(value, 2), axis=0).astype(BF16)
+def put_dirs(dirs_ref, at, value):
+    both = jnp.concatenate(pieces(value, 2), axis=0).astype(BF16)
+    for k in range(value.shape[1] // STRIP):
+        part = both[:, k * STRIP : (k + 1) * STRIP]
+        dirs_ref[at, :, 2 * k * STRIP : 2 * (k + 1) * STRIP] = jnp.concatenate(
+            [part, part], axis=1
+        )
+
+
+def put_own(own_ref, rows):
+    for c in range(own_ref.shape[0]):
+        own_ref[c] = rows[:, c * TILE : (c + 1) * TILE].astype(BF16)
 
 
 def shifted(value, stride, size, by):
@@ -68,14 +79,23 @@
     return [own], line, beside + across[:1], across[1:]
 
 
-def summed(value):
+def along_line(value):
     far, near = digits()
-    value = sum([shifted(value, 2 * near, far, by) for by in range(1, far)], value)
+    return [shifted(value, 2 * near, far, by) for by in range(1, far)]
+
+
+def over_quad(value):
+    _, near = digits()
+    length = lax.axis_size("row")
     quad = [shifted(value, 1, 2, 1)]
     for by in range(1, near):
-        beside = shifted(value, 2, near, by)
-        quad += [beside, shifted(beside, 1, 2, 1)]
-    return sum(quad, value)
+        quad.append(shifted(value, 2, near, by))
+        pairs = []
+        for i in range(length):
+            digit = (i // 2) % near
+            pairs.append((i, (i + ((digit - by) % near - digit) * 2) ^ 1))
+        quad.append(lax.ppermute(value, "row", pairs))
+    return quad
 
 
 def tables():
@@ -103,21 +123,37 @@
     return [jnp.concatenate(t) for t in (first, second, last_first, last_second)]
 
 
-def add_block(yt_ref, at, own_ref, dirs, acc_ref):
-    for c in range(own_ref.shape[1] // TILE):
-        cols = slice(c * TILE, (c + 1) * TILE)
-        expo = jnp.dot(yt_ref[at], own_ref[:, cols], preferred_element_type=F32)
-        weight = jnp.exp2(expo)
-        high = weight.astype(BF16)
-        low = (weight - high.astype(F32)).astype(BF16)
-        acc_ref[:, cols] += jnp.dot(
-            dirs, high, preferred_element_type=F32
-        ) + jnp.dot(dirs, low, preferred_element_type=F32)
+def add_blocks(yt_ref, own_ref, dirs_ref, acc_ref, count, block):
+    acc_ref[...] = jnp.zeros_like(acc_ref)
+    chunks = own_ref.shape[0]
+
+    def step(t, carry):
+        c = t % chunks
+        b = block(t // chunks)
+        own = own_ref[c]
+        total = acc_ref[c]
+        for k in range(yt_ref.shape[1] // STRIP):
+            rows = slice(k * STRIP, (k + 1) * STRIP)
+            expo = jnp.dot(yt_ref[b, rows, :], own, preferred_element_type=F32)
+            weight = jnp.exp2(expo)
+            high = weight.astype(BF16)
+            low = (weight - high.astype(F32)).astype(BF16)
+            total = total + jnp.dot(
+                dirs_ref[b, :, 2 * k * STRIP : 2 * (k + 1) * STRIP],
+                jnp.concatenate([high, low], axis=0),
+                preferred_element_type=F32,
+            )
+        acc_ref[c] = total
+        return carry
+
+    lax.fori_loop(0, count * chunks, step, 0)
 
 
 def folded(acc_ref):
-    nrhs = acc_ref.shape[0] // 2
-    return acc_ref[0:nrhs, :] + acc_ref[nrhs:, :]
+    nrhs = acc_ref.shape[1] // 2
+    return jnp.concatenate(
+        [acc_ref[c, 0:nrhs, :] + acc_ref[c, nrhs:, :] for c in range(acc_ref.shape[0])], axis=1
+    )
 
 
 def each(stacks, function):
@@ -144,24 +180,17 @@
     refs = refs[nstacks:]
     if first:
         own_ref = refs.pop(0)
-        own_ref[...] = exponent_rows(
-            stacks[0][0, 0:nfeat, :] / scale_ref[...], 1.0, False
-        ).astype(BF16)
+        points = stacks[0][0, 0:nfeat, :] / scale_ref[...]
+        put_own(own_ref, exponent_rows(points, 1.0, False))
     yt_ref, out_ref, dirs_ref, acc_ref = refs
 
     def prepare(b, value):
         rows = exponent_rows(value[0:nfeat, :] / scale_ref[...], LOG2E, True)
         yt_ref[b] = rows.T.astype(BF16)
-        dirs_ref[b] = stacked(value[nfeat:, :])
+        put_dirs(dirs_ref, b, value[nfeat:, :])
 
     each(stacks, prepare)
-    acc_ref[...] = jnp.zeros_like(acc_ref)
-
-    def step(b, carry):
-        add_block(yt_ref, b, own_ref, dirs_ref[b], acc_ref)
-        return carry
-
-    lax.fori_loop(0, yt_ref.shape[0], step, 0)
+    add_blocks(yt_ref, own_ref, dirs_ref, acc_ref, yt_ref.shape[0], lambda b: b)
     total = folded(acc_ref)
     if not first:
         total = total + sofar_ref[...]
@@ -183,17 +212,14 @@
     dirs_ref, acc_ref = refs
 
     def prepare(b, value):
-        dirs_ref[b] = stacked(value)
+        put_dirs(dirs_ref, b, value)
 
     each(stacks, prepare)
-    acc_ref[...] = jnp.zeros_like(acc_ref)
-
-    def step(s, carry):
-        b = table_ref[s] if table else s
-        add_block(yt_ref, b, own_ref, dirs_ref[b], acc_ref)
-        return carry
-
-    lax.fori_loop(0, table_ref.shape[0] if table else yt_ref.shape[0], step, 0)
+    add_blocks(
+        yt_ref, own_ref, dirs_ref, acc_ref,
+        table_ref.shape[0] if table else yt_ref.shape[0],
+        lambda s: table_ref[s] if table else s,
+    )
     total = folded(acc_ref)
     if sofar:
         total = total + sofar_ref[...]
@@ -274,8 +300,8 @@
             out_shape=out_shape,
             in_specs=[smem if table and k == 0 else vmem for k in range(len(operands))],
             scratch_shapes=[
-                pltpu.VMEM((blocks, 2 * nrhs, width), BF16),
-                pltpu.VMEM((2 * nrhs, width), F32),
+                pltpu.VMEM((blocks, 2 * nrhs, 2 * width), BF16),
+                pltpu.VMEM((width // TILE, 2 * nrhs, TILE), F32),
             ],
             compiler_params=pltpu.CompilerParams(
                 vmem_limit_bytes=min(16 * 1024 * 1024 + blocks * 1024 * width, 60 * 1024 * 1024)
@@ -294,7 +320,7 @@
 
     groups = gathered(jnp.concatenate([features, rhs], axis=0))
     mine = groups[0][0]
-    own_shape = jax.ShapeDtypeStruct((DEPTH, width), BF16)
+    own_shape = jax.ShapeDtypeStruct((width // TILE, DEPTH, TILE), BF16)
     own, points, total = call(
         functools.partial(over_points, nfeat, 1, True, None),
         1, 1, (own_shape, points_shape(groups[0]), field), (scale, mine), "own_block",
@@ -333,9 +359,14 @@
         3, (field, small), "across_half", sofar=(half,), table=last_first,
         form=(once, noise, image),
     )
-    form = summed(form)
+    parts = along_line(form)
     total = again(2, field, "beside_rest", sofar=(total,), table=second)
+    *parts, total = lax.optimization_barrier((*parts, total))
+    form = sum(parts, form)
+    parts = over_quad(form)
     total = again(3, field, "across_rest", sofar=(total,), table=last_second)
+    *parts, total = lax.optimization_barrier((*parts, total))
+    form = sum(parts, form)
     flat = [s for g in groups for s in g]
     flat_images = [s for g in images for s in g]
     scalars = pl.pallas_call(

time: 89.9 us -> 105 us (1.17)
  Pallas kernels: 57.1 us -> 78.7 us
  waiting for transfers between devices: 11.5 us -> 3.81 us
    pallas_call x10, Pallas kernels: 53 us -> 74.6 us  [call(): pl.pallas_call(kernel, out_shape=out_shape, in_specs=[smem if table and k...]
    ppermute x18 -> x17, waiting for transfers between devices: 11.5 us -> 3.81 us  [shifted(): return lax.ppermute(value, 'row', pairs)]
    ppermute x18 -> x17, starting transfers between devices: 17.1 us -> 17.8 us  [shifted(): return lax.ppermute(value, 'row', pairs)]
  transfers between devices with their start and end apart: 18 -> 18, of which waited for: 7 -> 3; matrix products, arithmetic and copies ran while one was open for 1% -> 1% of each run, Pallas kernels for 50% -> 60%
where the time goes in v6:
time: 105 us; the launch traced here: 104 us
  Pallas kernels  78.7 us (75%)
  starting transfers between devices  18.1 us (17%)
  waiting for transfers between devices  3.81 us (4%)
  other arithmetic  1.59 us (2%)
  local copies, waits for them, and re-layouts  1.4 us (1%)
    pallas_call x10, Pallas kernels, call(): pl.pallas_call(kernel, out_shape=out_shape, in_specs=[smem if table and k...  74.6 us
    ppermute x17, starting transfers between devices, shifted(): return lax.ppermute(value, 'row', pairs)  17.8 us
    ppermute x17, waiting for transfers between devices, shifted(): return lax.ppermute(value, 'row', pairs)  3.81 us
    pallas_call x1, Pallas kernels, shards(): pl.pallas_call(functools.partial(scalars_kernel, nfeat, len(flat)), out_s...  2.5 us
  transfers between devices with their start and end apart: 18, of which 3 were waited for; matrix products, arithmetic and copies ran while one was open for 1% of the time, Pallas kernels for 60%

profile of v6, /device:TPU:0, one launch (start us, length us, event | category | flops | bytes accessed | tf_op | source)
XLA Modules:
  0.0 104.5 jit_solution(16043798570843667558)
XLA Ops:
  0.6 0.8 maximum_bitcast_fusion.refs_1_.refs_4_.refs_0_.mine_ref
  1.4 5.1 %collective-permute-start = (f32[1,16,1024]{2,1,0:T(8,128)S(1)}, f32[1,16,1024]{2,1,0:T(8,128)S(1)}, u32[]{:S(2)}, u32[]{:S(2)}) collective-permute-start(f32[1,16,1024]{2,1,0:T(8,128)S(1)} %maximum_bitcast_fusion.refs_1_.refs_4_.refs_0_.mine_ref), channel_id=1, source_target_pairs={{0,12},{1,13},{2,14},{3,15},{4,0},{5,1},{6,2},{7,3},{8,4},{9,5},{1... | collective-permute-start | bytes 196616 | tf_op jit(solution)/shard_map/ppermute | solution.py:61
  6.5 0.0 collective-permute-start.1
  6.5 1.0 collective-permute-start.2
  7.5 0.7 copy.9.refs_0_
  8.3 2.4 %own_block.1 = (bf16[4,64,256]{2,1,0:T(8,128)(2,1)S(1)}, bf16[1,1024,64]{2,1,0:T(8,128)(2,1)S(1)}, f32[8,1024]{1,0:T(8,128)S(1)}) custom-call(f32[8,1]{1,0:T(8,128)S(1)} %copy.9.refs_0_, f32[1,16,1024]{2,1,0:T(8,128)S(1)} %maximum_bitcast_fusion.refs_1_.refs_4_.refs_0_.mine_ref), custom_call_target="tpu_custom_call" | custom-call | flops 2147483648 | bytes 1048576 | tf_op jit(solution)/shard_map/own_block/pallas_call | solution.py:298
  10.7 0.1 pad_add_fusion.refs_0_
  10.8 0.1 pad_add_fusion.1.refs_0_
  10.8 0.0 collective-permute-done.refs_3_.refs_1_
  10.8 2.1 %collective-permute-done.1.refs_4_.refs_2_ = f32[1,16,1024]{2,1,0:T(8,128)S(1)} collective-permute-done((f32[1,16,1024]{2,1,0:T(8,128)S(1)}, f32[1,16,1024]{2,1,0:T(8,128)S(1)}, u32[]{:S(2)}, u32[]{:S(2)}) %collective-permute-start.1) | collective-permute-done | bytes 65568 | tf_op jit(solution)/shard_map/ppermute | solution.py:61
  13.0 0.0 collective-permute-done.2.refs_5_.refs_3_
  13.0 1.6 %collective-permute-start.3 = (f32[4,16,1024]{2,1,0:T(8,128)S(1)}, f32[4,16,1024]{2,1,0:T(8,128)S(1)}, u32[]{:S(2)}, u32[]{:S(2)}) collective-permute-start(f32[4,16,1024]{2,1,0:T(8,128)S(1)} %pad_maximum_fusion), channel_id=1, source_target_pairs={{0,2},{1,3},{2,0},{3,1},{4,6},{5,7},{6,4},{7,5},{8,10},{9,11},{10,... | collective-permute-start | bytes 786440 | tf_op jit(solution)/shard_map/ppermute | solution.py:61
  14.6 0.0 collective-permute-start.4
  14.6 6.8 %blocks_0.1 = (bf16[3,1024,64]{2,1,0:T(8,128)(2,1)S(1)}, f32[8,1024]{1,0:T(8,128)S(1)}) custom-call(f32[8,1]{1,0:T(8,128)S(1)} %copy.9.refs_0_, bf16[4,64,256]{2,1,0:T(8,128)(2,1)S(1)} %get-tuple-element.21.refs_1_.refs_0_.refs_5_.refs_2_, f32[8,1024]{1,0:T(8,128)S(1)} %get-tuple-element.22.refs_2_, f32[1,16,1024]{2,1,0:T(8,128)S(1)} %collective-permute-done.refs_3_.refs_1_, ...), custom_call_target="tpu_custom_call" | custom-call | flops 6442450944 | bytes 1048576 | tf_op jit(solution)/shard_map/blocks_0/pallas_call | solution.py:298
  21.4 0.0 copy-done.5
  21.4 0.0 copy-done.6
  21.4 0.0 copy-done.7
  21.4 0.0 collective-permute-done.3.refs_3_.refs_4_
  21.5 0.6 collective-permute-start.5
  22.0 0.0 collective-permute-done.4.refs_4_.refs_5_
  22.0 19.0 %blocks_1.1 = (bf16[8,1024,64]{2,1,0:T(8,128)(2,1)S(1)}, f32[8,1024]{1,0:T(8,128)S(1)}) custom-call(f32[8,1]{1,0:T(8,128)S(1)} %copy.9.refs_0_, bf16[4,64,256]{2,1,0:T(8,128)(2,1)S(1)} %get-tuple-element.21.refs_1_.refs_0_.refs_5_.refs_2_, f32[8,1024]{1,0:T(8,128)S(1)} %get-tuple-element.23.refs_2_, ...), custom_call_target="tpu_custom_call" | custom-call | flops 17179869184 | bytes 1048576 | tf_op jit(solution)/shard_map/blocks_1/pallas_call | solution.py:298
  41.0 0.0 copy-done.2
  41.0 0.0 collective-permute-done.5.refs_5_.refs_6_
  41.1 9.5 %blocks_2.1 = (bf16[4,1024,64]{2,1,0:T(8,128)(2,1)S(1)}, f32[8,1024]{1,0:T(8,128)S(1)}) custom-call(f32[8,1]{1,0:T(8,128)S(1)} %copy.9.refs_0_, bf16[4,64,256]{2,1,0:T(8,128)(2,1)S(1)} %get-tuple-element.21.refs_1_.refs_0_.refs_5_.refs_2_, f32[8,1024]{1,0:T(8,128)S(1)} %get-tuple-element.24.refs_2_, f32[1,1024]{1,0:T(1,128)S(1)} %bitcast.14, ...), custom_call_target="tpu_custom_call" | custom-call | flops 8589934592 | bytes 1048576 | tf_op jit(solution)/shard_map/blocks_2/pallas_call | solution.py:298
  50.6 0.0 copy-done.4
  50.6 0.0 copy-start.1
  50.6 1.9 %collective-permute-start.6 = (f32[1,8,1024]{2,1,0:T(8,128)S(1)}, f32[1,8,1024]{2,1,0:T(8,128)S(1)}, u32[]{:S(2)}, u32[]{:S(2)}) collective-permute-start(f32[1,8,1024]{2,1,0:T(8,128)S(1)} %bitcast.5), channel_id=1, source_target_pairs={{0,12},{1,13},{2,14},{3,15},{4,0},{5,1},{6,2},{7,3},{8,4},{9,5},{1... | collective-permute-start | bytes 98312 | tf_op jit(solution)/shard_map/ppermute | solution.py:61
  52.5 0.0 collective-permute-start.7
  52.5 1.9 %collective-permute-start.8 = (f32[1,8,1024]{2,1,0:T(8,128)S(1)}, f32[1,8,1024]{2,1,0:T(8,128)S(1)}, u32[]{:S(2)}, u32[]{:S(2)}) collective-permute-start(f32[1,8,1024]{2,1,0:T(8,128)S(1)} %bitcast.7), channel_id=1, source_target_pairs={{0,4},{1,5},{2,6},{3,7},{4,8},{5,9},{6,10},{7,11},{8,12},{9,13},{1... | collective-permute-start | bytes 98312 | tf_op jit(solution)/shard_map/ppermute | solution.py:61
  54.4 2.2 %own_again.1.refs_0_ = f32[8,1024]{1,0:T(8,128)S(1)} custom-call(bf16[4,64,256]{2,1,0:T(8,128)(2,1)S(1)} %get-tuple-element.21.refs_1_.refs_0_.refs_5_.refs_2_, bf16[1,1024,64]{2,1,0:T(8,128)(2,1)S(1)} %get-tuple-element.27.refs_1_, f32[1,8,1024]{2,1,0:T(8,128)S(1)} %bitcast.8), custom_call_target="tpu_custom_call" | custom-call | flops 2147483648 | bytes 1048576 | tf_op jit(solution)/shard_map/own_again/pallas_call | solution.py:298
  56.6 0.0 collective-permute-done.6.refs_8_.refs_3_
  56.6 0.0 copy-start.12
  56.6 1.0 collective-permute-done.7.refs_9_.refs_4_
  57.6 0.6 collective-permute-done.8.refs_10_.refs_5_
  58.2 0.1 collective-permute-start.10
  58.3 0.6 collective-permute-start.9
  58.9 6.5 %line_again.1.refs_2_ = f32[8,1024]{1,0:T(8,128)S(1)} custom-call(f32[8,1024]{1,0:T(8,128)S(1)} %own_again.1.refs_0_, bf16[4,64,256]{2,1,0:T(8,128)(2,1)S(1)} %get-tuple-element.21.refs_1_.refs_0_.refs_5_.refs_2_, bf16[3,1024,64]{2,1,0:T(8,128)(2,1)S(1)} %get-tuple-element.28.refs_2_, f32[1,8,1024]{2,1,0:T(8,128)S(1)} %collective-permute-done.6.refs_8_.refs_3_, ...), custom_call_target="tpu_custom_call" | custom-call | flops 6442450944 | bytes 1048576 | tf_op jit(solution)/shard_map/line_again/pallas_call | solution.py:298
  65.4 0.0 copy-done.12
  65.4 0.0 collective-permute-done.9.refs_11_.refs_3_.refs_4_
  65.4 0.0 copy-start.11
  65.4 0.2 collective-permute-start.11
  65.7 0.0 collective-permute-done.10.refs_12_.refs_4_.refs_5_
  65.7 9.2 %beside_half.1.refs_1_ = f32[8,1024]{1,0:T(8,128)S(1)} custom-call(s32[4]{0:T(128)S(1)} %pad_add_fusion.refs_0_, bf16[4,64,256]{2,1,0:T(8,128)(2,1)S(1)} %get-tuple-element.21.refs_1_.refs_0_.refs_5_.refs_2_, bf16[8,1024,64]{2,1,0:T(8,128)(2,1)S(1)} %get-tuple-element.26.refs_2_.refs_3_, f32[4,8,1024]{2,1,0:T(8,128)S(1)} %collective-permute-done.9.refs_11_.refs_3_.refs_4_, ...), custom_call_target="tpu_custom_call" | custom-call | flops 8589934592 | bytes 1048576 | tf_op jit(solution)/shard_map/beside_half/pallas_call | solution.py:298
  74.9 0.0 collective-permute-done.11.refs_13_.refs_7_.refs_4_
  74.9 5.0 %across_half.1 = (f32[8,1024]{1,0:T(8,128)S(1)}, f32[8,128]{1,0:T(8,128)S(1)}) custom-call(s32[2]{0:T(128)S(1)} %fusion.2.refs_0_, f32[8,1024]{1,0:T(8,128)S(1)} %beside_half.1.refs_1_, f32[8,1024]{1,0:T(8,128)S(1)} %line_again.1.refs_2_, f32[1,1024]{1,0:T(1,128)S(1)} %bitcast.15, f32[1,8,1024]{2,1,0:T(8,128)S(1)} %bitcast.10, ...), custom_call_target="tpu_custom_call" | custom-call | flops 4294967296 | bytes 1048576 | tf_op jit(solution)/shard_map/across_half/pallas_call | solution.py:298
  79.9 1.2 %collective-permute-start.12 = (f32[8,128]{1,0:T(8,128)S(1)}, f32[8,128]{1,0:T(8,128)S(1)}, u32[]{:S(2)}, u32[]{:S(2)}) collective-permute-start(f32[8,128]{1,0:T(8,128)S(1)} %get-tuple-element.30), channel_id=1, source_target_pairs={{0,12},{1,13},{2,14},{3,15},{4,0},{5,1},{6,2},{7,3},{8,4},{9,5},{1... | collective-permute-start | bytes 12296 | tf_op jit(solution)/shard_map/ppermute | solution.py:61
  81.1 0.4 collective-permute-start.13
  81.5 1.6 %collective-permute-start.14 = (f32[8,128]{1,0:T(8,128)S(1)}, f32[8,128]{1,0:T(8,128)S(1)}, u32[]{:S(2)}, u32[]{:S(2)}) collective-permute-start(f32[8,128]{1,0:T(8,128)S(1)} %get-tuple-element.30), channel_id=1, source_target_pairs={{0,4},{1,5},{2,6},{3,7},{4,8},{5,9},{6,10},{7,11},{8,12},{9,13},{1... | collective-permute-start | bytes 12296 | tf_op jit(solution)/shard_map/ppermute | solution.py:61
  83.0 0.0 copy-done.11
  83.1 9.2 %beside_rest.1.refs_1_ = f32[8,1024]{1,0:T(8,128)S(1)} custom-call(s32[4]{0:T(128)S(1)} %pad_add_fusion.1.refs_0_, f32[8,1024]{1,0:T(8,128)S(1)} %get-tuple-element.31.refs_1_, bf16[4,64,256]{2,1,0:T(8,128)(2,1)S(1)} %get-tuple-element.21.refs_1_.refs_0_.refs_5_.refs_2_, bf16[8,1024,64]{2,1,0:T(8,128)(2,1)S(1)} %get-tuple-element.26.refs_2_.refs_3_, ...), custom_call_target="tpu_custom_call" | custom-call | flops 8589934592 | bytes 1048576 | tf_op jit(solution)/shard_map/beside_rest/pallas_call | solution.py:298
  92.3 2.5 %scalars.1.scalars_ref = f32[4,8,128]{2,1,0:T(8,128)} custom-call(f32[1,16,1024]{2,1,0:T(8,128)} %copy-done, f32[1,16,1024]{2,1,0:T(8,128)} %copy-done.5, f32[1,16,1024]{2,1,0:T(8,128)} %copy-done.6, f32[1,16,1024]{2,1,0:T(8,128)} %copy-done.7, f32[4,16,1024]{2,1,0:T(8,128)} %copy-done.2, f32[4,16,1024]{2,1,0:T(8,128)} %copy-done.3, ...), custom_call_target="tpu_custom_call" | custom-call | tf_op jit(solution)/shard_map/scalars/pallas_call | solution.py:372
  94.8 0.0 collective-permute-done.12
  94.8 0.0 collective-permute-done.13
  94.8 0.0 collective-permute-done.14
  94.8 0.1 collective-permute-start.15
  94.9 1.6 %collective-permute-start.16 = (f32[8,128]{1,0:T(8,128)S(1)}, f32[8,128]{1,0:T(8,128)S(1)}, u32[]{:S(2)}, u32[]{:S(2)}) collective-permute-start(f32[8,128]{1,0:T(8,128)S(1)} %add_add_fusion.1), channel_id=1, source_target_pairs={{0,2},{1,3},{2,0},{3,1},{4,6},{5,7},{6,4},{7,5},{8,10},{9,11},{10,... | collective-permute-start | bytes 12296 | tf_op jit(solution)/shard_map/ppermute | solution.py:61
  96.5 0.3 collective-permute-start.17
  96.8 4.9 %across_rest.1.total_ref = f32[8,1024]{1,0:T(8,128)S(1)} custom-call(s32[2]{0:T(128)S(1)} %fusion.3.refs_0_, f32[8,1024]{1,0:T(8,128)S(1)} %beside_rest.1.refs_1_, bf16[4,64,256]{2,1,0:T(8,128)(2,1)S(1)} %get-tuple-element.21.refs_1_.refs_0_.refs_5_.refs_2_, bf16[4,1024,64]{2,1,0:T(8,128)(2,1)S(1)} %get-tuple-element.29.refs_6_.refs_3_, ...), custom_call_target="tpu_custom_call" | custom-call | flops 4294967296 | bytes 1048576 | tf_op jit(solution)/shard_map/across_rest/pallas_call | solution.py:298
  101.7 0.6 copy-done.15
  102.3 0.0 collective-permute-done.15
  102.3 0.0 collective-permute-done.16
  102.3 0.0 collective-permute-done.17
  102.3 0.6 add_add_fusion.form_ref
  102.9 1.6 %last_update.1 = (f32[8,1024]{1,0:T(8,128)}, f32[8,1024]{1,0:T(8,128)}) custom-call(f32[4,8,128]{2,1,0:T(8,128)} %scalars.1.scalars_ref, f32[8,128]{1,0:T(8,128)} %add_add_fusion.form_ref, f32[8,1024]{1,0:T(8,128)} %copy-done.15, f32[1,1024]{1,0:T(1,128)} %bitcast.13, f32[1,16,1024]{2,1,0:T(8,128)} %copy-done, f32[1,8,1024]{2,1,0:T(8,128)} %bitcast.12), custom_call_target="tpu_custom_call" | custom-call | tf_op jit(solution)/shard_map/last_update/pallas_call | solution.py:377
  (30 shorter events, 0.1 us)
Async XLA Ops:
  1.4 39.6 %copy-start = (f32[1,16,1024]{2,1,0:T(8,128)}, f32[1,16,1024]{2,1,0:T(8,128)S(1)}, u32[]{:S(2)}) copy-start(f32[1,16,1024]{2,1,0:T(8,128)S(1)} %maximum_bitcast_fusion.refs_1_.refs_4_.refs_0_.mine_ref) | copy-start | bytes 196612
  1.4 9.4 %collective-permute-start = (f32[1,16,1024]{2,1,0:T(8,128)S(1)}, f32[1,16,1024]{2,1,0:T(8,128)S(1)}, u32[]{:S(2)}, u32[]{:S(2)}) collective-permute-start(f32[1,16,1024]{2,1,0:T(8,128)S(1)} %maximum_bitcast_fusion.refs_1_.refs_4_.refs_0_.mine_ref), channel_id=1, source_target_pairs={{0,12},{1,13},{2,14},{3,15},{4,0},{5,1},{6,2},{7,3},{8,4},{9,5},{1... | collective-permute-start | bytes 196616 | tf_op jit(solution)/shard_map/ppermute | solution.py:61
  6.5 6.5 %collective-permute-start.1 = (f32[1,16,1024]{2,1,0:T(8,128)S(1)}, f32[1,16,1024]{2,1,0:T(8,128)S(1)}, u32[]{:S(2)}, u32[]{:S(2)}) collective-permute-start(f32[1,16,1024]{2,1,0:T(8,128)S(1)} %maximum_bitcast_fusion.refs_1_.refs_4_.refs_0_.mine_ref), channel_id=1, source_target_pairs={{0,8},{1,9},{2,10},{3,11},{4,12},{5,13},{6,14},{7,15},{8,0},{9,1},... | collective-permute-start | bytes 196616 | tf_op jit(solution)/shard_map/ppermute | solution.py:61
  6.5 6.5 %collective-permute-start.2 = (f32[1,16,1024]{2,1,0:T(8,128)S(1)}, f32[1,16,1024]{2,1,0:T(8,128)S(1)}, u32[]{:S(2)}, u32[]{:S(2)}) collective-permute-start(f32[1,16,1024]{2,1,0:T(8,128)S(1)} %maximum_bitcast_fusion.refs_1_.refs_4_.refs_0_.mine_ref), channel_id=1, source_target_pairs={{0,4},{1,5},{2,6},{3,7},{4,8},{5,9},{6,10},{7,11},{8,12},{9,13},{1... | collective-permute-start | bytes 196616 | tf_op jit(solution)/shard_map/ppermute | solution.py:61
  10.8 10.6 %copy-start.5 = (f32[1,16,1024]{2,1,0:T(8,128)}, f32[1,16,1024]{2,1,0:T(8,128)S(1)}, u32[]{:S(2)}) copy-start(f32[1,16,1024]{2,1,0:T(8,128)S(1)} %collective-permute-done.refs_3_.refs_1_) | copy-start | bytes 196612
  13.0 8.4 %copy-start.6 = (f32[1,16,1024]{2,1,0:T(8,128)}, f32[1,16,1024]{2,1,0:T(8,128)S(1)}, u32[]{:S(2)}) copy-start(f32[1,16,1024]{2,1,0:T(8,128)S(1)} %collective-permute-done.1.refs_4_.refs_2_) | copy-start | bytes 196612
  13.0 8.5 %copy-start.7 = (f32[1,16,1024]{2,1,0:T(8,128)}, f32[1,16,1024]{2,1,0:T(8,128)S(1)}, u32[]{:S(2)}) copy-start(f32[1,16,1024]{2,1,0:T(8,128)S(1)} %collective-permute-done.2.refs_5_.refs_3_) | copy-start | bytes 196612
  13.0 8.4 %collective-permute-start.3 = (f32[4,16,1024]{2,1,0:T(8,128)S(1)}, f32[4,16,1024]{2,1,0:T(8,128)S(1)}, u32[]{:S(2)}, u32[]{:S(2)}) collective-permute-start(f32[4,16,1024]{2,1,0:T(8,128)S(1)} %pad_maximum_fusion), channel_id=1, source_target_pairs={{0,2},{1,3},{2,0},{3,1},{4,6},{5,7},{6,4},{7,5},{8,10},{9,11},{10,... | collective-permute-start | bytes 786440 | tf_op jit(solution)/shard_map/ppermute | solution.py:61
  14.6 7.4 %collective-permute-start.4 = (f32[4,16,1024]{2,1,0:T(8,128)S(1)}, f32[4,16,1024]{2,1,0:T(8,128)S(1)}, u32[]{:S(2)}, u32[]{:S(2)}) collective-permute-start(f32[4,16,1024]{2,1,0:T(8,128)S(1)} %pad_maximum_fusion), channel_id=1, source_target_pairs={{0,1},{1,0},{2,3},{3,2},{4,5},{5,4},{6,7},{7,6},{8,9},{9,8},{10,11... | collective-permute-start | bytes 786440 | tf_op jit(solution)/shard_map/ppermute | solution.py:61
  21.5 19.5 %copy-start.2 = (f32[4,16,1024]{2,1,0:T(8,128)}, f32[4,16,1024]{2,1,0:T(8,128)S(1)}, u32[]{:S(2)}) copy-start(f32[4,16,1024]{2,1,0:T(8,128)S(1)} %collective-permute-done.3.refs_3_.refs_4_) | copy-start | bytes 786436
  21.5 19.6 %collective-permute-start.5 = (f32[4,16,1024]{2,1,0:T(8,128)S(1)}, f32[4,16,1024]{2,1,0:T(8,128)S(1)}, u32[]{:S(2)}, u32[]{:S(2)}) collective-permute-start(f32[4,16,1024]{2,1,0:T(8,128)S(1)} %collective-permute-done.3.refs_3_.refs_4_), channel_id=1, source_target_pairs={{0,1},{1,0},{2,3},{3,2},{4,5},{5,4},{6,7},{7,6},{8,9},{9,8},{10,11... | collective-permute-start | bytes 786440 | tf_op jit(solution)/shard_map/ppermute | solution.py:61
  22.0 19.0 %copy-start.3 = (f32[4,16,1024]{2,1,0:T(8,128)}, f32[4,16,1024]{2,1,0:T(8,128)S(1)}, u32[]{:S(2)}) copy-start(f32[4,16,1024]{2,1,0:T(8,128)S(1)} %collective-permute-done.4.refs_4_.refs_5_) | copy-start | bytes 786436
  22.0 19.0 %copy-start.16 = (f32[1024]{0:T(1024)S(1)}, f32[1024]{0:T(1024)}, u32[]{:S(2)}) copy-start(f32[1024]{0:T(1024)} %param.6) | copy-start | bytes 12292
  41.0 9.5 %copy-start.4 = (f32[4,16,1024]{2,1,0:T(8,128)}, f32[4,16,1024]{2,1,0:T(8,128)S(1)}, u32[]{:S(2)}) copy-start(f32[4,16,1024]{2,1,0:T(8,128)S(1)} %collective-permute-done.5.refs_5_.refs_6_) | copy-start | bytes 786436
  50.6 24.3 %copy-start.1 = (f32[8,1024]{1,0:T(8,128)}, f32[8,1024]{1,0:T(8,128)S(1)}, u32[]{:S(2)}) copy-start(f32[8,1024]{1,0:T(8,128)S(1)} %get-tuple-element.25) | copy-start | bytes 98308
  50.6 6.0 %collective-permute-start.6 = (f32[1,8,1024]{2,1,0:T(8,128)S(1)}, f32[1,8,1024]{2,1,0:T(8,128)S(1)}, u32[]{:S(2)}, u32[]{:S(2)}) collective-permute-start(f32[1,8,1024]{2,1,0:T(8,128)S(1)} %bitcast.5), channel_id=1, source_target_pairs={{0,12},{1,13},{2,14},{3,15},{4,0},{5,1},{6,2},{7,3},{8,4},{9,5},{1... | collective-permute-start | bytes 98312 | tf_op jit(solution)/shard_map/ppermute | solution.py:61
  52.5 5.1 %collective-permute-start.7 = (f32[1,8,1024]{2,1,0:T(8,128)S(1)}, f32[1,8,1024]{2,1,0:T(8,128)S(1)}, u32[]{:S(2)}, u32[]{:S(2)}) collective-permute-start(f32[1,8,1024]{2,1,0:T(8,128)S(1)} %bitcast.6), channel_id=1, source_target_pairs={{0,8},{1,9},{2,10},{3,11},{4,12},{5,13},{6,14},{7,15},{8,0},{9,1},... | collective-permute-start | bytes 98312 | tf_op jit(solution)/shard_map/ppermute | solution.py:61
  52.5 5.7 %collective-permute-start.8 = (f32[1,8,1024]{2,1,0:T(8,128)S(1)}, f32[1,8,1024]{2,1,0:T(8,128)S(1)}, u32[]{:S(2)}, u32[]{:S(2)}) collective-permute-start(f32[1,8,1024]{2,1,0:T(8,128)S(1)} %bitcast.7), channel_id=1, source_target_pairs={{0,4},{1,5},{2,6},{3,7},{4,8},{5,9},{6,10},{7,11},{8,12},{9,13},{1... | collective-permute-start | bytes 98312 | tf_op jit(solution)/shard_map/ppermute | solution.py:61
  56.6 8.8 %copy-start.12 = (f32[1,8,1024]{2,1,0:T(8,128)}, f32[1,8,1024]{2,1,0:T(8,128)S(1)}, u32[]{:S(2)}) copy-start(f32[1,8,1024]{2,1,0:T(8,128)S(1)} %collective-permute-done.6.refs_8_.refs_3_) | copy-start | bytes 98308
  57.6 7.8 %copy-start.13 = (f32[1,8,1024]{2,1,0:T(8,128)}, f32[1,8,1024]{2,1,0:T(8,128)S(1)}, u32[]{:S(2)}) copy-start(f32[1,8,1024]{2,1,0:T(8,128)S(1)} %collective-permute-done.7.refs_9_.refs_4_) | copy-start | bytes 98308
  58.2 7.2 %copy-start.14 = (f32[1,8,1024]{2,1,0:T(8,128)}, f32[1,8,1024]{2,1,0:T(8,128)S(1)}, u32[]{:S(2)}) copy-start(f32[1,8,1024]{2,1,0:T(8,128)S(1)} %collective-permute-done.8.refs_10_.refs_5_) | copy-start | bytes 98308
  58.2 7.4 %collective-permute-start.10 = (f32[4,8,1024]{2,1,0:T(8,128)S(1)}, f32[4,8,1024]{2,1,0:T(8,128)S(1)}, u32[]{:S(2)}, u32[]{:S(2)}) collective-permute-start(f32[4,8,1024]{2,1,0:T(8,128)S(1)} %pad_maximum_fusion.1), channel_id=1, source_target_pairs={{0,1},{1,0},{2,3},{3,2},{4,5},{5,4},{6,7},{7,6},{8,9},{9,8},{10,11... | collective-permute-start | bytes 393224 | tf_op jit(solution)/shard_map/ppermute | solution.py:61
  58.3 7.1 %collective-permute-start.9 = (f32[4,8,1024]{2,1,0:T(8,128)S(1)}, f32[4,8,1024]{2,1,0:T(8,128)S(1)}, u32[]{:S(2)}, u32[]{:S(2)}) collective-permute-start(f32[4,8,1024]{2,1,0:T(8,128)S(1)} %pad_maximum_fusion.1), channel_id=1, source_target_pairs={{0,2},{1,3},{2,0},{3,1},{4,6},{5,7},{6,4},{7,5},{8,10},{9,11},{10,... | collective-permute-start | bytes 393224 | tf_op jit(solution)/shard_map/ppermute | solution.py:61
  65.4 17.6 %copy-start.11 = (f32[4,8,1024]{2,1,0:T(8,128)}, f32[4,8,1024]{2,1,0:T(8,128)S(1)}, u32[]{:S(2)}) copy-start(f32[4,8,1024]{2,1,0:T(8,128)S(1)} %collective-permute-done.9.refs_11_.refs_3_.refs_4_) | copy-start | bytes 393220
  65.4 9.5 %collective-permute-start.11 = (f32[4,8,1024]{2,1,0:T(8,128)S(1)}, f32[4,8,1024]{2,1,0:T(8,128)S(1)}, u32[]{:S(2)}, u32[]{:S(2)}) collective-permute-start(f32[4,8,1024]{2,1,0:T(8,128)S(1)} %collective-permute-done.9.refs_11_.refs_3_.refs_4_), channel_id=1, source_target_pairs={{0,1},{1,0},{2,3},{3,2},{4,5},{5,4},{6,7},{7,6},{8,9},{9,8},{10,11... | collective-permute-start | bytes 393224 | tf_op jit(solution)/shard_map/ppermute | solution.py:61
  65.7 17.4 %copy-start.10 = (f32[4,8,1024]{2,1,0:T(8,128)}, f32[4,8,1024]{2,1,0:T(8,128)S(1)}, u32[]{:S(2)}) copy-start(f32[4,8,1024]{2,1,0:T(8,128)S(1)} %collective-permute-done.10.refs_12_.refs_4_.refs_5_) | copy-start | bytes 393220
  74.9 5.0 %copy-start.8 = (f32[4,8,1024]{2,1,0:T(8,128)}, f32[4,8,1024]{2,1,0:T(8,128)S(1)}, u32[]{:S(2)}) copy-start(f32[4,8,1024]{2,1,0:T(8,128)S(1)} %collective-permute-done.11.refs_13_.refs_7_.refs_4_) | copy-start | bytes 393220
  79.9 14.9 %collective-permute-start.12 = (f32[8,128]{1,0:T(8,128)S(1)}, f32[8,128]{1,0:T(8,128)S(1)}, u32[]{:S(2)}, u32[]{:S(2)}) collective-permute-start(f32[8,128]{1,0:T(8,128)S(1)} %get-tuple-element.30), channel_id=1, source_target_pairs={{0,12},{1,13},{2,14},{3,15},{4,0},{5,1},{6,2},{7,3},{8,4},{9,5},{1... | collective-permute-start | bytes 12296 | tf_op jit(solution)/shard_map/ppermute | solution.py:61
  81.1 13.7 %collective-permute-start.13 = (f32[8,128]{1,0:T(8,128)S(1)}, f32[8,128]{1,0:T(8,128)S(1)}, u32[]{:S(2)}, u32[]{:S(2)}) collective-permute-start(f32[8,128]{1,0:T(8,128)S(1)} %get-tuple-element.30), channel_id=1, source_target_pairs={{0,8},{1,9},{2,10},{3,11},{4,12},{5,13},{6,14},{7,15},{8,0},{9,1},... | collective-permute-start | bytes 12296 | tf_op jit(solution)/shard_map/ppermute | solution.py:61
  81.5 13.3 %collective-permute-start.14 = (f32[8,128]{1,0:T(8,128)S(1)}, f32[8,128]{1,0:T(8,128)S(1)}, u32[]{:S(2)}, u32[]{:S(2)}) collective-permute-start(f32[8,128]{1,0:T(8,128)S(1)} %get-tuple-element.30), channel_id=1, source_target_pairs={{0,4},{1,5},{2,6},{3,7},{4,8},{5,9},{6,10},{7,11},{8,12},{9,13},{1... | collective-permute-start | bytes 12296 | tf_op jit(solution)/shard_map/ppermute | solution.py:61
  83.1 13.7 %copy-start.9 = (f32[4,8,1024]{2,1,0:T(8,128)S(1)}, f32[4,8,1024]{2,1,0:T(8,128)}, u32[]{:S(2)}) copy-start(f32[4,8,1024]{2,1,0:T(8,128)} %copy-done.8) | copy-start | bytes 393220
  94.8 7.4 %collective-permute-start.15 = (f32[8,128]{1,0:T(8,128)S(1)}, f32[8,128]{1,0:T(8,128)S(1)}, u32[]{:S(2)}, u32[]{:S(2)}) collective-permute-start(f32[8,128]{1,0:T(8,128)S(1)} %add_add_fusion.1), channel_id=1, source_target_pairs={{0,1},{1,0},{2,3},{3,2},{4,5},{5,4},{6,7},{7,6},{8,9},{9,8},{10,11... | collective-permute-start | bytes 12296 | tf_op jit(solution)/shard_map/ppermute | solution.py:61
  94.9 7.4 %collective-permute-start.16 = (f32[8,128]{1,0:T(8,128)S(1)}, f32[8,128]{1,0:T(8,128)S(1)}, u32[]{:S(2)}, u32[]{:S(2)}) collective-permute-start(f32[8,128]{1,0:T(8,128)S(1)} %add_add_fusion.1), channel_id=1, source_target_pairs={{0,2},{1,3},{2,0},{3,1},{4,6},{5,7},{6,4},{7,5},{8,10},{9,11},{10,... | collective-permute-start | bytes 12296 | tf_op jit(solution)/shard_map/ppermute | solution.py:61
  96.5 5.8 %collective-permute-start.17 = (f32[8,128]{1,0:T(8,128)S(1)}, f32[8,128]{1,0:T(8,128)S(1)}, u32[]{:S(2)}, u32[]{:S(2)}) collective-permute-start(f32[8,128]{1,0:T(8,128)S(1)} %add_add_fusion.1), channel_id=1, source_target_pairs={{0,3},{1,2},{2,1},{3,0},{4,7},{5,6},{6,5},{7,4},{8,11},{9,10},{10,... | collective-permute-start | bytes 12296 | tf_op jit(solution)/shard_map/ppermute | solution.py:97
  101.7 0.6 copy-start.15

commit v7 on v4

--- a/solution.py
+++ b/solution.py
@@ -11,6 +11,8 @@
 LOG2E = math.log2(math.e)
 DEPTH = 64
 TILE = 256
+MIB = 1024 * 1024
+KEPT_ORDER = (0, 1, 3, 2)
 F32 = jnp.float32
 BF16 = jnp.bfloat16
 
@@ -37,8 +39,9 @@
     return jnp.concatenate(order + [tail, jnp.zeros_like(tail)], axis=0)
 
 
-def stacked(value):
-    return jnp.concatenate(pieces(value, 2), axis=0).astype(BF16)
+def put_dirs(dirs_ref, at, value):
+    both = jnp.concatenate(pieces(value, 2), axis=0).astype(BF16)
+    dirs_ref[at] = jnp.concatenate([both, both], axis=1)
 
 
 def shifted(value, stride, size, by):
@@ -68,14 +71,23 @@
     return [own], line, beside + across[:1], across[1:]
 
 
-def summed(value):
+def along_line(value):
     far, near = digits()
-    value = sum([shifted(value, 2 * near, far, by) for by in range(1, far)], value)
+    return [shifted(value, 2 * near, far, by) for by in range(1, far)]
+
+
+def over_quad(value):
+    _, near = digits()
+    length = lax.axis_size("row")
     quad = [shifted(value, 1, 2, 1)]
     for by in range(1, near):
-        beside = shifted(value, 2, near, by)
-        quad += [beside, shifted(beside, 1, 2, 1)]
-    return sum(quad, value)
+        quad.append(shifted(value, 2, near, by))
+        pairs = []
+        for i in range(length):
+            digit = (i // 2) % near
+            pairs.append((i, (i + ((digit - by) % near - digit) * 2) ^ 1))
+        quad.append(lax.ppermute(value, "row", pairs))
+    return quad
 
 
 def tables():
@@ -103,16 +115,27 @@
     return [jnp.concatenate(t) for t in (first, second, last_first, last_second)]
 
 
-def add_block(yt_ref, at, own_ref, dirs, acc_ref):
-    for c in range(own_ref.shape[1] // TILE):
+def add_block(yt_ref, at, own_ref, dirs_ref, acc_ref, keep_ref):
+    width = own_ref.shape[1]
+    for c in range(width // TILE):
         cols = slice(c * TILE, (c + 1) * TILE)
         expo = jnp.dot(yt_ref[at], own_ref[:, cols], preferred_element_type=F32)
         weight = jnp.exp2(expo)
         high = weight.astype(BF16)
         low = (weight - high.astype(F32)).astype(BF16)
+        if keep_ref is not None:
+            keep_ref[at, c, 0:width, :] = high
+            keep_ref[at, c, width:, :] = low
         acc_ref[:, cols] += jnp.dot(
-            dirs, high, preferred_element_type=F32
-        ) + jnp.dot(dirs, low, preferred_element_type=F32)
+            dirs_ref[at, :, 0:width], high, preferred_element_type=F32
+        ) + jnp.dot(dirs_ref[at, :, 0:width], low, preferred_element_type=F32)
+
+
+def add_kept_block(keep_ref, at, dirs_ref, acc_ref):
+    for c in range(keep_ref.shape[1]):
+        acc_ref[:, c * TILE : (c + 1) * TILE] += jnp.dot(
+            dirs_ref[at], keep_ref[at, c], preferred_element_type=F32
+        )
 
 
 def folded(acc_ref):
@@ -135,7 +158,7 @@
         base += ref.shape[0]
 
 
-def over_points(nfeat, nstacks, first, amplitude, *refs):
+def over_points(nfeat, nstacks, first, amplitude, kept, *refs):
     scale_ref, *refs = refs
     own_ref = refs.pop(0) if not first else None
     sofar_ref = refs.pop(0) if not first else None
@@ -147,18 +170,19 @@
         own_ref[...] = exponent_rows(
             stacks[0][0, 0:nfeat, :] / scale_ref[...], 1.0, False
         ).astype(BF16)
-    yt_ref, out_ref, dirs_ref, acc_ref = refs
+    out_ref, yt_ref, dirs_ref, acc_ref = refs[:1] + refs[-3:]
+    keep_ref = refs[1] if kept else None
 
     def prepare(b, value):
         rows = exponent_rows(value[0:nfeat, :] / scale_ref[...], LOG2E, True)
         yt_ref[b] = rows.T.astype(BF16)
-        dirs_ref[b] = stacked(value[nfeat:, :])
+        put_dirs(dirs_ref, b, value[nfeat:, :])
 
     each(stacks, prepare)
     acc_ref[...] = jnp.zeros_like(acc_ref)
 
     def step(b, carry):
-        add_block(yt_ref, b, own_ref, dirs_ref[b], acc_ref)
+        add_block(yt_ref, b, own_ref, dirs_ref, acc_ref, keep_ref)
         return carry
 
     lax.fori_loop(0, yt_ref.shape[0], step, 0)
@@ -170,30 +194,34 @@
     out_ref[...] = total
 
 
-def over_images(nstacks, table, sofar, form, amplitude, *refs):
+def over_images(nstacks, table, sofar, form, amplitude, kept, *refs):
     refs = list(refs)
     table_ref = refs.pop(0) if table else None
     sofar_ref = refs.pop(0) if sofar else None
     if form:
         once_ref, noise_ref, mine_ref = refs.pop(0), refs.pop(0), refs.pop(0)
-    own_ref, yt_ref, *refs = refs
+    own_ref = None if kept else refs.pop(0)
+    source_ref, *refs = refs
     stacks = refs[:nstacks]
     out_ref, *refs = refs[nstacks:]
     form_ref = refs.pop(0) if form else None
     dirs_ref, acc_ref = refs
 
     def prepare(b, value):
-        dirs_ref[b] = stacked(value)
+        put_dirs(dirs_ref, b, value)
 
     each(stacks, prepare)
     acc_ref[...] = jnp.zeros_like(acc_ref)
 
     def step(s, carry):
         b = table_ref[s] if table else s
-        add_block(yt_ref, b, own_ref, dirs_ref[b], acc_ref)
+        if kept:
+            add_kept_block(source_ref, b, dirs_ref, acc_ref)
+        else:
+            add_block(source_ref, b, own_ref, dirs_ref, acc_ref, None)
         return carry
 
-    lax.fori_loop(0, table_ref.shape[0] if table else yt_ref.shape[0], step, 0)
+    lax.fori_loop(0, table_ref.shape[0] if table else source_ref.shape[0], step, 0)
     total = folded(acc_ref)
     if sofar:
         total = total + sofar_ref[...]
@@ -267,19 +295,21 @@
     smem = pl.BlockSpec(memory_space=pltpu.SMEM)
     vmem = pl.BlockSpec(memory_space=pltpu.VMEM)
 
-    def call(kernel, blocks, work, out_shape, operands, name, table=False):
+    def call(kernel, blocks, work, out_shape, operands, name, table=False, kept=0, fresh=0):
         entries = work * width * width
+        scratch = [
+            pltpu.VMEM((blocks, 2 * nrhs, 2 * width), BF16),
+            pltpu.VMEM((2 * nrhs, width), F32),
+        ]
+        if fresh:
+            scratch.insert(0, pltpu.VMEM((fresh, width, DEPTH), BF16))
+        limit = 8 * MIB + blocks * 768 * width + 4 * kept * width * width
         return pl.pallas_call(
             kernel,
             out_shape=out_shape,
             in_specs=[smem if table and k == 0 else vmem for k in range(len(operands))],
-            scratch_shapes=[
-                pltpu.VMEM((blocks, 2 * nrhs, width), BF16),
-                pltpu.VMEM((2 * nrhs, width), F32),
-            ],
-            compiler_params=pltpu.CompilerParams(
-                vmem_limit_bytes=min(16 * 1024 * 1024 + blocks * 1024 * width, 60 * 1024 * 1024)
-            ),
+            scratch_shapes=scratch,
+            compiler_params=pltpu.CompilerParams(vmem_limit_bytes=min(limit, 60 * MIB)),
             cost_estimate=pl.CostEstimate(
                 flops=2 * entries * 4 * TILE, bytes_accessed=1024 * width, transcendentals=entries
             ),
@@ -289,26 +319,35 @@
     def amount(stacks):
         return sum(s.shape[0] for s in stacks)
 
-    def points_shape(stacks):
-        return jax.ShapeDtypeStruct((amount(stacks), width, DEPTH), BF16)
-
     groups = gathered(jnp.concatenate([features, rhs], axis=0))
     mine = groups[0][0]
     own_shape = jax.ShapeDtypeStruct((DEPTH, width), BF16)
-    own, points, total = call(
-        functools.partial(over_points, nfeat, 1, True, None),
-        1, 1, (own_shape, points_shape(groups[0]), field), (scale, mine), "own_block",
-    )
-    prepared = [points]
-    for k, stacks in enumerate(groups[1:]):
-        final = k == 2
-        points, total = call(
-            functools.partial(over_points, nfeat, len(stacks), False, amplitude if final else None),
-            amount(stacks), amount(stacks), (points_shape(stacks), field),
-            (scale, own, total) + ((noise, mine) if final else ()) + tuple(stacks),
-            "blocks_%d" % k,
+    room = 40 * MIB - lax.axis_size("row") * 512 * width
+    keep = [False] * len(groups)
+    for k in KEPT_ORDER:
+        size = 4 * amount(groups[k]) * width * width
+        keep[k] = size <= room
+        room -= size if keep[k] else 0
+    own, total, prepared = None, None, []
+    for k, stacks in enumerate(groups):
+        blocks = amount(stacks)
+        final = k == len(groups) - 1
+        if keep[k]:
+            source = jax.ShapeDtypeStruct((blocks, width // TILE, 2 * width, TILE), BF16)
+        else:
+            source = jax.ShapeDtypeStruct((blocks, width, DEPTH), BF16)
+        out = (own_shape,) * (k == 0) + (field, source)
+        *made, total, source = call(
+            functools.partial(
+                over_points, nfeat, len(stacks), k == 0, amplitude if final else None, keep[k]
+            ),
+            blocks, blocks, out,
+            (scale,) + (() if k == 0 else (own, total)) + ((noise, mine) if final else ())
+            + tuple(stacks),
+            "blocks_%d" % k, kept=blocks * keep[k], fresh=blocks * keep[k],
         )
-        prepared.append(points)
+        own = made[0] if made else own
+        prepared.append(source)
     images = gathered(total)
     image = images[0][0]
 
@@ -318,11 +357,13 @@
         work = amount(stacks) if table is None else table.shape[0]
         return call(
             functools.partial(
-                over_images, len(stacks), table is not None, bool(sofar), bool(form), amplitude
+                over_images, len(stacks), table is not None, bool(sofar), bool(form), amplitude,
+                keep[group],
             ),
             amount(stacks), work, out,
-            listed + tuple(sofar) + tuple(form) + (own, prepared[group]) + tuple(stacks),
-            name, table is not None,
+            listed + tuple(sofar) + tuple(form) + (() if keep[group] else (own,))
+            + (prepared[group],) + tuple(stacks),
+            name, table is not None, kept=amount(stacks) * keep[group],
         )
 
     first, second, last_first, last_second = tables()
@@ -333,9 +374,14 @@
         3, (field, small), "across_half", sofar=(half,), table=last_first,
         form=(once, noise, image),
     )
-    form = summed(form)
+    parts = along_line(form)
     total = again(2, field, "beside_rest", sofar=(total,), table=second)
+    *parts, total = lax.optimization_barrier((*parts, total))
+    form = sum(parts, form)
+    parts = over_quad(form)
     total = again(3, field, "across_rest", sofar=(total,), table=last_second)
+    *parts, total = lax.optimization_barrier((*parts, total))
+    form = sum(parts, form)
     flat = [s for g in groups for s in g]
     flat_images = [s for g in images for s in g]
     scalars = pl.pallas_call(

time: 89.9 us -> 91.3 us (1.016)
  local copies, waits for them, and re-layouts: 1.43 us -> 12.7 us
  Pallas kernels: 57.1 us -> 50.6 us
  waiting for transfers between devices: 11.5 us -> 7.74 us
    unnamed x32 -> x42, local copies, waits for them, and re-layouts: 0.7 us -> 11.9 us
    pallas_call x10, Pallas kernels: 53 us -> 46.5 us  [call(): pl.pallas_call(kernel, out_shape=out_shape, in_specs=[smem if table and k...]
    ppermute x18 -> x17, waiting for transfers between devices: 11.5 us -> 7.73 us  [shifted(): return lax.ppermute(value, 'row', pairs)]
    ppermute x0 -> x1, starting transfers between devices: none -> 1.2 us  [over_quad(): quad.append(lax.ppermute(value, 'row', pairs))]
    ppermute x18 -> x17, starting transfers between devices: 17.1 us -> 16.2 us  [shifted(): return lax.ppermute(value, 'row', pairs)]
  transfers between devices with their start and end apart: 18 -> 18, of which waited for: 7 -> 4; matrix products, arithmetic and copies ran while one was open for 1% -> 1% of each run, Pallas kernels for 50% -> 44%
where the time goes in v7:
time: 91.3 us; the launch traced here: 91 us
  Pallas kernels  50.6 us (55%)
  starting transfers between devices  17.4 us (19%)
  local copies, waits for them, and re-layouts  12.7 us (14%)
  waiting for transfers between devices  7.74 us (8%)
  other arithmetic  1.59 us (2%)
  between operations  0.95 us (1%)
    pallas_call x10, Pallas kernels, call(): pl.pallas_call(kernel, out_shape=out_shape, in_specs=[smem if table and k...  46.5 us
    ppermute x17, starting transfers between devices, shifted(): return lax.ppermute(value, 'row', pairs)  16.2 us
    unnamed x42, local copies, waits for them, and re-layouts  11.9 us
    ppermute x17, waiting for transfers between devices, shifted(): return lax.ppermute(value, 'row', pairs)  7.73 us
    pallas_call x1, Pallas kernels, shards(): pl.pallas_call(functools.partial(scalars_kernel, nfeat, len(flat)), out_s...  2.5 us
  transfers between devices with their start and end apart: 18, of which 4 were waited for; matrix products, arithmetic and copies ran while one was open for 1% of the time, Pallas kernels for 44%

profile of v7, /device:TPU:0, one launch (start us, length us, event | category | flops | bytes accessed | tf_op | source)
XLA Modules:
  0.0 91.0 jit_solution(11007192284389496788)
XLA Ops:
  0.6 0.8 maximum_bitcast_fusion.refs_1_.refs_4_.refs_0_.mine_ref
  1.4 5.1 %collective-permute-start = (f32[1,16,1024]{2,1,0:T(8,128)S(1)}, f32[1,16,1024]{2,1,0:T(8,128)S(1)}, u32[]{:S(2)}, u32[]{:S(2)}) collective-permute-start(f32[1,16,1024]{2,1,0:T(8,128)S(1)} %maximum_bitcast_fusion.refs_1_.refs_4_.refs_0_.mine_ref), channel_id=1, source_target_pairs={{0,12},{1,13},{2,14},{3,15},{4,0},{5,1},{6,2},{7,3},{8,4},{9,5},{1... | collective-permute-start | bytes 196616 | tf_op jit(solution)/shard_map/ppermute | solution.py:53
  6.5 0.0 collective-permute-start.1
  6.5 1.0 %collective-permute-start.2 = (f32[1,16,1024]{2,1,0:T(8,128)S(1)}, f32[1,16,1024]{2,1,0:T(8,128)S(1)}, u32[]{:S(2)}, u32[]{:S(2)}) collective-permute-start(f32[1,16,1024]{2,1,0:T(8,128)S(1)} %maximum_bitcast_fusion.refs_1_.refs_4_.refs_0_.mine_ref), channel_id=1, source_target_pairs={{0,4},{1,5},{2,6},{3,7},{4,8},{5,9},{6,10},{7,11},{8,12},{9,13},{1... | collective-permute-start | bytes 196616 | tf_op jit(solution)/shard_map/ppermute | solution.py:53
  7.5 0.7 copy.9.refs_0_
  8.3 1.6 %blocks_0.1 = (bf16[64,1024]{1,0:T(8,128)(2,1)S(1)}, f32[8,1024]{1,0:T(8,128)S(1)}, bf16[1,4,2048,256]{3,2,1,0:T(8,128)(2,1)S(1)}) custom-call(f32[8,1]{1,0:T(8,128)S(1)} %copy.9.refs_0_, f32[1,16,1024]{2,1,0:T(8,128)S(1)} %maximum_bitcast_fusion.refs_1_.refs_4_.refs_0_.mine_ref), custom_call_target="tpu_custom_call" | custom-call | flops 2147483648 | bytes 1048576 | tf_op jit(solution)/shard_map/blocks_0/pallas_call | solution.py:307
  9.9 0.1 pad_add_fusion.refs_0_
  10.0 0.1 pad_add_fusion.1.refs_0_
  10.1 0.0 collective-permute-done.refs_3_.refs_1_
  10.1 2.9 %collective-permute-done.1.refs_4_.refs_2_ = f32[1,16,1024]{2,1,0:T(8,128)S(1)} collective-permute-done((f32[1,16,1024]{2,1,0:T(8,128)S(1)}, f32[1,16,1024]{2,1,0:T(8,128)S(1)}, u32[]{:S(2)}, u32[]{:S(2)}) %collective-permute-start.1) | collective-permute-done | bytes 65568 | tf_op jit(solution)/shard_map/ppermute | solution.py:53
  13.0 0.0 collective-permute-done.2.refs_5_.refs_3_
  13.0 1.6 %collective-permute-start.3 = (f32[4,16,1024]{2,1,0:T(8,128)S(1)}, f32[4,16,1024]{2,1,0:T(8,128)S(1)}, u32[]{:S(2)}, u32[]{:S(2)}) collective-permute-start(f32[4,16,1024]{2,1,0:T(8,128)S(1)} %pad_maximum_fusion), channel_id=1, source_target_pairs={{0,2},{1,3},{2,0},{3,1},{4,6},{5,7},{6,4},{7,5},{8,10},{9,11},{10,... | collective-permute-start | bytes 786440 | tf_op jit(solution)/shard_map/ppermute | solution.py:53
  14.6 0.0 collective-permute-start.4
  14.6 4.8 %blocks_1.1 = (f32[8,1024]{1,0:T(8,128)S(1)}, bf16[3,4,2048,256]{3,2,1,0:T(8,128)(2,1)S(1)}) custom-call(f32[8,1]{1,0:T(8,128)S(1)} %copy.9.refs_0_, bf16[64,1024]{1,0:T(8,128)(2,1)S(1)} %get-tuple-element.21.refs_1_.refs_2_, f32[8,1024]{1,0:T(8,128)S(1)} %get-tuple-element.22.refs_2_, f32[1,16,1024]{2,1,0:T(8,128)S(1)} %collective-permute-done.refs_3_.refs_1_, ...), custom_call_target="tpu_custom_call" | custom-call | flops 6442450944 | bytes 1048576 | tf_op jit(solution)/shard_map/blocks_1/pallas_call | solution.py:307
  19.4 0.0 copy-start.19
  19.4 1.7 %collective-permute-done.3.refs_3_.refs_4_ = f32[4,16,1024]{2,1,0:T(8,128)S(1)} collective-permute-done((f32[4,16,1024]{2,1,0:T(8,128)S(1)}, f32[4,16,1024]{2,1,0:T(8,128)S(1)}, u32[]{:S(2)}, u32[]{:S(2)}) %collective-permute-start.3) | collective-permute-done | bytes 262176 | tf_op jit(solution)/shard_map/ppermute | solution.py:53
  21.1 0.0 collective-permute-start.5
  21.1 0.0 collective-permute-done.4.refs_4_.refs_5_
  21.1 0.0 copy-start.18
  21.1 13.6 %blocks_2.1 = (f32[8,1024]{1,0:T(8,128)S(1)}, bf16[8,1024,64]{2,1,0:T(8,128)(2,1)S(1)}) custom-call(f32[8,1]{1,0:T(8,128)S(1)} %copy.9.refs_0_, bf16[64,1024]{1,0:T(8,128)(2,1)S(1)} %get-tuple-element.21.refs_1_.refs_2_, f32[8,1024]{1,0:T(8,128)S(1)} %get-tuple-element.23.refs_2_, f32[4,16,1024]{2,1,0:T(8,128)S(1)} %collective-permute-done.3.refs_3_.refs_4_, ...), custom_call_target="tpu_custom_call" | custom-call | flops 17179869184 | bytes 1048576 | tf_op jit(solution)/shard_map/blocks_2/pallas_call | solution.py:307
  34.8 0.0 copy-done.9
  34.8 0.0 collective-permute-done.5.refs_5_.refs_6_
  34.9 6.8 %blocks_3.1 = (f32[8,1024]{1,0:T(8,128)S(1)}, bf16[4,4,2048,256]{3,2,1,0:T(8,128)(2,1)S(1)}) custom-call(f32[8,1]{1,0:T(8,128)S(1)} %copy.9.refs_0_, bf16[64,1024]{1,0:T(8,128)(2,1)S(1)} %get-tuple-element.21.refs_1_.refs_2_, f32[8,1024]{1,0:T(8,128)S(1)} %get-tuple-element.24.refs_2_, f32[1,1024]{1,0:T(1,128)S(1)} %bitcast.14, ...), custom_call_target="tpu_custom_call" | custom-call | flops 8589934592 | bytes 1048576 | tf_op jit(solution)/shard_map/blocks_3/pallas_call | solution.py:307
  41.7 0.0 copy-done.8
  41.7 0.8 collective-permute-start.6
  42.5 0.7 collective-permute-start.7
  43.3 1.9 %collective-permute-start.8 = (f32[1,8,1024]{2,1,0:T(8,128)S(1)}, f32[1,8,1024]{2,1,0:T(8,128)S(1)}, u32[]{:S(2)}, u32[]{:S(2)}) collective-permute-start(f32[1,8,1024]{2,1,0:T(8,128)S(1)} %bitcast.7), channel_id=1, source_target_pairs={{0,4},{1,5},{2,6},{3,7},{4,8},{5,9},{6,10},{7,11},{8,12},{9,13},{1... | collective-permute-start | bytes 98312 | tf_op jit(solution)/shard_map/ppermute | solution.py:53
  45.2 0.6 own_again.1.refs_0_
  45.8 0.0 collective-permute-done.6.refs_8_.refs_2_
  45.9 1.7 %collective-permute-done.7.refs_9_.refs_3_ = f32[1,8,1024]{2,1,0:T(8,128)S(1)} collective-permute-done((f32[1,8,1024]{2,1,0:T(8,128)S(1)}, f32[1,8,1024]{2,1,0:T(8,128)S(1)}, u32[]{:S(2)}, u32[]{:S(2)}) %collective-permute-start.7) | collective-permute-done | bytes 32800 | tf_op jit(solution)/shard_map/ppermute | solution.py:53
  47.6 1.4 %collective-permute-done.8.refs_10_.refs_4_ = f32[1,8,1024]{2,1,0:T(8,128)S(1)} collective-permute-done((f32[1,8,1024]{2,1,0:T(8,128)S(1)}, f32[1,8,1024]{2,1,0:T(8,128)S(1)}, u32[]{:S(2)}, u32[]{:S(2)}) %collective-permute-start.8) | collective-permute-done | bytes 32800 | tf_op jit(solution)/shard_map/ppermute | solution.py:53
  49.0 0.1 collective-permute-start.10
  49.1 1.6 %collective-permute-start.9 = (f32[4,8,1024]{2,1,0:T(8,128)S(1)}, f32[4,8,1024]{2,1,0:T(8,128)S(1)}, u32[]{:S(2)}, u32[]{:S(2)}) collective-permute-start(f32[4,8,1024]{2,1,0:T(8,128)S(1)} %pad_maximum_fusion.1), channel_id=1, source_target_pairs={{0,2},{1,3},{2,0},{3,1},{4,6},{5,7},{6,4},{7,5},{8,10},{9,11},{10,... | collective-permute-start | bytes 393224 | tf_op jit(solution)/shard_map/ppermute | solution.py:53
  50.6 4.6 %copy-done.20 = bf16[3,4,2048,256]{3,2,1,0:T(8,128)(2,1)S(1)} copy-done((bf16[3,4,2048,256]{3,2,1,0:T(8,128)(2,1)S(1)}, bf16[3,4,2048,256]{3,2,1,0:T(8,128)(2,1)}, u32[]{:S(2)}) %copy-start.20) | copy-done | bytes 12582936
  55.2 2.0 %line_again.1.refs_2_ = f32[8,1024]{1,0:T(8,128)S(1)} custom-call(f32[8,1024]{1,0:T(8,128)S(1)} %own_again.1.refs_0_, bf16[3,4,2048,256]{3,2,1,0:T(8,128)(2,1)S(1)} %copy-done.20, f32[1,8,1024]{2,1,0:T(8,128)S(1)} %collective-permute-done.6.refs_8_.refs_2_, f32[1,8,1024]{2,1,0:T(8,128)S(1)} %collective-permute-done.7.refs_9_.refs_3_, ...), custom_call_target="tpu_custom_call" | custom-call | flops 6442450944 | bytes 1048576 | tf_op jit(solution)/shard_map/line_again/pallas_call | solution.py:307
  57.2 0.0 collective-permute-done.9.refs_11_.refs_3_.refs_4_
  57.2 0.2 collective-permute-start.11
  57.5 0.0 collective-permute-done.10.refs_12_.refs_4_.refs_5_
  57.5 6.6 %beside_half.1.refs_1_ = f32[8,1024]{1,0:T(8,128)S(1)} custom-call(s32[4]{0:T(128)S(1)} %pad_add_fusion.refs_0_, bf16[64,1024]{1,0:T(8,128)(2,1)S(1)} %get-tuple-element.21.refs_1_.refs_2_, bf16[8,1024,64]{2,1,0:T(8,128)(2,1)S(1)} %get-tuple-element.26.refs_2_.refs_3_, f32[4,8,1024]{2,1,0:T(8,128)S(1)} %collective-permute-done.9.refs_11_.refs_3_.refs_4_, ...), custom_call_target="tpu_custom_call" | custom-call | flops 8589934592 | bytes 1048576 | tf_op jit(solution)/shard_map/beside_half/pallas_call | solution.py:307
  64.0 0.0 copy-done.15
  64.1 0.0 collective-permute-done.11.refs_13_.refs_6_.refs_3_
  64.1 0.0 copy-done
  64.1 2.0 %across_half.1 = (f32[8,1024]{1,0:T(8,128)S(1)}, f32[8,128]{1,0:T(8,128)S(1)}) custom-call(s32[2]{0:T(128)S(1)} %fusion.2.refs_0_, f32[8,1024]{1,0:T(8,128)S(1)} %beside_half.1.refs_1_, f32[8,1024]{1,0:T(8,128)S(1)} %line_again.1.refs_2_, f32[1,1024]{1,0:T(1,128)S(1)} %bitcast.15, f32[1,8,1024]{2,1,0:T(8,128)S(1)} %bitcast.10, ...), custom_call_target="tpu_custom_call" | custom-call | flops 4294967296 | bytes 1048576 | tf_op jit(solution)/shard_map/across_half/pallas_call | solution.py:307
  66.1 1.1 %collective-permute-start.12 = (f32[8,128]{1,0:T(8,128)S(1)}, f32[8,128]{1,0:T(8,128)S(1)}, u32[]{:S(2)}, u32[]{:S(2)}) collective-permute-start(f32[8,128]{1,0:T(8,128)S(1)} %get-tuple-element.30), channel_id=1, source_target_pairs={{0,12},{1,13},{2,14},{3,15},{4,0},{5,1},{6,2},{7,3},{8,4},{9,5},{1... | collective-permute-start | bytes 12296 | tf_op jit(solution)/shard_map/ppermute | solution.py:53
  67.2 0.5 collective-permute-start.13
  67.7 0.8 collective-permute-start.14
  68.5 6.6 %beside_rest.1.refs_1_ = f32[8,1024]{1,0:T(8,128)S(1)} custom-call(s32[4]{0:T(128)S(1)} %pad_add_fusion.1.refs_0_, f32[8,1024]{1,0:T(8,128)S(1)} %get-tuple-element.31.refs_1_, bf16[64,1024]{1,0:T(8,128)(2,1)S(1)} %get-tuple-element.21.refs_1_.refs_2_, bf16[8,1024,64]{2,1,0:T(8,128)(2,1)S(1)} %get-tuple-element.26.refs_2_.refs_3_, ...), custom_call_target="tpu_custom_call" | custom-call | flops 8589934592 | bytes 1048576 | tf_op jit(solution)/shard_map/beside_rest/pallas_call | solution.py:307
  75.1 0.0 copy-done.2
  75.1 2.5 %scalars.1.scalars_ref = f32[4,8,128]{2,1,0:T(8,128)} custom-call(f32[1,16,1024]{2,1,0:T(8,128)} %copy-done.4, f32[1,16,1024]{2,1,0:T(8,128)} %copy-done.9, f32[1,16,1024]{2,1,0:T(8,128)} %copy-done.10, f32[1,16,1024]{2,1,0:T(8,128)} %copy-done.11, f32[4,16,1024]{2,1,0:T(8,128)} %copy-done.6, f32[4,16,1024]{2,1,0:T(8,128)} %copy-done.7, ...), custom_call_target="tpu_custom_call" | custom-call | tf_op jit(solution)/shard_map/scalars/pallas_call | solution.py:387
  77.6 0.0 collective-permute-done.12
  77.6 0.0 collective-permute-done.13
  77.6 0.0 collective-permute-done.14
  77.6 0.1 collective-permute-start.15
  77.7 0.7 collective-permute-start.16
  78.3 1.2 %collective-permute-start.17 = (f32[8,128]{1,0:T(8,128)S(1)}, f32[8,128]{1,0:T(8,128)S(1)}, u32[]{:S(2)}, u32[]{:S(2)}) collective-permute-start(f32[8,128]{1,0:T(8,128)S(1)} %add_add_fusion.1), channel_id=1, source_target_pairs={{0,3},{1,2},{2,1},{3,0},{4,7},{5,6},{6,5},{7,4},{8,11},{9,10},{10,... | collective-permute-start | bytes 12296 | tf_op jit(solution)/shard_map/ppermute | solution.py:89
  79.5 5.8 %copy-done.1 = bf16[4,4,2048,256]{3,2,1,0:T(8,128)(2,1)S(1)} copy-done((bf16[4,4,2048,256]{3,2,1,0:T(8,128)(2,1)S(1)}, bf16[4,4,2048,256]{3,2,1,0:T(8,128)(2,1)}, u32[]{:S(2)}) %copy-start.1) | copy-done | bytes 16777240
  85.3 0.9 copy-done.3
  86.2 1.9 %across_rest.1.total_ref = f32[8,1024]{1,0:T(8,128)S(1)} custom-call(s32[2]{0:T(128)S(1)} %fusion.3.refs_0_, f32[8,1024]{1,0:T(8,128)S(1)} %beside_rest.1.refs_1_, bf16[4,4,2048,256]{3,2,1,0:T(8,128)(2,1)S(1)} %copy-done.1, f32[4,8,1024]{2,1,0:T(8,128)S(1)} %copy-done.3), custom_call_target="tpu_custom_call" | custom-call | flops 4294967296 | bytes 1048576 | tf_op jit(solution)/shard_map/across_rest/pallas_call | solution.py:307
  88.1 0.6 copy-done.12
  88.7 0.0 collective-permute-done.15
  88.7 0.0 collective-permute-done.16
  88.7 0.0 collective-permute-done.17
  88.8 0.6 add_add_fusion.form_ref
  89.3 1.6 %last_update.1 = (f32[8,1024]{1,0:T(8,128)}, f32[8,1024]{1,0:T(8,128)}) custom-call(f32[4,8,128]{2,1,0:T(8,128)} %scalars.1.scalars_ref, f32[8,128]{1,0:T(8,128)} %add_add_fusion.form_ref, f32[8,1024]{1,0:T(8,128)} %copy-done.12, f32[1,1024]{1,0:T(1,128)} %bitcast.13, f32[1,16,1024]{2,1,0:T(8,128)} %copy-done.4, f32[1,8,1024]{2,1,0:T(8,128)} %bitcast.12), custom_call_target="tpu_custom_call" | custom-call | tf_op jit(solution)/shard_map/last_update/pallas_call | solution.py:392
  (38 shorter events, 0.1 us)
Async XLA Ops:
  1.4 33.4 %copy-start.4 = (f32[1,16,1024]{2,1,0:T(8,128)}, f32[1,16,1024]{2,1,0:T(8,128)S(1)}, u32[]{:S(2)}) copy-start(f32[1,16,1024]{2,1,0:T(8,128)S(1)} %maximum_bitcast_fusion.refs_1_.refs_4_.refs_0_.mine_ref) | copy-start | bytes 196612
  1.4 8.7 %collective-permute-start = (f32[1,16,1024]{2,1,0:T(8,128)S(1)}, f32[1,16,1024]{2,1,0:T(8,128)S(1)}, u32[]{:S(2)}, u32[]{:S(2)}) collective-permute-start(f32[1,16,1024]{2,1,0:T(8,128)S(1)} %maximum_bitcast_fusion.refs_1_.refs_4_.refs_0_.mine_ref), channel_id=1, source_target_pairs={{0,12},{1,13},{2,14},{3,15},{4,0},{5,1},{6,2},{7,3},{8,4},{9,5},{1... | collective-permute-start | bytes 196616 | tf_op jit(solution)/shard_map/ppermute | solution.py:53
  6.5 6.5 %collective-permute-start.1 = (f32[1,16,1024]{2,1,0:T(8,128)S(1)}, f32[1,16,1024]{2,1,0:T(8,128)S(1)}, u32[]{:S(2)}, u32[]{:S(2)}) collective-permute-start(f32[1,16,1024]{2,1,0:T(8,128)S(1)} %maximum_bitcast_fusion.refs_1_.refs_4_.refs_0_.mine_ref), channel_id=1, source_target_pairs={{0,8},{1,9},{2,10},{3,11},{4,12},{5,13},{6,14},{7,15},{8,0},{9,1},... | collective-permute-start | bytes 196616 | tf_op jit(solution)/shard_map/ppermute | solution.py:53
  6.5 6.5 %collective-permute-start.2 = (f32[1,16,1024]{2,1,0:T(8,128)S(1)}, f32[1,16,1024]{2,1,0:T(8,128)S(1)}, u32[]{:S(2)}, u32[]{:S(2)}) collective-permute-start(f32[1,16,1024]{2,1,0:T(8,128)S(1)} %maximum_bitcast_fusion.refs_1_.refs_4_.refs_0_.mine_ref), channel_id=1, source_target_pairs={{0,4},{1,5},{2,6},{3,7},{4,8},{5,9},{6,10},{7,11},{8,12},{9,13},{1... | collective-permute-start | bytes 196616 | tf_op jit(solution)/shard_map/ppermute | solution.py:53
  10.1 24.7 %copy-start.9 = (f32[1,16,1024]{2,1,0:T(8,128)}, f32[1,16,1024]{2,1,0:T(8,128)S(1)}, u32[]{:S(2)}) copy-start(f32[1,16,1024]{2,1,0:T(8,128)S(1)} %collective-permute-done.refs_3_.refs_1_) | copy-start | bytes 196612
  13.0 21.8 %copy-start.10 = (f32[1,16,1024]{2,1,0:T(8,128)}, f32[1,16,1024]{2,1,0:T(8,128)S(1)}, u32[]{:S(2)}) copy-start(f32[1,16,1024]{2,1,0:T(8,128)S(1)} %collective-permute-done.1.refs_4_.refs_2_) | copy-start | bytes 196612
  13.0 21.8 %copy-start.11 = (f32[1,16,1024]{2,1,0:T(8,128)}, f32[1,16,1024]{2,1,0:T(8,128)S(1)}, u32[]{:S(2)}) copy-start(f32[1,16,1024]{2,1,0:T(8,128)S(1)} %collective-permute-done.2.refs_5_.refs_3_) | copy-start | bytes 196612
  13.0 8.1 %collective-permute-start.3 = (f32[4,16,1024]{2,1,0:T(8,128)S(1)}, f32[4,16,1024]{2,1,0:T(8,128)S(1)}, u32[]{:S(2)}, u32[]{:S(2)}) collective-permute-start(f32[4,16,1024]{2,1,0:T(8,128)S(1)} %pad_maximum_fusion), channel_id=1, source_target_pairs={{0,2},{1,3},{2,0},{3,1},{4,6},{5,7},{6,4},{7,5},{8,10},{9,11},{10,... | collective-permute-start | bytes 786440 | tf_op jit(solution)/shard_map/ppermute | solution.py:53
  14.6 6.5 %collective-permute-start.4 = (f32[4,16,1024]{2,1,0:T(8,128)S(1)}, f32[4,16,1024]{2,1,0:T(8,128)S(1)}, u32[]{:S(2)}, u32[]{:S(2)}) collective-permute-start(f32[4,16,1024]{2,1,0:T(8,128)S(1)} %pad_maximum_fusion), channel_id=1, source_target_pairs={{0,1},{1,0},{2,3},{3,2},{4,5},{5,4},{6,7},{7,6},{8,9},{9,8},{10,11... | collective-permute-start | bytes 786440 | tf_op jit(solution)/shard_map/ppermute | solution.py:53
  19.4 15.4 %copy-start.19 = (bf16[3,4,2048,256]{3,2,1,0:T(8,128)(2,1)}, bf16[3,4,2048,256]{3,2,1,0:T(8,128)(2,1)S(1)}, u32[]{:S(2)}) copy-start(bf16[3,4,2048,256]{3,2,1,0:T(8,128)(2,1)S(1)} %get-tuple-element.28.refs_1_) | copy-start | bytes 37748740
  21.1 13.7 %copy-start.6 = (f32[4,16,1024]{2,1,0:T(8,128)}, f32[4,16,1024]{2,1,0:T(8,128)S(1)}, u32[]{:S(2)}) copy-start(f32[4,16,1024]{2,1,0:T(8,128)S(1)} %collective-permute-done.3.refs_3_.refs_4_) | copy-start | bytes 786436
  21.1 13.7 %collective-permute-start.5 = (f32[4,16,1024]{2,1,0:T(8,128)S(1)}, f32[4,16,1024]{2,1,0:T(8,128)S(1)}, u32[]{:S(2)}, u32[]{:S(2)}) collective-permute-start(f32[4,16,1024]{2,1,0:T(8,128)S(1)} %collective-permute-done.3.refs_3_.refs_4_), channel_id=1, source_target_pairs={{0,1},{1,0},{2,3},{3,2},{4,5},{5,4},{6,7},{7,6},{8,9},{9,8},{10,11... | collective-permute-start | bytes 786440 | tf_op jit(solution)/shard_map/ppermute | solution.py:53
  21.1 13.7 %copy-start.7 = (f32[4,16,1024]{2,1,0:T(8,128)}, f32[4,16,1024]{2,1,0:T(8,128)S(1)}, u32[]{:S(2)}) copy-start(f32[4,16,1024]{2,1,0:T(8,128)S(1)} %collective-permute-done.4.refs_4_.refs_5_) | copy-start | bytes 786436
  21.1 13.7 %copy-start.18 = (f32[1024]{0:T(1024)S(1)}, f32[1024]{0:T(1024)}, u32[]{:S(2)}) copy-start(f32[1024]{0:T(1024)} %param.6) | copy-start | bytes 12292
  34.8 6.8 %copy-start.8 = (f32[4,16,1024]{2,1,0:T(8,128)}, f32[4,16,1024]{2,1,0:T(8,128)S(1)}, u32[]{:S(2)}) copy-start(f32[4,16,1024]{2,1,0:T(8,128)S(1)} %collective-permute-done.5.refs_5_.refs_6_) | copy-start | bytes 786436
  41.7 22.4 %copy-start = (bf16[4,4,2048,256]{3,2,1,0:T(8,128)(2,1)}, bf16[4,4,2048,256]{3,2,1,0:T(8,128)(2,1)S(1)}, u32[]{:S(2)}) copy-start(bf16[4,4,2048,256]{3,2,1,0:T(8,128)(2,1)S(1)} %get-tuple-element.29.refs_5_.refs_2_) | copy-start | bytes 50331652
  41.7 22.4 %copy-start.5 = (f32[8,1024]{1,0:T(8,128)}, f32[8,1024]{1,0:T(8,128)S(1)}, u32[]{:S(2)}) copy-start(f32[8,1024]{1,0:T(8,128)S(1)} %get-tuple-element.25) | copy-start | bytes 98308
  41.7 4.2 %collective-permute-start.6 = (f32[1,8,1024]{2,1,0:T(8,128)S(1)}, f32[1,8,1024]{2,1,0:T(8,128)S(1)}, u32[]{:S(2)}, u32[]{:S(2)}) collective-permute-start(f32[1,8,1024]{2,1,0:T(8,128)S(1)} %bitcast.5), channel_id=1, source_target_pairs={{0,12},{1,13},{2,14},{3,15},{4,0},{5,1},{6,2},{7,3},{8,4},{9,5},{1... | collective-permute-start | bytes 98312 | tf_op jit(solution)/shard_map/ppermute | solution.py:53
  42.5 5.1 %collective-permute-start.7 = (f32[1,8,1024]{2,1,0:T(8,128)S(1)}, f32[1,8,1024]{2,1,0:T(8,128)S(1)}, u32[]{:S(2)}, u32[]{:S(2)}) collective-permute-start(f32[1,8,1024]{2,1,0:T(8,128)S(1)} %bitcast.6), channel_id=1, source_target_pairs={{0,8},{1,9},{2,10},{3,11},{4,12},{5,13},{6,14},{7,15},{8,0},{9,1},... | collective-permute-start | bytes 98312 | tf_op jit(solution)/shard_map/ppermute | solution.py:53
  43.3 5.7 %collective-permute-start.8 = (f32[1,8,1024]{2,1,0:T(8,128)S(1)}, f32[1,8,1024]{2,1,0:T(8,128)S(1)}, u32[]{:S(2)}, u32[]{:S(2)}) collective-permute-start(f32[1,8,1024]{2,1,0:T(8,128)S(1)} %bitcast.7), channel_id=1, source_target_pairs={{0,4},{1,5},{2,6},{3,7},{4,8},{5,9},{6,10},{7,11},{8,12},{9,13},{1... | collective-permute-start | bytes 98312 | tf_op jit(solution)/shard_map/ppermute | solution.py:53
  45.9 18.2 %copy-start.15 = (f32[1,8,1024]{2,1,0:T(8,128)}, f32[1,8,1024]{2,1,0:T(8,128)S(1)}, u32[]{:S(2)}) copy-start(f32[1,8,1024]{2,1,0:T(8,128)S(1)} %collective-permute-done.6.refs_8_.refs_2_) | copy-start | bytes 98308
  47.6 16.4 %copy-start.16 = (f32[1,8,1024]{2,1,0:T(8,128)}, f32[1,8,1024]{2,1,0:T(8,128)S(1)}, u32[]{:S(2)}) copy-start(f32[1,8,1024]{2,1,0:T(8,128)S(1)} %collective-permute-done.7.refs_9_.refs_3_) | copy-start | bytes 98308
  49.0 15.1 %copy-start.17 = (f32[1,8,1024]{2,1,0:T(8,128)}, f32[1,8,1024]{2,1,0:T(8,128)S(1)}, u32[]{:S(2)}) copy-start(f32[1,8,1024]{2,1,0:T(8,128)S(1)} %collective-permute-done.8.refs_10_.refs_4_) | copy-start | bytes 98308
  49.0 8.5 %collective-permute-start.10 = (f32[4,8,1024]{2,1,0:T(8,128)S(1)}, f32[4,8,1024]{2,1,0:T(8,128)S(1)}, u32[]{:S(2)}, u32[]{:S(2)}) collective-permute-start(f32[4,8,1024]{2,1,0:T(8,128)S(1)} %pad_maximum_fusion.1), channel_id=1, source_target_pairs={{0,1},{1,0},{2,3},{3,2},{4,5},{5,4},{6,7},{7,6},{8,9},{9,8},{10,11... | collective-permute-start | bytes 393224 | tf_op jit(solution)/shard_map/ppermute | solution.py:53
  49.1 8.2 %collective-permute-start.9 = (f32[4,8,1024]{2,1,0:T(8,128)S(1)}, f32[4,8,1024]{2,1,0:T(8,128)S(1)}, u32[]{:S(2)}, u32[]{:S(2)}) collective-permute-start(f32[4,8,1024]{2,1,0:T(8,128)S(1)} %pad_maximum_fusion.1), channel_id=1, source_target_pairs={{0,2},{1,3},{2,0},{3,1},{4,6},{5,7},{6,4},{7,5},{8,10},{9,11},{10,... | collective-permute-start | bytes 393224 | tf_op jit(solution)/shard_map/ppermute | solution.py:53
  50.6 4.6 %copy-start.20 = (bf16[3,4,2048,256]{3,2,1,0:T(8,128)(2,1)S(1)}, bf16[3,4,2048,256]{3,2,1,0:T(8,128)(2,1)}, u32[]{:S(2)}) copy-start(bf16[3,4,2048,256]{3,2,1,0:T(8,128)(2,1)} %copy-done.19) | copy-start | bytes 37748740
  57.2 11.3 %copy-start.14 = (f32[4,8,1024]{2,1,0:T(8,128)}, f32[4,8,1024]{2,1,0:T(8,128)S(1)}, u32[]{:S(2)}) copy-start(f32[4,8,1024]{2,1,0:T(8,128)S(1)} %collective-permute-done.9.refs_11_.refs_3_.refs_4_) | copy-start | bytes 393220
  57.2 6.8 %collective-permute-start.11 = (f32[4,8,1024]{2,1,0:T(8,128)S(1)}, f32[4,8,1024]{2,1,0:T(8,128)S(1)}, u32[]{:S(2)}, u32[]{:S(2)}) collective-permute-start(f32[4,8,1024]{2,1,0:T(8,128)S(1)} %collective-permute-done.9.refs_11_.refs_3_.refs_4_), channel_id=1, source_target_pairs={{0,1},{1,0},{2,3},{3,2},{4,5},{5,4},{6,7},{7,6},{8,9},{9,8},{10,11... | collective-permute-start | bytes 393224 | tf_op jit(solution)/shard_map/ppermute | solution.py:53
  57.5 11.0 %copy-start.13 = (f32[4,8,1024]{2,1,0:T(8,128)}, f32[4,8,1024]{2,1,0:T(8,128)S(1)}, u32[]{:S(2)}) copy-start(f32[4,8,1024]{2,1,0:T(8,128)S(1)} %collective-permute-done.10.refs_12_.refs_4_.refs_5_) | copy-start | bytes 393220
  64.1 11.0 %copy-start.2 = (f32[4,8,1024]{2,1,0:T(8,128)}, f32[4,8,1024]{2,1,0:T(8,128)S(1)}, u32[]{:S(2)}) copy-start(f32[4,8,1024]{2,1,0:T(8,128)S(1)} %collective-permute-done.11.refs_13_.refs_6_.refs_3_) | copy-start | bytes 393220
  66.1 11.5 %collective-permute-start.12 = (f32[8,128]{1,0:T(8,128)S(1)}, f32[8,128]{1,0:T(8,128)S(1)}, u32[]{:S(2)}, u32[]{:S(2)}) collective-permute-start(f32[8,128]{1,0:T(8,128)S(1)} %get-tuple-element.30), channel_id=1, source_target_pairs={{0,12},{1,13},{2,14},{3,15},{4,0},{5,1},{6,2},{7,3},{8,4},{9,5},{1... | collective-permute-start | bytes 12296 | tf_op jit(solution)/shard_map/ppermute | solution.py:53
  67.2 10.3 %collective-permute-start.13 = (f32[8,128]{1,0:T(8,128)S(1)}, f32[8,128]{1,0:T(8,128)S(1)}, u32[]{:S(2)}, u32[]{:S(2)}) collective-permute-start(f32[8,128]{1,0:T(8,128)S(1)} %get-tuple-element.30), channel_id=1, source_target_pairs={{0,8},{1,9},{2,10},{3,11},{4,12},{5,13},{6,14},{7,15},{8,0},{9,1},... | collective-permute-start | bytes 12296 | tf_op jit(solution)/shard_map/ppermute | solution.py:53
  67.7 9.9 %collective-permute-start.14 = (f32[8,128]{1,0:T(8,128)S(1)}, f32[8,128]{1,0:T(8,128)S(1)}, u32[]{:S(2)}, u32[]{:S(2)}) collective-permute-start(f32[8,128]{1,0:T(8,128)S(1)} %get-tuple-element.30), channel_id=1, source_target_pairs={{0,4},{1,5},{2,6},{3,7},{4,8},{5,9},{6,10},{7,11},{8,12},{9,13},{1... | collective-permute-start | bytes 12296 | tf_op jit(solution)/shard_map/ppermute | solution.py:53
  77.6 11.1 %collective-permute-start.15 = (f32[8,128]{1,0:T(8,128)S(1)}, f32[8,128]{1,0:T(8,128)S(1)}, u32[]{:S(2)}, u32[]{:S(2)}) collective-permute-start(f32[8,128]{1,0:T(8,128)S(1)} %add_add_fusion.1), channel_id=1, source_target_pairs={{0,1},{1,0},{2,3},{3,2},{4,5},{5,4},{6,7},{7,6},{8,9},{9,8},{10,11... | collective-permute-start | bytes 12296 | tf_op jit(solution)/shard_map/ppermute | solution.py:53
  77.7 11.1 %collective-permute-start.16 = (f32[8,128]{1,0:T(8,128)S(1)}, f32[8,128]{1,0:T(8,128)S(1)}, u32[]{:S(2)}, u32[]{:S(2)}) collective-permute-start(f32[8,128]{1,0:T(8,128)S(1)} %add_add_fusion.1), channel_id=1, source_target_pairs={{0,2},{1,3},{2,0},{3,1},{4,6},{5,7},{6,4},{7,5},{8,10},{9,11},{10,... | collective-permute-start | bytes 12296 | tf_op jit(solution)/shard_map/ppermute | solution.py:53
  78.3 10.4 %collective-permute-start.17 = (f32[8,128]{1,0:T(8,128)S(1)}, f32[8,128]{1,0:T(8,128)S(1)}, u32[]{:S(2)}, u32[]{:S(2)}) collective-permute-start(f32[8,128]{1,0:T(8,128)S(1)} %add_add_fusion.1), channel_id=1, source_target_pairs={{0,3},{1,2},{2,1},{3,0},{4,7},{5,6},{6,5},{7,4},{8,11},{9,10},{10,... | collective-permute-start | bytes 12296 | tf_op jit(solution)/shard_map/ppermute | solution.py:89
  79.5 5.8 %copy-start.1 = (bf16[4,4,2048,256]{3,2,1,0:T(8,128)(2,1)S(1)}, bf16[4,4,2048,256]{3,2,1,0:T(8,128)(2,1)}, u32[]{:S(2)}) copy-start(bf16[4,4,2048,256]{3,2,1,0:T(8,128)(2,1)} %copy-done) | copy-start | bytes 50331652
  85.3 0.9 copy-start.3
  88.1 0.6 copy-start.12

commit v8 on v7

--- a/solution.py
+++ b/solution.py
@@ -185,7 +185,8 @@
         add_block(yt_ref, b, own_ref, dirs_ref, acc_ref, keep_ref)
         return carry
 
-    lax.fori_loop(0, yt_ref.shape[0], step, 0)
+    blocks = yt_ref.shape[0]
+    lax.fori_loop(0, blocks, step, 0, unroll=2 if blocks % 2 == 0 else min(blocks, 3))
     total = folded(acc_ref)
     if not first:
         total = total + sofar_ref[...]
@@ -221,7 +222,8 @@
             add_block(source_ref, b, own_ref, dirs_ref, acc_ref, None)
         return carry
 
-    lax.fori_loop(0, table_ref.shape[0] if table else source_ref.shape[0], step, 0)
+    blocks = table_ref.shape[0] if table else source_ref.shape[0]
+    lax.fori_loop(0, blocks, step, 0, unroll=2 if blocks % 2 == 0 else min(blocks, 3))
     total = folded(acc_ref)
     if sofar:
         total = total + sofar_ref[...]
@@ -295,7 +297,7 @@
     smem = pl.BlockSpec(memory_space=pltpu.SMEM)
     vmem = pl.BlockSpec(memory_space=pltpu.VMEM)
 
-    def call(kernel, blocks, work, out_shape, operands, name, table=False, kept=0, fresh=0):
+    def call(kernel, blocks, work, out_shape, operands, name, table=False, fresh=0):
         entries = work * width * width
         scratch = [
             pltpu.VMEM((blocks, 2 * nrhs, 2 * width), BF16),
@@ -303,7 +305,7 @@
         ]
         if fresh:
             scratch.insert(0, pltpu.VMEM((fresh, width, DEPTH), BF16))
-        limit = 8 * MIB + blocks * 768 * width + 4 * kept * width * width
+        limit = 8 * MIB + blocks * 640 * width
         return pl.pallas_call(
             kernel,
             out_shape=out_shape,
@@ -333,7 +335,7 @@
         blocks = amount(stacks)
         final = k == len(groups) - 1
         if keep[k]:
-            source = jax.ShapeDtypeStruct((blocks, width // TILE, 2 * width, TILE), BF16)
+            source = pltpu.VMEM((blocks, width // TILE, 2 * width, TILE), BF16)
         else:
             source = jax.ShapeDtypeStruct((blocks, width, DEPTH), BF16)
         out = (own_shape,) * (k == 0) + (field, source)
@@ -344,7 +346,7 @@
             blocks, blocks, out,
             (scale,) + (() if k == 0 else (own, total)) + ((noise, mine) if final else ())
             + tuple(stacks),
-            "blocks_%d" % k, kept=blocks * keep[k], fresh=blocks * keep[k],
+            "blocks_%d" % k, fresh=blocks * keep[k],
         )
         own = made[0] if made else own
         prepared.append(source)
@@ -355,6 +357,9 @@
         stacks = images[group]
         listed = () if table is None else (table,)
         work = amount(stacks) if table is None else table.shape[0]
+        source = prepared[group]
+        if keep[group]:
+            source = pltpu.with_memory_space_constraint(source, pltpu.VMEM)
         return call(
             functools.partial(
                 over_images, len(stacks), table is not None, bool(sofar), bool(form), amplitude,
@@ -362,8 +367,8 @@
             ),
             amount(stacks), work, out,
             listed + tuple(sofar) + tuple(form) + (() if keep[group] else (own,))
-            + (prepared[group],) + tuple(stacks),
-            name, table is not None, kept=amount(stacks) * keep[group],
+            + (source,) + tuple(stacks),
+            name, table is not None,
         )
 
     first, second, last_first, last_second = tables()

time: 91.3 us -> 84.6 us (0.927)
  Pallas kernels: 50.6 us -> 45.2 us
  local copies, waits for them, and re-layouts: 12.7 us -> 8.09 us
  waiting for transfers between devices: 7.74 us -> 11.3 us
    pallas_call x10, Pallas kernels: 46.5 us -> 41.1 us  [call(): pl.pallas_call(kernel, out_shape=out_shape, in_specs=[smem if table and k...]
    unnamed x42 -> x38, local copies, waits for them, and re-layouts: 11.9 us -> 7.36 us
    ppermute x17, waiting for transfers between devices: 7.73 us -> 11.3 us  [shifted(): return lax.ppermute(value, 'row', pairs)]
    ppermute x1, starting transfers between devices: 1.2 us -> 0.28 us  [over_quad(): quad.append(lax.ppermute(value, 'row', pairs))]
  transfers between devices with their start and end apart: 18 -> 18, of which waited for: 4 -> 5; matrix products, arithmetic and copies ran while one was open for 1% -> 1% of each run, Pallas kernels for 44% -> 42%
where the time goes in v8:
time: 84.6 us; the launch traced here: 84.3 us
  Pallas kernels  45.2 us (53%)
  starting transfers between devices  17.2 us (20%)
  waiting for transfers between devices  11.3 us (13%)
  local copies, waits for them, and re-layouts  8.09 us (10%)
  other arithmetic  1.59 us (2%)
  between operations  0.91 us (1%)
    pallas_call x10, Pallas kernels, call(): pl.pallas_call(kernel, out_shape=out_shape, in_specs=[smem if table and k...  41.1 us
    ppermute x17, starting transfers between devices, shifted(): return lax.ppermute(value, 'row', pairs)  16.9 us
    ppermute x17, waiting for transfers between devices, shifted(): return lax.ppermute(value, 'row', pairs)  11.3 us
    unnamed x38, local copies, waits for them, and re-layouts  7.36 us
    pallas_call x1, Pallas kernels, shards(): pl.pallas_call(functools.partial(scalars_kernel, nfeat, len(flat)), out_s...  2.5 us
  transfers between devices with their start and end apart: 18, of which 5 were waited for; matrix products, arithmetic and copies ran while one was open for 1% of the time, Pallas kernels for 42%

profile of v8, /device:TPU:0, one launch (start us, length us, event | category | flops | bytes accessed | tf_op | source)
XLA Modules:
  0.0 84.3 jit_solution(2026579198512158517)
XLA Ops:
  0.6 0.8 maximum_bitcast_fusion.refs_1_.refs_4_.refs_0_.mine_ref
  1.4 5.1 %collective-permute-start = (f32[1,16,1024]{2,1,0:T(8,128)S(1)}, f32[1,16,1024]{2,1,0:T(8,128)S(1)}, u32[]{:S(2)}, u32[]{:S(2)}) collective-permute-start(f32[1,16,1024]{2,1,0:T(8,128)S(1)} %maximum_bitcast_fusion.refs_1_.refs_4_.refs_0_.mine_ref), channel_id=1, source_target_pairs={{0,12},{1,13},{2,14},{3,15},{4,0},{5,1},{6,2},{7,3},{8,4},{9,5},{1... | collective-permute-start | bytes 196616 | tf_op jit(solution)/shard_map/ppermute | solution.py:53
  6.5 0.0 collective-permute-start.1
  6.5 1.0 %collective-permute-start.2 = (f32[1,16,1024]{2,1,0:T(8,128)S(1)}, f32[1,16,1024]{2,1,0:T(8,128)S(1)}, u32[]{:S(2)}, u32[]{:S(2)}) collective-permute-start(f32[1,16,1024]{2,1,0:T(8,128)S(1)} %maximum_bitcast_fusion.refs_1_.refs_4_.refs_0_.mine_ref), channel_id=1, source_target_pairs={{0,4},{1,5},{2,6},{3,7},{4,8},{5,9},{6,10},{7,11},{8,12},{9,13},{1... | collective-permute-start | bytes 196616 | tf_op jit(solution)/shard_map/ppermute | solution.py:53
  7.5 0.7 copy.9.refs_0_
  8.3 1.6 %blocks_0.1 = (bf16[64,1024]{1,0:T(8,128)(2,1)S(1)}, f32[8,1024]{1,0:T(8,128)S(1)}, bf16[1,4,2048,256]{3,2,1,0:T(8,128)(2,1)S(1)}) custom-call(f32[8,1]{1,0:T(8,128)S(1)} %copy.9.refs_0_, f32[1,16,1024]{2,1,0:T(8,128)S(1)} %maximum_bitcast_fusion.refs_1_.refs_4_.refs_0_.mine_ref), custom_call_target="tpu_custom_call" | custom-call | flops 2147483648 | bytes 1048576 | tf_op jit(solution)/shard_map/blocks_0/pallas_call | solution.py:309
  9.9 0.1 pad_add_fusion.refs_0_
  10.0 0.1 pad_add_fusion.1.refs_0_
  10.1 0.0 collective-permute-done.refs_3_.refs_1_
  10.1 2.9 %collective-permute-done.1.refs_4_.refs_2_ = f32[1,16,1024]{2,1,0:T(8,128)S(1)} collective-permute-done((f32[1,16,1024]{2,1,0:T(8,128)S(1)}, f32[1,16,1024]{2,1,0:T(8,128)S(1)}, u32[]{:S(2)}, u32[]{:S(2)}) %collective-permute-start.1) | collective-permute-done | bytes 65568 | tf_op jit(solution)/shard_map/ppermute | solution.py:53
  13.0 0.0 collective-permute-done.2.refs_5_.refs_3_
  13.0 1.6 %collective-permute-start.3 = (f32[4,16,1024]{2,1,0:T(8,128)S(1)}, f32[4,16,1024]{2,1,0:T(8,128)S(1)}, u32[]{:S(2)}, u32[]{:S(2)}) collective-permute-start(f32[4,16,1024]{2,1,0:T(8,128)S(1)} %pad_maximum_fusion), channel_id=1, source_target_pairs={{0,2},{1,3},{2,0},{3,1},{4,6},{5,7},{6,4},{7,5},{8,10},{9,11},{10,... | collective-permute-start | bytes 786440 | tf_op jit(solution)/shard_map/ppermute | solution.py:53
  14.6 0.0 collective-permute-start.4
  14.6 3.8 %blocks_1.1 = (f32[8,1024]{1,0:T(8,128)S(1)}, bf16[3,4,2048,256]{3,2,1,0:T(8,128)(2,1)S(1)}) custom-call(f32[8,1]{1,0:T(8,128)S(1)} %copy.9.refs_0_, bf16[64,1024]{1,0:T(8,128)(2,1)S(1)} %get-tuple-element.21.refs_1_.refs_2_, f32[8,1024]{1,0:T(8,128)S(1)} %get-tuple-element.22.refs_2_, f32[1,16,1024]{2,1,0:T(8,128)S(1)} %collective-permute-done.refs_3_.refs_1_, ...), custom_call_target="tpu_custom_call" | custom-call | flops 6442450944 | bytes 1048576 | tf_op jit(solution)/shard_map/blocks_1/pallas_call | solution.py:309
  18.4 2.7 %collective-permute-done.3.refs_3_.refs_4_ = f32[4,16,1024]{2,1,0:T(8,128)S(1)} collective-permute-done((f32[4,16,1024]{2,1,0:T(8,128)S(1)}, f32[4,16,1024]{2,1,0:T(8,128)S(1)}, u32[]{:S(2)}, u32[]{:S(2)}) %collective-permute-start.3) | collective-permute-done | bytes 262176 | tf_op jit(solution)/shard_map/ppermute | solution.py:53
  21.1 0.0 collective-permute-start.5
  21.1 0.0 collective-permute-done.4.refs_4_.refs_5_
  21.1 0.0 copy-start.18
  21.1 12.0 %blocks_2.1 = (f32[8,1024]{1,0:T(8,128)S(1)}, bf16[8,1024,64]{2,1,0:T(8,128)(2,1)S(1)}) custom-call(f32[8,1]{1,0:T(8,128)S(1)} %copy.9.refs_0_, bf16[64,1024]{1,0:T(8,128)(2,1)S(1)} %get-tuple-element.21.refs_1_.refs_2_, f32[8,1024]{1,0:T(8,128)S(1)} %get-tuple-element.23.refs_2_, f32[4,16,1024]{2,1,0:T(8,128)S(1)} %collective-permute-done.3.refs_3_.refs_4_, ...), custom_call_target="tpu_custom_call" | custom-call | flops 17179869184 | bytes 1048576 | tf_op jit(solution)/shard_map/blocks_2/pallas_call | solution.py:309
  33.2 0.0 copy-done.9
  33.2 0.0 collective-permute-done.5.refs_5_.refs_6_
  33.3 0.0 copy-start.8
  33.3 0.0 copy-done.4
  33.3 0.0 copy-done.18
  33.3 6.0 %blocks_3.1 = (f32[8,1024]{1,0:T(8,128)S(1)}, bf16[4,4,2048,256]{3,2,1,0:T(8,128)(2,1)S(1)}) custom-call(f32[8,1]{1,0:T(8,128)S(1)} %copy.9.refs_0_, bf16[64,1024]{1,0:T(8,128)(2,1)S(1)} %get-tuple-element.21.refs_1_.refs_2_, f32[8,1024]{1,0:T(8,128)S(1)} %get-tuple-element.24.refs_2_, f32[1,1024]{1,0:T(1,128)S(1)} %bitcast.14, ...), custom_call_target="tpu_custom_call" | custom-call | flops 8589934592 | bytes 1048576 | tf_op jit(solution)/shard_map/blocks_3/pallas_call | solution.py:309
  39.3 0.3 collective-permute-start.6
  39.6 1.3 %collective-permute-start.7 = (f32[1,8,1024]{2,1,0:T(8,128)S(1)}, f32[1,8,1024]{2,1,0:T(8,128)S(1)}, u32[]{:S(2)}, u32[]{:S(2)}) collective-permute-start(f32[1,8,1024]{2,1,0:T(8,128)S(1)} %bitcast.6), channel_id=1, source_target_pairs={{0,8},{1,9},{2,10},{3,11},{4,12},{5,13},{6,14},{7,15},{8,0},{9,1},... | collective-permute-start | bytes 98312 | tf_op jit(solution)/shard_map/ppermute | solution.py:53
  40.9 1.9 %collective-permute-start.8 = (f32[1,8,1024]{2,1,0:T(8,128)S(1)}, f32[1,8,1024]{2,1,0:T(8,128)S(1)}, u32[]{:S(2)}, u32[]{:S(2)}) collective-permute-start(f32[1,8,1024]{2,1,0:T(8,128)S(1)} %bitcast.7), channel_id=1, source_target_pairs={{0,4},{1,5},{2,6},{3,7},{4,8},{5,9},{6,10},{7,11},{8,12},{9,13},{1... | collective-permute-start | bytes 98312 | tf_op jit(solution)/shard_map/ppermute | solution.py:53
  42.8 0.6 own_again.1.refs_0_
  43.5 0.0 collective-permute-done.6.refs_8_.refs_2_
  43.5 0.9 %collective-permute-done.7.refs_9_.refs_3_ = f32[1,8,1024]{2,1,0:T(8,128)S(1)} collective-permute-done((f32[1,8,1024]{2,1,0:T(8,128)S(1)}, f32[1,8,1024]{2,1,0:T(8,128)S(1)}, u32[]{:S(2)}, u32[]{:S(2)}) %collective-permute-start.7) | collective-permute-done | bytes 32800 | tf_op jit(solution)/shard_map/ppermute | solution.py:53
  44.4 2.2 %collective-permute-done.8.refs_10_.refs_4_ = f32[1,8,1024]{2,1,0:T(8,128)S(1)} collective-permute-done((f32[1,8,1024]{2,1,0:T(8,128)S(1)}, f32[1,8,1024]{2,1,0:T(8,128)S(1)}, u32[]{:S(2)}, u32[]{:S(2)}) %collective-permute-start.8) | collective-permute-done | bytes 32800 | tf_op jit(solution)/shard_map/ppermute | solution.py:53
  46.6 0.1 collective-permute-start.10
  46.7 1.6 %collective-permute-start.9 = (f32[4,8,1024]{2,1,0:T(8,128)S(1)}, f32[4,8,1024]{2,1,0:T(8,128)S(1)}, u32[]{:S(2)}, u32[]{:S(2)}) collective-permute-start(f32[4,8,1024]{2,1,0:T(8,128)S(1)} %pad_maximum_fusion.1), channel_id=1, source_target_pairs={{0,2},{1,3},{2,0},{3,1},{4,6},{5,7},{6,4},{7,5},{8,10},{9,11},{10,... | collective-permute-start | bytes 393224 | tf_op jit(solution)/shard_map/ppermute | solution.py:53
  48.3 1.7 %line_again.1.refs_2_ = f32[8,1024]{1,0:T(8,128)S(1)} custom-call(f32[8,1024]{1,0:T(8,128)S(1)} %own_again.1.refs_0_, bf16[3,4,2048,256]{3,2,1,0:T(8,128)(2,1)S(1)} %get-tuple-element.28.refs_1_, f32[1,8,1024]{2,1,0:T(8,128)S(1)} %collective-permute-done.6.refs_8_.refs_2_, f32[1,8,1024]{2,1,0:T(8,128)S(1)} %collective-permute-done.7.refs_9_.refs_3_, ...), custom_call_target="tpu_custom_call" | custom-call | flops 6442450944 | bytes 1048576 | tf_op jit(solution)/shard_map/line_again/pallas_call | solution.py:309
  50.0 2.6 %collective-permute-done.9.refs_11_.refs_3_.refs_4_ = f32[4,8,1024]{2,1,0:T(8,128)S(1)} collective-permute-done((f32[4,8,1024]{2,1,0:T(8,128)S(1)}, f32[4,8,1024]{2,1,0:T(8,128)S(1)}, u32[]{:S(2)}, u32[]{:S(2)}) %collective-permute-start.9) | collective-permute-done | bytes 131104 | tf_op jit(solution)/shard_map/ppermute | solution.py:53
  52.6 0.0 collective-permute-start.11
  52.6 0.0 collective-permute-done.10.refs_12_.refs_4_.refs_5_
  52.6 5.8 %beside_half.1.refs_1_ = f32[8,1024]{1,0:T(8,128)S(1)} custom-call(s32[4]{0:T(128)S(1)} %pad_add_fusion.refs_0_, bf16[64,1024]{1,0:T(8,128)(2,1)S(1)} %get-tuple-element.21.refs_1_.refs_2_, bf16[8,1024,64]{2,1,0:T(8,128)(2,1)S(1)} %get-tuple-element.26.refs_2_.refs_3_, f32[4,8,1024]{2,1,0:T(8,128)S(1)} %collective-permute-done.9.refs_11_.refs_3_.refs_4_, ...), custom_call_target="tpu_custom_call" | custom-call | flops 8589934592 | bytes 1048576 | tf_op jit(solution)/shard_map/beside_half/pallas_call | solution.py:309
  58.4 0.0 copy-done.15
  58.4 0.0 collective-permute-done.11.refs_13_.refs_6_.refs_3_
  58.5 0.0 copy-done
  58.5 1.9 %across_half.1 = (f32[8,1024]{1,0:T(8,128)S(1)}, f32[8,128]{1,0:T(8,128)S(1)}) custom-call(s32[2]{0:T(128)S(1)} %fusion.2.refs_0_, f32[8,1024]{1,0:T(8,128)S(1)} %beside_half.1.refs_1_, f32[8,1024]{1,0:T(8,128)S(1)} %line_again.1.refs_2_, f32[1,1024]{1,0:T(1,128)S(1)} %bitcast.15, f32[1,8,1024]{2,1,0:T(8,128)S(1)} %bitcast.10, ...), custom_call_target="tpu_custom_call" | custom-call | flops 4294967296 | bytes 1048576 | tf_op jit(solution)/shard_map/across_half/pallas_call | solution.py:309
  60.3 1.1 %collective-permute-start.12 = (f32[8,128]{1,0:T(8,128)S(1)}, f32[8,128]{1,0:T(8,128)S(1)}, u32[]{:S(2)}, u32[]{:S(2)}) collective-permute-start(f32[8,128]{1,0:T(8,128)S(1)} %get-tuple-element.30), channel_id=1, source_target_pairs={{0,12},{1,13},{2,14},{3,15},{4,0},{5,1},{6,2},{7,3},{8,4},{9,5},{1... | collective-permute-start | bytes 12296 | tf_op jit(solution)/shard_map/ppermute | solution.py:53
  61.5 0.5 collective-permute-start.13
  62.0 0.8 collective-permute-start.14
  62.8 5.8 %beside_rest.1.refs_1_ = f32[8,1024]{1,0:T(8,128)S(1)} custom-call(s32[4]{0:T(128)S(1)} %pad_add_fusion.1.refs_0_, f32[8,1024]{1,0:T(8,128)S(1)} %get-tuple-element.31.refs_1_, bf16[64,1024]{1,0:T(8,128)(2,1)S(1)} %get-tuple-element.21.refs_1_.refs_2_, bf16[8,1024,64]{2,1,0:T(8,128)(2,1)S(1)} %get-tuple-element.26.refs_2_.refs_3_, ...), custom_call_target="tpu_custom_call" | custom-call | flops 8589934592 | bytes 1048576 | tf_op jit(solution)/shard_map/beside_rest/pallas_call | solution.py:309
  68.5 0.0 copy-done.2
  68.5 2.5 %scalars.1.scalars_ref = f32[4,8,128]{2,1,0:T(8,128)} custom-call(f32[1,16,1024]{2,1,0:T(8,128)} %copy-done.4, f32[1,16,1024]{2,1,0:T(8,128)} %copy-done.9, f32[1,16,1024]{2,1,0:T(8,128)} %copy-done.10, f32[1,16,1024]{2,1,0:T(8,128)} %copy-done.11, f32[4,16,1024]{2,1,0:T(8,128)} %copy-done.6, f32[4,16,1024]{2,1,0:T(8,128)} %copy-done.7, ...), custom_call_target="tpu_custom_call" | custom-call | tf_op jit(solution)/shard_map/scalars/pallas_call | solution.py:392
  71.0 0.0 collective-permute-done.12
  71.1 0.0 collective-permute-done.13
  71.1 0.0 collective-permute-done.14
  71.1 0.1 collective-permute-start.15
  71.2 1.6 %collective-permute-start.16 = (f32[8,128]{1,0:T(8,128)S(1)}, f32[8,128]{1,0:T(8,128)S(1)}, u32[]{:S(2)}, u32[]{:S(2)}) collective-permute-start(f32[8,128]{1,0:T(8,128)S(1)} %add_add_fusion.1), channel_id=1, source_target_pairs={{0,2},{1,3},{2,0},{3,1},{4,6},{5,7},{6,4},{7,5},{8,10},{9,11},{10,... | collective-permute-start | bytes 12296 | tf_op jit(solution)/shard_map/ppermute | solution.py:53
  72.7 0.3 collective-permute-start.17
  73.0 5.8 %copy-done.1 = bf16[4,4,2048,256]{3,2,1,0:T(8,128)(2,1)S(1)} copy-done((bf16[4,4,2048,256]{3,2,1,0:T(8,128)(2,1)S(1)}, bf16[4,4,2048,256]{3,2,1,0:T(8,128)(2,1)}, u32[]{:S(2)}) %copy-start.1) | copy-done | bytes 16777240
  78.8 0.9 %copy-done.3 = f32[4,8,1024]{2,1,0:T(8,128)S(1)} copy-done((f32[4,8,1024]{2,1,0:T(8,128)S(1)}, f32[4,8,1024]{2,1,0:T(8,128)}, u32[]{:S(2)}) %copy-start.3) | copy-done | bytes 131096
  79.7 1.8 %across_rest.1.total_ref = f32[8,1024]{1,0:T(8,128)S(1)} custom-call(s32[2]{0:T(128)S(1)} %fusion.3.refs_0_, f32[8,1024]{1,0:T(8,128)S(1)} %beside_rest.1.refs_1_, bf16[4,4,2048,256]{3,2,1,0:T(8,128)(2,1)S(1)} %copy-done.1, f32[4,8,1024]{2,1,0:T(8,128)S(1)} %copy-done.3), custom_call_target="tpu_custom_call" | custom-call | flops 4294967296 | bytes 1048576 | tf_op jit(solution)/shard_map/across_rest/pallas_call | solution.py:309
  81.5 0.6 copy-done.12
  82.1 0.0 collective-permute-done.15
  82.1 0.0 collective-permute-done.16
  82.1 0.0 collective-permute-done.17
  82.1 0.6 add_add_fusion.form_ref
  82.7 1.6 %last_update.1 = (f32[8,1024]{1,0:T(8,128)}, f32[8,1024]{1,0:T(8,128)}) custom-call(f32[4,8,128]{2,1,0:T(8,128)} %scalars.1.scalars_ref, f32[8,128]{1,0:T(8,128)} %add_add_fusion.form_ref, f32[8,1024]{1,0:T(8,128)} %copy-done.12, f32[1,1024]{1,0:T(1,128)} %bitcast.13, f32[1,16,1024]{2,1,0:T(8,128)} %copy-done.4, f32[1,8,1024]{2,1,0:T(8,128)} %bitcast.12), custom_call_target="tpu_custom_call" | custom-call | tf_op jit(solution)/shard_map/last_update/pallas_call | solution.py:397
  (34 shorter events, 0.1 us)
Async XLA Ops:
  1.4 31.9 %copy-start.4 = (f32[1,16,1024]{2,1,0:T(8,128)}, f32[1,16,1024]{2,1,0:T(8,128)S(1)}, u32[]{:S(2)}) copy-start(f32[1,16,1024]{2,1,0:T(8,128)S(1)} %maximum_bitcast_fusion.refs_1_.refs_4_.refs_0_.mine_ref) | copy-start | bytes 196612
  1.4 8.7 %collective-permute-start = (f32[1,16,1024]{2,1,0:T(8,128)S(1)}, f32[1,16,1024]{2,1,0:T(8,128)S(1)}, u32[]{:S(2)}, u32[]{:S(2)}) collective-permute-start(f32[1,16,1024]{2,1,0:T(8,128)S(1)} %maximum_bitcast_fusion.refs_1_.refs_4_.refs_0_.mine_ref), channel_id=1, source_target_pairs={{0,12},{1,13},{2,14},{3,15},{4,0},{5,1},{6,2},{7,3},{8,4},{9,5},{1... | collective-permute-start | bytes 196616 | tf_op jit(solution)/shard_map/ppermute | solution.py:53
  6.5 6.5 %collective-permute-start.1 = (f32[1,16,1024]{2,1,0:T(8,128)S(1)}, f32[1,16,1024]{2,1,0:T(8,128)S(1)}, u32[]{:S(2)}, u32[]{:S(2)}) collective-permute-start(f32[1,16,1024]{2,1,0:T(8,128)S(1)} %maximum_bitcast_fusion.refs_1_.refs_4_.refs_0_.mine_ref), channel_id=1, source_target_pairs={{0,8},{1,9},{2,10},{3,11},{4,12},{5,13},{6,14},{7,15},{8,0},{9,1},... | collective-permute-start | bytes 196616 | tf_op jit(solution)/shard_map/ppermute | solution.py:53
  6.5 6.5 %collective-permute-start.2 = (f32[1,16,1024]{2,1,0:T(8,128)S(1)}, f32[1,16,1024]{2,1,0:T(8,128)S(1)}, u32[]{:S(2)}, u32[]{:S(2)}) collective-permute-start(f32[1,16,1024]{2,1,0:T(8,128)S(1)} %maximum_bitcast_fusion.refs_1_.refs_4_.refs_0_.mine_ref), channel_id=1, source_target_pairs={{0,4},{1,5},{2,6},{3,7},{4,8},{5,9},{6,10},{7,11},{8,12},{9,13},{1... | collective-permute-start | bytes 196616 | tf_op jit(solution)/shard_map/ppermute | solution.py:53
  10.1 23.1 %copy-start.9 = (f32[1,16,1024]{2,1,0:T(8,128)}, f32[1,16,1024]{2,1,0:T(8,128)S(1)}, u32[]{:S(2)}) copy-start(f32[1,16,1024]{2,1,0:T(8,128)S(1)} %collective-permute-done.refs_3_.refs_1_) | copy-start | bytes 196612
  13.0 20.2 %copy-start.10 = (f32[1,16,1024]{2,1,0:T(8,128)}, f32[1,16,1024]{2,1,0:T(8,128)S(1)}, u32[]{:S(2)}) copy-start(f32[1,16,1024]{2,1,0:T(8,128)S(1)} %collective-permute-done.1.refs_4_.refs_2_) | copy-start | bytes 196612
  13.0 20.2 %copy-start.11 = (f32[1,16,1024]{2,1,0:T(8,128)}, f32[1,16,1024]{2,1,0:T(8,128)S(1)}, u32[]{:S(2)}) copy-start(f32[1,16,1024]{2,1,0:T(8,128)S(1)} %collective-permute-done.2.refs_5_.refs_3_) | copy-start | bytes 196612
  13.0 8.1 %collective-permute-start.3 = (f32[4,16,1024]{2,1,0:T(8,128)S(1)}, f32[4,16,1024]{2,1,0:T(8,128)S(1)}, u32[]{:S(2)}, u32[]{:S(2)}) collective-permute-start(f32[4,16,1024]{2,1,0:T(8,128)S(1)} %pad_maximum_fusion), channel_id=1, source_target_pairs={{0,2},{1,3},{2,0},{3,1},{4,6},{5,7},{6,4},{7,5},{8,10},{9,11},{10,... | collective-permute-start | bytes 786440 | tf_op jit(solution)/shard_map/ppermute | solution.py:53
  14.6 6.5 %collective-permute-start.4 = (f32[4,16,1024]{2,1,0:T(8,128)S(1)}, f32[4,16,1024]{2,1,0:T(8,128)S(1)}, u32[]{:S(2)}, u32[]{:S(2)}) collective-permute-start(f32[4,16,1024]{2,1,0:T(8,128)S(1)} %pad_maximum_fusion), channel_id=1, source_target_pairs={{0,1},{1,0},{2,3},{3,2},{4,5},{5,4},{6,7},{7,6},{8,9},{9,8},{10,11... | collective-permute-start | bytes 786440 | tf_op jit(solution)/shard_map/ppermute | solution.py:53
  21.1 12.1 %copy-start.6 = (f32[4,16,1024]{2,1,0:T(8,128)}, f32[4,16,1024]{2,1,0:T(8,128)S(1)}, u32[]{:S(2)}) copy-start(f32[4,16,1024]{2,1,0:T(8,128)S(1)} %collective-permute-done.3.refs_3_.refs_4_) | copy-start | bytes 786436
  21.1 12.1 %collective-permute-start.5 = (f32[4,16,1024]{2,1,0:T(8,128)S(1)}, f32[4,16,1024]{2,1,0:T(8,128)S(1)}, u32[]{:S(2)}, u32[]{:S(2)}) collective-permute-start(f32[4,16,1024]{2,1,0:T(8,128)S(1)} %collective-permute-done.3.refs_3_.refs_4_), channel_id=1, source_target_pairs={{0,1},{1,0},{2,3},{3,2},{4,5},{5,4},{6,7},{7,6},{8,9},{9,8},{10,11... | collective-permute-start | bytes 786440 | tf_op jit(solution)/shard_map/ppermute | solution.py:53
  21.1 12.1 %copy-start.7 = (f32[4,16,1024]{2,1,0:T(8,128)}, f32[4,16,1024]{2,1,0:T(8,128)S(1)}, u32[]{:S(2)}) copy-start(f32[4,16,1024]{2,1,0:T(8,128)S(1)} %collective-permute-done.4.refs_4_.refs_5_) | copy-start | bytes 786436
  21.1 12.1 %copy-start.18 = (f32[1024]{0:T(1024)S(1)}, f32[1024]{0:T(1024)}, u32[]{:S(2)}) copy-start(f32[1024]{0:T(1024)} %param.6) | copy-start | bytes 12292
  33.3 6.1 %copy-start.8 = (f32[4,16,1024]{2,1,0:T(8,128)}, f32[4,16,1024]{2,1,0:T(8,128)S(1)}, u32[]{:S(2)}) copy-start(f32[4,16,1024]{2,1,0:T(8,128)S(1)} %collective-permute-done.5.refs_5_.refs_6_) | copy-start | bytes 786436
  39.3 19.1 %copy-start = (bf16[4,4,2048,256]{3,2,1,0:T(8,128)(2,1)}, bf16[4,4,2048,256]{3,2,1,0:T(8,128)(2,1)S(1)}, u32[]{:S(2)}) copy-start(bf16[4,4,2048,256]{3,2,1,0:T(8,128)(2,1)S(1)} %get-tuple-element.29.refs_5_.refs_2_) | copy-start | bytes 50331652
  39.3 19.1 %copy-start.5 = (f32[8,1024]{1,0:T(8,128)}, f32[8,1024]{1,0:T(8,128)S(1)}, u32[]{:S(2)}) copy-start(f32[8,1024]{1,0:T(8,128)S(1)} %get-tuple-element.25) | copy-start | bytes 98308
  39.3 4.2 %collective-permute-start.6 = (f32[1,8,1024]{2,1,0:T(8,128)S(1)}, f32[1,8,1024]{2,1,0:T(8,128)S(1)}, u32[]{:S(2)}, u32[]{:S(2)}) collective-permute-start(f32[1,8,1024]{2,1,0:T(8,128)S(1)} %bitcast.5), channel_id=1, source_target_pairs={{0,12},{1,13},{2,14},{3,15},{4,0},{5,1},{6,2},{7,3},{8,4},{9,5},{1... | collective-permute-start | bytes 98312 | tf_op jit(solution)/shard_map/ppermute | solution.py:53
  39.6 4.8 %collective-permute-start.7 = (f32[1,8,1024]{2,1,0:T(8,128)S(1)}, f32[1,8,1024]{2,1,0:T(8,128)S(1)}, u32[]{:S(2)}, u32[]{:S(2)}) collective-permute-start(f32[1,8,1024]{2,1,0:T(8,128)S(1)} %bitcast.6), channel_id=1, source_target_pairs={{0,8},{1,9},{2,10},{3,11},{4,12},{5,13},{6,14},{7,15},{8,0},{9,1},... | collective-permute-start | bytes 98312 | tf_op jit(solution)/shard_map/ppermute | solution.py:53
  40.9 5.7 %collective-permute-start.8 = (f32[1,8,1024]{2,1,0:T(8,128)S(1)}, f32[1,8,1024]{2,1,0:T(8,128)S(1)}, u32[]{:S(2)}, u32[]{:S(2)}) collective-permute-start(f32[1,8,1024]{2,1,0:T(8,128)S(1)} %bitcast.7), channel_id=1, source_target_pairs={{0,4},{1,5},{2,6},{3,7},{4,8},{5,9},{6,10},{7,11},{8,12},{9,13},{1... | collective-permute-start | bytes 98312 | tf_op jit(solution)/shard_map/ppermute | solution.py:53
  43.5 14.9 %copy-start.15 = (f32[1,8,1024]{2,1,0:T(8,128)}, f32[1,8,1024]{2,1,0:T(8,128)S(1)}, u32[]{:S(2)}) copy-start(f32[1,8,1024]{2,1,0:T(8,128)S(1)} %collective-permute-done.6.refs_8_.refs_2_) | copy-start | bytes 98308
  44.4 14.0 %copy-start.16 = (f32[1,8,1024]{2,1,0:T(8,128)}, f32[1,8,1024]{2,1,0:T(8,128)S(1)}, u32[]{:S(2)}) copy-start(f32[1,8,1024]{2,1,0:T(8,128)S(1)} %collective-permute-done.7.refs_9_.refs_3_) | copy-start | bytes 98308
  46.6 11.8 %copy-start.17 = (f32[1,8,1024]{2,1,0:T(8,128)}, f32[1,8,1024]{2,1,0:T(8,128)S(1)}, u32[]{:S(2)}) copy-start(f32[1,8,1024]{2,1,0:T(8,128)S(1)} %collective-permute-done.8.refs_10_.refs_4_) | copy-start | bytes 98308
  46.6 6.0 %collective-permute-start.10 = (f32[4,8,1024]{2,1,0:T(8,128)S(1)}, f32[4,8,1024]{2,1,0:T(8,128)S(1)}, u32[]{:S(2)}, u32[]{:S(2)}) collective-permute-start(f32[4,8,1024]{2,1,0:T(8,128)S(1)} %pad_maximum_fusion.1), channel_id=1, source_target_pairs={{0,1},{1,0},{2,3},{3,2},{4,5},{5,4},{6,7},{7,6},{8,9},{9,8},{10,11... | collective-permute-start | bytes 393224 | tf_op jit(solution)/shard_map/ppermute | solution.py:53
  46.7 5.9 %collective-permute-start.9 = (f32[4,8,1024]{2,1,0:T(8,128)S(1)}, f32[4,8,1024]{2,1,0:T(8,128)S(1)}, u32[]{:S(2)}, u32[]{:S(2)}) collective-permute-start(f32[4,8,1024]{2,1,0:T(8,128)S(1)} %pad_maximum_fusion.1), channel_id=1, source_target_pairs={{0,2},{1,3},{2,0},{3,1},{4,6},{5,7},{6,4},{7,5},{8,10},{9,11},{10,... | collective-permute-start | bytes 393224 | tf_op jit(solution)/shard_map/ppermute | solution.py:53
  52.6 10.1 %copy-start.14 = (f32[4,8,1024]{2,1,0:T(8,128)}, f32[4,8,1024]{2,1,0:T(8,128)S(1)}, u32[]{:S(2)}) copy-start(f32[4,8,1024]{2,1,0:T(8,128)S(1)} %collective-permute-done.9.refs_11_.refs_3_.refs_4_) | copy-start | bytes 393220
  52.6 5.8 %collective-permute-start.11 = (f32[4,8,1024]{2,1,0:T(8,128)S(1)}, f32[4,8,1024]{2,1,0:T(8,128)S(1)}, u32[]{:S(2)}, u32[]{:S(2)}) collective-permute-start(f32[4,8,1024]{2,1,0:T(8,128)S(1)} %collective-permute-done.9.refs_11_.refs_3_.refs_4_), channel_id=1, source_target_pairs={{0,1},{1,0},{2,3},{3,2},{4,5},{5,4},{6,7},{7,6},{8,9},{9,8},{10,11... | collective-permute-start | bytes 393224 | tf_op jit(solution)/shard_map/ppermute | solution.py:53
  52.6 10.1 %copy-start.13 = (f32[4,8,1024]{2,1,0:T(8,128)}, f32[4,8,1024]{2,1,0:T(8,128)S(1)}, u32[]{:S(2)}) copy-start(f32[4,8,1024]{2,1,0:T(8,128)S(1)} %collective-permute-done.10.refs_12_.refs_4_.refs_5_) | copy-start | bytes 393220
  58.5 10.1 %copy-start.2 = (f32[4,8,1024]{2,1,0:T(8,128)}, f32[4,8,1024]{2,1,0:T(8,128)S(1)}, u32[]{:S(2)}) copy-start(f32[4,8,1024]{2,1,0:T(8,128)S(1)} %collective-permute-done.11.refs_13_.refs_6_.refs_3_) | copy-start | bytes 393220
  60.3 10.7 %collective-permute-start.12 = (f32[8,128]{1,0:T(8,128)S(1)}, f32[8,128]{1,0:T(8,128)S(1)}, u32[]{:S(2)}, u32[]{:S(2)}) collective-permute-start(f32[8,128]{1,0:T(8,128)S(1)} %get-tuple-element.30), channel_id=1, source_target_pairs={{0,12},{1,13},{2,14},{3,15},{4,0},{5,1},{6,2},{7,3},{8,4},{9,5},{1... | collective-permute-start | bytes 12296 | tf_op jit(solution)/shard_map/ppermute | solution.py:53
  61.5 9.6 %collective-permute-start.13 = (f32[8,128]{1,0:T(8,128)S(1)}, f32[8,128]{1,0:T(8,128)S(1)}, u32[]{:S(2)}, u32[]{:S(2)}) collective-permute-start(f32[8,128]{1,0:T(8,128)S(1)} %get-tuple-element.30), channel_id=1, source_target_pairs={{0,8},{1,9},{2,10},{3,11},{4,12},{5,13},{6,14},{7,15},{8,0},{9,1},... | collective-permute-start | bytes 12296 | tf_op jit(solution)/shard_map/ppermute | solution.py:53
  62.0 9.1 %collective-permute-start.14 = (f32[8,128]{1,0:T(8,128)S(1)}, f32[8,128]{1,0:T(8,128)S(1)}, u32[]{:S(2)}, u32[]{:S(2)}) collective-permute-start(f32[8,128]{1,0:T(8,128)S(1)} %get-tuple-element.30), channel_id=1, source_target_pairs={{0,4},{1,5},{2,6},{3,7},{4,8},{5,9},{6,10},{7,11},{8,12},{9,13},{1... | collective-permute-start | bytes 12296 | tf_op jit(solution)/shard_map/ppermute | solution.py:53
  71.1 11.0 %collective-permute-start.15 = (f32[8,128]{1,0:T(8,128)S(1)}, f32[8,128]{1,0:T(8,128)S(1)}, u32[]{:S(2)}, u32[]{:S(2)}) collective-permute-start(f32[8,128]{1,0:T(8,128)S(1)} %add_add_fusion.1), channel_id=1, source_target_pairs={{0,1},{1,0},{2,3},{3,2},{4,5},{5,4},{6,7},{7,6},{8,9},{9,8},{10,11... | collective-permute-start | bytes 12296 | tf_op jit(solution)/shard_map/ppermute | solution.py:53
  71.2 10.9 %collective-permute-start.16 = (f32[8,128]{1,0:T(8,128)S(1)}, f32[8,128]{1,0:T(8,128)S(1)}, u32[]{:S(2)}, u32[]{:S(2)}) collective-permute-start(f32[8,128]{1,0:T(8,128)S(1)} %add_add_fusion.1), channel_id=1, source_target_pairs={{0,2},{1,3},{2,0},{3,1},{4,6},{5,7},{6,4},{7,5},{8,10},{9,11},{10,... | collective-permute-start | bytes 12296 | tf_op jit(solution)/shard_map/ppermute | solution.py:53
  72.7 9.3 %collective-permute-start.17 = (f32[8,128]{1,0:T(8,128)S(1)}, f32[8,128]{1,0:T(8,128)S(1)}, u32[]{:S(2)}, u32[]{:S(2)}) collective-permute-start(f32[8,128]{1,0:T(8,128)S(1)} %add_add_fusion.1), channel_id=1, source_target_pairs={{0,3},{1,2},{2,1},{3,0},{4,7},{5,6},{6,5},{7,4},{8,11},{9,10},{10,... | collective-permute-start | bytes 12296 | tf_op jit(solution)/shard_map/ppermute | solution.py:89
  73.0 5.8 %copy-start.1 = (bf16[4,4,2048,256]{3,2,1,0:T(8,128)(2,1)S(1)}, bf16[4,4,2048,256]{3,2,1,0:T(8,128)(2,1)}, u32[]{:S(2)}) copy-start(bf16[4,4,2048,256]{3,2,1,0:T(8,128)(2,1)} %copy-done) | copy-start | bytes 50331652
  78.8 0.9 %copy-start.3 = (f32[4,8,1024]{2,1,0:T(8,128)S(1)}, f32[4,8,1024]{2,1,0:T(8,128)}, u32[]{:S(2)}) copy-start(f32[4,8,1024]{2,1,0:T(8,128)} %copy-done.2) | copy-start | bytes 393220
  81.5 0.6 copy-start.12

commit v9 on v8

--- a/solution.py
+++ b/solution.py
@@ -12,7 +12,7 @@
 DEPTH = 64
 TILE = 256
 MIB = 1024 * 1024
-KEPT_ORDER = (0, 1, 3, 2)
+KEPT_ORDER = (0, 2, 4, 1, 3)
 F32 = jnp.float32
 BF16 = jnp.bfloat16
 
@@ -68,7 +68,7 @@
     group = jnp.concatenate([own] + line, axis=0)
     beside = [shifted(group, 2, near, by) for by in range(1, near)]
     across = [shifted(g, 1, 2, 1) for g in [group] + beside]
-    return [own], line, beside + across[:1], across[1:]
+    return [own], line, beside, across[:1], across[1:]
 
 
 def along_line(value):
@@ -106,13 +106,12 @@
         else:
             whole = base + jnp.arange(far, dtype=jnp.int32)
             (first if 2 * shift < near else second).append(whole)
-    base = (near - 1) * far
-    first.append(base + picks + core)
-    second.append(base + picks + 1 - core)
-    for k in range(near - 1):
-        last_first.append(k * far + picks + core)
-        last_second.append(k * far + picks + 1 - core)
-    return [jnp.concatenate(t) for t in (first, second, last_first, last_second)]
+        last_first.append(base + picks + core)
+        last_second.append(base + picks + 1 - core)
+    return (
+        [jnp.concatenate(first), picks + core, jnp.concatenate(last_first)],
+        [jnp.concatenate(second), picks + 1 - core, jnp.concatenate(last_second)],
+    )
 
 
 def add_block(yt_ref, at, own_ref, dirs_ref, acc_ref, keep_ref):
@@ -143,6 +142,10 @@
     return acc_ref[0:nrhs, :] + acc_ref[nrhs:, :]
 
 
+def unrolled(steps):
+    return next(n for n in (4, 3, 2, 1) if steps % n == 0)
+
+
 def each(stacks, function):
     base = 0
     for ref in stacks:
@@ -186,7 +189,7 @@
         return carry
 
     blocks = yt_ref.shape[0]
-    lax.fori_loop(0, blocks, step, 0, unroll=2 if blocks % 2 == 0 else min(blocks, 3))
+    lax.fori_loop(0, blocks, step, 0, unroll=unrolled(blocks))
     total = folded(acc_ref)
     if not first:
         total = total + sofar_ref[...]
@@ -211,11 +214,15 @@
     def prepare(b, value):
         put_dirs(dirs_ref, b, value)
 
-    each(stacks, prepare)
+    alone = nstacks == 1
+    if not alone:
+        each(stacks, prepare)
     acc_ref[...] = jnp.zeros_like(acc_ref)
 
     def step(s, carry):
         b = table_ref[s] if table else s
+        if alone:
+            prepare(b, stacks[0][b])
         if kept:
             add_kept_block(source_ref, b, dirs_ref, acc_ref)
         else:
@@ -223,7 +230,7 @@
         return carry
 
     blocks = table_ref.shape[0] if table else source_ref.shape[0]
-    lax.fori_loop(0, blocks, step, 0, unroll=2 if blocks % 2 == 0 else min(blocks, 3))
+    lax.fori_loop(0, blocks, step, 0, unroll=unrolled(blocks))
     total = folded(acc_ref)
     if sofar:
         total = total + sofar_ref[...]
@@ -250,7 +257,8 @@
             def block(k, carry, b_ref=b_ref, m_ref=m_ref):
                 return function(carry, b_ref[k, nfeat:, :], m_ref[k])
 
-            carry = lax.fori_loop(0, b_ref.shape[0], block, carry)
+            steps = b_ref.shape[0]
+            carry = lax.fori_loop(0, steps, block, carry, unroll=unrolled(steps))
         return carry
 
     def total(value):
@@ -305,7 +313,7 @@
         ]
         if fresh:
             scratch.insert(0, pltpu.VMEM((fresh, width, DEPTH), BF16))
-        limit = 8 * MIB + blocks * 640 * width
+        limit = 4 * MIB + blocks * 512 * width
         return pl.pallas_call(
             kernel,
             out_shape=out_shape,
@@ -324,7 +332,7 @@
     groups = gathered(jnp.concatenate([features, rhs], axis=0))
     mine = groups[0][0]
     own_shape = jax.ShapeDtypeStruct((DEPTH, width), BF16)
-    room = 40 * MIB - lax.axis_size("row") * 512 * width
+    room = 52 * MIB - lax.axis_size("row") * 512 * width
     keep = [False] * len(groups)
     for k in KEPT_ORDER:
         size = 4 * amount(groups[k]) * width * width
@@ -371,20 +379,21 @@
             name, table is not None,
         )
 
-    first, second, last_first, last_second = tables()
+    halves, rests = tables()
     once = again(0, field, "own_again")
     once = again(1, field, "line_again", sofar=(once,))
-    half = again(2, field, "beside_half", table=first)
+    half = again(2, field, "beside_half", table=halves[0])
+    half = again(3, field, "across_half", sofar=(half,), table=halves[1])
     total, form = again(
-        3, (field, small), "across_half", sofar=(half,), table=last_first,
-        form=(once, noise, image),
+        4, (field, small), "far_half", sofar=(half,), table=halves[2], form=(once, noise, image)
     )
     parts = along_line(form)
-    total = again(2, field, "beside_rest", sofar=(total,), table=second)
+    total = again(2, field, "beside_rest", sofar=(total,), table=rests[0])
+    total = again(3, field, "across_rest", sofar=(total,), table=rests[1])
     *parts, total = lax.optimization_barrier((*parts, total))
     form = sum(parts, form)
     parts = over_quad(form)
-    total = again(3, field, "across_rest", sofar=(total,), table=last_second)
+    total = again(4, field, "far_rest", sofar=(total,), table=rests[2])
     *parts, total = lax.optimization_barrier((*parts, total))
     form = sum(parts, form)
     flat = [s for g in groups for s in g]
@@ -392,11 +401,15 @@
     scalars = pl.pallas_call(
         functools.partial(scalars_kernel, nfeat, len(flat)),
         out_shape=jax.ShapeDtypeStruct((4, nrhs, 128), F32),
+        compiler_params=pltpu.CompilerParams(
+            vmem_limit_bytes=4 * MIB + 96 * lax.axis_size("row") * width
+        ),
         name="scalars",
     )(*flat, *flat_images)
     return pl.pallas_call(
         functools.partial(last_kernel, nfeat, amplitude),
         out_shape=(field, field),
+        compiler_params=pltpu.CompilerParams(vmem_limit_bytes=4 * MIB),
         name="last_update",
     )(scalars, form, total, noise, mine, image)
 

time: 84.6 us -> 71.2 us (0.84)
  local copies, waits for them, and re-layouts: 8.09 us -> 2.69 us
  Pallas kernels: 45.2 us -> 41.3 us
  waiting for transfers between devices: 11.3 us -> 7.86 us
    unnamed x38 -> x6, local copies, waits for them, and re-layouts: 7.36 us -> 1.96 us
    ppermute x17, waiting for transfers between devices: 11.3 us -> 7.47 us  [shifted(): return lax.ppermute(value, 'row', pairs)]
    pallas_call x1, Pallas kernels: 2.5 us -> 0.36 us  [shards(): pl.pallas_call(functools.partial(scalars_kernel, nfeat, len(flat)), out_s...]
    pallas_call x1, Pallas kernels: 1.61 us -> 0.71 us  [shards(): pl.pallas_call(functools.partial(last_kernel, nfeat, amplitude), out_shap...]
    pallas_call x10 -> x13, Pallas kernels: 41.1 us -> 40.2 us  [call(): pl.pallas_call(kernel, out_shape=out_shape, in_specs=[smem if table and k...]
  transfers between devices with their start and end apart: 18 -> 18, of which waited for: 5 -> 6; matrix products, arithmetic and copies ran while one was open for 1% -> 1% of each run, Pallas kernels for 42% -> 46%
where the time goes in v9:
time: 71.2 us; the launch traced here: 71 us
  Pallas kernels  41.3 us (58%)
  starting transfers between devices  17.6 us (25%)
  waiting for transfers between devices  7.86 us (11%)
  local copies, waits for them, and re-layouts  2.69 us (4%)
  other arithmetic  0.84 us (1%)
  between operations  0.72 us (1%)
    pallas_call x13, Pallas kernels, call(): pl.pallas_call(kernel, out_shape=out_shape, in_specs=[smem if table and k...  40.2 us
    ppermute x17, starting transfers between devices, shifted(): return lax.ppermute(value, 'row', pairs)  16.7 us
    ppermute x17, waiting for transfers between devices, shifted(): return lax.ppermute(value, 'row', pairs)  7.47 us
    unnamed x6, local copies, waits for them, and re-layouts  1.96 us
  transfers between devices with their start and end apart: 18, of which 6 were waited for; matrix products, arithmetic and copies ran while one was open for 1% of the time, Pallas kernels for 46%

profile of v9, /device:TPU:0, one launch (start us, length us, event | category | flops | bytes accessed | tf_op | source)
XLA Modules:
  0.0 71.0 jit_solution(17191319018011818874)
XLA Ops:
  0.6 0.8 %maximum_bitcast_fusion.refs_1_.refs_4_.refs_0_.mine_ref = f32[1,16,1024]{2,1,0:T(8,128)S(1)} fusion(f32[8,1024]{1,0:T(8,128)} %param.7, f32[8,1024]{1,0:T(8,128)} %param.4), kind=kLoop, calls=%fused_computation.2 | loop fusion | flops 16384 | bytes 131072 | tf_op jit(solution)/shard_map/broadcast_in_dim | solution.py:66
  1.4 5.0 %collective-permute-start = (f32[1,16,1024]{2,1,0:T(8,128)S(1)}, f32[1,16,1024]{2,1,0:T(8,128)S(1)}, u32[]{:S(2)}, u32[]{:S(2)}) collective-permute-start(f32[1,16,1024]{2,1,0:T(8,128)S(1)} %maximum_bitcast_fusion.refs_1_.refs_4_.refs_0_.mine_ref), channel_id=1, source_target_pairs={{0,12},{1,13},{2,14},{3,15},{4,0},{5,1},{6,2},{7,3},{8,4},{9,5},{1... | collective-permute-start | bytes 196616 | tf_op jit(solution)/shard_map/ppermute | solution.py:53
  6.5 0.0 collective-permute-start.1
  6.5 1.0 %collective-permute-start.2 = (f32[1,16,1024]{2,1,0:T(8,128)S(1)}, f32[1,16,1024]{2,1,0:T(8,128)S(1)}, u32[]{:S(2)}, u32[]{:S(2)}) collective-permute-start(f32[1,16,1024]{2,1,0:T(8,128)S(1)} %maximum_bitcast_fusion.refs_1_.refs_4_.refs_0_.mine_ref), channel_id=1, source_target_pairs={{0,4},{1,5},{2,6},{3,7},{4,8},{5,9},{6,10},{7,11},{8,12},{9,13},{1... | collective-permute-start | bytes 196616 | tf_op jit(solution)/shard_map/ppermute | solution.py:53
  7.5 0.7 %copy.10.refs_0_ = f32[8,1]{1,0:T(8,128)S(1)} copy(f32[8,1]{0,1:T(1,128)} %bitcast.16) | data formatting | bytes 64 | tf_op jit(solution)/shard_map/broadcast_in_dim | solution.py:301
  8.2 1.6 %blocks_0.1 = (bf16[64,1024]{1,0:T(8,128)(2,1)S(1)}, f32[8,1024]{1,0:T(8,128)S(1)}, bf16[1,4,2048,256]{3,2,1,0:T(8,128)(2,1)S(1)}) custom-call(f32[8,1]{1,0:T(8,128)S(1)} %copy.10.refs_0_, f32[1,16,1024]{2,1,0:T(8,128)S(1)} %maximum_bitcast_fusion.refs_1_.refs_4_.refs_0_.mine_ref), custom_call_target="tpu_custom_call" | custom-call | flops 2147483648 | bytes 1048576 | tf_op jit(solution)/shard_map/blocks_0/pallas_call | solution.py:317
  9.8 0.0 copy-start.1
  9.8 2.0 %copy-done.1 = bf16[1,4,2048,256]{3,2,1,0:T(8,128)(2,1)} copy-done((bf16[1,4,2048,256]{3,2,1,0:T(8,128)(2,1)}, bf16[1,4,2048,256]{3,2,1,0:T(8,128)(2,1)S(1)}, u32[]{:S(2)}) %copy-start.1) | copy-done | bytes 4194328
  11.8 0.0 collective-permute-done.refs_3_.refs_1_
  11.8 1.1 %collective-permute-done.1.refs_4_.refs_2_ = f32[1,16,1024]{2,1,0:T(8,128)S(1)} collective-permute-done((f32[1,16,1024]{2,1,0:T(8,128)S(1)}, f32[1,16,1024]{2,1,0:T(8,128)S(1)}, u32[]{:S(2)}, u32[]{:S(2)}) %collective-permute-start.1) | collective-permute-done | bytes 65568 | tf_op jit(solution)/shard_map/ppermute | solution.py:53
  12.9 0.0 collective-permute-done.2.refs_5_.refs_3_
  13.0 1.6 %collective-permute-start.3 = (f32[4,16,1024]{2,1,0:T(8,128)S(1)}, f32[4,16,1024]{2,1,0:T(8,128)S(1)}, u32[]{:S(2)}, u32[]{:S(2)}) collective-permute-start(f32[4,16,1024]{2,1,0:T(8,128)S(1)} %pad_maximum_fusion), channel_id=1, source_target_pairs={{0,2},{1,3},{2,0},{3,1},{4,6},{5,7},{6,4},{7,5},{8,10},{9,11},{10,... | collective-permute-start | bytes 786440 | tf_op jit(solution)/shard_map/ppermute | solution.py:53
  14.5 0.0 collective-permute-start.4
  14.5 3.9 %blocks_1.1 = (f32[8,1024]{1,0:T(8,128)S(1)}, bf16[3,1024,64]{2,1,0:T(8,128)(2,1)S(1)}) custom-call(f32[8,1]{1,0:T(8,128)S(1)} %copy.10.refs_0_, bf16[64,1024]{1,0:T(8,128)(2,1)S(1)} %get-tuple-element.23.refs_1_.refs_2_, f32[8,1024]{1,0:T(8,128)S(1)} %get-tuple-element.24.refs_2_, f32[1,16,1024]{2,1,0:T(8,128)S(1)} %collective-permute-done.refs_3_.refs_1_, ...), custom_call_target="tpu_custom_call" | custom-call | flops 6442450944 | bytes 1048576 | tf_op jit(solution)/shard_map/blocks_1/pallas_call | solution.py:317
  18.4 2.6 %collective-permute-done.3.refs_3_.refs_4_ = f32[4,16,1024]{2,1,0:T(8,128)S(1)} collective-permute-done((f32[4,16,1024]{2,1,0:T(8,128)S(1)}, f32[4,16,1024]{2,1,0:T(8,128)S(1)}, u32[]{:S(2)}, u32[]{:S(2)}) %collective-permute-start.3) | collective-permute-done | bytes 262176 | tf_op jit(solution)/shard_map/ppermute | solution.py:53
  21.1 0.0 collective-permute-start.5
  21.1 5.6 %blocks_2.1 = (f32[8,1024]{1,0:T(8,128)S(1)}, bf16[4,4,2048,256]{3,2,1,0:T(8,128)(2,1)S(1)}) custom-call(f32[8,1]{1,0:T(8,128)S(1)} %copy.10.refs_0_, bf16[64,1024]{1,0:T(8,128)(2,1)S(1)} %get-tuple-element.23.refs_1_.refs_2_, f32[8,1024]{1,0:T(8,128)S(1)} %get-tuple-element.25.refs_2_, f32[4,16,1024]{2,1,0:T(8,128)S(1)} %collective-permute-done.3.refs_3_.refs_4_), custom_call_target="tpu_custom_call" | custom-call | flops 8589934592 | bytes 1048576 | tf_op jit(solution)/shard_map/blocks_2/pallas_call | solution.py:317
  26.7 0.0 copy-start
  26.7 0.0 collective-permute-done.4.refs_3_.refs_5_
  26.7 5.6 %blocks_3.1 = (f32[8,1024]{1,0:T(8,128)S(1)}, bf16[4,1024,64]{2,1,0:T(8,128)(2,1)S(1)}) custom-call(f32[8,1]{1,0:T(8,128)S(1)} %copy.10.refs_0_, bf16[64,1024]{1,0:T(8,128)(2,1)S(1)} %get-tuple-element.23.refs_1_.refs_2_, f32[8,1024]{1,0:T(8,128)S(1)} %get-tuple-element.26.refs_2_, f32[4,16,1024]{2,1,0:T(8,128)S(1)} %collective-permute-done.4.refs_3_.refs_5_), custom_call_target="tpu_custom_call" | custom-call | flops 8589934592 | bytes 1048576 | tf_op jit(solution)/shard_map/blocks_3/pallas_call | solution.py:317
  32.3 0.0 copy-start.2
  32.3 0.0 collective-permute-done.5.refs_5_.refs_6_
  32.4 0.0 copy-done
  32.4 5.8 %blocks_4.1 = (f32[8,1024]{1,0:T(8,128)S(1)}, bf16[4,4,2048,256]{3,2,1,0:T(8,128)(2,1)S(1)}) custom-call(f32[8,1]{1,0:T(8,128)S(1)} %copy.10.refs_0_, bf16[64,1024]{1,0:T(8,128)(2,1)S(1)} %get-tuple-element.23.refs_1_.refs_2_, f32[8,1024]{1,0:T(8,128)S(1)} %get-tuple-element.27.refs_2_, f32[1,1024]{1,0:T(1,128)S(1)} %bitcast.13, ...), custom_call_target="tpu_custom_call" | custom-call | flops 8589934592 | bytes 1048576 | tf_op jit(solution)/shard_map/blocks_4/pallas_call | solution.py:317
  38.2 1.2 %collective-permute-start.6 = (f32[1,8,1024]{2,1,0:T(8,128)S(1)}, f32[1,8,1024]{2,1,0:T(8,128)S(1)}, u32[]{:S(2)}, u32[]{:S(2)}) collective-permute-start(f32[1,8,1024]{2,1,0:T(8,128)S(1)} %bitcast.5), channel_id=1, source_target_pairs={{0,12},{1,13},{2,14},{3,15},{4,0},{5,1},{6,2},{7,3},{8,4},{9,5},{1... | collective-permute-start | bytes 98312 | tf_op jit(solution)/shard_map/ppermute | solution.py:53
  39.4 0.8 %collective-permute-start.7 = (f32[1,8,1024]{2,1,0:T(8,128)S(1)}, f32[1,8,1024]{2,1,0:T(8,128)S(1)}, u32[]{:S(2)}, u32[]{:S(2)}) collective-permute-start(f32[1,8,1024]{2,1,0:T(8,128)S(1)} %bitcast.6), channel_id=1, source_target_pairs={{0,8},{1,9},{2,10},{3,11},{4,12},{5,13},{6,14},{7,15},{8,0},{9,1},... | collective-permute-start | bytes 98312 | tf_op jit(solution)/shard_map/ppermute | solution.py:53
  40.2 1.4 %collective-permute-start.8 = (f32[1,8,1024]{2,1,0:T(8,128)S(1)}, f32[1,8,1024]{2,1,0:T(8,128)S(1)}, u32[]{:S(2)}, u32[]{:S(2)}) collective-permute-start(f32[1,8,1024]{2,1,0:T(8,128)S(1)} %bitcast.7), channel_id=1, source_target_pairs={{0,4},{1,5},{2,6},{3,7},{4,8},{5,9},{6,10},{7,11},{8,12},{9,13},{1... | collective-permute-start | bytes 98312 | tf_op jit(solution)/shard_map/ppermute | solution.py:53
  41.7 0.0 copy-done.2
  41.7 0.6 own_again.1.refs_0_
  42.3 0.0 collective-permute-done.6.refs_8_.refs_3_
  42.3 2.2 %collective-permute-done.7.refs_9_.refs_4_ = f32[1,8,1024]{2,1,0:T(8,128)S(1)} collective-permute-done((f32[1,8,1024]{2,1,0:T(8,128)S(1)}, f32[1,8,1024]{2,1,0:T(8,128)S(1)}, u32[]{:S(2)}, u32[]{:S(2)}) %collective-permute-start.7) | collective-permute-done | bytes 32800 | tf_op jit(solution)/shard_map/ppermute | solution.py:53
  44.6 1.4 %collective-permute-done.8.refs_10_.refs_5_ = f32[1,8,1024]{2,1,0:T(8,128)S(1)} collective-permute-done((f32[1,8,1024]{2,1,0:T(8,128)S(1)}, f32[1,8,1024]{2,1,0:T(8,128)S(1)}, u32[]{:S(2)}, u32[]{:S(2)}) %collective-permute-start.8) | collective-permute-done | bytes 32800 | tf_op jit(solution)/shard_map/ppermute | solution.py:53
  46.0 1.6 %collective-permute-start.9 = (f32[4,8,1024]{2,1,0:T(8,128)S(1)}, f32[4,8,1024]{2,1,0:T(8,128)S(1)}, u32[]{:S(2)}, u32[]{:S(2)}) collective-permute-start(f32[4,8,1024]{2,1,0:T(8,128)S(1)} %pad_maximum_fusion.1), channel_id=1, source_target_pairs={{0,2},{1,3},{2,0},{3,1},{4,6},{5,7},{6,4},{7,5},{8,10},{9,11},{10,... | collective-permute-start | bytes 393224 | tf_op jit(solution)/shard_map/ppermute | solution.py:53
  47.6 0.0 collective-permute-start.10
  47.6 3.7 %line_again.1.refs_2_ = f32[8,1024]{1,0:T(8,128)S(1)} custom-call(f32[8,1024]{1,0:T(8,128)S(1)} %own_again.1.refs_0_, bf16[64,1024]{1,0:T(8,128)(2,1)S(1)} %get-tuple-element.23.refs_1_.refs_2_, bf16[3,1024,64]{2,1,0:T(8,128)(2,1)S(1)} %get-tuple-element.32.refs_2_, f32[1,8,1024]{2,1,0:T(8,128)S(1)} %collective-permute-done.6.refs_8_.refs_3_, ...), custom_call_target="tpu_custom_call" | custom-call | flops 6442450944 | bytes 1048576 | tf_op jit(solution)/shard_map/line_again/pallas_call | solution.py:317
  51.2 0.0 collective-permute-done.9.refs_11_.refs_2_.refs_3_
  51.2 0.5 collective-permute-start.11
  51.8 1.7 %beside_half.1.refs_1_ = f32[8,1024]{1,0:T(8,128)S(1)} custom-call(s32[2]{0:T(128)S(1)} %fusion.1.refs_0_, bf16[4,4,2048,256]{3,2,1,0:T(8,128)(2,1)S(1)} %get-tuple-element.29.refs_1_.refs_2_, f32[4,8,1024]{2,1,0:T(8,128)S(1)} %collective-permute-done.9.refs_11_.refs_2_.refs_3_), custom_call_target="tpu_custom_call" | custom-call | flops 4294967296 | bytes 1048576 | tf_op jit(solution)/shard_map/beside_half/pallas_call | solution.py:317
  53.5 0.0 collective-permute-done.10.refs_12_.refs_4_
  53.5 3.1 %across_half.1.refs_1_ = f32[8,1024]{1,0:T(8,128)S(1)} custom-call(s32[2]{0:T(128)S(1)} %fusion.2.refs_0_, f32[8,1024]{1,0:T(8,128)S(1)} %beside_half.1.refs_1_, bf16[64,1024]{1,0:T(8,128)(2,1)S(1)} %get-tuple-element.23.refs_1_.refs_2_, bf16[4,1024,64]{2,1,0:T(8,128)(2,1)S(1)} %get-tuple-element.30.refs_3_, ...), custom_call_target="tpu_custom_call" | custom-call | flops 4294967296 | bytes 1048576 | tf_op jit(solution)/shard_map/across_half/pallas_call | solution.py:317
  56.6 0.0 collective-permute-done.11.refs_13_.refs_6_.refs_3_
  56.6 1.8 %far_half.1 = (f32[8,1024]{1,0:T(8,128)S(1)}, f32[8,128]{1,0:T(8,128)S(1)}) custom-call(s32[2]{0:T(128)S(1)} %fusion.2.refs_0_, f32[8,1024]{1,0:T(8,128)S(1)} %across_half.1.refs_1_, f32[8,1024]{1,0:T(8,128)S(1)} %line_again.1.refs_2_, f32[1,1024]{1,0:T(1,128)S(1)} %bitcast.14, f32[1,8,1024]{2,1,0:T(8,128)S(1)} %bitcast.10, ...), custom_call_target="tpu_custom_call" | custom-call | flops 4294967296 | bytes 1048576 | tf_op jit(solution)/shard_map/far_half/pallas_call | solution.py:317
  58.5 0.9 %collective-permute-start.12 = (f32[8,128]{1,0:T(8,128)S(1)}, f32[8,128]{1,0:T(8,128)S(1)}, u32[]{:S(2)}, u32[]{:S(2)}) collective-permute-start(f32[8,128]{1,0:T(8,128)S(1)} %get-tuple-element.34), channel_id=1, source_target_pairs={{0,12},{1,13},{2,14},{3,15},{4,0},{5,1},{6,2},{7,3},{8,4},{9,5},{1... | collective-permute-start | bytes 12296 | tf_op jit(solution)/shard_map/ppermute | solution.py:53
  59.4 0.2 collective-permute-start.13
  59.6 1.3 %collective-permute-start.14 = (f32[8,128]{1,0:T(8,128)S(1)}, f32[8,128]{1,0:T(8,128)S(1)}, u32[]{:S(2)}, u32[]{:S(2)}) collective-permute-start(f32[8,128]{1,0:T(8,128)S(1)} %get-tuple-element.34), channel_id=1, source_target_pairs={{0,4},{1,5},{2,6},{3,7},{4,8},{5,9},{6,10},{7,11},{8,12},{9,13},{1... | collective-permute-start | bytes 12296 | tf_op jit(solution)/shard_map/ppermute | solution.py:53
  60.9 1.7 %beside_rest.1.refs_1_ = f32[8,1024]{1,0:T(8,128)S(1)} custom-call(s32[2]{0:T(128)S(1)} %fusion.3.refs_0_, f32[8,1024]{1,0:T(8,128)S(1)} %get-tuple-element.35.refs_1_, bf16[4,4,2048,256]{3,2,1,0:T(8,128)(2,1)S(1)} %get-tuple-element.29.refs_1_.refs_2_, f32[4,8,1024]{2,1,0:T(8,128)S(1)} %collective-permute-done.9.refs_11_.refs_2_.refs_3_), custom_call_target="tpu_custom_call" | custom-call | flops 4294967296 | bytes 1048576 | tf_op jit(solution)/shard_map/beside_rest/pallas_call | solution.py:317
  62.6 3.1 %across_rest.1.refs_1_ = f32[8,1024]{1,0:T(8,128)S(1)} custom-call(s32[2]{0:T(128)S(1)} %fusion.4.refs_0_, f32[8,1024]{1,0:T(8,128)S(1)} %beside_rest.1.refs_1_, bf16[64,1024]{1,0:T(8,128)(2,1)S(1)} %get-tuple-element.23.refs_1_.refs_2_, bf16[4,1024,64]{2,1,0:T(8,128)(2,1)S(1)} %get-tuple-element.30.refs_3_, ...), custom_call_target="tpu_custom_call" | custom-call | flops 4294967296 | bytes 1048576 | tf_op jit(solution)/shard_map/across_rest/pallas_call | solution.py:317
  65.7 0.4 scalars.1.scalars_ref
  66.1 0.0 collective-permute-done.12
  66.1 0.0 collective-permute-done.13
  66.1 0.0 collective-permute-done.14
  66.1 0.1 collective-permute-start.15
  66.2 1.0 %collective-permute-start.16 = (f32[8,128]{1,0:T(8,128)S(1)}, f32[8,128]{1,0:T(8,128)S(1)}, u32[]{:S(2)}, u32[]{:S(2)}) collective-permute-start(f32[8,128]{1,0:T(8,128)S(1)} %add_add_fusion.1), channel_id=1, source_target_pairs={{0,2},{1,3},{2,0},{3,1},{4,6},{5,7},{6,4},{7,5},{8,10},{9,11},{10,... | collective-permute-start | bytes 12296 | tf_op jit(solution)/shard_map/ppermute | solution.py:53
  67.2 0.8 %collective-permute-start.17 = (f32[8,128]{1,0:T(8,128)S(1)}, f32[8,128]{1,0:T(8,128)S(1)}, u32[]{:S(2)}, u32[]{:S(2)}) collective-permute-start(f32[8,128]{1,0:T(8,128)S(1)} %add_add_fusion.1), channel_id=1, source_target_pairs={{0,3},{1,2},{2,1},{3,0},{4,7},{5,6},{6,5},{7,4},{8,11},{9,10},{10,... | collective-permute-start | bytes 12296 | tf_op jit(solution)/shard_map/ppermute | solution.py:89
  68.1 1.7 %far_rest.1.total_ref = f32[8,1024]{1,0:T(8,128)S(1)} custom-call(s32[2]{0:T(128)S(1)} %fusion.4.refs_0_, f32[8,1024]{1,0:T(8,128)S(1)} %across_rest.1.refs_1_, bf16[4,4,2048,256]{3,2,1,0:T(8,128)(2,1)S(1)} %get-tuple-element.33.refs_5_.refs_2_, f32[4,8,1024]{2,1,0:T(8,128)S(1)} %collective-permute-done.11.refs_13_.refs_6_.refs_3_), custom_call_target="tpu_custom_call" | custom-call | flops 4294967296 | bytes 1048576 | tf_op jit(solution)/shard_map/far_rest/pallas_call | solution.py:317
  69.8 0.0 collective-permute-done.15
  69.8 0.1 collective-permute-done.16
  69.9 0.4 collective-permute-done.17
  70.3 0.7 %last_update.1 = (f32[8,1024]{1,0:T(8,128)}, f32[8,1024]{1,0:T(8,128)}) custom-call(f32[4,8,128]{2,1,0:T(8,128)S(1)} %scalars.1.scalars_ref, f32[8,128]{1,0:T(8,128)S(1)} %add_add_fusion.form_ref, f32[8,1024]{1,0:T(8,128)S(1)} %far_rest.1.total_ref, f32[1,1024]{1,0:T(1,128)S(1)} %bitcast.15, ...), custom_call_target="tpu_custom_call" | custom-call | tf_op jit(solution)/shard_map/last_update/pallas_call | solution.py:409
  (8 shorter events, 0.1 us)
Async XLA Ops:
  1.4 10.4 %collective-permute-start = (f32[1,16,1024]{2,1,0:T(8,128)S(1)}, f32[1,16,1024]{2,1,0:T(8,128)S(1)}, u32[]{:S(2)}, u32[]{:S(2)}) collective-permute-start(f32[1,16,1024]{2,1,0:T(8,128)S(1)} %maximum_bitcast_fusion.refs_1_.refs_4_.refs_0_.mine_ref), channel_id=1, source_target_pairs={{0,12},{1,13},{2,14},{3,15},{4,0},{5,1},{6,2},{7,3},{8,4},{9,5},{1... | collective-permute-start | bytes 196616 | tf_op jit(solution)/shard_map/ppermute | solution.py:53
  6.5 6.5 %collective-permute-start.1 = (f32[1,16,1024]{2,1,0:T(8,128)S(1)}, f32[1,16,1024]{2,1,0:T(8,128)S(1)}, u32[]{:S(2)}, u32[]{:S(2)}) collective-permute-start(f32[1,16,1024]{2,1,0:T(8,128)S(1)} %maximum_bitcast_fusion.refs_1_.refs_4_.refs_0_.mine_ref), channel_id=1, source_target_pairs={{0,8},{1,9},{2,10},{3,11},{4,12},{5,13},{6,14},{7,15},{8,0},{9,1},... | collective-permute-start | bytes 196616 | tf_op jit(solution)/shard_map/ppermute | solution.py:53
  6.5 6.5 %collective-permute-start.2 = (f32[1,16,1024]{2,1,0:T(8,128)S(1)}, f32[1,16,1024]{2,1,0:T(8,128)S(1)}, u32[]{:S(2)}, u32[]{:S(2)}) collective-permute-start(f32[1,16,1024]{2,1,0:T(8,128)S(1)} %maximum_bitcast_fusion.refs_1_.refs_4_.refs_0_.mine_ref), channel_id=1, source_target_pairs={{0,4},{1,5},{2,6},{3,7},{4,8},{5,9},{6,10},{7,11},{8,12},{9,13},{1... | collective-permute-start | bytes 196616 | tf_op jit(solution)/shard_map/ppermute | solution.py:53
  9.8 2.0 %copy-start.1 = (bf16[1,4,2048,256]{3,2,1,0:T(8,128)(2,1)}, bf16[1,4,2048,256]{3,2,1,0:T(8,128)(2,1)S(1)}, u32[]{:S(2)}) copy-start(bf16[1,4,2048,256]{3,2,1,0:T(8,128)(2,1)S(1)} %get-tuple-element.31.refs_0_) | copy-start | bytes 12582916
  13.0 8.1 %collective-permute-start.3 = (f32[4,16,1024]{2,1,0:T(8,128)S(1)}, f32[4,16,1024]{2,1,0:T(8,128)S(1)}, u32[]{:S(2)}, u32[]{:S(2)}) collective-permute-start(f32[4,16,1024]{2,1,0:T(8,128)S(1)} %pad_maximum_fusion), channel_id=1, source_target_pairs={{0,2},{1,3},{2,0},{3,1},{4,6},{5,7},{6,4},{7,5},{8,10},{9,11},{10,... | collective-permute-start | bytes 786440 | tf_op jit(solution)/shard_map/ppermute | solution.py:53
  14.5 12.2 %collective-permute-start.4 = (f32[4,16,1024]{2,1,0:T(8,128)S(1)}, f32[4,16,1024]{2,1,0:T(8,128)S(1)}, u32[]{:S(2)}, u32[]{:S(2)}) collective-permute-start(f32[4,16,1024]{2,1,0:T(8,128)S(1)} %pad_maximum_fusion), channel_id=1, source_target_pairs={{0,1},{1,0},{2,3},{3,2},{4,5},{5,4},{6,7},{7,6},{8,9},{9,8},{10,11... | collective-permute-start | bytes 786440 | tf_op jit(solution)/shard_map/ppermute | solution.py:53
  21.1 11.3 %collective-permute-start.5 = (f32[4,16,1024]{2,1,0:T(8,128)S(1)}, f32[4,16,1024]{2,1,0:T(8,128)S(1)}, u32[]{:S(2)}, u32[]{:S(2)}) collective-permute-start(f32[4,16,1024]{2,1,0:T(8,128)S(1)} %collective-permute-done.3.refs_3_.refs_4_), channel_id=1, source_target_pairs={{0,1},{1,0},{2,3},{3,2},{4,5},{5,4},{6,7},{7,6},{8,9},{9,8},{10,11... | collective-permute-start | bytes 786440 | tf_op jit(solution)/shard_map/ppermute | solution.py:53
  26.7 5.7 %copy-start = (f32[1024]{0:T(1024)S(1)}, f32[1024]{0:T(1024)}, u32[]{:S(2)}) copy-start(f32[1024]{0:T(1024)} %param.6) | copy-start | bytes 12292
  32.3 9.3 %copy-start.2 = (bf16[1,4,2048,256]{3,2,1,0:T(8,128)(2,1)S(1)}, bf16[1,4,2048,256]{3,2,1,0:T(8,128)(2,1)}, u32[]{:S(2)}) copy-start(bf16[1,4,2048,256]{3,2,1,0:T(8,128)(2,1)} %copy-done.1) | copy-start | bytes 12582916
  38.2 4.1 %collective-permute-start.6 = (f32[1,8,1024]{2,1,0:T(8,128)S(1)}, f32[1,8,1024]{2,1,0:T(8,128)S(1)}, u32[]{:S(2)}, u32[]{:S(2)}) collective-permute-start(f32[1,8,1024]{2,1,0:T(8,128)S(1)} %bitcast.5), channel_id=1, source_target_pairs={{0,12},{1,13},{2,14},{3,15},{4,0},{5,1},{6,2},{7,3},{8,4},{9,5},{1... | collective-permute-start | bytes 98312 | tf_op jit(solution)/shard_map/ppermute | solution.py:53
  39.4 5.2 %collective-permute-start.7 = (f32[1,8,1024]{2,1,0:T(8,128)S(1)}, f32[1,8,1024]{2,1,0:T(8,128)S(1)}, u32[]{:S(2)}, u32[]{:S(2)}) collective-permute-start(f32[1,8,1024]{2,1,0:T(8,128)S(1)} %bitcast.6), channel_id=1, source_target_pairs={{0,8},{1,9},{2,10},{3,11},{4,12},{5,13},{6,14},{7,15},{8,0},{9,1},... | collective-permute-start | bytes 98312 | tf_op jit(solution)/shard_map/ppermute | solution.py:53
  40.2 5.7 %collective-permute-start.8 = (f32[1,8,1024]{2,1,0:T(8,128)S(1)}, f32[1,8,1024]{2,1,0:T(8,128)S(1)}, u32[]{:S(2)}, u32[]{:S(2)}) collective-permute-start(f32[1,8,1024]{2,1,0:T(8,128)S(1)} %bitcast.7), channel_id=1, source_target_pairs={{0,4},{1,5},{2,6},{3,7},{4,8},{5,9},{6,10},{7,11},{8,12},{9,13},{1... | collective-permute-start | bytes 98312 | tf_op jit(solution)/shard_map/ppermute | solution.py:53
  46.0 5.3 %collective-permute-start.9 = (f32[4,8,1024]{2,1,0:T(8,128)S(1)}, f32[4,8,1024]{2,1,0:T(8,128)S(1)}, u32[]{:S(2)}, u32[]{:S(2)}) collective-permute-start(f32[4,8,1024]{2,1,0:T(8,128)S(1)} %pad_maximum_fusion.1), channel_id=1, source_target_pairs={{0,2},{1,3},{2,0},{3,1},{4,6},{5,7},{6,4},{7,5},{8,10},{9,11},{10,... | collective-permute-start | bytes 393224 | tf_op jit(solution)/shard_map/ppermute | solution.py:53
  47.6 6.0 %collective-permute-start.10 = (f32[4,8,1024]{2,1,0:T(8,128)S(1)}, f32[4,8,1024]{2,1,0:T(8,128)S(1)}, u32[]{:S(2)}, u32[]{:S(2)}) collective-permute-start(f32[4,8,1024]{2,1,0:T(8,128)S(1)} %pad_maximum_fusion.1), channel_id=1, source_target_pairs={{0,1},{1,0},{2,3},{3,2},{4,5},{5,4},{6,7},{7,6},{8,9},{9,8},{10,11... | collective-permute-start | bytes 393224 | tf_op jit(solution)/shard_map/ppermute | solution.py:53
  51.2 5.4 %collective-permute-start.11 = (f32[4,8,1024]{2,1,0:T(8,128)S(1)}, f32[4,8,1024]{2,1,0:T(8,128)S(1)}, u32[]{:S(2)}, u32[]{:S(2)}) collective-permute-start(f32[4,8,1024]{2,1,0:T(8,128)S(1)} %collective-permute-done.9.refs_11_.refs_2_.refs_3_), channel_id=1, source_target_pairs={{0,1},{1,0},{2,3},{3,2},{4,5},{5,4},{6,7},{7,6},{8,9},{9,8},{10,11... | collective-permute-start | bytes 393224 | tf_op jit(solution)/shard_map/ppermute | solution.py:53
  58.5 7.6 %collective-permute-start.12 = (f32[8,128]{1,0:T(8,128)S(1)}, f32[8,128]{1,0:T(8,128)S(1)}, u32[]{:S(2)}, u32[]{:S(2)}) collective-permute-start(f32[8,128]{1,0:T(8,128)S(1)} %get-tuple-element.34), channel_id=1, source_target_pairs={{0,12},{1,13},{2,14},{3,15},{4,0},{5,1},{6,2},{7,3},{8,4},{9,5},{1... | collective-permute-start | bytes 12296 | tf_op jit(solution)/shard_map/ppermute | solution.py:53
  59.4 6.7 %collective-permute-start.13 = (f32[8,128]{1,0:T(8,128)S(1)}, f32[8,128]{1,0:T(8,128)S(1)}, u32[]{:S(2)}, u32[]{:S(2)}) collective-permute-start(f32[8,128]{1,0:T(8,128)S(1)} %get-tuple-element.34), channel_id=1, source_target_pairs={{0,8},{1,9},{2,10},{3,11},{4,12},{5,13},{6,14},{7,15},{8,0},{9,1},... | collective-permute-start | bytes 12296 | tf_op jit(solution)/shard_map/ppermute | solution.py:53
  59.6 6.5 %collective-permute-start.14 = (f32[8,128]{1,0:T(8,128)S(1)}, f32[8,128]{1,0:T(8,128)S(1)}, u32[]{:S(2)}, u32[]{:S(2)}) collective-permute-start(f32[8,128]{1,0:T(8,128)S(1)} %get-tuple-element.34), channel_id=1, source_target_pairs={{0,4},{1,5},{2,6},{3,7},{4,8},{5,9},{6,10},{7,11},{8,12},{9,13},{1... | collective-permute-start | bytes 12296 | tf_op jit(solution)/shard_map/ppermute | solution.py:53
  66.1 3.7 %collective-permute-start.15 = (f32[8,128]{1,0:T(8,128)S(1)}, f32[8,128]{1,0:T(8,128)S(1)}, u32[]{:S(2)}, u32[]{:S(2)}) collective-permute-start(f32[8,128]{1,0:T(8,128)S(1)} %add_add_fusion.1), channel_id=1, source_target_pairs={{0,1},{1,0},{2,3},{3,2},{4,5},{5,4},{6,7},{7,6},{8,9},{9,8},{10,11... | collective-permute-start | bytes 12296 | tf_op jit(solution)/shard_map/ppermute | solution.py:53
  66.2 3.7 %collective-permute-start.16 = (f32[8,128]{1,0:T(8,128)S(1)}, f32[8,128]{1,0:T(8,128)S(1)}, u32[]{:S(2)}, u32[]{:S(2)}) collective-permute-start(f32[8,128]{1,0:T(8,128)S(1)} %add_add_fusion.1), channel_id=1, source_target_pairs={{0,2},{1,3},{2,0},{3,1},{4,6},{5,7},{6,4},{7,5},{8,10},{9,11},{10,... | collective-permute-start | bytes 12296 | tf_op jit(solution)/shard_map/ppermute | solution.py:53
  67.2 3.0 %collective-permute-start.17 = (f32[8,128]{1,0:T(8,128)S(1)}, f32[8,128]{1,0:T(8,128)S(1)}, u32[]{:S(2)}, u32[]{:S(2)}) collective-permute-start(f32[8,128]{1,0:T(8,128)S(1)} %add_add_fusion.1), channel_id=1, source_target_pairs={{0,3},{1,2},{2,1},{3,0},{4,7},{5,6},{6,5},{7,4},{8,11},{9,10},{10,... | collective-permute-start | bytes 12296 | tf_op jit(solution)/shard_map/ppermute | solution.py:89

commit v10 on v9

--- a/solution.py
+++ b/solution.py
@@ -12,7 +12,8 @@
 DEPTH = 64
 TILE = 256
 MIB = 1024 * 1024
-KEPT_ORDER = (0, 2, 4, 1, 3)
+KEPT_ORDER = (0, 1, 4, 3, 2)
+KEPT_ROOM = 52 * MIB
 F32 = jnp.float32
 BF16 = jnp.bfloat16
 
@@ -44,13 +45,11 @@
     dirs_ref[at] = jnp.concatenate([both, both], axis=1)
 
 
-def shifted(value, stride, size, by):
+def swapped(value, far_by, near_by, core_by):
     length = lax.axis_size("row")
-    pairs = []
-    for i in range(length):
-        digit = (i // stride) % size
-        pairs.append((i, i + ((digit - by) % size - digit) * stride))
-    return lax.ppermute(value, "row", pairs)
+    _, near = digits()
+    by = (far_by * near + near_by) * 2 + core_by
+    return lax.ppermute(value, "row", [(i, i ^ by) for i in range(length)])
 
 
 def digits():
@@ -64,57 +63,44 @@
 def gathered(value):
     far, near = digits()
     own = value[None]
-    line = [shifted(own, 2 * near, far, by) for by in range(1, far)]
+    line = [swapped(own, by, 0, 0) for by in range(1, far)]
     group = jnp.concatenate([own] + line, axis=0)
-    beside = [shifted(group, 2, near, by) for by in range(1, near)]
-    across = [shifted(g, 1, 2, 1) for g in [group] + beside]
-    return [own], line, beside, across[:1], across[1:]
+    across = swapped(group, 0, 0, 1)
+    beside = [swapped(group, 0, by, 0) for by in range(1, near)]
+    return [own], line, [across], beside, [swapped(g, 0, 0, 1) for g in beside]
 
 
 def along_line(value):
-    far, near = digits()
-    return [shifted(value, 2 * near, far, by) for by in range(1, far)]
+    far, _ = digits()
+    return [swapped(value, by, 0, 0) for by in range(1, far)]
 
 
 def over_quad(value):
     _, near = digits()
-    length = lax.axis_size("row")
-    quad = [shifted(value, 1, 2, 1)]
-    for by in range(1, near):
-        quad.append(shifted(value, 2, near, by))
-        pairs = []
-        for i in range(length):
-            digit = (i // 2) % near
-            pairs.append((i, (i + ((digit - by) % near - digit) * 2) ^ 1))
-        quad.append(lax.ppermute(value, "row", pairs))
-    return quad
+    return [swapped(value, 0, by // 2, by % 2) for by in range(1, 2 * near)]
 
 
 def tables():
     far, near = digits()
     place = lax.axis_index("row")
     core = place % 2
-    side = (place // 2 % near) // (near // 2)
     picks = jnp.arange(far // 2, dtype=jnp.int32) * 2
-    first, second, last_first, last_second = [], [], [], []
-    for k in range(near - 1):
-        base = k * far
-        shift = k + 1
-        if 2 * shift == near:
-            first.append(base + picks + side)
-            second.append(base + picks + 1 - side)
-        else:
-            whole = base + jnp.arange(far, dtype=jnp.int32)
-            (first if 2 * shift < near else second).append(whole)
-        last_first.append(base + picks + core)
-        last_second.append(base + picks + 1 - core)
-    return (
-        [jnp.concatenate(first), picks + core, jnp.concatenate(last_first)],
-        [jnp.concatenate(second), picks + 1 - core, jnp.concatenate(last_second)],
-    )
-
-
-def add_block(yt_ref, at, own_ref, dirs_ref, acc_ref, keep_ref):
+    sides = [(place // 2 // (by & -by)) % 2 for by in range(1, near)]
+
+    def listed(flip):
+        def one(k, side):
+            return k * far + picks + (side + flip) % 2
+
+        return [
+            one(0, core),
+            jnp.concatenate([one(k, side) for k, side in enumerate(sides)]),
+            jnp.concatenate([one(k, core) for k in range(near - 1)]),
+        ]
+
+    return listed(0), listed(1)
+
+
+def add_block(yt_ref, at, own_ref, dirs_ref, slot, acc_ref, keep_ref=None, kept_at=None):
     width = own_ref.shape[1]
     for c in range(width // TILE):
         cols = slice(c * TILE, (c + 1) * TILE)
@@ -123,17 +109,17 @@
         high = weight.astype(BF16)
         low = (weight - high.astype(F32)).astype(BF16)
         if keep_ref is not None:
-            keep_ref[at, c, 0:width, :] = high
-            keep_ref[at, c, width:, :] = low
+            keep_ref[kept_at, c, 0:width, :] = high
+            keep_ref[kept_at, c, width:, :] = low
         acc_ref[:, cols] += jnp.dot(
-            dirs_ref[at, :, 0:width], high, preferred_element_type=F32
-        ) + jnp.dot(dirs_ref[at, :, 0:width], low, preferred_element_type=F32)
-
-
-def add_kept_block(keep_ref, at, dirs_ref, acc_ref):
+            dirs_ref[slot, :, 0:width], high, preferred_element_type=F32
+        ) + jnp.dot(dirs_ref[slot, :, 0:width], low, preferred_element_type=F32)
+
+
+def add_kept_block(keep_ref, at, dirs_ref, slot, acc_ref):
     for c in range(keep_ref.shape[1]):
         acc_ref[:, c * TILE : (c + 1) * TILE] += jnp.dot(
-            dirs_ref[at], keep_ref[at, c], preferred_element_type=F32
+            dirs_ref[slot], keep_ref[at, c], preferred_element_type=F32
         )
 
 
@@ -146,18 +132,23 @@
     return next(n for n in (4, 3, 2, 1) if steps % n == 0)
 
 
+def repeated(steps, function):
+    if steps <= 4:
+        for k in range(steps):
+            function(k)
+    else:
+
+        def step(k, carry):
+            function(k)
+            return carry
+
+        lax.fori_loop(0, steps, step, 0, unroll=unrolled(steps))
+
+
 def each(stacks, function):
     base = 0
     for ref in stacks:
-
-        def block(b, carry, ref=ref, base=base):
-            function(base + b, ref[b])
-            return carry
-
-        if ref.shape[0] == 1:
-            block(0, 0)
-        else:
-            lax.fori_loop(0, ref.shape[0], block, 0)
+        repeated(ref.shape[0], lambda b, ref=ref, base=base: function(base + b, ref[b]))
         base += ref.shape[0]
 
 
@@ -168,28 +159,29 @@
     noise_ref, mine_ref = (refs.pop(0), refs.pop(0)) if amplitude else (None, None)
     stacks = refs[:nstacks]
     refs = refs[nstacks:]
+    blocks = sum(ref.shape[0] for ref in stacks)
     if first:
         own_ref = refs.pop(0)
         own_ref[...] = exponent_rows(
             stacks[0][0, 0:nfeat, :] / scale_ref[...], 1.0, False
         ).astype(BF16)
-    out_ref, yt_ref, dirs_ref, acc_ref = refs[:1] + refs[-3:]
-    keep_ref = refs[1] if kept else None
-
-    def prepare(b, value):
+    out_ref = refs.pop(0)
+    keep_ref = refs.pop(0) if kept else None
+    yt_ref = refs.pop(0) if kept < blocks else None
+    dirs_ref, acc_ref, *fresh = refs
+    acc_ref[...] = jnp.zeros_like(acc_ref)
+
+    def step(b, value):
         rows = exponent_rows(value[0:nfeat, :] / scale_ref[...], LOG2E, True)
-        yt_ref[b] = rows.T.astype(BF16)
         put_dirs(dirs_ref, b, value[nfeat:, :])
-
-    each(stacks, prepare)
-    acc_ref[...] = jnp.zeros_like(acc_ref)
-
-    def step(b, carry):
-        add_block(yt_ref, b, own_ref, dirs_ref, acc_ref, keep_ref)
-        return carry
-
-    blocks = yt_ref.shape[0]
-    lax.fori_loop(0, blocks, step, 0, unroll=unrolled(blocks))
+        if kept and b < kept:
+            fresh[0][b] = rows.T.astype(BF16)
+            add_block(fresh[0], b, own_ref, dirs_ref, b, acc_ref, keep_ref, b)
+        else:
+            yt_ref[b - kept] = rows.T.astype(BF16)
+            add_block(yt_ref, b - kept, own_ref, dirs_ref, b, acc_ref)
+
+    each(stacks, step)
     total = folded(acc_ref)
     if not first:
         total = total + sofar_ref[...]
@@ -198,39 +190,44 @@
     out_ref[...] = total
 
 
-def over_images(nstacks, table, sofar, form, amplitude, kept, *refs):
+def over_images(nstacks, table, sofar, form, amplitude, kept, blocks, *refs):
     refs = list(refs)
     table_ref = refs.pop(0) if table else None
     sofar_ref = refs.pop(0) if sofar else None
     if form:
         once_ref, noise_ref, mine_ref = refs.pop(0), refs.pop(0), refs.pop(0)
-    own_ref = None if kept else refs.pop(0)
-    source_ref, *refs = refs
+    keep_ref = refs.pop(0) if kept else None
+    own_ref, yt_ref = (refs.pop(0), refs.pop(0)) if kept < blocks else (None, None)
     stacks = refs[:nstacks]
     out_ref, *refs = refs[nstacks:]
     form_ref = refs.pop(0) if form else None
     dirs_ref, acc_ref = refs
-
-    def prepare(b, value):
-        put_dirs(dirs_ref, b, value)
-
-    alone = nstacks == 1
-    if not alone:
-        each(stacks, prepare)
     acc_ref[...] = jnp.zeros_like(acc_ref)
 
-    def step(s, carry):
-        b = table_ref[s] if table else s
-        if alone:
-            prepare(b, stacks[0][b])
-        if kept:
-            add_kept_block(source_ref, b, dirs_ref, acc_ref)
+    def add(at, slot, is_kept):
+        if is_kept:
+            add_kept_block(keep_ref, at, dirs_ref, slot, acc_ref)
         else:
-            add_block(source_ref, b, own_ref, dirs_ref, acc_ref, None)
-        return carry
-
-    blocks = table_ref.shape[0] if table else source_ref.shape[0]
-    lax.fori_loop(0, blocks, step, 0, unroll=unrolled(blocks))
+            add_block(yt_ref, at - kept, own_ref, dirs_ref, slot, acc_ref)
+
+    if table:
+        if nstacks > 1:
+            each(stacks, lambda b, value: put_dirs(dirs_ref, b, value))
+
+        def step(s):
+            b = table_ref[s]
+            if nstacks == 1:
+                put_dirs(dirs_ref, s, stacks[0][b])
+            add(b, s if nstacks == 1 else b, bool(kept) and 2 * s + 1 < kept)
+
+        repeated(table_ref.shape[0], step)
+    else:
+
+        def direct(b, value):
+            put_dirs(dirs_ref, b, value)
+            add(b, b, bool(kept) and b < kept)
+
+        each(stacks, direct)
     total = folded(acc_ref)
     if sofar:
         total = total + sofar_ref[...]
@@ -312,7 +309,7 @@
             pltpu.VMEM((2 * nrhs, width), F32),
         ]
         if fresh:
-            scratch.insert(0, pltpu.VMEM((fresh, width, DEPTH), BF16))
+            scratch.append(pltpu.VMEM((fresh, width, DEPTH), BF16))
         limit = 4 * MIB + blocks * 512 * width
         return pl.pallas_call(
             kernel,
@@ -332,64 +329,69 @@
     groups = gathered(jnp.concatenate([features, rhs], axis=0))
     mine = groups[0][0]
     own_shape = jax.ShapeDtypeStruct((DEPTH, width), BF16)
-    room = 52 * MIB - lax.axis_size("row") * 512 * width
-    keep = [False] * len(groups)
+    room = KEPT_ROOM - lax.axis_size("row") * 512 * width
+    keep = [0] * len(groups)
     for k in KEPT_ORDER:
-        size = 4 * amount(groups[k]) * width * width
-        keep[k] = size <= room
-        room -= size if keep[k] else 0
+        fit = max(room, 0) // (4 * width * width)
+        blocks = amount(groups[k])
+        keep[k] = blocks if blocks <= fit else fit // 2 * 2 if blocks <= 4 else 0
+        room -= 4 * keep[k] * width * width
     own, total, prepared = None, None, []
     for k, stacks in enumerate(groups):
         blocks = amount(stacks)
         final = k == len(groups) - 1
+        made = (own_shape,) * (k == 0) + (field,)
         if keep[k]:
-            source = pltpu.VMEM((blocks, width // TILE, 2 * width, TILE), BF16)
-        else:
-            source = jax.ShapeDtypeStruct((blocks, width, DEPTH), BF16)
-        out = (own_shape,) * (k == 0) + (field, source)
-        *made, total, source = call(
+            made += (pltpu.VMEM((keep[k], width // TILE, 2 * width, TILE), BF16),)
+        if keep[k] < blocks:
+            made += (jax.ShapeDtypeStruct((blocks - keep[k], width, DEPTH), BF16),)
+        made = call(
             functools.partial(
                 over_points, nfeat, len(stacks), k == 0, amplitude if final else None, keep[k]
             ),
-            blocks, blocks, out,
+            blocks, blocks, made,
             (scale,) + (() if k == 0 else (own, total)) + ((noise, mine) if final else ())
             + tuple(stacks),
-            "blocks_%d" % k, fresh=blocks * keep[k],
+            "blocks_%d" % k, fresh=keep[k],
         )
-        own = made[0] if made else own
-        prepared.append(source)
+        if k == 0:
+            own, *made = made
+        total, *sources = made
+        prepared.append(sources)
     images = gathered(total)
     image = images[0][0]
 
     def again(group, out, name, sofar=(), table=None, form=()):
         stacks = images[group]
+        blocks = amount(stacks)
         listed = () if table is None else (table,)
-        work = amount(stacks) if table is None else table.shape[0]
-        source = prepared[group]
+        work = blocks if table is None else table.shape[0]
+        sources = list(prepared[group])
         if keep[group]:
-            source = pltpu.with_memory_space_constraint(source, pltpu.VMEM)
+            sources[0] = pltpu.with_memory_space_constraint(sources[0], pltpu.VMEM)
+        if keep[group] < blocks:
+            sources.insert(len(sources) - 1, own)
         return call(
             functools.partial(
                 over_images, len(stacks), table is not None, bool(sofar), bool(form), amplitude,
-                keep[group],
+                keep[group], blocks,
             ),
-            amount(stacks), work, out,
-            listed + tuple(sofar) + tuple(form) + (() if keep[group] else (own,))
-            + (source,) + tuple(stacks),
+            blocks, work, out,
+            listed + tuple(sofar) + tuple(form) + tuple(sources) + tuple(stacks),
             name, table is not None,
         )
 
     halves, rests = tables()
     once = again(0, field, "own_again")
     once = again(1, field, "line_again", sofar=(once,))
-    half = again(2, field, "beside_half", table=halves[0])
-    half = again(3, field, "across_half", sofar=(half,), table=halves[1])
+    half = again(2, field, "across_half", table=halves[0])
+    half = again(3, field, "beside_half", sofar=(half,), table=halves[1])
     total, form = again(
         4, (field, small), "far_half", sofar=(half,), table=halves[2], form=(once, noise, image)
     )
     parts = along_line(form)
-    total = again(2, field, "beside_rest", sofar=(total,), table=rests[0])
-    total = again(3, field, "across_rest", sofar=(total,), table=rests[1])
+    total = again(2, field, "across_rest", sofar=(total,), table=rests[0])
+    total = again(3, field, "beside_rest", sofar=(total,), table=rests[1])
     *parts, total = lax.optimization_barrier((*parts, total))
     form = sum(parts, form)
     parts = over_quad(form)

time: 71.2 us -> 74.8 us (1.051)
  waiting for transfers between devices: 7.86 us -> 12 us
  Pallas kernels: 41.3 us -> 38.6 us
  starting transfers between devices: 17.6 us -> 19.6 us
    ppermute x18, waiting for transfers between devices: 7.86 us -> 12 us  [swapped(): return lax.ppermute(value, 'row', [(i, i ^ by) for i in range(length)])]
    pallas_call x13, Pallas kernels: 40.2 us -> 37.5 us  [call(): pl.pallas_call(kernel, out_shape=out_shape, in_specs=[smem if table and k...]
    ppermute x18, starting transfers between devices: 17.6 us -> 19.6 us  [swapped(): return lax.ppermute(value, 'row', [(i, i ^ by) for i in range(length)])]
  transfers between devices with their start and end apart: 18 -> 18, of which waited for: 6 -> 7; matrix products, arithmetic and copies ran while one was open for 1% -> 1% of each run, Pallas kernels for 46% -> 42%
where the time goes in v10:
time: 74.8 us; the launch traced here: 74.6 us
  Pallas kernels  38.6 us (52%)
  starting transfers between devices  19.6 us (26%)
  waiting for transfers between devices  12 us (16%)
  local copies, waits for them, and re-layouts  2.7 us (4%)
  other arithmetic  0.84 us (1%)
  between operations  0.76 us (1%)
    pallas_call x13, Pallas kernels, call(): pl.pallas_call(kernel, out_shape=out_shape, in_specs=[smem if table and k...  37.5 us
    ppermute x18, starting transfers between devices, swapped(): return lax.ppermute(value, 'row', [(i, i ^ by) for i in range(length)])  19.6 us
    ppermute x18, waiting for transfers between devices, swapped(): return lax.ppermute(value, 'row', [(i, i ^ by) for i in range(length)])  12 us
    unnamed x6, local copies, waits for them, and re-layouts  1.97 us
  transfers between devices with their start and end apart: 18, of which 7 were waited for; matrix products, arithmetic and copies ran while one was open for 1% of the time, Pallas kernels for 42%

profile of v10, /device:TPU:0, one launch (start us, length us, event | category | flops | bytes accessed | tf_op | source)
XLA Modules:
  0.0 74.6 jit_solution(3658129650547774061)
XLA Ops:
  0.6 0.8 %maximum_bitcast_fusion.refs_1_.refs_4_.refs_0_.mine_ref = f32[1,16,1024]{2,1,0:T(8,128)S(1)} fusion(f32[8,1024]{1,0:T(8,128)} %param.7, f32[8,1024]{1,0:T(8,128)} %param.4), kind=kLoop, calls=%fused_computation.2 | loop fusion | flops 16384 | bytes 131072 | tf_op jit(solution)/shard_map/broadcast_in_dim | solution.py:65
  1.4 3.0 %collective-permute-start = (f32[1,16,1024]{2,1,0:T(8,128)S(1)}, f32[1,16,1024]{2,1,0:T(8,128)S(1)}, u32[]{:S(2)}, u32[]{:S(2)}) collective-permute-start(f32[1,16,1024]{2,1,0:T(8,128)S(1)} %maximum_bitcast_fusion.refs_1_.refs_4_.refs_0_.mine_ref), channel_id=1, source_target_pairs={{0,4},{1,5},{2,6},{3,7},{4,0},{5,1},{6,2},{7,3},{8,12},{9,13},{10,... | collective-permute-start | bytes 196616 | tf_op jit(solution)/shard_map/ppermute | solution.py:52
  4.4 2.6 %collective-permute-start.1 = (f32[1,16,1024]{2,1,0:T(8,128)S(1)}, f32[1,16,1024]{2,1,0:T(8,128)S(1)}, u32[]{:S(2)}, u32[]{:S(2)}) collective-permute-start(f32[1,16,1024]{2,1,0:T(8,128)S(1)} %maximum_bitcast_fusion.refs_1_.refs_4_.refs_0_.mine_ref), channel_id=1, source_target_pairs={{0,8},{1,9},{2,10},{3,11},{4,12},{5,13},{6,14},{7,15},{8,0},{9,1},... | collective-permute-start | bytes 196616 | tf_op jit(solution)/shard_map/ppermute | solution.py:52
  7.0 0.0 collective-permute-start.2
  7.0 0.7 copy.10.refs_0_
  7.8 1.6 %blocks_0.1 = (bf16[64,1024]{1,0:T(8,128)(2,1)S(1)}, f32[8,1024]{1,0:T(8,128)S(1)}, bf16[1,4,2048,256]{3,2,1,0:T(8,128)(2,1)S(1)}) custom-call(f32[8,1]{1,0:T(8,128)S(1)} %copy.10.refs_0_, f32[1,16,1024]{2,1,0:T(8,128)S(1)} %maximum_bitcast_fusion.refs_1_.refs_4_.refs_0_.mine_ref), custom_call_target="tpu_custom_call" | custom-call | flops 2147483648 | bytes 1048576 | tf_op jit(solution)/shard_map/blocks_0/pallas_call | solution.py:314
  9.4 0.0 copy-start.1
  9.4 2.0 %copy-done.1 = bf16[1,4,2048,256]{3,2,1,0:T(8,128)(2,1)} copy-done((bf16[1,4,2048,256]{3,2,1,0:T(8,128)(2,1)}, bf16[1,4,2048,256]{3,2,1,0:T(8,128)(2,1)S(1)}, u32[]{:S(2)}) %copy-start.1) | copy-done | bytes 4194328
  11.4 0.0 collective-permute-done.refs_3_.refs_1_
  11.4 0.3 collective-permute-done.1.refs_4_.refs_2_
  11.7 1.4 %collective-permute-done.2.refs_5_.refs_3_ = f32[1,16,1024]{2,1,0:T(8,128)S(1)} collective-permute-done((f32[1,16,1024]{2,1,0:T(8,128)S(1)}, f32[1,16,1024]{2,1,0:T(8,128)S(1)}, u32[]{:S(2)}, u32[]{:S(2)}) %collective-permute-start.2) | collective-permute-done | bytes 65568 | tf_op jit(solution)/shard_map/ppermute | solution.py:52
  13.1 0.1 collective-permute-start.3
  13.2 1.6 %collective-permute-start.4 = (f32[4,16,1024]{2,1,0:T(8,128)S(1)}, f32[4,16,1024]{2,1,0:T(8,128)S(1)}, u32[]{:S(2)}, u32[]{:S(2)}) collective-permute-start(f32[4,16,1024]{2,1,0:T(8,128)S(1)} %pad_maximum_fusion), channel_id=1, source_target_pairs={{0,2},{1,3},{2,0},{3,1},{4,6},{5,7},{6,4},{7,5},{8,10},{9,11},{10,... | collective-permute-start | bytes 786440 | tf_op jit(solution)/shard_map/ppermute | solution.py:52
  14.8 3.8 %blocks_1.1 = (f32[8,1024]{1,0:T(8,128)S(1)}, bf16[3,4,2048,256]{3,2,1,0:T(8,128)(2,1)S(1)}) custom-call(f32[8,1]{1,0:T(8,128)S(1)} %copy.10.refs_0_, bf16[64,1024]{1,0:T(8,128)(2,1)S(1)} %get-tuple-element.24.refs_1_.refs_3_.refs_2_, f32[8,1024]{1,0:T(8,128)S(1)} %get-tuple-element.25.refs_2_, f32[1,16,1024]{2,1,0:T(8,128)S(1)} %collective-permute-done.refs_3_.refs_1_, ...), custom_call_target="tpu_custom_call" | custom-call | flops 6442450944 | bytes 1048576 | tf_op jit(solution)/shard_map/blocks_1/pallas_call | solution.py:314
  18.6 3.3 %collective-permute-done.4.refs_3_.refs_5_ = f32[4,16,1024]{2,1,0:T(8,128)S(1)} collective-permute-done((f32[4,16,1024]{2,1,0:T(8,128)S(1)}, f32[4,16,1024]{2,1,0:T(8,128)S(1)}, u32[]{:S(2)}, u32[]{:S(2)}) %collective-permute-start.4) | collective-permute-done | bytes 262176 | tf_op jit(solution)/shard_map/ppermute | solution.py:52
  21.9 0.0 collective-permute-start.5
  21.9 0.0 collective-permute-done.3.refs_3_.refs_4_
  21.9 4.9 %blocks_2.1 = (f32[8,1024]{1,0:T(8,128)S(1)}, bf16[4,1024,64]{2,1,0:T(8,128)(2,1)S(1)}) custom-call(f32[8,1]{1,0:T(8,128)S(1)} %copy.10.refs_0_, bf16[64,1024]{1,0:T(8,128)(2,1)S(1)} %get-tuple-element.24.refs_1_.refs_3_.refs_2_, f32[8,1024]{1,0:T(8,128)S(1)} %get-tuple-element.26.refs_2_, f32[4,16,1024]{2,1,0:T(8,128)S(1)} %collective-permute-done.3.refs_3_.refs_4_), custom_call_target="tpu_custom_call" | custom-call | flops 8589934592 | bytes 1048576 | tf_op jit(solution)/shard_map/blocks_2/pallas_call | solution.py:314
  26.9 0.0 copy-start
  26.9 5.1 %blocks_3.1 = (f32[8,1024]{1,0:T(8,128)S(1)}, bf16[2,4,2048,256]{3,2,1,0:T(8,128)(2,1)S(1)}, bf16[2,1024,64]{2,1,0:T(8,128)(2,1)S(1)}) custom-call(f32[8,1]{1,0:T(8,128)S(1)} %copy.10.refs_0_, bf16[64,1024]{1,0:T(8,128)(2,1)S(1)} %get-tuple-element.24.refs_1_.refs_3_.refs_2_, f32[8,1024]{1,0:T(8,128)S(1)} %get-tuple-element.27.refs_2_, ...), custom_call_target="tpu_custom_call" | custom-call | flops 8589934592 | bytes 1048576 | tf_op jit(solution)/shard_map/blocks_3/pallas_call | solution.py:314
  32.0 0.0 collective-permute-done.5.refs_5_.refs_6_
  32.0 0.0 copy-done
  32.0 0.0 copy-start.2
  32.1 4.9 %blocks_4.1 = (f32[8,1024]{1,0:T(8,128)S(1)}, bf16[4,4,2048,256]{3,2,1,0:T(8,128)(2,1)S(1)}) custom-call(f32[8,1]{1,0:T(8,128)S(1)} %copy.10.refs_0_, bf16[64,1024]{1,0:T(8,128)(2,1)S(1)} %get-tuple-element.24.refs_1_.refs_3_.refs_2_, f32[8,1024]{1,0:T(8,128)S(1)} %get-tuple-element.28.refs_2_, f32[1,1024]{1,0:T(1,128)S(1)} %bitcast.13, ...), custom_call_target="tpu_custom_call" | custom-call | flops 8589934592 | bytes 1048576 | tf_op jit(solution)/shard_map/blocks_4/pallas_call | solution.py:314
  37.0 0.0 collective-permute-start.6
  37.0 2.7 %collective-permute-start.7 = (f32[1,8,1024]{2,1,0:T(8,128)S(1)}, f32[1,8,1024]{2,1,0:T(8,128)S(1)}, u32[]{:S(2)}, u32[]{:S(2)}) collective-permute-start(f32[1,8,1024]{2,1,0:T(8,128)S(1)} %bitcast.6), channel_id=1, source_target_pairs={{0,8},{1,9},{2,10},{3,11},{4,12},{5,13},{6,14},{7,15},{8,0},{9,1},... | collective-permute-start | bytes 98312 | tf_op jit(solution)/shard_map/ppermute | solution.py:52
  39.7 1.7 %collective-permute-start.8 = (f32[1,8,1024]{2,1,0:T(8,128)S(1)}, f32[1,8,1024]{2,1,0:T(8,128)S(1)}, u32[]{:S(2)}, u32[]{:S(2)}) collective-permute-start(f32[1,8,1024]{2,1,0:T(8,128)S(1)} %bitcast.7), channel_id=1, source_target_pairs={{0,12},{1,13},{2,14},{3,15},{4,8},{5,9},{6,10},{7,11},{8,4},{9,5},... | collective-permute-start | bytes 98312 | tf_op jit(solution)/shard_map/ppermute | solution.py:52
  41.4 0.0 copy-done.2
  41.4 0.6 own_again.1.refs_0_
  42.1 0.0 collective-permute-done.6.refs_8_.refs_2_
  42.1 0.0 collective-permute-done.7.refs_9_.refs_3_
  42.1 3.4 %collective-permute-done.8.refs_10_.refs_4_ = f32[1,8,1024]{2,1,0:T(8,128)S(1)} collective-permute-done((f32[1,8,1024]{2,1,0:T(8,128)S(1)}, f32[1,8,1024]{2,1,0:T(8,128)S(1)}, u32[]{:S(2)}, u32[]{:S(2)}) %collective-permute-start.8) | collective-permute-done | bytes 32800 | tf_op jit(solution)/shard_map/ppermute | solution.py:52
  45.4 0.1 collective-permute-start.9
  45.5 1.6 %collective-permute-start.10 = (f32[4,8,1024]{2,1,0:T(8,128)S(1)}, f32[4,8,1024]{2,1,0:T(8,128)S(1)}, u32[]{:S(2)}, u32[]{:S(2)}) collective-permute-start(f32[4,8,1024]{2,1,0:T(8,128)S(1)} %pad_maximum_fusion.1), channel_id=1, source_target_pairs={{0,2},{1,3},{2,0},{3,1},{4,6},{5,7},{6,4},{7,5},{8,10},{9,11},{10,... | collective-permute-start | bytes 393224 | tf_op jit(solution)/shard_map/ppermute | solution.py:52
  47.1 1.7 %line_again.1.refs_2_ = f32[8,1024]{1,0:T(8,128)S(1)} custom-call(f32[8,1024]{1,0:T(8,128)S(1)} %own_again.1.refs_0_, bf16[3,4,2048,256]{3,2,1,0:T(8,128)(2,1)S(1)} %get-tuple-element.34.refs_1_, f32[1,8,1024]{2,1,0:T(8,128)S(1)} %collective-permute-done.6.refs_8_.refs_2_, f32[1,8,1024]{2,1,0:T(8,128)S(1)} %collective-permute-done.7.refs_9_.refs_3_, ...), custom_call_target="tpu_custom_call" | custom-call | flops 6442450944 | bytes 1048576 | tf_op jit(solution)/shard_map/line_again/pallas_call | solution.py:314
  48.8 2.6 %collective-permute-done.10.refs_12_.refs_5_ = f32[4,8,1024]{2,1,0:T(8,128)S(1)} collective-permute-done((f32[4,8,1024]{2,1,0:T(8,128)S(1)}, f32[4,8,1024]{2,1,0:T(8,128)S(1)}, u32[]{:S(2)}, u32[]{:S(2)}) %collective-permute-start.10) | collective-permute-done | bytes 131104 | tf_op jit(solution)/shard_map/ppermute | solution.py:52
  51.4 0.0 collective-permute-start.11
  51.4 0.0 collective-permute-done.9.refs_11_.refs_3_.refs_4_
  51.4 3.3 %across_half.1.refs_1_ = f32[8,1024]{1,0:T(8,128)S(1)} custom-call(s32[2]{0:T(128)S(1)} %fusion.3.refs_0_, bf16[64,1024]{1,0:T(8,128)(2,1)S(1)} %get-tuple-element.24.refs_1_.refs_3_.refs_2_, bf16[4,1024,64]{2,1,0:T(8,128)(2,1)S(1)} %get-tuple-element.30.refs_2_.refs_3_, f32[4,8,1024]{2,1,0:T(8,128)S(1)} %collective-permute-done.9.refs_11_.refs_3_.refs_4_), custom_call_target="tpu_custom_call" | custom-call | flops 4294967296 | bytes 1048576 | tf_op jit(solution)/shard_map/across_half/pallas_call | solution.py:314
  54.8 2.3 %beside_half.1.refs_1_ = f32[8,1024]{1,0:T(8,128)S(1)} custom-call(s32[2]{0:T(128)S(1)} %fusion.2.refs_0_, f32[8,1024]{1,0:T(8,128)S(1)} %across_half.1.refs_1_, bf16[2,4,2048,256]{3,2,1,0:T(8,128)(2,1)S(1)} %get-tuple-element.31.refs_2_, bf16[64,1024]{1,0:T(8,128)(2,1)S(1)} %get-tuple-element.24.refs_1_.refs_3_.refs_2_, ...), custom_call_target="tpu_custom_call" | custom-call | flops 4294967296 | bytes 1048576 | tf_op jit(solution)/shard_map/beside_half/pallas_call | solution.py:314
  57.1 0.0 collective-permute-done.11.refs_13_.refs_6_.refs_3_
  57.1 1.8 %far_half.1 = (f32[8,1024]{1,0:T(8,128)S(1)}, f32[8,128]{1,0:T(8,128)S(1)}) custom-call(s32[2]{0:T(128)S(1)} %fusion.3.refs_0_, f32[8,1024]{1,0:T(8,128)S(1)} %beside_half.1.refs_1_, f32[8,1024]{1,0:T(8,128)S(1)} %line_again.1.refs_2_, f32[1,1024]{1,0:T(1,128)S(1)} %bitcast.14, f32[1,8,1024]{2,1,0:T(8,128)S(1)} %bitcast.10, ...), custom_call_target="tpu_custom_call" | custom-call | flops 4294967296 | bytes 1048576 | tf_op jit(solution)/shard_map/far_half/pallas_call | solution.py:314
  58.9 0.0 collective-permute-start.12
  59.0 2.2 %collective-permute-start.13 = (f32[8,128]{1,0:T(8,128)S(1)}, f32[8,128]{1,0:T(8,128)S(1)}, u32[]{:S(2)}, u32[]{:S(2)}) collective-permute-start(f32[8,128]{1,0:T(8,128)S(1)} %get-tuple-element.36), channel_id=1, source_target_pairs={{0,8},{1,9},{2,10},{3,11},{4,12},{5,13},{6,14},{7,15},{8,0},{9,1},... | collective-permute-start | bytes 12296 | tf_op jit(solution)/shard_map/ppermute | solution.py:52
  61.2 2.1 %collective-permute-start.14 = (f32[8,128]{1,0:T(8,128)S(1)}, f32[8,128]{1,0:T(8,128)S(1)}, u32[]{:S(2)}, u32[]{:S(2)}) collective-permute-start(f32[8,128]{1,0:T(8,128)S(1)} %get-tuple-element.36), channel_id=1, source_target_pairs={{0,12},{1,13},{2,14},{3,15},{4,8},{5,9},{6,10},{7,11},{8,4},{9,5},... | collective-permute-start | bytes 12296 | tf_op jit(solution)/shard_map/ppermute | solution.py:52
  63.3 3.1 %across_rest.1.refs_1_ = f32[8,1024]{1,0:T(8,128)S(1)} custom-call(s32[2]{0:T(128)S(1)} %fusion.refs_0_, f32[8,1024]{1,0:T(8,128)S(1)} %get-tuple-element.37.refs_1_, bf16[64,1024]{1,0:T(8,128)(2,1)S(1)} %get-tuple-element.24.refs_1_.refs_3_.refs_2_, bf16[4,1024,64]{2,1,0:T(8,128)(2,1)S(1)} %get-tuple-element.30.refs_2_.refs_3_, ...), custom_call_target="tpu_custom_call" | custom-call | flops 4294967296 | bytes 1048576 | tf_op jit(solution)/shard_map/across_rest/pallas_call | solution.py:314
  66.4 2.3 %beside_rest.1.refs_1_ = f32[8,1024]{1,0:T(8,128)S(1)} custom-call(s32[2]{0:T(128)S(1)} %fusion.1.refs_0_, f32[8,1024]{1,0:T(8,128)S(1)} %across_rest.1.refs_1_, bf16[2,4,2048,256]{3,2,1,0:T(8,128)(2,1)S(1)} %get-tuple-element.31.refs_2_, bf16[64,1024]{1,0:T(8,128)(2,1)S(1)} %get-tuple-element.24.refs_1_.refs_3_.refs_2_, ...), custom_call_target="tpu_custom_call" | custom-call | flops 4294967296 | bytes 1048576 | tf_op jit(solution)/shard_map/beside_rest/pallas_call | solution.py:314
  68.8 0.3 scalars.1.scalars_ref
  69.1 0.0 collective-permute-done.12
  69.1 0.0 collective-permute-done.13
  69.1 0.0 collective-permute-done.14
  69.2 0.1 collective-permute-start.15
  69.2 1.6 %collective-permute-start.16 = (f32[8,128]{1,0:T(8,128)S(1)}, f32[8,128]{1,0:T(8,128)S(1)}, u32[]{:S(2)}, u32[]{:S(2)}) collective-permute-start(f32[8,128]{1,0:T(8,128)S(1)} %add_add_fusion.1), channel_id=1, source_target_pairs={{0,2},{1,3},{2,0},{3,1},{4,6},{5,7},{6,4},{7,5},{8,10},{9,11},{10,... | collective-permute-start | bytes 12296 | tf_op jit(solution)/shard_map/ppermute | solution.py:52
  70.8 0.3 collective-permute-start.17
  71.1 1.7 %far_rest.1.total_ref = f32[8,1024]{1,0:T(8,128)S(1)} custom-call(s32[2]{0:T(128)S(1)} %fusion.refs_0_, f32[8,1024]{1,0:T(8,128)S(1)} %beside_rest.1.refs_1_, bf16[4,4,2048,256]{3,2,1,0:T(8,128)(2,1)S(1)} %get-tuple-element.35.refs_5_.refs_2_, f32[4,8,1024]{2,1,0:T(8,128)S(1)} %collective-permute-done.11.refs_13_.refs_6_.refs_3_), custom_call_target="tpu_custom_call" | custom-call | flops 4294967296 | bytes 1048576 | tf_op jit(solution)/shard_map/far_rest/pallas_call | solution.py:314
  72.8 0.0 collective-permute-done.15
  72.8 0.1 collective-permute-done.16
  72.9 0.9 %collective-permute-done.17 = f32[8,128]{1,0:T(8,128)S(1)} collective-permute-done((f32[8,128]{1,0:T(8,128)S(1)}, f32[8,128]{1,0:T(8,128)S(1)}, u32[]{:S(2)}, u32[]{:S(2)}) %collective-permute-start.17) | collective-permute-done | bytes 4128 | tf_op jit(solution)/shard_map/ppermute | solution.py:52
  73.9 0.7 last_update.1
  (8 shorter events, 0.1 us)
Async XLA Ops:
  1.4 10.0 %collective-permute-start = (f32[1,16,1024]{2,1,0:T(8,128)S(1)}, f32[1,16,1024]{2,1,0:T(8,128)S(1)}, u32[]{:S(2)}, u32[]{:S(2)}) collective-permute-start(f32[1,16,1024]{2,1,0:T(8,128)S(1)} %maximum_bitcast_fusion.refs_1_.refs_4_.refs_0_.mine_ref), channel_id=1, source_target_pairs={{0,4},{1,5},{2,6},{3,7},{4,0},{5,1},{6,2},{7,3},{8,12},{9,13},{10,... | collective-permute-start | bytes 196616 | tf_op jit(solution)/shard_map/ppermute | solution.py:52
  4.4 7.3 %collective-permute-start.1 = (f32[1,16,1024]{2,1,0:T(8,128)S(1)}, f32[1,16,1024]{2,1,0:T(8,128)S(1)}, u32[]{:S(2)}, u32[]{:S(2)}) collective-permute-start(f32[1,16,1024]{2,1,0:T(8,128)S(1)} %maximum_bitcast_fusion.refs_1_.refs_4_.refs_0_.mine_ref), channel_id=1, source_target_pairs={{0,8},{1,9},{2,10},{3,11},{4,12},{5,13},{6,14},{7,15},{8,0},{9,1},... | collective-permute-start | bytes 196616 | tf_op jit(solution)/shard_map/ppermute | solution.py:52
  7.0 6.1 %collective-permute-start.2 = (f32[1,16,1024]{2,1,0:T(8,128)S(1)}, f32[1,16,1024]{2,1,0:T(8,128)S(1)}, u32[]{:S(2)}, u32[]{:S(2)}) collective-permute-start(f32[1,16,1024]{2,1,0:T(8,128)S(1)} %maximum_bitcast_fusion.refs_1_.refs_4_.refs_0_.mine_ref), channel_id=1, source_target_pairs={{0,12},{1,13},{2,14},{3,15},{4,8},{5,9},{6,10},{7,11},{8,4},{9,5},... | collective-permute-start | bytes 196616 | tf_op jit(solution)/shard_map/ppermute | solution.py:52
  9.4 2.0 %copy-start.1 = (bf16[1,4,2048,256]{3,2,1,0:T(8,128)(2,1)}, bf16[1,4,2048,256]{3,2,1,0:T(8,128)(2,1)S(1)}, u32[]{:S(2)}) copy-start(bf16[1,4,2048,256]{3,2,1,0:T(8,128)(2,1)S(1)} %get-tuple-element.33.refs_0_) | copy-start | bytes 12582916
  13.1 8.8 %collective-permute-start.3 = (f32[4,16,1024]{2,1,0:T(8,128)S(1)}, f32[4,16,1024]{2,1,0:T(8,128)S(1)}, u32[]{:S(2)}, u32[]{:S(2)}) collective-permute-start(f32[4,16,1024]{2,1,0:T(8,128)S(1)} %pad_maximum_fusion), channel_id=1, source_target_pairs={{0,1},{1,0},{2,3},{3,2},{4,5},{5,4},{6,7},{7,6},{8,9},{9,8},{10,11... | collective-permute-start | bytes 786440 | tf_op jit(solution)/shard_map/ppermute | solution.py:52
  13.2 8.7 %collective-permute-start.4 = (f32[4,16,1024]{2,1,0:T(8,128)S(1)}, f32[4,16,1024]{2,1,0:T(8,128)S(1)}, u32[]{:S(2)}, u32[]{:S(2)}) collective-permute-start(f32[4,16,1024]{2,1,0:T(8,128)S(1)} %pad_maximum_fusion), channel_id=1, source_target_pairs={{0,2},{1,3},{2,0},{3,1},{4,6},{5,7},{6,4},{7,5},{8,10},{9,11},{10,... | collective-permute-start | bytes 786440 | tf_op jit(solution)/shard_map/ppermute | solution.py:52
  21.9 10.1 %collective-permute-start.5 = (f32[4,16,1024]{2,1,0:T(8,128)S(1)}, f32[4,16,1024]{2,1,0:T(8,128)S(1)}, u32[]{:S(2)}, u32[]{:S(2)}) collective-permute-start(f32[4,16,1024]{2,1,0:T(8,128)S(1)} %collective-permute-done.4.refs_3_.refs_5_), channel_id=1, source_target_pairs={{0,1},{1,0},{2,3},{3,2},{4,5},{5,4},{6,7},{7,6},{8,9},{9,8},{10,11... | collective-permute-start | bytes 786440 | tf_op jit(solution)/shard_map/ppermute | solution.py:52
  26.9 5.2 %copy-start = (f32[1024]{0:T(1024)S(1)}, f32[1024]{0:T(1024)}, u32[]{:S(2)}) copy-start(f32[1024]{0:T(1024)} %param.6) | copy-start | bytes 12292
  32.0 9.4 %copy-start.2 = (bf16[1,4,2048,256]{3,2,1,0:T(8,128)(2,1)S(1)}, bf16[1,4,2048,256]{3,2,1,0:T(8,128)(2,1)}, u32[]{:S(2)}) copy-start(bf16[1,4,2048,256]{3,2,1,0:T(8,128)(2,1)} %copy-done.1) | copy-start | bytes 12582916
  37.0 5.1 %collective-permute-start.6 = (f32[1,8,1024]{2,1,0:T(8,128)S(1)}, f32[1,8,1024]{2,1,0:T(8,128)S(1)}, u32[]{:S(2)}, u32[]{:S(2)}) collective-permute-start(f32[1,8,1024]{2,1,0:T(8,128)S(1)} %bitcast.5), channel_id=1, source_target_pairs={{0,4},{1,5},{2,6},{3,7},{4,0},{5,1},{6,2},{7,3},{8,12},{9,13},{10,... | collective-permute-start | bytes 98312 | tf_op jit(solution)/shard_map/ppermute | solution.py:52
  37.0 5.0 %collective-permute-start.7 = (f32[1,8,1024]{2,1,0:T(8,128)S(1)}, f32[1,8,1024]{2,1,0:T(8,128)S(1)}, u32[]{:S(2)}, u32[]{:S(2)}) collective-permute-start(f32[1,8,1024]{2,1,0:T(8,128)S(1)} %bitcast.6), channel_id=1, source_target_pairs={{0,8},{1,9},{2,10},{3,11},{4,12},{5,13},{6,14},{7,15},{8,0},{9,1},... | collective-permute-start | bytes 98312 | tf_op jit(solution)/shard_map/ppermute | solution.py:52
  39.7 5.7 %collective-permute-start.8 = (f32[1,8,1024]{2,1,0:T(8,128)S(1)}, f32[1,8,1024]{2,1,0:T(8,128)S(1)}, u32[]{:S(2)}, u32[]{:S(2)}) collective-permute-start(f32[1,8,1024]{2,1,0:T(8,128)S(1)} %bitcast.7), channel_id=1, source_target_pairs={{0,12},{1,13},{2,14},{3,15},{4,8},{5,9},{6,10},{7,11},{8,4},{9,5},... | collective-permute-start | bytes 98312 | tf_op jit(solution)/shard_map/ppermute | solution.py:52
  45.4 6.0 %collective-permute-start.9 = (f32[4,8,1024]{2,1,0:T(8,128)S(1)}, f32[4,8,1024]{2,1,0:T(8,128)S(1)}, u32[]{:S(2)}, u32[]{:S(2)}) collective-permute-start(f32[4,8,1024]{2,1,0:T(8,128)S(1)} %pad_maximum_fusion.1), channel_id=1, source_target_pairs={{0,1},{1,0},{2,3},{3,2},{4,5},{5,4},{6,7},{7,6},{8,9},{9,8},{10,11... | collective-permute-start | bytes 393224 | tf_op jit(solution)/shard_map/ppermute | solution.py:52
  45.5 5.9 %collective-permute-start.10 = (f32[4,8,1024]{2,1,0:T(8,128)S(1)}, f32[4,8,1024]{2,1,0:T(8,128)S(1)}, u32[]{:S(2)}, u32[]{:S(2)}) collective-permute-start(f32[4,8,1024]{2,1,0:T(8,128)S(1)} %pad_maximum_fusion.1), channel_id=1, source_target_pairs={{0,2},{1,3},{2,0},{3,1},{4,6},{5,7},{6,4},{7,5},{8,10},{9,11},{10,... | collective-permute-start | bytes 393224 | tf_op jit(solution)/shard_map/ppermute | solution.py:52
  51.4 5.7 %collective-permute-start.11 = (f32[4,8,1024]{2,1,0:T(8,128)S(1)}, f32[4,8,1024]{2,1,0:T(8,128)S(1)}, u32[]{:S(2)}, u32[]{:S(2)}) collective-permute-start(f32[4,8,1024]{2,1,0:T(8,128)S(1)} %collective-permute-done.10.refs_12_.refs_5_), channel_id=1, source_target_pairs={{0,1},{1,0},{2,3},{3,2},{4,5},{5,4},{6,7},{7,6},{8,9},{9,8},{10,11... | collective-permute-start | bytes 393224 | tf_op jit(solution)/shard_map/ppermute | solution.py:52
  58.9 10.2 %collective-permute-start.12 = (f32[8,128]{1,0:T(8,128)S(1)}, f32[8,128]{1,0:T(8,128)S(1)}, u32[]{:S(2)}, u32[]{:S(2)}) collective-permute-start(f32[8,128]{1,0:T(8,128)S(1)} %get-tuple-element.36), channel_id=1, source_target_pairs={{0,4},{1,5},{2,6},{3,7},{4,0},{5,1},{6,2},{7,3},{8,12},{9,13},{10,... | collective-permute-start | bytes 12296 | tf_op jit(solution)/shard_map/ppermute | solution.py:52
  59.0 10.2 %collective-permute-start.13 = (f32[8,128]{1,0:T(8,128)S(1)}, f32[8,128]{1,0:T(8,128)S(1)}, u32[]{:S(2)}, u32[]{:S(2)}) collective-permute-start(f32[8,128]{1,0:T(8,128)S(1)} %get-tuple-element.36), channel_id=1, source_target_pairs={{0,8},{1,9},{2,10},{3,11},{4,12},{5,13},{6,14},{7,15},{8,0},{9,1},... | collective-permute-start | bytes 12296 | tf_op jit(solution)/shard_map/ppermute | solution.py:52
  61.2 7.9 %collective-permute-start.14 = (f32[8,128]{1,0:T(8,128)S(1)}, f32[8,128]{1,0:T(8,128)S(1)}, u32[]{:S(2)}, u32[]{:S(2)}) collective-permute-start(f32[8,128]{1,0:T(8,128)S(1)} %get-tuple-element.36), channel_id=1, source_target_pairs={{0,12},{1,13},{2,14},{3,15},{4,8},{5,9},{6,10},{7,11},{8,4},{9,5},... | collective-permute-start | bytes 12296 | tf_op jit(solution)/shard_map/ppermute | solution.py:52
  69.2 3.7 %collective-permute-start.15 = (f32[8,128]{1,0:T(8,128)S(1)}, f32[8,128]{1,0:T(8,128)S(1)}, u32[]{:S(2)}, u32[]{:S(2)}) collective-permute-start(f32[8,128]{1,0:T(8,128)S(1)} %add_add_fusion.1), channel_id=1, source_target_pairs={{0,1},{1,0},{2,3},{3,2},{4,5},{5,4},{6,7},{7,6},{8,9},{9,8},{10,11... | collective-permute-start | bytes 12296 | tf_op jit(solution)/shard_map/ppermute | solution.py:52
  69.2 3.7 %collective-permute-start.16 = (f32[8,128]{1,0:T(8,128)S(1)}, f32[8,128]{1,0:T(8,128)S(1)}, u32[]{:S(2)}, u32[]{:S(2)}) collective-permute-start(f32[8,128]{1,0:T(8,128)S(1)} %add_add_fusion.1), channel_id=1, source_target_pairs={{0,2},{1,3},{2,0},{3,1},{4,6},{5,7},{6,4},{7,5},{8,10},{9,11},{10,... | collective-permute-start | bytes 12296 | tf_op jit(solution)/shard_map/ppermute | solution.py:52
  70.8 3.0 %collective-permute-start.17 = (f32[8,128]{1,0:T(8,128)S(1)}, f32[8,128]{1,0:T(8,128)S(1)}, u32[]{:S(2)}, u32[]{:S(2)}) collective-permute-start(f32[8,128]{1,0:T(8,128)S(1)} %add_add_fusion.1), channel_id=1, source_target_pairs={{0,3},{1,2},{2,1},{3,0},{4,7},{5,6},{6,5},{7,4},{8,11},{9,10},{10,... | collective-permute-start | bytes 12296 | tf_op jit(solution)/shard_map/ppermute | solution.py:52

commit v11 on v10

--- a/solution.py
+++ b/solution.py
@@ -52,6 +52,13 @@
     return lax.ppermute(value, "row", [(i, i ^ by) for i in range(length)])
 
 
+def turned(value, by):
+    length = lax.axis_size("row")
+    far, _ = digits()
+    step = length // far
+    return lax.ppermute(value, "row", [(i, (i - by * step) % length) for i in range(length)])
+
+
 def digits():
     chips = lax.axis_size("row") // 2
     near = 1
@@ -63,16 +70,21 @@
 def gathered(value):
     far, near = digits()
     own = value[None]
-    line = [swapped(own, by, 0, 0) for by in range(1, far)]
+    line = [turned(own, by) for by in range(1, far)]
     group = jnp.concatenate([own] + line, axis=0)
     across = swapped(group, 0, 0, 1)
     beside = [swapped(group, 0, by, 0) for by in range(1, near)]
-    return [own], line, [across], beside, [swapped(g, 0, 0, 1) for g in beside]
+    return [[own], line, [across], beside]
+
+
+def held_back(groups, value):
+    *beside, value = lax.optimization_barrier((*groups[3], value))
+    return groups[:3] + [beside, [swapped(g, 0, 0, 1) for g in beside]], value
 
 
 def along_line(value):
     far, _ = digits()
-    return [swapped(value, by, 0, 0) for by in range(1, far)]
+    return [turned(value, by) for by in range(1, far)]
 
 
 def over_quad(value):
@@ -330,16 +342,20 @@
     mine = groups[0][0]
     own_shape = jax.ShapeDtypeStruct((DEPTH, width), BF16)
     room = KEPT_ROOM - lax.axis_size("row") * 512 * width
-    keep = [0] * len(groups)
+    sizes = [amount(g) for g in groups]
+    sizes.append(sizes[3])
+    keep = [0] * len(sizes)
     for k in KEPT_ORDER:
         fit = max(room, 0) // (4 * width * width)
-        blocks = amount(groups[k])
+        blocks = sizes[k]
         keep[k] = blocks if blocks <= fit else fit // 2 * 2 if blocks <= 4 else 0
         room -= 4 * keep[k] * width * width
     own, total, prepared = None, None, []
-    for k, stacks in enumerate(groups):
-        blocks = amount(stacks)
-        final = k == len(groups) - 1
+    for k, blocks in enumerate(sizes):
+        if k == 3:
+            groups, total = held_back(groups, total)
+        stacks = groups[k]
+        final = k == len(sizes) - 1
         made = (own_shape,) * (k == 0) + (field,)
         if keep[k]:
             made += (pltpu.VMEM((keep[k], width // TILE, 2 * width, TILE), BF16),)
@@ -385,6 +401,7 @@
     once = again(0, field, "own_again")
     once = again(1, field, "line_again", sofar=(once,))
     half = again(2, field, "across_half", table=halves[0])
+    images, half = held_back(images, half)
     half = again(3, field, "beside_half", sofar=(half,), table=halves[1])
     total, form = again(
         4, (field, small), "far_half", sofar=(half,), table=halves[2], form=(once, noise, image)

time: 74.8 us -> 65.9 us (0.88)
  waiting for transfers between devices: 12 us -> 6.45 us
  starting transfers between devices: 19.6 us -> 16.5 us
    ppermute x18 -> x9, starting transfers between devices: 19.6 us -> 4.46 us  [swapped(): return lax.ppermute(value, 'row', [(i, i ^ by) for i in range(length)])]
    ppermute x0 -> x9, starting transfers between devices: none -> 12.1 us  [turned(): lax.ppermute(value, 'row', [(i, (i - by * step) % length) for i in range(...]
    ppermute x18 -> x9, waiting for transfers between devices: 12 us -> 1.22 us  [swapped(): return lax.ppermute(value, 'row', [(i, i ^ by) for i in range(length)])]
    ppermute x0 -> x9, waiting for transfers between devices: none -> 5.24 us  [turned(): lax.ppermute(value, 'row', [(i, (i - by * step) % length) for i in range(...]
  transfers between devices with their start and end apart: 18 -> 18, of which waited for: 7 -> 6; matrix products, arithmetic and copies ran while one was open for 1% -> 1% of each run, Pallas kernels for 42% -> 47%
where the time goes in v11:
time: 65.9 us; the launch traced here: 65.7 us
  Pallas kernels  38.4 us (58%)
  starting transfers between devices  16.5 us (25%)
  waiting for transfers between devices  6.45 us (10%)
  local copies, waits for them, and re-layouts  2.71 us (4%)
  other arithmetic  0.84 us (1%)
  between operations  0.75 us (1%)
    pallas_call x13, Pallas kernels, call(): pl.pallas_call(kernel, out_shape=out_shape, in_specs=[smem if table and k...  37.3 us
    ppermute x9, starting transfers between devices, turned(): lax.ppermute(value, 'row', [(i, (i - by * step) % length) for i in range(...  12.1 us
    ppermute x9, waiting for transfers between devices, turned(): lax.ppermute(value, 'row', [(i, (i - by * step) % length) for i in range(...  5.24 us
    ppermute x9, starting transfers between devices, swapped(): return lax.ppermute(value, 'row', [(i, i ^ by) for i in range(length)])  4.46 us
    unnamed x6, local copies, waits for them, and re-layouts  1.98 us
  transfers between devices with their start and end apart: 18, of which 6 were waited for; matrix products, arithmetic and copies ran while one was open for 1% of the time, Pallas kernels for 47%

profile of v11, /device:TPU:0, one launch (start us, length us, event | category | flops | bytes accessed | tf_op | source)
XLA Modules:
  0.0 65.7 jit_solution(8983363577751492061)
XLA Ops:
  0.6 0.8 %maximum_bitcast_fusion.refs_1_.refs_4_.refs_0_.mine_ref = f32[1,16,1024]{2,1,0:T(8,128)S(1)} fusion(f32[8,1024]{1,0:T(8,128)} %param.7, f32[8,1024]{1,0:T(8,128)} %param.4), kind=kLoop, calls=%fused_computation.2 | loop fusion | flops 16384 | bytes 131072 | tf_op jit(solution)/shard_map/broadcast_in_dim | solution.py:72
  1.4 5.0 %collective-permute-start = (f32[1,16,1024]{2,1,0:T(8,128)S(1)}, f32[1,16,1024]{2,1,0:T(8,128)S(1)}, u32[]{:S(2)}, u32[]{:S(2)}) collective-permute-start(f32[1,16,1024]{2,1,0:T(8,128)S(1)} %maximum_bitcast_fusion.refs_1_.refs_4_.refs_0_.mine_ref), channel_id=1, source_target_pairs={{0,12},{1,13},{2,14},{3,15},{4,0},{5,1},{6,2},{7,3},{8,4},{9,5},{1... | collective-permute-start | bytes 196616 | tf_op jit(solution)/shard_map/ppermute | solution.py:59
  6.5 0.0 collective-permute-start.1
  6.5 1.0 %collective-permute-start.2 = (f32[1,16,1024]{2,1,0:T(8,128)S(1)}, f32[1,16,1024]{2,1,0:T(8,128)S(1)}, u32[]{:S(2)}, u32[]{:S(2)}) collective-permute-start(f32[1,16,1024]{2,1,0:T(8,128)S(1)} %maximum_bitcast_fusion.refs_1_.refs_4_.refs_0_.mine_ref), channel_id=1, source_target_pairs={{0,4},{1,5},{2,6},{3,7},{4,8},{5,9},{6,10},{7,11},{8,12},{9,13},{1... | collective-permute-start | bytes 196616 | tf_op jit(solution)/shard_map/ppermute | solution.py:59
  7.5 0.7 %copy.8.refs_0_ = f32[8,1]{1,0:T(8,128)S(1)} copy(f32[8,1]{0,1:T(1,128)} %bitcast.16) | data formatting | bytes 64 | tf_op jit(solution)/shard_map/broadcast_in_dim | solution.py:310
  8.2 1.6 %blocks_0.1 = (bf16[64,1024]{1,0:T(8,128)(2,1)S(1)}, f32[8,1024]{1,0:T(8,128)S(1)}, bf16[1,4,2048,256]{3,2,1,0:T(8,128)(2,1)S(1)}) custom-call(f32[8,1]{1,0:T(8,128)S(1)} %copy.8.refs_0_, f32[1,16,1024]{2,1,0:T(8,128)S(1)} %maximum_bitcast_fusion.refs_1_.refs_4_.refs_0_.mine_ref), custom_call_target="tpu_custom_call" | custom-call | flops 2147483648 | bytes 1048576 | tf_op jit(solution)/shard_map/blocks_0/pallas_call | solution.py:326
  9.8 0.0 copy-start.1
  9.8 2.0 %copy-done.1 = bf16[1,4,2048,256]{3,2,1,0:T(8,128)(2,1)} copy-done((bf16[1,4,2048,256]{3,2,1,0:T(8,128)(2,1)}, bf16[1,4,2048,256]{3,2,1,0:T(8,128)(2,1)S(1)}, u32[]{:S(2)}) %copy-start.1) | copy-done | bytes 4194328
  11.8 0.0 collective-permute-done.refs_3_.refs_1_
  11.8 1.1 %collective-permute-done.1.refs_4_.refs_2_ = f32[1,16,1024]{2,1,0:T(8,128)S(1)} collective-permute-done((f32[1,16,1024]{2,1,0:T(8,128)S(1)}, f32[1,16,1024]{2,1,0:T(8,128)S(1)}, u32[]{:S(2)}, u32[]{:S(2)}) %collective-permute-start.1) | collective-permute-done | bytes 65568 | tf_op jit(solution)/shard_map/ppermute | solution.py:59
  12.9 0.0 collective-permute-done.2.refs_5_.refs_3_
  13.0 0.1 collective-permute-start.3
  13.0 1.6 %collective-permute-start.4 = (f32[4,16,1024]{2,1,0:T(8,128)S(1)}, f32[4,16,1024]{2,1,0:T(8,128)S(1)}, u32[]{:S(2)}, u32[]{:S(2)}) collective-permute-start(f32[4,16,1024]{2,1,0:T(8,128)S(1)} %pad_maximum_fusion), channel_id=1, source_target_pairs={{0,2},{1,3},{2,0},{3,1},{4,6},{5,7},{6,4},{7,5},{8,10},{9,11},{10,... | collective-permute-start | bytes 786440 | tf_op jit(solution)/shard_map/ppermute | solution.py:52
  14.6 3.8 %blocks_1.1 = (f32[8,1024]{1,0:T(8,128)S(1)}, bf16[3,4,2048,256]{3,2,1,0:T(8,128)(2,1)S(1)}) custom-call(f32[8,1]{1,0:T(8,128)S(1)} %copy.8.refs_0_, bf16[64,1024]{1,0:T(8,128)(2,1)S(1)} %get-tuple-element.28.refs_1_.refs_3_.refs_2_, f32[8,1024]{1,0:T(8,128)S(1)} %get-tuple-element.29.refs_2_, f32[1,16,1024]{2,1,0:T(8,128)S(1)} %collective-permute-done.refs_3_.refs_1_, ...), custom_call_target="tpu_custom_call" | custom-call | flops 6442450944 | bytes 1048576 | tf_op jit(solution)/shard_map/blocks_1/pallas_call | solution.py:326
  18.5 0.0 collective-permute-done.3.refs_3_.refs_4_
  18.5 5.0 %blocks_2.1 = (f32[8,1024]{1,0:T(8,128)S(1)}, bf16[4,1024,64]{2,1,0:T(8,128)(2,1)S(1)}) custom-call(f32[8,1]{1,0:T(8,128)S(1)} %copy.8.refs_0_, bf16[64,1024]{1,0:T(8,128)(2,1)S(1)} %get-tuple-element.28.refs_1_.refs_3_.refs_2_, f32[8,1024]{1,0:T(8,128)S(1)} %get-tuple-element.30.refs_2_, f32[4,16,1024]{2,1,0:T(8,128)S(1)} %collective-permute-done.3.refs_3_.refs_4_), custom_call_target="tpu_custom_call" | custom-call | flops 8589934592 | bytes 1048576 | tf_op jit(solution)/shard_map/blocks_2/pallas_call | solution.py:326
  23.4 0.0 collective-permute-done.4.refs_3_.refs_5_
  23.4 0.0 copy-start
  23.5 0.2 collective-permute-start.5
  23.7 5.1 %blocks_3.1 = (f32[8,1024]{1,0:T(8,128)S(1)}, bf16[2,4,2048,256]{3,2,1,0:T(8,128)(2,1)S(1)}, bf16[2,1024,64]{2,1,0:T(8,128)(2,1)S(1)}) custom-call(f32[8,1]{1,0:T(8,128)S(1)} %copy.8.refs_0_, bf16[64,1024]{1,0:T(8,128)(2,1)S(1)} %get-tuple-element.28.refs_1_.refs_3_.refs_2_, f32[8,1024]{1,0:T(8,128)S(1)} %get-tuple-element.33.refs_2_, ...), custom_call_target="tpu_custom_call" | custom-call | flops 8589934592 | bytes 1048576 | tf_op jit(solution)/shard_map/blocks_3/pallas_call | solution.py:326
  28.8 0.0 collective-permute-done.5.refs_5_.refs_6_
  28.8 0.0 copy-done
  28.8 0.0 copy-start.2
  28.8 4.9 %blocks_4.1 = (f32[8,1024]{1,0:T(8,128)S(1)}, bf16[4,4,2048,256]{3,2,1,0:T(8,128)(2,1)S(1)}) custom-call(f32[8,1]{1,0:T(8,128)S(1)} %copy.8.refs_0_, bf16[64,1024]{1,0:T(8,128)(2,1)S(1)} %get-tuple-element.28.refs_1_.refs_3_.refs_2_, f32[8,1024]{1,0:T(8,128)S(1)} %get-tuple-element.34.refs_2_, f32[1,1024]{1,0:T(1,128)S(1)} %bitcast.13, ...), custom_call_target="tpu_custom_call" | custom-call | flops 8589934592 | bytes 1048576 | tf_op jit(solution)/shard_map/blocks_4/pallas_call | solution.py:326
  33.8 1.9 %collective-permute-start.6 = (f32[1,8,1024]{2,1,0:T(8,128)S(1)}, f32[1,8,1024]{2,1,0:T(8,128)S(1)}, u32[]{:S(2)}, u32[]{:S(2)}) collective-permute-start(f32[1,8,1024]{2,1,0:T(8,128)S(1)} %bitcast.5), channel_id=1, source_target_pairs={{0,12},{1,13},{2,14},{3,15},{4,0},{5,1},{6,2},{7,3},{8,4},{9,5},{1... | collective-permute-start | bytes 98312 | tf_op jit(solution)/shard_map/ppermute | solution.py:59
  35.7 1.0 %collective-permute-start.7 = (f32[1,8,1024]{2,1,0:T(8,128)S(1)}, f32[1,8,1024]{2,1,0:T(8,128)S(1)}, u32[]{:S(2)}, u32[]{:S(2)}) collective-permute-start(f32[1,8,1024]{2,1,0:T(8,128)S(1)} %bitcast.6), channel_id=1, source_target_pairs={{0,8},{1,9},{2,10},{3,11},{4,12},{5,13},{6,14},{7,15},{8,0},{9,1},... | collective-permute-start | bytes 98312 | tf_op jit(solution)/shard_map/ppermute | solution.py:59
  36.7 0.9 %collective-permute-start.8 = (f32[1,8,1024]{2,1,0:T(8,128)S(1)}, f32[1,8,1024]{2,1,0:T(8,128)S(1)}, u32[]{:S(2)}, u32[]{:S(2)}) collective-permute-start(f32[1,8,1024]{2,1,0:T(8,128)S(1)} %bitcast.7), channel_id=1, source_target_pairs={{0,4},{1,5},{2,6},{3,7},{4,8},{5,9},{6,10},{7,11},{8,12},{9,13},{1... | collective-permute-start | bytes 98312 | tf_op jit(solution)/shard_map/ppermute | solution.py:59
  37.6 0.0 copy-done.2
  37.6 0.6 own_again.1.refs_0_
  38.3 0.0 collective-permute-done.6.refs_8_.refs_2_
  38.3 2.3 %collective-permute-done.7.refs_9_.refs_3_ = f32[1,8,1024]{2,1,0:T(8,128)S(1)} collective-permute-done((f32[1,8,1024]{2,1,0:T(8,128)S(1)}, f32[1,8,1024]{2,1,0:T(8,128)S(1)}, u32[]{:S(2)}, u32[]{:S(2)}) %collective-permute-start.7) | collective-permute-done | bytes 32800 | tf_op jit(solution)/shard_map/ppermute | solution.py:59
  40.5 1.9 %collective-permute-done.8.refs_10_.refs_4_ = f32[1,8,1024]{2,1,0:T(8,128)S(1)} collective-permute-done((f32[1,8,1024]{2,1,0:T(8,128)S(1)}, f32[1,8,1024]{2,1,0:T(8,128)S(1)}, u32[]{:S(2)}, u32[]{:S(2)}) %collective-permute-start.8) | collective-permute-done | bytes 32800 | tf_op jit(solution)/shard_map/ppermute | solution.py:59
  42.4 0.1 collective-permute-start.9
  42.5 0.6 collective-permute-start.10
  43.1 1.7 %line_again.1.refs_2_ = f32[8,1024]{1,0:T(8,128)S(1)} custom-call(f32[8,1024]{1,0:T(8,128)S(1)} %own_again.1.refs_0_, bf16[3,4,2048,256]{3,2,1,0:T(8,128)(2,1)S(1)} %get-tuple-element.42.refs_1_, f32[1,8,1024]{2,1,0:T(8,128)S(1)} %collective-permute-done.6.refs_8_.refs_2_, f32[1,8,1024]{2,1,0:T(8,128)S(1)} %collective-permute-done.7.refs_9_.refs_3_, ...), custom_call_target="tpu_custom_call" | custom-call | flops 6442450944 | bytes 1048576 | tf_op jit(solution)/shard_map/line_again/pallas_call | solution.py:326
  44.8 0.0 collective-permute-done.9.refs_3_.refs_11_.refs_4_
  44.8 3.1 %across_half.1.refs_1_ = f32[8,1024]{1,0:T(8,128)S(1)} custom-call(s32[2]{0:T(128)S(1)} %fusion.3.refs_0_, bf16[64,1024]{1,0:T(8,128)(2,1)S(1)} %get-tuple-element.28.refs_1_.refs_3_.refs_2_, bf16[4,1024,64]{2,1,0:T(8,128)(2,1)S(1)} %get-tuple-element.36.refs_2_.refs_3_, f32[4,8,1024]{2,1,0:T(8,128)S(1)} %collective-permute-done.9.refs_3_.refs_11_.refs_4_), custom_call_target="tpu_custom_call" | custom-call | flops 4294967296 | bytes 1048576 | tf_op jit(solution)/shard_map/across_half/pallas_call | solution.py:326
  47.9 0.5 collective-permute-done.10.refs_12_.refs_5_
  48.4 0.0 collective-permute-start.11
  48.4 2.3 %beside_half.1.refs_1_ = f32[8,1024]{1,0:T(8,128)S(1)} custom-call(s32[2]{0:T(128)S(1)} %fusion.2.refs_0_, f32[8,1024]{1,0:T(8,128)S(1)} %across_half.1.refs_1_, bf16[2,4,2048,256]{3,2,1,0:T(8,128)(2,1)S(1)} %get-tuple-element.39.refs_2_, bf16[64,1024]{1,0:T(8,128)(2,1)S(1)} %get-tuple-element.28.refs_1_.refs_3_.refs_2_, ...), custom_call_target="tpu_custom_call" | custom-call | flops 4294967296 | bytes 1048576 | tf_op jit(solution)/shard_map/beside_half/pallas_call | solution.py:326
  50.7 0.0 collective-permute-done.11.refs_13_.refs_6_.refs_3_
  50.7 1.8 %far_half.1 = (f32[8,1024]{1,0:T(8,128)S(1)}, f32[8,128]{1,0:T(8,128)S(1)}) custom-call(s32[2]{0:T(128)S(1)} %fusion.3.refs_0_, f32[8,1024]{1,0:T(8,128)S(1)} %beside_half.1.refs_1_, f32[8,1024]{1,0:T(8,128)S(1)} %line_again.1.refs_2_, f32[1,1024]{1,0:T(1,128)S(1)} %bitcast.14, f32[1,8,1024]{2,1,0:T(8,128)S(1)} %bitcast.10, ...), custom_call_target="tpu_custom_call" | custom-call | flops 4294967296 | bytes 1048576 | tf_op jit(solution)/shard_map/far_half/pallas_call | solution.py:326
  52.6 0.4 collective-permute-start.12
  53.0 0.2 collective-permute-start.13
  53.2 1.6 %collective-permute-start.14 = (f32[8,128]{1,0:T(8,128)S(1)}, f32[8,128]{1,0:T(8,128)S(1)}, u32[]{:S(2)}, u32[]{:S(2)}) collective-permute-start(f32[8,128]{1,0:T(8,128)S(1)} %get-tuple-element.44), channel_id=1, source_target_pairs={{0,4},{1,5},{2,6},{3,7},{4,8},{5,9},{6,10},{7,11},{8,12},{9,13},{1... | collective-permute-start | bytes 12296 | tf_op jit(solution)/shard_map/ppermute | solution.py:59
  54.8 3.1 %across_rest.1.refs_1_ = f32[8,1024]{1,0:T(8,128)S(1)} custom-call(s32[2]{0:T(128)S(1)} %fusion.refs_0_, f32[8,1024]{1,0:T(8,128)S(1)} %get-tuple-element.45.refs_1_, bf16[64,1024]{1,0:T(8,128)(2,1)S(1)} %get-tuple-element.28.refs_1_.refs_3_.refs_2_, bf16[4,1024,64]{2,1,0:T(8,128)(2,1)S(1)} %get-tuple-element.36.refs_2_.refs_3_, ...), custom_call_target="tpu_custom_call" | custom-call | flops 4294967296 | bytes 1048576 | tf_op jit(solution)/shard_map/across_rest/pallas_call | solution.py:326
  57.8 2.3 %beside_rest.1.refs_1_ = f32[8,1024]{1,0:T(8,128)S(1)} custom-call(s32[2]{0:T(128)S(1)} %fusion.1.refs_0_, f32[8,1024]{1,0:T(8,128)S(1)} %across_rest.1.refs_1_, bf16[2,4,2048,256]{3,2,1,0:T(8,128)(2,1)S(1)} %get-tuple-element.39.refs_2_, bf16[64,1024]{1,0:T(8,128)(2,1)S(1)} %get-tuple-element.28.refs_1_.refs_3_.refs_2_, ...), custom_call_target="tpu_custom_call" | custom-call | flops 4294967296 | bytes 1048576 | tf_op jit(solution)/shard_map/beside_rest/pallas_call | solution.py:326
  60.2 0.3 scalars.1.scalars_ref
  60.5 0.0 collective-permute-done.12
  60.5 0.0 collective-permute-done.13
  60.5 0.0 collective-permute-done.14
  60.6 0.1 collective-permute-start.15
  60.7 1.3 %collective-permute-start.16 = (f32[8,128]{1,0:T(8,128)S(1)}, f32[8,128]{1,0:T(8,128)S(1)}, u32[]{:S(2)}, u32[]{:S(2)}) collective-permute-start(f32[8,128]{1,0:T(8,128)S(1)} %add_add_fusion.1), channel_id=1, source_target_pairs={{0,2},{1,3},{2,0},{3,1},{4,6},{5,7},{6,4},{7,5},{8,10},{9,11},{10,... | collective-permute-start | bytes 12296 | tf_op jit(solution)/shard_map/ppermute | solution.py:52
  61.9 0.6 collective-permute-start.17
  62.5 1.7 %far_rest.1.total_ref = f32[8,1024]{1,0:T(8,128)S(1)} custom-call(s32[2]{0:T(128)S(1)} %fusion.refs_0_, f32[8,1024]{1,0:T(8,128)S(1)} %beside_rest.1.refs_1_, bf16[4,4,2048,256]{3,2,1,0:T(8,128)(2,1)S(1)} %get-tuple-element.43.refs_5_.refs_2_, f32[4,8,1024]{2,1,0:T(8,128)S(1)} %collective-permute-done.11.refs_13_.refs_6_.refs_3_), custom_call_target="tpu_custom_call" | custom-call | flops 4294967296 | bytes 1048576 | tf_op jit(solution)/shard_map/far_rest/pallas_call | solution.py:326
  64.2 0.0 collective-permute-done.15
  64.2 0.1 collective-permute-done.16
  64.3 0.6 collective-permute-done.17
  65.0 0.7 %last_update.1 = (f32[8,1024]{1,0:T(8,128)}, f32[8,1024]{1,0:T(8,128)}) custom-call(f32[4,8,128]{2,1,0:T(8,128)S(1)} %scalars.1.scalars_ref, f32[8,128]{1,0:T(8,128)S(1)} %add_add_fusion.form_ref, f32[8,1024]{1,0:T(8,128)S(1)} %far_rest.1.total_ref, f32[1,1024]{1,0:T(1,128)S(1)} %bitcast.15, ...), custom_call_target="tpu_custom_call" | custom-call | tf_op jit(solution)/shard_map/last_update/pallas_call | solution.py:428
  (8 shorter events, 0.1 us)
Async XLA Ops:
  1.4 10.4 %collective-permute-start = (f32[1,16,1024]{2,1,0:T(8,128)S(1)}, f32[1,16,1024]{2,1,0:T(8,128)S(1)}, u32[]{:S(2)}, u32[]{:S(2)}) collective-permute-start(f32[1,16,1024]{2,1,0:T(8,128)S(1)} %maximum_bitcast_fusion.refs_1_.refs_4_.refs_0_.mine_ref), channel_id=1, source_target_pairs={{0,12},{1,13},{2,14},{3,15},{4,0},{5,1},{6,2},{7,3},{8,4},{9,5},{1... | collective-permute-start | bytes 196616 | tf_op jit(solution)/shard_map/ppermute | solution.py:59
  6.5 6.5 %collective-permute-start.1 = (f32[1,16,1024]{2,1,0:T(8,128)S(1)}, f32[1,16,1024]{2,1,0:T(8,128)S(1)}, u32[]{:S(2)}, u32[]{:S(2)}) collective-permute-start(f32[1,16,1024]{2,1,0:T(8,128)S(1)} %maximum_bitcast_fusion.refs_1_.refs_4_.refs_0_.mine_ref), channel_id=1, source_target_pairs={{0,8},{1,9},{2,10},{3,11},{4,12},{5,13},{6,14},{7,15},{8,0},{9,1},... | collective-permute-start | bytes 196616 | tf_op jit(solution)/shard_map/ppermute | solution.py:59
  6.5 6.5 %collective-permute-start.2 = (f32[1,16,1024]{2,1,0:T(8,128)S(1)}, f32[1,16,1024]{2,1,0:T(8,128)S(1)}, u32[]{:S(2)}, u32[]{:S(2)}) collective-permute-start(f32[1,16,1024]{2,1,0:T(8,128)S(1)} %maximum_bitcast_fusion.refs_1_.refs_4_.refs_0_.mine_ref), channel_id=1, source_target_pairs={{0,4},{1,5},{2,6},{3,7},{4,8},{5,9},{6,10},{7,11},{8,12},{9,13},{1... | collective-permute-start | bytes 196616 | tf_op jit(solution)/shard_map/ppermute | solution.py:59
  9.8 2.0 %copy-start.1 = (bf16[1,4,2048,256]{3,2,1,0:T(8,128)(2,1)}, bf16[1,4,2048,256]{3,2,1,0:T(8,128)(2,1)S(1)}, u32[]{:S(2)}) copy-start(bf16[1,4,2048,256]{3,2,1,0:T(8,128)(2,1)S(1)} %get-tuple-element.41.refs_0_) | copy-start | bytes 12582916
  13.0 5.5 %collective-permute-start.3 = (f32[4,16,1024]{2,1,0:T(8,128)S(1)}, f32[4,16,1024]{2,1,0:T(8,128)S(1)}, u32[]{:S(2)}, u32[]{:S(2)}) collective-permute-start(f32[4,16,1024]{2,1,0:T(8,128)S(1)} %pad_maximum_fusion), channel_id=1, source_target_pairs={{0,1},{1,0},{2,3},{3,2},{4,5},{5,4},{6,7},{7,6},{8,9},{9,8},{10,11... | collective-permute-start | bytes 786440 | tf_op jit(solution)/shard_map/ppermute | solution.py:52
  13.0 10.4 %collective-permute-start.4 = (f32[4,16,1024]{2,1,0:T(8,128)S(1)}, f32[4,16,1024]{2,1,0:T(8,128)S(1)}, u32[]{:S(2)}, u32[]{:S(2)}) collective-permute-start(f32[4,16,1024]{2,1,0:T(8,128)S(1)} %pad_maximum_fusion), channel_id=1, source_target_pairs={{0,2},{1,3},{2,0},{3,1},{4,6},{5,7},{6,4},{7,5},{8,10},{9,11},{10,... | collective-permute-start | bytes 786440 | tf_op jit(solution)/shard_map/ppermute | solution.py:52
  23.4 5.4 %copy-start = (f32[1024]{0:T(1024)S(1)}, f32[1024]{0:T(1024)}, u32[]{:S(2)}) copy-start(f32[1024]{0:T(1024)} %param.6) | copy-start | bytes 12292
  23.5 5.4 %collective-permute-start.5 = (f32[4,16,1024]{2,1,0:T(8,128)S(1)}, f32[4,16,1024]{2,1,0:T(8,128)S(1)}, u32[]{:S(2)}, u32[]{:S(2)}) collective-permute-start(f32[4,16,1024]{2,1,0:T(8,128)S(1)} %collective-permute-done.4.refs_3_.refs_5_), channel_id=1, source_target_pairs={{0,1},{1,0},{2,3},{3,2},{4,5},{5,4},{6,7},{7,6},{8,9},{9,8},{10,11... | collective-permute-start | bytes 786440 | tf_op jit(solution)/shard_map/ppermute | solution.py:52
  28.8 8.8 %copy-start.2 = (bf16[1,4,2048,256]{3,2,1,0:T(8,128)(2,1)S(1)}, bf16[1,4,2048,256]{3,2,1,0:T(8,128)(2,1)}, u32[]{:S(2)}) copy-start(bf16[1,4,2048,256]{3,2,1,0:T(8,128)(2,1)} %copy-done.1) | copy-start | bytes 12582916
  33.8 4.5 %collective-permute-start.6 = (f32[1,8,1024]{2,1,0:T(8,128)S(1)}, f32[1,8,1024]{2,1,0:T(8,128)S(1)}, u32[]{:S(2)}, u32[]{:S(2)}) collective-permute-start(f32[1,8,1024]{2,1,0:T(8,128)S(1)} %bitcast.5), channel_id=1, source_target_pairs={{0,12},{1,13},{2,14},{3,15},{4,0},{5,1},{6,2},{7,3},{8,4},{9,5},{1... | collective-permute-start | bytes 98312 | tf_op jit(solution)/shard_map/ppermute | solution.py:59
  35.7 4.8 %collective-permute-start.7 = (f32[1,8,1024]{2,1,0:T(8,128)S(1)}, f32[1,8,1024]{2,1,0:T(8,128)S(1)}, u32[]{:S(2)}, u32[]{:S(2)}) collective-permute-start(f32[1,8,1024]{2,1,0:T(8,128)S(1)} %bitcast.6), channel_id=1, source_target_pairs={{0,8},{1,9},{2,10},{3,11},{4,12},{5,13},{6,14},{7,15},{8,0},{9,1},... | collective-permute-start | bytes 98312 | tf_op jit(solution)/shard_map/ppermute | solution.py:59
  36.7 5.7 %collective-permute-start.8 = (f32[1,8,1024]{2,1,0:T(8,128)S(1)}, f32[1,8,1024]{2,1,0:T(8,128)S(1)}, u32[]{:S(2)}, u32[]{:S(2)}) collective-permute-start(f32[1,8,1024]{2,1,0:T(8,128)S(1)} %bitcast.7), channel_id=1, source_target_pairs={{0,4},{1,5},{2,6},{3,7},{4,8},{5,9},{6,10},{7,11},{8,12},{9,13},{1... | collective-permute-start | bytes 98312 | tf_op jit(solution)/shard_map/ppermute | solution.py:59
  42.4 2.4 %collective-permute-start.9 = (f32[4,8,1024]{2,1,0:T(8,128)S(1)}, f32[4,8,1024]{2,1,0:T(8,128)S(1)}, u32[]{:S(2)}, u32[]{:S(2)}) collective-permute-start(f32[4,8,1024]{2,1,0:T(8,128)S(1)} %pad_maximum_fusion.1), channel_id=1, source_target_pairs={{0,1},{1,0},{2,3},{3,2},{4,5},{5,4},{6,7},{7,6},{8,9},{9,8},{10,11... | collective-permute-start | bytes 393224 | tf_op jit(solution)/shard_map/ppermute | solution.py:52
  42.5 5.9 %collective-permute-start.10 = (f32[4,8,1024]{2,1,0:T(8,128)S(1)}, f32[4,8,1024]{2,1,0:T(8,128)S(1)}, u32[]{:S(2)}, u32[]{:S(2)}) collective-permute-start(f32[4,8,1024]{2,1,0:T(8,128)S(1)} %pad_maximum_fusion.1), channel_id=1, source_target_pairs={{0,2},{1,3},{2,0},{3,1},{4,6},{5,7},{6,4},{7,5},{8,10},{9,11},{10,... | collective-permute-start | bytes 393224 | tf_op jit(solution)/shard_map/ppermute | solution.py:52
  48.4 2.3 %collective-permute-start.11 = (f32[4,8,1024]{2,1,0:T(8,128)S(1)}, f32[4,8,1024]{2,1,0:T(8,128)S(1)}, u32[]{:S(2)}, u32[]{:S(2)}) collective-permute-start(f32[4,8,1024]{2,1,0:T(8,128)S(1)} %collective-permute-done.10.refs_12_.refs_5_), channel_id=1, source_target_pairs={{0,1},{1,0},{2,3},{3,2},{4,5},{5,4},{6,7},{7,6},{8,9},{9,8},{10,11... | collective-permute-start | bytes 393224 | tf_op jit(solution)/shard_map/ppermute | solution.py:52
  52.6 8.0 %collective-permute-start.12 = (f32[8,128]{1,0:T(8,128)S(1)}, f32[8,128]{1,0:T(8,128)S(1)}, u32[]{:S(2)}, u32[]{:S(2)}) collective-permute-start(f32[8,128]{1,0:T(8,128)S(1)} %get-tuple-element.44), channel_id=1, source_target_pairs={{0,12},{1,13},{2,14},{3,15},{4,0},{5,1},{6,2},{7,3},{8,4},{9,5},{1... | collective-permute-start | bytes 12296 | tf_op jit(solution)/shard_map/ppermute | solution.py:59
  53.0 7.5 %collective-permute-start.13 = (f32[8,128]{1,0:T(8,128)S(1)}, f32[8,128]{1,0:T(8,128)S(1)}, u32[]{:S(2)}, u32[]{:S(2)}) collective-permute-start(f32[8,128]{1,0:T(8,128)S(1)} %get-tuple-element.44), channel_id=1, source_target_pairs={{0,8},{1,9},{2,10},{3,11},{4,12},{5,13},{6,14},{7,15},{8,0},{9,1},... | collective-permute-start | bytes 12296 | tf_op jit(solution)/shard_map/ppermute | solution.py:59
  53.2 7.4 %collective-permute-start.14 = (f32[8,128]{1,0:T(8,128)S(1)}, f32[8,128]{1,0:T(8,128)S(1)}, u32[]{:S(2)}, u32[]{:S(2)}) collective-permute-start(f32[8,128]{1,0:T(8,128)S(1)} %get-tuple-element.44), channel_id=1, source_target_pairs={{0,4},{1,5},{2,6},{3,7},{4,8},{5,9},{6,10},{7,11},{8,12},{9,13},{1... | collective-permute-start | bytes 12296 | tf_op jit(solution)/shard_map/ppermute | solution.py:59
  60.6 3.7 %collective-permute-start.15 = (f32[8,128]{1,0:T(8,128)S(1)}, f32[8,128]{1,0:T(8,128)S(1)}, u32[]{:S(2)}, u32[]{:S(2)}) collective-permute-start(f32[8,128]{1,0:T(8,128)S(1)} %add_add_fusion.1), channel_id=1, source_target_pairs={{0,1},{1,0},{2,3},{3,2},{4,5},{5,4},{6,7},{7,6},{8,9},{9,8},{10,11... | collective-permute-start | bytes 12296 | tf_op jit(solution)/shard_map/ppermute | solution.py:52
  60.7 3.7 %collective-permute-start.16 = (f32[8,128]{1,0:T(8,128)S(1)}, f32[8,128]{1,0:T(8,128)S(1)}, u32[]{:S(2)}, u32[]{:S(2)}) collective-permute-start(f32[8,128]{1,0:T(8,128)S(1)} %add_add_fusion.1), channel_id=1, source_target_pairs={{0,2},{1,3},{2,0},{3,1},{4,6},{5,7},{6,4},{7,5},{8,10},{9,11},{10,... | collective-permute-start | bytes 12296 | tf_op jit(solution)/shard_map/ppermute | solution.py:52
  61.9 3.0 %collective-permute-start.17 = (f32[8,128]{1,0:T(8,128)S(1)}, f32[8,128]{1,0:T(8,128)S(1)}, u32[]{:S(2)}, u32[]{:S(2)}) collective-permute-start(f32[8,128]{1,0:T(8,128)S(1)} %add_add_fusion.1), channel_id=1, source_target_pairs={{0,3},{1,2},{2,1},{3,0},{4,7},{5,6},{6,5},{7,4},{8,11},{9,10},{10,... | collective-permute-start | bytes 12296 | tf_op jit(solution)/shard_map/ppermute | solution.py:52

commit v12 on v11

--- a/solution.py
+++ b/solution.py
@@ -67,14 +67,20 @@
     return chips // near, near
 
 
-def gathered(value):
+def gathered(value, at_once):
     far, near = digits()
-    own = value[None]
-    line = [turned(own, by) for by in range(1, far)]
-    group = jnp.concatenate([own] + line, axis=0)
+    step = 2 * near
+    if at_once:
+        lines = [[step * z + k for z in range(far)] for k in range(step)]
+        group = lax.all_gather(value, "row", axis_index_groups=lines)
+        group = jnp.concatenate([group, group[:-1]], axis=0)
+        group = lax.dynamic_slice_in_dim(group, lax.axis_index("row") // step, far, 0)
+    else:
+        own = value[None]
+        group = jnp.concatenate([own] + [turned(own, by) for by in range(1, far)], axis=0)
     across = swapped(group, 0, 0, 1)
     beside = [swapped(group, 0, by, 0) for by in range(1, near)]
-    return [[own], line, [across], beside]
+    return [[value[None]], [group], [across], beside]
 
 
 def held_back(groups, value):
@@ -109,7 +115,8 @@
             jnp.concatenate([one(k, core) for k in range(near - 1)]),
         ]
 
-    return listed(0), listed(1)
+    others = 1 + jnp.arange(far - 1, dtype=jnp.int32)
+    return others, listed(0), listed(1)
 
 
 def add_block(yt_ref, at, own_ref, dirs_ref, slot, acc_ref, keep_ref=None, kept_at=None):
@@ -164,14 +171,16 @@
         base += ref.shape[0]
 
 
-def over_points(nfeat, nstacks, first, amplitude, kept, *refs):
-    scale_ref, *refs = refs
+def over_points(nfeat, nstacks, first, amplitude, kept, table, *refs):
+    refs = list(refs)
+    table_ref = refs.pop(0) if table else None
+    scale_ref = refs.pop(0)
     own_ref = refs.pop(0) if not first else None
     sofar_ref = refs.pop(0) if not first else None
     noise_ref, mine_ref = (refs.pop(0), refs.pop(0)) if amplitude else (None, None)
     stacks = refs[:nstacks]
     refs = refs[nstacks:]
-    blocks = sum(ref.shape[0] for ref in stacks)
+    blocks = table_ref.shape[0] if table else sum(ref.shape[0] for ref in stacks)
     if first:
         own_ref = refs.pop(0)
         own_ref[...] = exponent_rows(
@@ -193,7 +202,10 @@
             yt_ref[b - kept] = rows.T.astype(BF16)
             add_block(yt_ref, b - kept, own_ref, dirs_ref, b, acc_ref)
 
-    each(stacks, step)
+    if table:
+        repeated(blocks, lambda s: step(s, stacks[0][table_ref[s]]))
+    else:
+        each(stacks, step)
     total = folded(acc_ref)
     if not first:
         total = total + sofar_ref[...]
@@ -202,7 +214,7 @@
     out_ref[...] = total
 
 
-def over_images(nstacks, table, sofar, form, amplitude, kept, blocks, *refs):
+def over_images(nstacks, table, line, sofar, form, amplitude, kept, blocks, *refs):
     refs = list(refs)
     table_ref = refs.pop(0) if table else None
     sofar_ref = refs.pop(0) if sofar else None
@@ -222,7 +234,14 @@
         else:
             add_block(yt_ref, at - kept, own_ref, dirs_ref, slot, acc_ref)
 
-    if table:
+    if line:
+
+        def other(s):
+            put_dirs(dirs_ref, s, stacks[0][table_ref[s]])
+            add(s, s, bool(kept) and s < kept)
+
+        repeated(blocks, other)
+    elif table:
         if nstacks > 1:
             each(stacks, lambda b, value: put_dirs(dirs_ref, b, value))
 
@@ -338,11 +357,13 @@
     def amount(stacks):
         return sum(s.shape[0] for s in stacks)
 
-    groups = gathered(jnp.concatenate([features, rhs], axis=0))
+    groups = gathered(jnp.concatenate([features, rhs], axis=0), False)
     mine = groups[0][0]
     own_shape = jax.ShapeDtypeStruct((DEPTH, width), BF16)
     room = KEPT_ROOM - lax.axis_size("row") * 512 * width
+    others, halves, rests = tables()
     sizes = [amount(g) for g in groups]
+    sizes[1] -= 1
     sizes.append(sizes[3])
     keep = [0] * len(sizes)
     for k in KEPT_ORDER:
@@ -363,23 +384,24 @@
             made += (jax.ShapeDtypeStruct((blocks - keep[k], width, DEPTH), BF16),)
         made = call(
             functools.partial(
-                over_points, nfeat, len(stacks), k == 0, amplitude if final else None, keep[k]
+                over_points, nfeat, len(stacks), k == 0, amplitude if final else None, keep[k],
+                k == 1,
             ),
             blocks, blocks, made,
-            (scale,) + (() if k == 0 else (own, total)) + ((noise, mine) if final else ())
+            ((others,) if k == 1 else ()) + (scale,) + (() if k == 0 else (own, total)) + ((noise, mine) if final else ())
             + tuple(stacks),
-            "blocks_%d" % k, fresh=keep[k],
+            "blocks_%d" % k, k == 1, fresh=keep[k],
         )
         if k == 0:
             own, *made = made
         total, *sources = made
         prepared.append(sources)
-    images = gathered(total)
+    images = gathered(total, True)
     image = images[0][0]
 
     def again(group, out, name, sofar=(), table=None, form=()):
         stacks = images[group]
-        blocks = amount(stacks)
+        blocks = sizes[group]
         listed = () if table is None else (table,)
         work = blocks if table is None else table.shape[0]
         sources = list(prepared[group])
@@ -389,17 +411,16 @@
             sources.insert(len(sources) - 1, own)
         return call(
             functools.partial(
-                over_images, len(stacks), table is not None, bool(sofar), bool(form), amplitude,
-                keep[group], blocks,
+                over_images, len(stacks), table is not None, group == 1, bool(sofar), bool(form),
+                amplitude, keep[group], blocks,
             ),
             blocks, work, out,
             listed + tuple(sofar) + tuple(form) + tuple(sources) + tuple(stacks),
             name, table is not None,
         )
 
-    halves, rests = tables()
     once = again(0, field, "own_again")
-    once = again(1, field, "line_again", sofar=(once,))
+    once = again(1, field, "line_again", sofar=(once,), table=others)
     half = again(2, field, "across_half", table=halves[0])
     images, half = held_back(images, half)
     half = again(3, field, "beside_half", sofar=(half,), table=halves[1])
@@ -415,8 +436,8 @@
     total = again(4, field, "far_rest", sofar=(total,), table=rests[2])
     *parts, total = lax.optimization_barrier((*parts, total))
     form = sum(parts, form)
-    flat = [s for g in groups for s in g]
-    flat_images = [s for g in images for s in g]
+    flat = [s for g in groups[1:] for s in g]
+    flat_images = [s for g in images[1:] for s in g]
     scalars = pl.pallas_call(
         functools.partial(scalars_kernel, nfeat, len(flat)),
         out_shape=jax.ShapeDtypeStruct((4, nrhs, 128), F32),

time: 65.9 us -> 75 us (1.14)
  blocking collectives: 0 us -> 13.6 us
  waiting for transfers between devices: 6.45 us -> 2.14 us
  starting transfers between devices: 16.5 us -> 15.1 us
  Pallas kernels: 38.4 us -> 39.6 us
    all_gather x0 -> x1, blocking collectives: none -> 13.6 us  [gathered(): group = lax.all_gather(value, 'row', axis_index_groups=lines)]
    ppermute x9 -> x6, waiting for transfers between devices: 5.24 us -> 1.1 us  [turned(): lax.ppermute(value, 'row', [(i, (i - by * step) % length) for i in range(...]
    ppermute x9 -> x6, starting transfers between devices: 12.1 us -> 10.5 us  [turned(): lax.ppermute(value, 'row', [(i, (i - by * step) % length) for i in range(...]
    pallas_call x13, Pallas kernels: 37.3 us -> 38.5 us  [call(): pl.pallas_call(kernel, out_shape=out_shape, in_specs=[smem if table and k...]
  transfers between devices with their start and end apart: 18 -> 15, of which waited for: 6 -> 3; matrix products, arithmetic and copies ran while one was open for 1% -> 1% of each run, Pallas kernels for 47% -> 43%
where the time goes in v12:
time: 75 us; the launch traced here: 74.8 us
  Pallas kernels  39.6 us (53%)
  starting transfers between devices  15.1 us (20%)
  blocking collectives  13.6 us (18%)
  local copies, waits for them, and re-layouts  2.72 us (4%)
  waiting for transfers between devices  2.14 us (3%)
  other arithmetic  0.87 us (1%)
  between operations  0.76 us (1%)
    pallas_call x13, Pallas kernels, call(): pl.pallas_call(kernel, out_shape=out_shape, in_specs=[smem if table and k...  38.5 us
    all_gather x1, blocking collectives, gathered(): group = lax.all_gather(value, 'row', axis_index_groups=lines)  13.6 us
    ppermute x6, starting transfers between devices, turned(): lax.ppermute(value, 'row', [(i, (i - by * step) % length) for i in range(...  10.5 us
    ppermute x9, starting transfers between devices, swapped(): return lax.ppermute(value, 'row', [(i, i ^ by) for i in range(length)])  4.65 us
    unnamed x6, local copies, waits for them, and re-layouts  1.98 us
  transfers between devices with their start and end apart: 15, of which 3 were waited for; matrix products, arithmetic and copies ran while one was open for 1% of the time, Pallas kernels for 43%

profile of v12, /device:TPU:0, one launch (start us, length us, event | category | flops | bytes accessed | tf_op | source)
XLA Modules:
  0.0 74.8 jit_solution(8222973459224007491)
XLA Ops:
  0.6 0.8 %maximum_bitcast_fusion.refs_1_.refs_4_.mine_ref = f32[1,16,1024]{2,1,0:T(8,128)S(1)} fusion(f32[8,1024]{1,0:T(8,128)} %param.7, f32[8,1024]{1,0:T(8,128)} %param.4), kind=kLoop, calls=%fused_computation.5 | loop fusion | flops 16384 | bytes 131072 | tf_op jit(solution)/shard_map/broadcast_in_dim | solution.py:79
  1.4 5.0 %collective-permute-start = (f32[1,16,1024]{2,1,0:T(8,128)S(1)}, f32[1,16,1024]{2,1,0:T(8,128)S(1)}, u32[]{:S(2)}, u32[]{:S(2)}) collective-permute-start(f32[1,16,1024]{2,1,0:T(8,128)S(1)} %maximum_bitcast_fusion.refs_1_.refs_4_.mine_ref), channel_id=1, source_target_pairs={{0,12},{1,13},{2,14},{3,15},{4,0},{5,1},{6,2},{7,3},{8,4},{9,5},{1... | collective-permute-start | bytes 196616 | tf_op jit(solution)/shard_map/ppermute | solution.py:59
  6.5 0.0 collective-permute-start.1
  6.5 1.0 %collective-permute-start.2 = (f32[1,16,1024]{2,1,0:T(8,128)S(1)}, f32[1,16,1024]{2,1,0:T(8,128)S(1)}, u32[]{:S(2)}, u32[]{:S(2)}) collective-permute-start(f32[1,16,1024]{2,1,0:T(8,128)S(1)} %maximum_bitcast_fusion.refs_1_.refs_4_.mine_ref), channel_id=1, source_target_pairs={{0,4},{1,5},{2,6},{3,7},{4,8},{5,9},{6,10},{7,11},{8,12},{9,13},{1... | collective-permute-start | bytes 196616 | tf_op jit(solution)/shard_map/ppermute | solution.py:59
  7.5 0.7 copy.8.refs_0_.refs_1_
  8.2 1.6 %blocks_0.1 = (bf16[64,1024]{1,0:T(8,128)(2,1)S(1)}, f32[8,1024]{1,0:T(8,128)S(1)}, bf16[1,4,2048,256]{3,2,1,0:T(8,128)(2,1)S(1)}) custom-call(f32[8,1]{1,0:T(8,128)S(1)} %copy.8.refs_0_.refs_1_, f32[1,16,1024]{2,1,0:T(8,128)S(1)} %maximum_bitcast_fusion.refs_1_.refs_4_.mine_ref), custom_call_target="tpu_custom_call" | custom-call | flops 2147483648 | bytes 1048576 | tf_op jit(solution)/shard_map/blocks_0/pallas_call | solution.py:345
  9.8 0.0 copy-start.1
  9.8 1.9 %copy-done.1 = bf16[1,4,2048,256]{3,2,1,0:T(8,128)(2,1)} copy-done((bf16[1,4,2048,256]{3,2,1,0:T(8,128)(2,1)}, bf16[1,4,2048,256]{3,2,1,0:T(8,128)(2,1)S(1)}, u32[]{:S(2)}) %copy-start.1) | copy-done | bytes 4194328
  11.8 0.0 collective-permute-done
  11.8 1.1 %collective-permute-done.1 = f32[1,16,1024]{2,1,0:T(8,128)S(1)} collective-permute-done((f32[1,16,1024]{2,1,0:T(8,128)S(1)}, f32[1,16,1024]{2,1,0:T(8,128)S(1)}, u32[]{:S(2)}, u32[]{:S(2)}) %collective-permute-start.1) | collective-permute-done | bytes 65568 | tf_op jit(solution)/shard_map/ppermute | solution.py:59
  12.9 0.0 collective-permute-done.2
  13.0 0.1 collective-permute-start.3
  13.0 1.6 %collective-permute-start.4 = (f32[4,16,1024]{2,1,0:T(8,128)S(1)}, f32[4,16,1024]{2,1,0:T(8,128)S(1)}, u32[]{:S(2)}, u32[]{:S(2)}) collective-permute-start(f32[4,16,1024]{2,1,0:T(8,128)S(1)} %pad_maximum_fusion.refs_4_.refs_0_), channel_id=1, source_target_pairs={{0,2},{1,3},{2,0},{3,1},{4,6},{5,7},{6,4},{7,5},{8,10},{9,11},{10,... | collective-permute-start | bytes 786440 | tf_op jit(solution)/shard_map/ppermute | solution.py:52
  14.6 4.4 %blocks_1.1 = (f32[8,1024]{1,0:T(8,128)S(1)}, bf16[3,4,2048,256]{3,2,1,0:T(8,128)(2,1)S(1)}) custom-call(s32[3]{0:T(128)S(1)} %iota_add_fusion.refs_0_, f32[8,1]{1,0:T(8,128)S(1)} %copy.8.refs_0_.refs_1_, bf16[64,1024]{1,0:T(8,128)(2,1)S(1)} %get-tuple-element.28.refs_2_.refs_1_.refs_3_, f32[8,1024]{1,0:T(8,128)S(1)} %get-tuple-element.29.refs_3_, ...), custom_call_target="tpu_custom_call" | custom-call | flops 6442450944 | bytes 1048576 | tf_op jit(solution)/shard_map/blocks_1/pallas_call | solution.py:345
  19.0 0.0 collective-permute-done.3.refs_3_.refs_1_
  19.0 5.0 %blocks_2.1 = (f32[8,1024]{1,0:T(8,128)S(1)}, bf16[4,1024,64]{2,1,0:T(8,128)(2,1)S(1)}) custom-call(f32[8,1]{1,0:T(8,128)S(1)} %copy.8.refs_0_.refs_1_, bf16[64,1024]{1,0:T(8,128)(2,1)S(1)} %get-tuple-element.28.refs_2_.refs_1_.refs_3_, f32[8,1024]{1,0:T(8,128)S(1)} %get-tuple-element.30.refs_2_, f32[4,16,1024]{2,1,0:T(8,128)S(1)} %collective-permute-done.3.refs_3_.refs_1_), custom_call_target="tpu_custom_call" | custom-call | flops 8589934592 | bytes 1048576 | tf_op jit(solution)/shard_map/blocks_2/pallas_call | solution.py:345
  24.0 0.0 collective-permute-done.4.refs_3_.refs_2_
  24.0 0.0 copy-start
  24.1 0.2 collective-permute-start.5
  24.3 5.1 %blocks_3.1 = (f32[8,1024]{1,0:T(8,128)S(1)}, bf16[2,4,2048,256]{3,2,1,0:T(8,128)(2,1)S(1)}, bf16[2,1024,64]{2,1,0:T(8,128)(2,1)S(1)}) custom-call(f32[8,1]{1,0:T(8,128)S(1)} %copy.8.refs_0_.refs_1_, bf16[64,1024]{1,0:T(8,128)(2,1)S(1)} %get-tuple-element.28.refs_2_.refs_1_.refs_3_, f32[8,1024]{1,0:T(8,128)S(1)} %get-tuple-element.33.refs_2_, ...), custom_call_target="tpu_custom_call" | custom-call | flops 8589934592 | bytes 1048576 | tf_op jit(solution)/shard_map/blocks_3/pallas_call | solution.py:345
  29.4 0.0 collective-permute-done.5.refs_5_.refs_3_
  29.4 0.0 copy-done
  29.5 0.0 copy-start.2
  29.5 5.0 %blocks_4.1 = (f32[8,1024]{1,0:T(8,128)S(1)}, bf16[4,4,2048,256]{3,2,1,0:T(8,128)(2,1)S(1)}) custom-call(f32[8,1]{1,0:T(8,128)S(1)} %copy.8.refs_0_.refs_1_, bf16[64,1024]{1,0:T(8,128)(2,1)S(1)} %get-tuple-element.28.refs_2_.refs_1_.refs_3_, f32[8,1024]{1,0:T(8,128)S(1)} %get-tuple-element.34.refs_2_, f32[1,1024]{1,0:T(1,128)S(1)} %bitcast.11, ...), custom_call_target="tpu_custom_call" | custom-call | flops 8589934592 | bytes 1048576 | tf_op jit(solution)/shard_map/blocks_4/pallas_call | solution.py:345
  34.4 13.6 %all-gather = f32[32,1024]{1,0:T(8,128)S(1)} all-gather(f32[8,1024]{1,0:T(8,128)S(1)} %get-tuple-element.35), channel_id=2, replica_groups={{0,4,8,12},{1,5,9,13},{2,6,10,14},{3,7,11,15},{16,20,24,28},{17,21,25,2..., dimensions={0}, use_global_device_ids=true | all-gather | bytes 163840 | tf_op jit(solution)/shard_map/all_gather | solution.py:75
  48.0 0.1 collective-permute-start.6
  48.1 0.6 collective-permute-start.7
  48.7 0.0 copy-done.2
  48.7 0.6 own_again.1.refs_1_
  49.3 2.3 %line_again.1.refs_2_ = f32[8,1024]{1,0:T(8,128)S(1)} custom-call(s32[3]{0:T(128)S(1)} %iota_add_fusion.refs_0_, f32[8,1024]{1,0:T(8,128)S(1)} %own_again.1.refs_1_, bf16[3,4,2048,256]{3,2,1,0:T(8,128)(2,1)S(1)} %get-tuple-element.42.refs_2_, f32[4,8,1024]{2,1,0:T(8,128)S(1)} %fusion.refs_4_.refs_3_), custom_call_target="tpu_custom_call" | custom-call | flops 6442450944 | bytes 1048576 | tf_op jit(solution)/shard_map/line_again/pallas_call | solution.py:345
  51.6 0.0 collective-permute-done.6.refs_3_.refs_5_.refs_4_
  51.6 3.1 %across_half.1.refs_1_ = f32[8,1024]{1,0:T(8,128)S(1)} custom-call(s32[2]{0:T(128)S(1)} %fusion.4.refs_0_, bf16[64,1024]{1,0:T(8,128)(2,1)S(1)} %get-tuple-element.28.refs_2_.refs_1_.refs_3_, bf16[4,1024,64]{2,1,0:T(8,128)(2,1)S(1)} %get-tuple-element.36.refs_2_.refs_3_, f32[4,8,1024]{2,1,0:T(8,128)S(1)} %collective-permute-done.6.refs_3_.refs_5_.refs_4_), custom_call_target="tpu_custom_call" | custom-call | flops 4294967296 | bytes 1048576 | tf_op jit(solution)/shard_map/across_half/pallas_call | solution.py:345
  54.7 0.0 collective-permute-done.7.refs_6_.refs_5_
  54.7 0.2 collective-permute-start.8
  54.9 2.3 %beside_half.1.refs_1_ = f32[8,1024]{1,0:T(8,128)S(1)} custom-call(s32[2]{0:T(128)S(1)} %fusion.3.refs_0_, f32[8,1024]{1,0:T(8,128)S(1)} %across_half.1.refs_1_, bf16[2,4,2048,256]{3,2,1,0:T(8,128)(2,1)S(1)} %get-tuple-element.39.refs_2_, bf16[64,1024]{1,0:T(8,128)(2,1)S(1)} %get-tuple-element.28.refs_2_.refs_1_.refs_3_, ...), custom_call_target="tpu_custom_call" | custom-call | flops 4294967296 | bytes 1048576 | tf_op jit(solution)/shard_map/beside_half/pallas_call | solution.py:345
  57.3 0.0 collective-permute-done.8.refs_7_.refs_6_.refs_3_
  57.3 1.8 %far_half.1 = (f32[8,1024]{1,0:T(8,128)S(1)}, f32[8,128]{1,0:T(8,128)S(1)}) custom-call(s32[2]{0:T(128)S(1)} %fusion.4.refs_0_, f32[8,1024]{1,0:T(8,128)S(1)} %beside_half.1.refs_1_, f32[8,1024]{1,0:T(8,128)S(1)} %line_again.1.refs_2_, f32[1,1024]{1,0:T(1,128)S(1)} %bitcast.12, f32[1,8,1024]{2,1,0:T(8,128)S(1)} %bitcast.9, ...), custom_call_target="tpu_custom_call" | custom-call | flops 4294967296 | bytes 1048576 | tf_op jit(solution)/shard_map/far_half/pallas_call | solution.py:345
  59.1 0.6 collective-permute-start.10
  59.7 1.9 %collective-permute-start.11 = (f32[8,128]{1,0:T(8,128)S(1)}, f32[8,128]{1,0:T(8,128)S(1)}, u32[]{:S(2)}, u32[]{:S(2)}) collective-permute-start(f32[8,128]{1,0:T(8,128)S(1)} %get-tuple-element.44), channel_id=1, source_target_pairs={{0,4},{1,5},{2,6},{3,7},{4,8},{5,9},{6,10},{7,11},{8,12},{9,13},{1... | collective-permute-start | bytes 12296 | tf_op jit(solution)/shard_map/ppermute | solution.py:59
  61.6 1.9 %collective-permute-start.9 = (f32[8,128]{1,0:T(8,128)S(1)}, f32[8,128]{1,0:T(8,128)S(1)}, u32[]{:S(2)}, u32[]{:S(2)}) collective-permute-start(f32[8,128]{1,0:T(8,128)S(1)} %get-tuple-element.44), channel_id=1, source_target_pairs={{0,12},{1,13},{2,14},{3,15},{4,0},{5,1},{6,2},{7,3},{8,4},{9,5},{1... | collective-permute-start | bytes 12296 | tf_op jit(solution)/shard_map/ppermute | solution.py:59
  63.5 3.1 %across_rest.1.refs_1_ = f32[8,1024]{1,0:T(8,128)S(1)} custom-call(s32[2]{0:T(128)S(1)} %fusion.1.refs_0_, f32[8,1024]{1,0:T(8,128)S(1)} %get-tuple-element.45.refs_1_, bf16[64,1024]{1,0:T(8,128)(2,1)S(1)} %get-tuple-element.28.refs_2_.refs_1_.refs_3_, bf16[4,1024,64]{2,1,0:T(8,128)(2,1)S(1)} %get-tuple-element.36.refs_2_.refs_3_, ...), custom_call_target="tpu_custom_call" | custom-call | flops 4294967296 | bytes 1048576 | tf_op jit(solution)/shard_map/across_rest/pallas_call | solution.py:345
  66.6 2.3 %beside_rest.1.refs_1_ = f32[8,1024]{1,0:T(8,128)S(1)} custom-call(s32[2]{0:T(128)S(1)} %fusion.2.refs_0_, f32[8,1024]{1,0:T(8,128)S(1)} %across_rest.1.refs_1_, bf16[2,4,2048,256]{3,2,1,0:T(8,128)(2,1)S(1)} %get-tuple-element.39.refs_2_, bf16[64,1024]{1,0:T(8,128)(2,1)S(1)} %get-tuple-element.28.refs_2_.refs_1_.refs_3_, ...), custom_call_target="tpu_custom_call" | custom-call | flops 4294967296 | bytes 1048576 | tf_op jit(solution)/shard_map/beside_rest/pallas_call | solution.py:345
  69.0 0.4 scalars.1.scalars_ref
  69.3 0.0 collective-permute-done.10
  69.3 0.0 collective-permute-done.11
  69.3 0.0 collective-permute-done.9
  69.4 0.1 collective-permute-start.12
  69.4 1.6 %collective-permute-start.13 = (f32[8,128]{1,0:T(8,128)S(1)}, f32[8,128]{1,0:T(8,128)S(1)}, u32[]{:S(2)}, u32[]{:S(2)}) collective-permute-start(f32[8,128]{1,0:T(8,128)S(1)} %add_add_fusion.1), channel_id=1, source_target_pairs={{0,2},{1,3},{2,0},{3,1},{4,6},{5,7},{6,4},{7,5},{8,10},{9,11},{10,... | collective-permute-start | bytes 12296 | tf_op jit(solution)/shard_map/ppermute | solution.py:52
  71.0 0.3 collective-permute-start.14
  71.3 1.7 %far_rest.1.total_ref = f32[8,1024]{1,0:T(8,128)S(1)} custom-call(s32[2]{0:T(128)S(1)} %fusion.1.refs_0_, f32[8,1024]{1,0:T(8,128)S(1)} %beside_rest.1.refs_1_, bf16[4,4,2048,256]{3,2,1,0:T(8,128)(2,1)S(1)} %get-tuple-element.43.refs_5_.refs_2_, f32[4,8,1024]{2,1,0:T(8,128)S(1)} %collective-permute-done.8.refs_7_.refs_6_.refs_3_), custom_call_target="tpu_custom_call" | custom-call | flops 4294967296 | bytes 1048576 | tf_op jit(solution)/shard_map/far_rest/pallas_call | solution.py:345
  73.0 0.0 collective-permute-done.12
  73.0 0.1 collective-permute-done.13
  73.1 0.9 %collective-permute-done.14 = f32[8,128]{1,0:T(8,128)S(1)} collective-permute-done((f32[8,128]{1,0:T(8,128)S(1)}, f32[8,128]{1,0:T(8,128)S(1)}, u32[]{:S(2)}, u32[]{:S(2)}) %collective-permute-start.14) | collective-permute-done | bytes 4128 | tf_op jit(solution)/shard_map/ppermute | solution.py:52
  74.1 0.7 last_update.1
  (10 shorter events, 0.1 us)
Async XLA Ops:
  1.4 10.4 %collective-permute-start = (f32[1,16,1024]{2,1,0:T(8,128)S(1)}, f32[1,16,1024]{2,1,0:T(8,128)S(1)}, u32[]{:S(2)}, u32[]{:S(2)}) collective-permute-start(f32[1,16,1024]{2,1,0:T(8,128)S(1)} %maximum_bitcast_fusion.refs_1_.refs_4_.mine_ref), channel_id=1, source_target_pairs={{0,12},{1,13},{2,14},{3,15},{4,0},{5,1},{6,2},{7,3},{8,4},{9,5},{1... | collective-permute-start | bytes 196616 | tf_op jit(solution)/shard_map/ppermute | solution.py:59
  6.5 6.5 %collective-permute-start.1 = (f32[1,16,1024]{2,1,0:T(8,128)S(1)}, f32[1,16,1024]{2,1,0:T(8,128)S(1)}, u32[]{:S(2)}, u32[]{:S(2)}) collective-permute-start(f32[1,16,1024]{2,1,0:T(8,128)S(1)} %maximum_bitcast_fusion.refs_1_.refs_4_.mine_ref), channel_id=1, source_target_pairs={{0,8},{1,9},{2,10},{3,11},{4,12},{5,13},{6,14},{7,15},{8,0},{9,1},... | collective-permute-start | bytes 196616 | tf_op jit(solution)/shard_map/ppermute | solution.py:59
  6.5 6.5 %collective-permute-start.2 = (f32[1,16,1024]{2,1,0:T(8,128)S(1)}, f32[1,16,1024]{2,1,0:T(8,128)S(1)}, u32[]{:S(2)}, u32[]{:S(2)}) collective-permute-start(f32[1,16,1024]{2,1,0:T(8,128)S(1)} %maximum_bitcast_fusion.refs_1_.refs_4_.mine_ref), channel_id=1, source_target_pairs={{0,4},{1,5},{2,6},{3,7},{4,8},{5,9},{6,10},{7,11},{8,12},{9,13},{1... | collective-permute-start | bytes 196616 | tf_op jit(solution)/shard_map/ppermute | solution.py:59
  9.8 2.0 %copy-start.1 = (bf16[1,4,2048,256]{3,2,1,0:T(8,128)(2,1)}, bf16[1,4,2048,256]{3,2,1,0:T(8,128)(2,1)S(1)}, u32[]{:S(2)}) copy-start(bf16[1,4,2048,256]{3,2,1,0:T(8,128)(2,1)S(1)} %get-tuple-element.41.refs_0_) | copy-start | bytes 12582916
  13.0 6.1 %collective-permute-start.3 = (f32[4,16,1024]{2,1,0:T(8,128)S(1)}, f32[4,16,1024]{2,1,0:T(8,128)S(1)}, u32[]{:S(2)}, u32[]{:S(2)}) collective-permute-start(f32[4,16,1024]{2,1,0:T(8,128)S(1)} %pad_maximum_fusion.refs_4_.refs_0_), channel_id=1, source_target_pairs={{0,1},{1,0},{2,3},{3,2},{4,5},{5,4},{6,7},{7,6},{8,9},{9,8},{10,11... | collective-permute-start | bytes 786440 | tf_op jit(solution)/shard_map/ppermute | solution.py:52
  13.0 11.0 %collective-permute-start.4 = (f32[4,16,1024]{2,1,0:T(8,128)S(1)}, f32[4,16,1024]{2,1,0:T(8,128)S(1)}, u32[]{:S(2)}, u32[]{:S(2)}) collective-permute-start(f32[4,16,1024]{2,1,0:T(8,128)S(1)} %pad_maximum_fusion.refs_4_.refs_0_), channel_id=1, source_target_pairs={{0,2},{1,3},{2,0},{3,1},{4,6},{5,7},{6,4},{7,5},{8,10},{9,11},{10,... | collective-permute-start | bytes 786440 | tf_op jit(solution)/shard_map/ppermute | solution.py:52
  24.0 5.4 %copy-start = (f32[1024]{0:T(1024)S(1)}, f32[1024]{0:T(1024)}, u32[]{:S(2)}) copy-start(f32[1024]{0:T(1024)} %param.6) | copy-start | bytes 12292
  24.1 5.4 %collective-permute-start.5 = (f32[4,16,1024]{2,1,0:T(8,128)S(1)}, f32[4,16,1024]{2,1,0:T(8,128)S(1)}, u32[]{:S(2)}, u32[]{:S(2)}) collective-permute-start(f32[4,16,1024]{2,1,0:T(8,128)S(1)} %collective-permute-done.4.refs_3_.refs_2_), channel_id=1, source_target_pairs={{0,1},{1,0},{2,3},{3,2},{4,5},{5,4},{6,7},{7,6},{8,9},{9,8},{10,11... | collective-permute-start | bytes 786440 | tf_op jit(solution)/shard_map/ppermute | solution.py:52
  29.5 19.2 %copy-start.2 = (bf16[1,4,2048,256]{3,2,1,0:T(8,128)(2,1)S(1)}, bf16[1,4,2048,256]{3,2,1,0:T(8,128)(2,1)}, u32[]{:S(2)}) copy-start(bf16[1,4,2048,256]{3,2,1,0:T(8,128)(2,1)} %copy-done.1) | copy-start | bytes 12582916
  48.0 3.6 %collective-permute-start.6 = (f32[4,8,1024]{2,1,0:T(8,128)S(1)}, f32[4,8,1024]{2,1,0:T(8,128)S(1)}, u32[]{:S(2)}, u32[]{:S(2)}) collective-permute-start(f32[4,8,1024]{2,1,0:T(8,128)S(1)} %fusion.refs_4_.refs_3_), channel_id=1, source_target_pairs={{0,1},{1,0},{2,3},{3,2},{4,5},{5,4},{6,7},{7,6},{8,9},{9,8},{10,11... | collective-permute-start | bytes 393224 | tf_op jit(solution)/shard_map/ppermute | solution.py:52
  48.1 6.6 %collective-permute-start.7 = (f32[4,8,1024]{2,1,0:T(8,128)S(1)}, f32[4,8,1024]{2,1,0:T(8,128)S(1)}, u32[]{:S(2)}, u32[]{:S(2)}) collective-permute-start(f32[4,8,1024]{2,1,0:T(8,128)S(1)} %fusion.refs_4_.refs_3_), channel_id=1, source_target_pairs={{0,2},{1,3},{2,0},{3,1},{4,6},{5,7},{6,4},{7,5},{8,10},{9,11},{10,... | collective-permute-start | bytes 393224 | tf_op jit(solution)/shard_map/ppermute | solution.py:52
  54.7 2.5 %collective-permute-start.8 = (f32[4,8,1024]{2,1,0:T(8,128)S(1)}, f32[4,8,1024]{2,1,0:T(8,128)S(1)}, u32[]{:S(2)}, u32[]{:S(2)}) collective-permute-start(f32[4,8,1024]{2,1,0:T(8,128)S(1)} %collective-permute-done.7.refs_6_.refs_5_), channel_id=1, source_target_pairs={{0,1},{1,0},{2,3},{3,2},{4,5},{5,4},{6,7},{7,6},{8,9},{9,8},{10,11... | collective-permute-start | bytes 393224 | tf_op jit(solution)/shard_map/ppermute | solution.py:52
  59.1 10.2 %collective-permute-start.10 = (f32[8,128]{1,0:T(8,128)S(1)}, f32[8,128]{1,0:T(8,128)S(1)}, u32[]{:S(2)}, u32[]{:S(2)}) collective-permute-start(f32[8,128]{1,0:T(8,128)S(1)} %get-tuple-element.44), channel_id=1, source_target_pairs={{0,8},{1,9},{2,10},{3,11},{4,12},{5,13},{6,14},{7,15},{8,0},{9,1},... | collective-permute-start | bytes 12296 | tf_op jit(solution)/shard_map/ppermute | solution.py:59
  59.7 9.6 %collective-permute-start.11 = (f32[8,128]{1,0:T(8,128)S(1)}, f32[8,128]{1,0:T(8,128)S(1)}, u32[]{:S(2)}, u32[]{:S(2)}) collective-permute-start(f32[8,128]{1,0:T(8,128)S(1)} %get-tuple-element.44), channel_id=1, source_target_pairs={{0,4},{1,5},{2,6},{3,7},{4,8},{5,9},{6,10},{7,11},{8,12},{9,13},{1... | collective-permute-start | bytes 12296 | tf_op jit(solution)/shard_map/ppermute | solution.py:59
  61.6 7.7 %collective-permute-start.9 = (f32[8,128]{1,0:T(8,128)S(1)}, f32[8,128]{1,0:T(8,128)S(1)}, u32[]{:S(2)}, u32[]{:S(2)}) collective-permute-start(f32[8,128]{1,0:T(8,128)S(1)} %get-tuple-element.44), channel_id=1, source_target_pairs={{0,12},{1,13},{2,14},{3,15},{4,0},{5,1},{6,2},{7,3},{8,4},{9,5},{1... | collective-permute-start | bytes 12296 | tf_op jit(solution)/shard_map/ppermute | solution.py:59
  69.4 3.7 %collective-permute-start.12 = (f32[8,128]{1,0:T(8,128)S(1)}, f32[8,128]{1,0:T(8,128)S(1)}, u32[]{:S(2)}, u32[]{:S(2)}) collective-permute-start(f32[8,128]{1,0:T(8,128)S(1)} %add_add_fusion.1), channel_id=1, source_target_pairs={{0,1},{1,0},{2,3},{3,2},{4,5},{5,4},{6,7},{7,6},{8,9},{9,8},{10,11... | collective-permute-start | bytes 12296 | tf_op jit(solution)/shard_map/ppermute | solution.py:52
  69.4 3.7 %collective-permute-start.13 = (f32[8,128]{1,0:T(8,128)S(1)}, f32[8,128]{1,0:T(8,128)S(1)}, u32[]{:S(2)}, u32[]{:S(2)}) collective-permute-start(f32[8,128]{1,0:T(8,128)S(1)} %add_add_fusion.1), channel_id=1, source_target_pairs={{0,2},{1,3},{2,0},{3,1},{4,6},{5,7},{6,4},{7,5},{8,10},{9,11},{10,... | collective-permute-start | bytes 12296 | tf_op jit(solution)/shard_map/ppermute | solution.py:52
  71.0 3.0 %collective-permute-start.14 = (f32[8,128]{1,0:T(8,128)S(1)}, f32[8,128]{1,0:T(8,128)S(1)}, u32[]{:S(2)}, u32[]{:S(2)}) collective-permute-start(f32[8,128]{1,0:T(8,128)S(1)} %add_add_fusion.1), channel_id=1, source_target_pairs={{0,3},{1,2},{2,1},{3,0},{4,7},{5,6},{6,5},{7,4},{8,11},{9,10},{10,... | collective-permute-start | bytes 12296 | tf_op jit(solution)/shard_map/ppermute | solution.py:52

commit v13 on v11

--- a/solution.py
+++ b/solution.py
@@ -12,8 +12,8 @@
 DEPTH = 64
 TILE = 256
 MIB = 1024 * 1024
-KEPT_ORDER = (0, 1, 4, 3, 2)
-KEPT_ROOM = 52 * MIB
+KEPT_ORDER = (1, 4, 3)
+KEPT_ROOM = 44 * MIB
 F32 = jnp.float32
 BF16 = jnp.bfloat16
 
@@ -165,7 +165,7 @@
 
 
 def over_points(nfeat, nstacks, first, amplitude, kept, *refs):
-    scale_ref, *refs = refs
+    refs = list(refs)
     own_ref = refs.pop(0) if not first else None
     sofar_ref = refs.pop(0) if not first else None
     noise_ref, mine_ref = (refs.pop(0), refs.pop(0)) if amplitude else (None, None)
@@ -175,7 +175,7 @@
     if first:
         own_ref = refs.pop(0)
         own_ref[...] = exponent_rows(
-            stacks[0][0, 0:nfeat, :] / scale_ref[...], 1.0, False
+            stacks[0][0, 0:nfeat, :], 1.0, False
         ).astype(BF16)
     out_ref = refs.pop(0)
     keep_ref = refs.pop(0) if kept else None
@@ -184,7 +184,7 @@
     acc_ref[...] = jnp.zeros_like(acc_ref)
 
     def step(b, value):
-        rows = exponent_rows(value[0:nfeat, :] / scale_ref[...], LOG2E, True)
+        rows = exponent_rows(value[0:nfeat, :], LOG2E, True)
         put_dirs(dirs_ref, b, value[nfeat:, :])
         if kept and b < kept:
             fresh[0][b] = rows.T.astype(BF16)
@@ -307,7 +307,7 @@
     nfeat, width = features.shape
     nrhs = rhs.shape[0]
     amplitude = 1.0 / math.sqrt(width * lax.axis_size("row"))
-    scale = lengthscale[:, None]
+    scaled = features / lengthscale[:, None]
     noise = noise[None, :]
     field = jax.ShapeDtypeStruct((nrhs, width), F32)
     small = jax.ShapeDtypeStruct((nrhs, 128), F32)
@@ -338,7 +338,7 @@
     def amount(stacks):
         return sum(s.shape[0] for s in stacks)
 
-    groups = gathered(jnp.concatenate([features, rhs], axis=0))
+    groups = gathered(jnp.concatenate([scaled, rhs], axis=0))
     mine = groups[0][0]
     own_shape = jax.ShapeDtypeStruct((DEPTH, width), BF16)
     room = KEPT_ROOM - lax.axis_size("row") * 512 * width
@@ -366,7 +366,7 @@
                 over_points, nfeat, len(stacks), k == 0, amplitude if final else None, keep[k]
             ),
             blocks, blocks, made,
-            (scale,) + (() if k == 0 else (own, total)) + ((noise, mine) if final else ())
+            (() if k == 0 else (own, total)) + ((noise, mine) if final else ())
             + tuple(stacks),
             "blocks_%d" % k, fresh=keep[k],
         )

time: 65.9 us -> 66.4 us (level)
  local copies, waits for them, and re-layouts: 2.71 us -> 0.03 us
  starting transfers between devices: 16.5 us -> 17.5 us
  waiting for transfers between devices: 6.45 us -> 7.39 us
  other arithmetic: 0.84 us -> 1.67 us
    unnamed x6 -> x2, local copies, waits for them, and re-layouts: 1.98 us -> 0.03 us
    ppermute x9, starting transfers between devices: 12.1 us -> 13 us  [turned(): lax.ppermute(value, 'row', [(i, (i - by * step) % length) for i in range(...]
    ppermute x9, waiting for transfers between devices: 5.24 us -> 6.18 us  [turned(): lax.ppermute(value, 'row', [(i, (i - by * step) % length) for i in range(...]
    div x0 -> x1, other arithmetic: none -> 0.83 us  [shards(): scaled = features / lengthscale[:, None]]
    broadcast_in_dim x1 -> x0, local copies, waits for them, and re-layouts: 0.73 us -> none  [shards(): scale = lengthscale[:, None]]
  transfers between devices with their start and end apart: 18 -> 18, of which waited for: 6 -> 6; matrix products, arithmetic and copies ran while one was open for 1% -> 0% of each run, Pallas kernels for 47% -> 47%
where the time goes in v13:
time: 66.4 us; the launch traced here: 66.2 us
  Pallas kernels  38.8 us (58%)
  starting transfers between devices  17.5 us (26%)
  waiting for transfers between devices  7.39 us (11%)
  other arithmetic  1.67 us (3%)
  between operations  0.76 us (1%)
    pallas_call x13, Pallas kernels, call(): pl.pallas_call(kernel, out_shape=out_shape, in_specs=[smem if table and k...  37.8 us
    ppermute x9, starting transfers between devices, turned(): lax.ppermute(value, 'row', [(i, (i - by * step) % length) for i in range(...  13 us
    ppermute x9, waiting for transfers between devices, turned(): lax.ppermute(value, 'row', [(i, (i - by * step) % length) for i in range(...  6.18 us
    ppermute x9, starting transfers between devices, swapped(): return lax.ppermute(value, 'row', [(i, i ^ by) for i in range(length)])  4.46 us
  transfers between devices with their start and end apart: 18, of which 6 were waited for; matrix products, arithmetic and copies ran while one was open for 0% of the time, Pallas kernels for 47%

profile of v13, /device:TPU:0, one launch (start us, length us, event | category | flops | bytes accessed | tf_op | source)
XLA Modules:
  0.0 66.2 jit_solution(14429949238045613879)
XLA Ops:
  0.6 0.8 %broadcast_divide_fusion = f32[8,1024]{1,0:T(8,128)S(1)} fusion(f32[8,1024]{1,0:T(8,128)} %param.4, f32[8]{0:T(128)} %param.5), kind=kLoop, calls=%fused_computation.3 | loop fusion | flops 8192 | bytes 65568 | tf_op jit(solution)/shard_map/div | solution.py:310
  1.5 0.8 %maximum_bitcast_fusion.refs_0_.refs_3_.mine_ref = f32[1,16,1024]{2,1,0:T(8,128)S(1)} fusion(f32[8,1024]{1,0:T(8,128)} %param.7, f32[8,1024]{1,0:T(8,128)S(1)} %broadcast_divide_fusion), kind=kLoop, calls=%fused_computation.2 | loop fusion | flops 16384 | bytes 131072 | tf_op jit(solution)/shard_map/broadcast_in_dim | solution.py:72
  2.2 5.0 %collective-permute-start = (f32[1,16,1024]{2,1,0:T(8,128)S(1)}, f32[1,16,1024]{2,1,0:T(8,128)S(1)}, u32[]{:S(2)}, u32[]{:S(2)}) collective-permute-start(f32[1,16,1024]{2,1,0:T(8,128)S(1)} %maximum_bitcast_fusion.refs_0_.refs_3_.mine_ref), channel_id=1, source_target_pairs={{0,12},{1,13},{2,14},{3,15},{4,0},{5,1},{6,2},{7,3},{8,4},{9,5},{1... | collective-permute-start | bytes 196616 | tf_op jit(solution)/shard_map/ppermute | solution.py:59
  7.3 0.0 collective-permute-start.1
  7.3 1.0 %collective-permute-start.2 = (f32[1,16,1024]{2,1,0:T(8,128)S(1)}, f32[1,16,1024]{2,1,0:T(8,128)S(1)}, u32[]{:S(2)}, u32[]{:S(2)}) collective-permute-start(f32[1,16,1024]{2,1,0:T(8,128)S(1)} %maximum_bitcast_fusion.refs_0_.refs_3_.mine_ref), channel_id=1, source_target_pairs={{0,4},{1,5},{2,6},{3,7},{4,8},{5,9},{6,10},{7,11},{8,12},{9,13},{1... | collective-permute-start | bytes 196616 | tf_op jit(solution)/shard_map/ppermute | solution.py:59
  8.3 1.6 %blocks_0.1 = (bf16[64,1024]{1,0:T(8,128)(2,1)S(1)}, f32[8,1024]{1,0:T(8,128)S(1)}, bf16[1,1024,64]{2,1,0:T(8,128)(2,1)S(1)}) custom-call(f32[1,16,1024]{2,1,0:T(8,128)S(1)} %maximum_bitcast_fusion.refs_0_.refs_3_.mine_ref), custom_call_target="tpu_custom_call" | custom-call | flops 2147483648 | bytes 1048576 | tf_op jit(solution)/shard_map/blocks_0/pallas_call | solution.py:326
  9.9 0.0 collective-permute-done.refs_2_.refs_1_
  9.9 3.8 %collective-permute-done.1.refs_3_.refs_2_ = f32[1,16,1024]{2,1,0:T(8,128)S(1)} collective-permute-done((f32[1,16,1024]{2,1,0:T(8,128)S(1)}, f32[1,16,1024]{2,1,0:T(8,128)S(1)}, u32[]{:S(2)}, u32[]{:S(2)}) %collective-permute-start.1) | collective-permute-done | bytes 65568 | tf_op jit(solution)/shard_map/ppermute | solution.py:59
  13.8 0.0 collective-permute-done.2.refs_4_.refs_3_
  13.8 0.1 collective-permute-start.3
  13.9 1.6 %collective-permute-start.4 = (f32[4,16,1024]{2,1,0:T(8,128)S(1)}, f32[4,16,1024]{2,1,0:T(8,128)S(1)}, u32[]{:S(2)}, u32[]{:S(2)}) collective-permute-start(f32[4,16,1024]{2,1,0:T(8,128)S(1)} %pad_maximum_fusion), channel_id=1, source_target_pairs={{0,2},{1,3},{2,0},{3,1},{4,6},{5,7},{6,4},{7,5},{8,10},{9,11},{10,... | collective-permute-start | bytes 786440 | tf_op jit(solution)/shard_map/ppermute | solution.py:52
  15.4 3.7 %blocks_1.1 = (f32[8,1024]{1,0:T(8,128)S(1)}, bf16[3,4,2048,256]{3,2,1,0:T(8,128)(2,1)S(1)}) custom-call(bf16[64,1024]{1,0:T(8,128)(2,1)S(1)} %get-tuple-element.28.refs_0_.refs_1_.refs_3_.refs_2_, f32[8,1024]{1,0:T(8,128)S(1)} %get-tuple-element.29.refs_1_, f32[1,16,1024]{2,1,0:T(8,128)S(1)} %collective-permute-done.refs_2_.refs_1_, ...), custom_call_target="tpu_custom_call" | custom-call | flops 6442450944 | bytes 1048576 | tf_op jit(solution)/shard_map/blocks_1/pallas_call | solution.py:326
  19.2 0.0 collective-permute-done.3.refs_2_.refs_4_
  19.2 4.9 %blocks_2.1 = (f32[8,1024]{1,0:T(8,128)S(1)}, bf16[4,1024,64]{2,1,0:T(8,128)(2,1)S(1)}) custom-call(bf16[64,1024]{1,0:T(8,128)(2,1)S(1)} %get-tuple-element.28.refs_0_.refs_1_.refs_3_.refs_2_, f32[8,1024]{1,0:T(8,128)S(1)} %get-tuple-element.30.refs_1_, f32[4,16,1024]{2,1,0:T(8,128)S(1)} %collective-permute-done.3.refs_2_.refs_4_), custom_call_target="tpu_custom_call" | custom-call | flops 8589934592 | bytes 1048576 | tf_op jit(solution)/shard_map/blocks_2/pallas_call | solution.py:326
  24.1 0.0 collective-permute-done.4.refs_2_.refs_5_
  24.1 0.0 copy-start
  24.1 0.2 collective-permute-start.5
  24.4 5.1 %blocks_3.1 = (f32[8,1024]{1,0:T(8,128)S(1)}, bf16[2,4,2048,256]{3,2,1,0:T(8,128)(2,1)S(1)}, bf16[2,1024,64]{2,1,0:T(8,128)(2,1)S(1)}) custom-call(bf16[64,1024]{1,0:T(8,128)(2,1)S(1)} %get-tuple-element.28.refs_0_.refs_1_.refs_3_.refs_2_, f32[8,1024]{1,0:T(8,128)S(1)} %get-tuple-element.33.refs_1_, f32[4,16,1024]{2,1,0:T(8,128)S(1)} %collective-permute-done.4.refs_2_.refs_5_), custom_call_target="tpu_custom_call" | custom-call | flops 8589934592 | bytes 1048576 | tf_op jit(solution)/shard_map/blocks_3/pallas_call | solution.py:326
  29.4 0.0 collective-permute-done.5.refs_4_.refs_6_
  29.4 0.0 copy-done
  29.4 4.8 %blocks_4.1 = (f32[8,1024]{1,0:T(8,128)S(1)}, bf16[4,4,2048,256]{3,2,1,0:T(8,128)(2,1)S(1)}) custom-call(bf16[64,1024]{1,0:T(8,128)(2,1)S(1)} %get-tuple-element.28.refs_0_.refs_1_.refs_3_.refs_2_, f32[8,1024]{1,0:T(8,128)S(1)} %get-tuple-element.34.refs_1_, f32[1,1024]{1,0:T(1,128)S(1)} %bitcast.12, ...), custom_call_target="tpu_custom_call" | custom-call | flops 8589934592 | bytes 1048576 | tf_op jit(solution)/shard_map/blocks_4/pallas_call | solution.py:326
  34.3 1.9 %collective-permute-start.6 = (f32[1,8,1024]{2,1,0:T(8,128)S(1)}, f32[1,8,1024]{2,1,0:T(8,128)S(1)}, u32[]{:S(2)}, u32[]{:S(2)}) collective-permute-start(f32[1,8,1024]{2,1,0:T(8,128)S(1)} %bitcast.4), channel_id=1, source_target_pairs={{0,12},{1,13},{2,14},{3,15},{4,0},{5,1},{6,2},{7,3},{8,4},{9,5},{1... | collective-permute-start | bytes 98312 | tf_op jit(solution)/shard_map/ppermute | solution.py:59
  36.2 0.0 collective-permute-start.7
  36.2 1.9 %collective-permute-start.8 = (f32[1,8,1024]{2,1,0:T(8,128)S(1)}, f32[1,8,1024]{2,1,0:T(8,128)S(1)}, u32[]{:S(2)}, u32[]{:S(2)}) collective-permute-start(f32[1,8,1024]{2,1,0:T(8,128)S(1)} %bitcast.6), channel_id=1, source_target_pairs={{0,4},{1,5},{2,6},{3,7},{4,8},{5,9},{6,10},{7,11},{8,12},{9,13},{1... | collective-permute-start | bytes 98312 | tf_op jit(solution)/shard_map/ppermute | solution.py:59
  38.1 1.5 %own_again.1.refs_0_ = f32[8,1024]{1,0:T(8,128)S(1)} custom-call(bf16[64,1024]{1,0:T(8,128)(2,1)S(1)} %get-tuple-element.28.refs_0_.refs_1_.refs_3_.refs_2_, bf16[1,1024,64]{2,1,0:T(8,128)(2,1)S(1)} %get-tuple-element.41.refs_1_, f32[1,8,1024]{2,1,0:T(8,128)S(1)} %bitcast.7), custom_call_target="tpu_custom_call" | custom-call | flops 2147483648 | bytes 1048576 | tf_op jit(solution)/shard_map/own_again/pallas_call | solution.py:326
  39.6 0.0 collective-permute-done.6.refs_8_.refs_2_
  39.6 1.8 %collective-permute-done.7.refs_9_.refs_3_ = f32[1,8,1024]{2,1,0:T(8,128)S(1)} collective-permute-done((f32[1,8,1024]{2,1,0:T(8,128)S(1)}, f32[1,8,1024]{2,1,0:T(8,128)S(1)}, u32[]{:S(2)}, u32[]{:S(2)}) %collective-permute-start.7) | collective-permute-done | bytes 32800 | tf_op jit(solution)/shard_map/ppermute | solution.py:59
  41.4 0.6 collective-permute-done.8.refs_10_.refs_4_
  41.9 0.1 collective-permute-start.9
  42.0 0.6 collective-permute-start.10
  42.6 1.7 %line_again.1.refs_2_ = f32[8,1024]{1,0:T(8,128)S(1)} custom-call(f32[8,1024]{1,0:T(8,128)S(1)} %own_again.1.refs_0_, bf16[3,4,2048,256]{3,2,1,0:T(8,128)(2,1)S(1)} %get-tuple-element.42.refs_1_, f32[1,8,1024]{2,1,0:T(8,128)S(1)} %collective-permute-done.6.refs_8_.refs_2_, f32[1,8,1024]{2,1,0:T(8,128)S(1)} %collective-permute-done.7.refs_9_.refs_3_, ...), custom_call_target="tpu_custom_call" | custom-call | flops 6442450944 | bytes 1048576 | tf_op jit(solution)/shard_map/line_again/pallas_call | solution.py:326
  44.3 0.0 collective-permute-done.9.refs_3_.refs_11_.refs_4_
  44.3 3.1 %across_half.1.refs_1_ = f32[8,1024]{1,0:T(8,128)S(1)} custom-call(s32[2]{0:T(128)S(1)} %fusion.3.refs_0_, bf16[64,1024]{1,0:T(8,128)(2,1)S(1)} %get-tuple-element.28.refs_0_.refs_1_.refs_3_.refs_2_, bf16[4,1024,64]{2,1,0:T(8,128)(2,1)S(1)} %get-tuple-element.36.refs_2_.refs_3_, f32[4,8,1024]{2,1,0:T(8,128)S(1)} %collective-permute-done.9.refs_3_.refs_11_.refs_4_), custom_call_target="tpu_custom_call" | custom-call | flops 4294967296 | bytes 1048576 | tf_op jit(solution)/shard_map/across_half/pallas_call | solution.py:326
  47.4 0.5 collective-permute-done.10.refs_12_.refs_5_
  47.9 0.0 collective-permute-start.11
  47.9 2.3 %beside_half.1.refs_1_ = f32[8,1024]{1,0:T(8,128)S(1)} custom-call(s32[2]{0:T(128)S(1)} %fusion.2.refs_0_, f32[8,1024]{1,0:T(8,128)S(1)} %across_half.1.refs_1_, bf16[2,4,2048,256]{3,2,1,0:T(8,128)(2,1)S(1)} %get-tuple-element.39.refs_2_, bf16[64,1024]{1,0:T(8,128)(2,1)S(1)} %get-tuple-element.28.refs_0_.refs_1_.refs_3_.refs_2_, ...), custom_call_target="tpu_custom_call" | custom-call | flops 4294967296 | bytes 1048576 | tf_op jit(solution)/shard_map/beside_half/pallas_call | solution.py:326
  50.2 0.0 collective-permute-done.11.refs_13_.refs_6_.refs_3_
  50.3 1.8 %far_half.1 = (f32[8,1024]{1,0:T(8,128)S(1)}, f32[8,128]{1,0:T(8,128)S(1)}) custom-call(s32[2]{0:T(128)S(1)} %fusion.3.refs_0_, f32[8,1024]{1,0:T(8,128)S(1)} %beside_half.1.refs_1_, f32[8,1024]{1,0:T(8,128)S(1)} %line_again.1.refs_2_, f32[1,1024]{1,0:T(1,128)S(1)} %bitcast.13, f32[1,8,1024]{2,1,0:T(8,128)S(1)} %bitcast.9, ...), custom_call_target="tpu_custom_call" | custom-call | flops 4294967296 | bytes 1048576 | tf_op jit(solution)/shard_map/far_half/pallas_call | solution.py:326
  52.1 1.3 %collective-permute-start.12 = (f32[8,128]{1,0:T(8,128)S(1)}, f32[8,128]{1,0:T(8,128)S(1)}, u32[]{:S(2)}, u32[]{:S(2)}) collective-permute-start(f32[8,128]{1,0:T(8,128)S(1)} %get-tuple-element.44), channel_id=1, source_target_pairs={{0,12},{1,13},{2,14},{3,15},{4,0},{5,1},{6,2},{7,3},{8,4},{9,5},{1... | collective-permute-start | bytes 12296 | tf_op jit(solution)/shard_map/ppermute | solution.py:59
  53.4 0.3 collective-permute-start.13
  53.7 1.6 %collective-permute-start.14 = (f32[8,128]{1,0:T(8,128)S(1)}, f32[8,128]{1,0:T(8,128)S(1)}, u32[]{:S(2)}, u32[]{:S(2)}) collective-permute-start(f32[8,128]{1,0:T(8,128)S(1)} %get-tuple-element.44), channel_id=1, source_target_pairs={{0,4},{1,5},{2,6},{3,7},{4,8},{5,9},{6,10},{7,11},{8,12},{9,13},{1... | collective-permute-start | bytes 12296 | tf_op jit(solution)/shard_map/ppermute | solution.py:59
  55.2 3.1 %across_rest.1.refs_1_ = f32[8,1024]{1,0:T(8,128)S(1)} custom-call(s32[2]{0:T(128)S(1)} %fusion.refs_0_, f32[8,1024]{1,0:T(8,128)S(1)} %get-tuple-element.45.refs_1_, bf16[64,1024]{1,0:T(8,128)(2,1)S(1)} %get-tuple-element.28.refs_0_.refs_1_.refs_3_.refs_2_, bf16[4,1024,64]{2,1,0:T(8,128)(2,1)S(1)} %get-tuple-element.36.refs_2_.refs_3_, ...), custom_call_target="tpu_custom_call" | custom-call | flops 4294967296 | bytes 1048576 | tf_op jit(solution)/shard_map/across_rest/pallas_call | solution.py:326
  58.3 2.3 %beside_rest.1.refs_1_ = f32[8,1024]{1,0:T(8,128)S(1)} custom-call(s32[2]{0:T(128)S(1)} %fusion.1.refs_0_, f32[8,1024]{1,0:T(8,128)S(1)} %across_rest.1.refs_1_, bf16[2,4,2048,256]{3,2,1,0:T(8,128)(2,1)S(1)} %get-tuple-element.39.refs_2_, bf16[64,1024]{1,0:T(8,128)(2,1)S(1)} %get-tuple-element.28.refs_0_.refs_1_.refs_3_.refs_2_, ...), custom_call_target="tpu_custom_call" | custom-call | flops 4294967296 | bytes 1048576 | tf_op jit(solution)/shard_map/beside_rest/pallas_call | solution.py:326
  60.7 0.3 scalars.1.scalars_ref
  61.0 0.0 collective-permute-done.12
  61.0 0.0 collective-permute-done.13
  61.0 0.0 collective-permute-done.14
  61.1 0.1 collective-permute-start.15
  61.1 1.3 %collective-permute-start.16 = (f32[8,128]{1,0:T(8,128)S(1)}, f32[8,128]{1,0:T(8,128)S(1)}, u32[]{:S(2)}, u32[]{:S(2)}) collective-permute-start(f32[8,128]{1,0:T(8,128)S(1)} %add_add_fusion.1), channel_id=1, source_target_pairs={{0,2},{1,3},{2,0},{3,1},{4,6},{5,7},{6,4},{7,5},{8,10},{9,11},{10,... | collective-permute-start | bytes 12296 | tf_op jit(solution)/shard_map/ppermute | solution.py:52
  62.4 0.6 collective-permute-start.17
  63.0 1.7 %far_rest.1.total_ref = f32[8,1024]{1,0:T(8,128)S(1)} custom-call(s32[2]{0:T(128)S(1)} %fusion.refs_0_, f32[8,1024]{1,0:T(8,128)S(1)} %beside_rest.1.refs_1_, bf16[4,4,2048,256]{3,2,1,0:T(8,128)(2,1)S(1)} %get-tuple-element.43.refs_5_.refs_2_, f32[4,8,1024]{2,1,0:T(8,128)S(1)} %collective-permute-done.11.refs_13_.refs_6_.refs_3_), custom_call_target="tpu_custom_call" | custom-call | flops 4294967296 | bytes 1048576 | tf_op jit(solution)/shard_map/far_rest/pallas_call | solution.py:326
  64.7 0.0 collective-permute-done.15
  64.7 0.1 collective-permute-done.16
  64.8 0.6 collective-permute-done.17
  65.5 0.7 %last_update.1 = (f32[8,1024]{1,0:T(8,128)}, f32[8,1024]{1,0:T(8,128)}) custom-call(f32[4,8,128]{2,1,0:T(8,128)S(1)} %scalars.1.scalars_ref, f32[8,128]{1,0:T(8,128)S(1)} %add_add_fusion.form_ref, f32[8,1024]{1,0:T(8,128)S(1)} %far_rest.1.total_ref, f32[1,1024]{1,0:T(1,128)S(1)} %bitcast.14, f32[1,16,1024]{2,1,0:T(8,128)S(1)} %maximum_bitcast_fusion.refs_0_.refs_3_.mine_ref, ...), custom_call_target="tpu_custom_call" | custom-call | tf_op jit(solution)/shard_map/last_update/pallas_call | solution.py:428
  (8 shorter events, 0.1 us)
Async XLA Ops:
  2.2 7.7 %collective-permute-start = (f32[1,16,1024]{2,1,0:T(8,128)S(1)}, f32[1,16,1024]{2,1,0:T(8,128)S(1)}, u32[]{:S(2)}, u32[]{:S(2)}) collective-permute-start(f32[1,16,1024]{2,1,0:T(8,128)S(1)} %maximum_bitcast_fusion.refs_0_.refs_3_.mine_ref), channel_id=1, source_target_pairs={{0,12},{1,13},{2,14},{3,15},{4,0},{5,1},{6,2},{7,3},{8,4},{9,5},{1... | collective-permute-start | bytes 196616 | tf_op jit(solution)/shard_map/ppermute | solution.py:59
  7.3 6.5 %collective-permute-start.1 = (f32[1,16,1024]{2,1,0:T(8,128)S(1)}, f32[1,16,1024]{2,1,0:T(8,128)S(1)}, u32[]{:S(2)}, u32[]{:S(2)}) collective-permute-start(f32[1,16,1024]{2,1,0:T(8,128)S(1)} %maximum_bitcast_fusion.refs_0_.refs_3_.mine_ref), channel_id=1, source_target_pairs={{0,8},{1,9},{2,10},{3,11},{4,12},{5,13},{6,14},{7,15},{8,0},{9,1},... | collective-permute-start | bytes 196616 | tf_op jit(solution)/shard_map/ppermute | solution.py:59
  7.3 6.5 %collective-permute-start.2 = (f32[1,16,1024]{2,1,0:T(8,128)S(1)}, f32[1,16,1024]{2,1,0:T(8,128)S(1)}, u32[]{:S(2)}, u32[]{:S(2)}) collective-permute-start(f32[1,16,1024]{2,1,0:T(8,128)S(1)} %maximum_bitcast_fusion.refs_0_.refs_3_.mine_ref), channel_id=1, source_target_pairs={{0,4},{1,5},{2,6},{3,7},{4,8},{5,9},{6,10},{7,11},{8,12},{9,13},{1... | collective-permute-start | bytes 196616 | tf_op jit(solution)/shard_map/ppermute | solution.py:59
  13.8 5.4 %collective-permute-start.3 = (f32[4,16,1024]{2,1,0:T(8,128)S(1)}, f32[4,16,1024]{2,1,0:T(8,128)S(1)}, u32[]{:S(2)}, u32[]{:S(2)}) collective-permute-start(f32[4,16,1024]{2,1,0:T(8,128)S(1)} %pad_maximum_fusion), channel_id=1, source_target_pairs={{0,1},{1,0},{2,3},{3,2},{4,5},{5,4},{6,7},{7,6},{8,9},{9,8},{10,11... | collective-permute-start | bytes 786440 | tf_op jit(solution)/shard_map/ppermute | solution.py:52
  13.9 10.3 %collective-permute-start.4 = (f32[4,16,1024]{2,1,0:T(8,128)S(1)}, f32[4,16,1024]{2,1,0:T(8,128)S(1)}, u32[]{:S(2)}, u32[]{:S(2)}) collective-permute-start(f32[4,16,1024]{2,1,0:T(8,128)S(1)} %pad_maximum_fusion), channel_id=1, source_target_pairs={{0,2},{1,3},{2,0},{3,1},{4,6},{5,7},{6,4},{7,5},{8,10},{9,11},{10,... | collective-permute-start | bytes 786440 | tf_op jit(solution)/shard_map/ppermute | solution.py:52
  24.1 5.3 %copy-start = (f32[1024]{0:T(1024)S(1)}, f32[1024]{0:T(1024)}, u32[]{:S(2)}) copy-start(f32[1024]{0:T(1024)} %param.6) | copy-start | bytes 12292
  24.1 5.3 %collective-permute-start.5 = (f32[4,16,1024]{2,1,0:T(8,128)S(1)}, f32[4,16,1024]{2,1,0:T(8,128)S(1)}, u32[]{:S(2)}, u32[]{:S(2)}) collective-permute-start(f32[4,16,1024]{2,1,0:T(8,128)S(1)} %collective-permute-done.4.refs_2_.refs_5_), channel_id=1, source_target_pairs={{0,1},{1,0},{2,3},{3,2},{4,5},{5,4},{6,7},{7,6},{8,9},{9,8},{10,11... | collective-permute-start | bytes 786440 | tf_op jit(solution)/shard_map/ppermute | solution.py:52
  34.3 5.3 %collective-permute-start.6 = (f32[1,8,1024]{2,1,0:T(8,128)S(1)}, f32[1,8,1024]{2,1,0:T(8,128)S(1)}, u32[]{:S(2)}, u32[]{:S(2)}) collective-permute-start(f32[1,8,1024]{2,1,0:T(8,128)S(1)} %bitcast.4), channel_id=1, source_target_pairs={{0,12},{1,13},{2,14},{3,15},{4,0},{5,1},{6,2},{7,3},{8,4},{9,5},{1... | collective-permute-start | bytes 98312 | tf_op jit(solution)/shard_map/ppermute | solution.py:59
  36.2 5.2 %collective-permute-start.7 = (f32[1,8,1024]{2,1,0:T(8,128)S(1)}, f32[1,8,1024]{2,1,0:T(8,128)S(1)}, u32[]{:S(2)}, u32[]{:S(2)}) collective-permute-start(f32[1,8,1024]{2,1,0:T(8,128)S(1)} %bitcast.5), channel_id=1, source_target_pairs={{0,8},{1,9},{2,10},{3,11},{4,12},{5,13},{6,14},{7,15},{8,0},{9,1},... | collective-permute-start | bytes 98312 | tf_op jit(solution)/shard_map/ppermute | solution.py:59
  36.2 5.7 %collective-permute-start.8 = (f32[1,8,1024]{2,1,0:T(8,128)S(1)}, f32[1,8,1024]{2,1,0:T(8,128)S(1)}, u32[]{:S(2)}, u32[]{:S(2)}) collective-permute-start(f32[1,8,1024]{2,1,0:T(8,128)S(1)} %bitcast.6), channel_id=1, source_target_pairs={{0,4},{1,5},{2,6},{3,7},{4,8},{5,9},{6,10},{7,11},{8,12},{9,13},{1... | collective-permute-start | bytes 98312 | tf_op jit(solution)/shard_map/ppermute | solution.py:59
  41.9 2.4 %collective-permute-start.9 = (f32[4,8,1024]{2,1,0:T(8,128)S(1)}, f32[4,8,1024]{2,1,0:T(8,128)S(1)}, u32[]{:S(2)}, u32[]{:S(2)}) collective-permute-start(f32[4,8,1024]{2,1,0:T(8,128)S(1)} %pad_maximum_fusion.1), channel_id=1, source_target_pairs={{0,1},{1,0},{2,3},{3,2},{4,5},{5,4},{6,7},{7,6},{8,9},{9,8},{10,11... | collective-permute-start | bytes 393224 | tf_op jit(solution)/shard_map/ppermute | solution.py:52
  42.0 5.9 %collective-permute-start.10 = (f32[4,8,1024]{2,1,0:T(8,128)S(1)}, f32[4,8,1024]{2,1,0:T(8,128)S(1)}, u32[]{:S(2)}, u32[]{:S(2)}) collective-permute-start(f32[4,8,1024]{2,1,0:T(8,128)S(1)} %pad_maximum_fusion.1), channel_id=1, source_target_pairs={{0,2},{1,3},{2,0},{3,1},{4,6},{5,7},{6,4},{7,5},{8,10},{9,11},{10,... | collective-permute-start | bytes 393224 | tf_op jit(solution)/shard_map/ppermute | solution.py:52
  47.9 2.3 %collective-permute-start.11 = (f32[4,8,1024]{2,1,0:T(8,128)S(1)}, f32[4,8,1024]{2,1,0:T(8,128)S(1)}, u32[]{:S(2)}, u32[]{:S(2)}) collective-permute-start(f32[4,8,1024]{2,1,0:T(8,128)S(1)} %collective-permute-done.10.refs_12_.refs_5_), channel_id=1, source_target_pairs={{0,1},{1,0},{2,3},{3,2},{4,5},{5,4},{6,7},{7,6},{8,9},{9,8},{10,11... | collective-permute-start | bytes 393224 | tf_op jit(solution)/shard_map/ppermute | solution.py:52
  52.1 9.0 %collective-permute-start.12 = (f32[8,128]{1,0:T(8,128)S(1)}, f32[8,128]{1,0:T(8,128)S(1)}, u32[]{:S(2)}, u32[]{:S(2)}) collective-permute-start(f32[8,128]{1,0:T(8,128)S(1)} %get-tuple-element.44), channel_id=1, source_target_pairs={{0,12},{1,13},{2,14},{3,15},{4,0},{5,1},{6,2},{7,3},{8,4},{9,5},{1... | collective-permute-start | bytes 12296 | tf_op jit(solution)/shard_map/ppermute | solution.py:59
  53.4 7.7 %collective-permute-start.13 = (f32[8,128]{1,0:T(8,128)S(1)}, f32[8,128]{1,0:T(8,128)S(1)}, u32[]{:S(2)}, u32[]{:S(2)}) collective-permute-start(f32[8,128]{1,0:T(8,128)S(1)} %get-tuple-element.44), channel_id=1, source_target_pairs={{0,8},{1,9},{2,10},{3,11},{4,12},{5,13},{6,14},{7,15},{8,0},{9,1},... | collective-permute-start | bytes 12296 | tf_op jit(solution)/shard_map/ppermute | solution.py:59
  53.7 7.4 %collective-permute-start.14 = (f32[8,128]{1,0:T(8,128)S(1)}, f32[8,128]{1,0:T(8,128)S(1)}, u32[]{:S(2)}, u32[]{:S(2)}) collective-permute-start(f32[8,128]{1,0:T(8,128)S(1)} %get-tuple-element.44), channel_id=1, source_target_pairs={{0,4},{1,5},{2,6},{3,7},{4,8},{5,9},{6,10},{7,11},{8,12},{9,13},{1... | collective-permute-start | bytes 12296 | tf_op jit(solution)/shard_map/ppermute | solution.py:59
  61.1 3.7 %collective-permute-start.15 = (f32[8,128]{1,0:T(8,128)S(1)}, f32[8,128]{1,0:T(8,128)S(1)}, u32[]{:S(2)}, u32[]{:S(2)}) collective-permute-start(f32[8,128]{1,0:T(8,128)S(1)} %add_add_fusion.1), channel_id=1, source_target_pairs={{0,1},{1,0},{2,3},{3,2},{4,5},{5,4},{6,7},{7,6},{8,9},{9,8},{10,11... | collective-permute-start | bytes 12296 | tf_op jit(solution)/shard_map/ppermute | solution.py:52
  61.1 3.7 %collective-permute-start.16 = (f32[8,128]{1,0:T(8,128)S(1)}, f32[8,128]{1,0:T(8,128)S(1)}, u32[]{:S(2)}, u32[]{:S(2)}) collective-permute-start(f32[8,128]{1,0:T(8,128)S(1)} %add_add_fusion.1), channel_id=1, source_target_pairs={{0,2},{1,3},{2,0},{3,1},{4,6},{5,7},{6,4},{7,5},{8,10},{9,11},{10,... | collective-permute-start | bytes 12296 | tf_op jit(solution)/shard_map/ppermute | solution.py:52
  62.4 3.0 %collective-permute-start.17 = (f32[8,128]{1,0:T(8,128)S(1)}, f32[8,128]{1,0:T(8,128)S(1)}, u32[]{:S(2)}, u32[]{:S(2)}) collective-permute-start(f32[8,128]{1,0:T(8,128)S(1)} %add_add_fusion.1), channel_id=1, source_target_pairs={{0,3},{1,2},{2,1},{3,0},{4,7},{5,6},{6,5},{7,4},{8,11},{9,10},{10,... | collective-permute-start | bytes 12296 | tf_op jit(solution)/shard_map/ppermute | solution.py:52

commit v14 on v13

--- a/solution.py
+++ b/solution.py
@@ -162,6 +162,16 @@
     for ref in stacks:
         repeated(ref.shape[0], lambda b, ref=ref, base=base: function(base + b, ref[b]))
         base += ref.shape[0]
+
+
+def join_kernel(scale_ref, features_ref, rhs_ref, out_ref):
+    nfeat = features_ref.shape[0]
+    row = lax.broadcasted_iota(jnp.int32, (nfeat, 128), 0)
+    scale = jnp.zeros((nfeat, 128), F32)
+    for k in range(nfeat):
+        scale = jnp.where(row == k, scale_ref[k], scale)
+    out_ref[0:nfeat, :] = features_ref[...] / scale[:, 0:1]
+    out_ref[nfeat:, :] = rhs_ref[...]
 
 
 def over_points(nfeat, nstacks, first, amplitude, kept, *refs):
@@ -307,7 +317,6 @@
     nfeat, width = features.shape
     nrhs = rhs.shape[0]
     amplitude = 1.0 / math.sqrt(width * lax.axis_size("row"))
-    scaled = features / lengthscale[:, None]
     noise = noise[None, :]
     field = jax.ShapeDtypeStruct((nrhs, width), F32)
     small = jax.ShapeDtypeStruct((nrhs, 128), F32)
@@ -338,7 +347,14 @@
     def amount(stacks):
         return sum(s.shape[0] for s in stacks)
 
-    groups = gathered(jnp.concatenate([scaled, rhs], axis=0))
+    joined = pl.pallas_call(
+        join_kernel,
+        out_shape=jax.ShapeDtypeStruct((nfeat + nrhs, width), F32),
+        in_specs=[smem, vmem, vmem],
+        compiler_params=pltpu.CompilerParams(vmem_limit_bytes=4 * MIB),
+        name="join",
+    )(lengthscale, features, rhs)
+    groups = gathered(joined)
     mine = groups[0][0]
     own_shape = jax.ShapeDtypeStruct((DEPTH, width), BF16)
     room = KEPT_ROOM - lax.axis_size("row") * 512 * width

time: 66.4 us -> 67.6 us (1.018)
  local copies, waits for them, and re-layouts: 0.03 us -> 2.19 us
  other arithmetic: 1.67 us -> 0.07 us
    unnamed x2 -> x8, local copies, waits for them, and re-layouts: 0.03 us -> 2.19 us
    div x1 -> x0, other arithmetic: 0.83 us -> none  [shards(): scaled = features / lengthscale[:, None]]
    broadcast_in_dim x1 -> x0, other arithmetic: 0.77 us -> none  [gathered(): own = value[None]]
where the time goes in v14:
time: 67.6 us; the launch traced here: 67.4 us
  Pallas kernels  39.4 us (58%)
  starting transfers between devices  17.5 us (26%)
  waiting for transfers between devices  7.39 us (11%)
  local copies, waits for them, and re-layouts  2.19 us (3%)
  between operations  0.78 us (1%)
    pallas_call x13, Pallas kernels, call(): pl.pallas_call(kernel, out_shape=out_shape, in_specs=[smem if table and k...  37.8 us
    ppermute x9, starting transfers between devices, turned(): lax.ppermute(value, 'row', [(i, (i - by * step) % length) for i in range(...  13.1 us
    ppermute x9, waiting for transfers between devices, turned(): lax.ppermute(value, 'row', [(i, (i - by * step) % length) for i in range(...  6.18 us
    ppermute x9, starting transfers between devices, swapped(): return lax.ppermute(value, 'row', [(i, i ^ by) for i in range(length)])  4.47 us
    unnamed x8, local copies, waits for them, and re-layouts  2.19 us
  transfers between devices with their start and end apart: 18, of which 6 were waited for; matrix products, arithmetic and copies ran while one was open for 0% of the time, Pallas kernels for 47%

profile of v14, /device:TPU:0, one launch (start us, length us, event | category | flops | bytes accessed | tf_op | source)
XLA Modules:
  0.0 67.4 jit_solution(5688767747762027071)
XLA Ops:
  0.6 0.0 copy-start
  0.6 0.7 %copy-done = f32[8,1024]{1,0:T(8,128)S(1)} copy-done((f32[8,1024]{1,0:T(8,128)S(1)}, f32[8,1024]{1,0:T(8,128)}, u32[]{:S(2)}) %copy-start) | copy-done | bytes 32792
  1.4 0.0 copy-start.1
  1.4 0.8 %copy-done.1 = f32[8,1024]{1,0:T(8,128)S(1)} copy-done((f32[8,1024]{1,0:T(8,128)S(1)}, f32[8,1024]{1,0:T(8,128)}, u32[]{:S(2)}) %copy-start.1) | copy-done | bytes 32792
  2.1 0.0 copy-start.3
  2.1 0.7 copy-done.3
  2.8 0.6 join.1
  3.4 5.1 %collective-permute-start = (f32[1,16,1024]{2,1,0:T(8,128)S(1)}, f32[1,16,1024]{2,1,0:T(8,128)S(1)}, u32[]{:S(2)}, u32[]{:S(2)}) collective-permute-start(f32[1,16,1024]{2,1,0:T(8,128)S(1)} %bitcast.3), channel_id=1, source_target_pairs={{0,12},{1,13},{2,14},{3,15},{4,0},{5,1},{6,2},{7,3},{8,4},{9,5},{1... | collective-permute-start | bytes 196616 | tf_op jit(solution)/shard_map/ppermute | solution.py:59
  8.5 0.0 collective-permute-start.1
  8.5 1.0 %collective-permute-start.2 = (f32[1,16,1024]{2,1,0:T(8,128)S(1)}, f32[1,16,1024]{2,1,0:T(8,128)S(1)}, u32[]{:S(2)}, u32[]{:S(2)}) collective-permute-start(f32[1,16,1024]{2,1,0:T(8,128)S(1)} %bitcast.5), channel_id=1, source_target_pairs={{0,4},{1,5},{2,6},{3,7},{4,8},{5,9},{6,10},{7,11},{8,12},{9,13},{1... | collective-permute-start | bytes 196616 | tf_op jit(solution)/shard_map/ppermute | solution.py:59
  9.5 1.6 %blocks_0.1 = (bf16[64,1024]{1,0:T(8,128)(2,1)S(1)}, f32[8,1024]{1,0:T(8,128)S(1)}, bf16[1,1024,64]{2,1,0:T(8,128)(2,1)S(1)}) custom-call(f32[1,16,1024]{2,1,0:T(8,128)S(1)} %bitcast.6), custom_call_target="tpu_custom_call" | custom-call | flops 2147483648 | bytes 1048576 | tf_op jit(solution)/shard_map/blocks_0/pallas_call | solution.py:335
  11.1 0.0 collective-permute-done.refs_2_.refs_1_
  11.1 3.8 %collective-permute-done.1.refs_3_.refs_2_ = f32[1,16,1024]{2,1,0:T(8,128)S(1)} collective-permute-done((f32[1,16,1024]{2,1,0:T(8,128)S(1)}, f32[1,16,1024]{2,1,0:T(8,128)S(1)}, u32[]{:S(2)}, u32[]{:S(2)}) %collective-permute-start.1) | collective-permute-done | bytes 65568 | tf_op jit(solution)/shard_map/ppermute | solution.py:59
  14.9 0.0 collective-permute-done.2.refs_4_.refs_3_
  15.0 0.1 collective-permute-start.3
  15.0 1.6 %collective-permute-start.4 = (f32[4,16,1024]{2,1,0:T(8,128)S(1)}, f32[4,16,1024]{2,1,0:T(8,128)S(1)}, u32[]{:S(2)}, u32[]{:S(2)}) collective-permute-start(f32[4,16,1024]{2,1,0:T(8,128)S(1)} %pad_maximum_fusion), channel_id=1, source_target_pairs={{0,2},{1,3},{2,0},{3,1},{4,6},{5,7},{6,4},{7,5},{8,10},{9,11},{10,... | collective-permute-start | bytes 786440 | tf_op jit(solution)/shard_map/ppermute | solution.py:52
  16.6 3.7 %blocks_1.1 = (f32[8,1024]{1,0:T(8,128)S(1)}, bf16[3,4,2048,256]{3,2,1,0:T(8,128)(2,1)S(1)}) custom-call(bf16[64,1024]{1,0:T(8,128)(2,1)S(1)} %get-tuple-element.28.refs_0_.refs_1_.refs_3_.refs_2_, f32[8,1024]{1,0:T(8,128)S(1)} %get-tuple-element.29.refs_1_, f32[1,16,1024]{2,1,0:T(8,128)S(1)} %collective-permute-done.refs_2_.refs_1_, ...), custom_call_target="tpu_custom_call" | custom-call | flops 6442450944 | bytes 1048576 | tf_op jit(solution)/shard_map/blocks_1/pallas_call | solution.py:335
  20.4 0.0 collective-permute-done.3.refs_2_.refs_4_
  20.4 4.9 %blocks_2.1 = (f32[8,1024]{1,0:T(8,128)S(1)}, bf16[4,1024,64]{2,1,0:T(8,128)(2,1)S(1)}) custom-call(bf16[64,1024]{1,0:T(8,128)(2,1)S(1)} %get-tuple-element.28.refs_0_.refs_1_.refs_3_.refs_2_, f32[8,1024]{1,0:T(8,128)S(1)} %get-tuple-element.30.refs_1_, f32[4,16,1024]{2,1,0:T(8,128)S(1)} %collective-permute-done.3.refs_2_.refs_4_), custom_call_target="tpu_custom_call" | custom-call | flops 8589934592 | bytes 1048576 | tf_op jit(solution)/shard_map/blocks_2/pallas_call | solution.py:335
  25.3 0.0 collective-permute-done.4.refs_2_.refs_5_
  25.3 0.0 copy-start.2
  25.3 0.2 collective-permute-start.5
  25.5 5.1 %blocks_3.1 = (f32[8,1024]{1,0:T(8,128)S(1)}, bf16[2,4,2048,256]{3,2,1,0:T(8,128)(2,1)S(1)}, bf16[2,1024,64]{2,1,0:T(8,128)(2,1)S(1)}) custom-call(bf16[64,1024]{1,0:T(8,128)(2,1)S(1)} %get-tuple-element.28.refs_0_.refs_1_.refs_3_.refs_2_, f32[8,1024]{1,0:T(8,128)S(1)} %get-tuple-element.33.refs_1_, f32[4,16,1024]{2,1,0:T(8,128)S(1)} %collective-permute-done.4.refs_2_.refs_5_), custom_call_target="tpu_custom_call" | custom-call | flops 8589934592 | bytes 1048576 | tf_op jit(solution)/shard_map/blocks_3/pallas_call | solution.py:335
  30.6 0.0 collective-permute-done.5.refs_4_.refs_6_
  30.6 0.0 copy-done.2
  30.6 4.8 %blocks_4.1 = (f32[8,1024]{1,0:T(8,128)S(1)}, bf16[4,4,2048,256]{3,2,1,0:T(8,128)(2,1)S(1)}) custom-call(bf16[64,1024]{1,0:T(8,128)(2,1)S(1)} %get-tuple-element.28.refs_0_.refs_1_.refs_3_.refs_2_, f32[8,1024]{1,0:T(8,128)S(1)} %get-tuple-element.34.refs_1_, f32[1,1024]{1,0:T(1,128)S(1)} %bitcast.19, f32[1,16,1024]{2,1,0:T(8,128)S(1)} %bitcast.8, ...), custom_call_target="tpu_custom_call" | custom-call | flops 8589934592 | bytes 1048576 | tf_op jit(solution)/shard_map/blocks_4/pallas_call | solution.py:335
  35.5 1.9 %collective-permute-start.6 = (f32[1,8,1024]{2,1,0:T(8,128)S(1)}, f32[1,8,1024]{2,1,0:T(8,128)S(1)}, u32[]{:S(2)}, u32[]{:S(2)}) collective-permute-start(f32[1,8,1024]{2,1,0:T(8,128)S(1)} %bitcast.11), channel_id=1, source_target_pairs={{0,12},{1,13},{2,14},{3,15},{4,0},{5,1},{6,2},{7,3},{8,4},{9,5},{1... | collective-permute-start | bytes 98312 | tf_op jit(solution)/shard_map/ppermute | solution.py:59
  37.4 0.0 collective-permute-start.7
  37.4 1.9 %collective-permute-start.8 = (f32[1,8,1024]{2,1,0:T(8,128)S(1)}, f32[1,8,1024]{2,1,0:T(8,128)S(1)}, u32[]{:S(2)}, u32[]{:S(2)}) collective-permute-start(f32[1,8,1024]{2,1,0:T(8,128)S(1)} %bitcast.13), channel_id=1, source_target_pairs={{0,4},{1,5},{2,6},{3,7},{4,8},{5,9},{6,10},{7,11},{8,12},{9,13},{1... | collective-permute-start | bytes 98312 | tf_op jit(solution)/shard_map/ppermute | solution.py:59
  39.3 1.5 %own_again.1.refs_0_ = f32[8,1024]{1,0:T(8,128)S(1)} custom-call(bf16[64,1024]{1,0:T(8,128)(2,1)S(1)} %get-tuple-element.28.refs_0_.refs_1_.refs_3_.refs_2_, bf16[1,1024,64]{2,1,0:T(8,128)(2,1)S(1)} %get-tuple-element.41.refs_1_, f32[1,8,1024]{2,1,0:T(8,128)S(1)} %bitcast.14), custom_call_target="tpu_custom_call" | custom-call | flops 2147483648 | bytes 1048576 | tf_op jit(solution)/shard_map/own_again/pallas_call | solution.py:335
  40.8 0.0 collective-permute-done.6.refs_8_.refs_2_
  40.8 1.8 %collective-permute-done.7.refs_9_.refs_3_ = f32[1,8,1024]{2,1,0:T(8,128)S(1)} collective-permute-done((f32[1,8,1024]{2,1,0:T(8,128)S(1)}, f32[1,8,1024]{2,1,0:T(8,128)S(1)}, u32[]{:S(2)}, u32[]{:S(2)}) %collective-permute-start.7) | collective-permute-done | bytes 32800 | tf_op jit(solution)/shard_map/ppermute | solution.py:59
  42.5 0.6 collective-permute-done.8.refs_10_.refs_4_
  43.1 0.1 collective-permute-start.9
  43.2 0.6 collective-permute-start.10
  43.8 1.7 %line_again.1.refs_2_ = f32[8,1024]{1,0:T(8,128)S(1)} custom-call(f32[8,1024]{1,0:T(8,128)S(1)} %own_again.1.refs_0_, bf16[3,4,2048,256]{3,2,1,0:T(8,128)(2,1)S(1)} %get-tuple-element.42.refs_1_, f32[1,8,1024]{2,1,0:T(8,128)S(1)} %collective-permute-done.6.refs_8_.refs_2_, f32[1,8,1024]{2,1,0:T(8,128)S(1)} %collective-permute-done.7.refs_9_.refs_3_, ...), custom_call_target="tpu_custom_call" | custom-call | flops 6442450944 | bytes 1048576 | tf_op jit(solution)/shard_map/line_again/pallas_call | solution.py:335
  45.5 0.0 collective-permute-done.9.refs_3_.refs_11_.refs_4_
  45.5 3.1 %across_half.1.refs_1_ = f32[8,1024]{1,0:T(8,128)S(1)} custom-call(s32[2]{0:T(128)S(1)} %fusion.3.refs_0_, bf16[64,1024]{1,0:T(8,128)(2,1)S(1)} %get-tuple-element.28.refs_0_.refs_1_.refs_3_.refs_2_, bf16[4,1024,64]{2,1,0:T(8,128)(2,1)S(1)} %get-tuple-element.36.refs_2_.refs_3_, f32[4,8,1024]{2,1,0:T(8,128)S(1)} %collective-permute-done.9.refs_3_.refs_11_.refs_4_), custom_call_target="tpu_custom_call" | custom-call | flops 4294967296 | bytes 1048576 | tf_op jit(solution)/shard_map/across_half/pallas_call | solution.py:335
  48.6 0.5 collective-permute-done.10.refs_12_.refs_5_
  49.1 0.0 collective-permute-start.11
  49.1 2.3 %beside_half.1.refs_1_ = f32[8,1024]{1,0:T(8,128)S(1)} custom-call(s32[2]{0:T(128)S(1)} %fusion.2.refs_0_, f32[8,1024]{1,0:T(8,128)S(1)} %across_half.1.refs_1_, bf16[2,4,2048,256]{3,2,1,0:T(8,128)(2,1)S(1)} %get-tuple-element.39.refs_2_, bf16[64,1024]{1,0:T(8,128)(2,1)S(1)} %get-tuple-element.28.refs_0_.refs_1_.refs_3_.refs_2_, ...), custom_call_target="tpu_custom_call" | custom-call | flops 4294967296 | bytes 1048576 | tf_op jit(solution)/shard_map/beside_half/pallas_call | solution.py:335
  51.4 0.0 collective-permute-done.11.refs_13_.refs_6_.refs_3_
  51.4 1.8 %far_half.1 = (f32[8,1024]{1,0:T(8,128)S(1)}, f32[8,128]{1,0:T(8,128)S(1)}) custom-call(s32[2]{0:T(128)S(1)} %fusion.3.refs_0_, f32[8,1024]{1,0:T(8,128)S(1)} %beside_half.1.refs_1_, f32[8,1024]{1,0:T(8,128)S(1)} %line_again.1.refs_2_, f32[1,1024]{1,0:T(1,128)S(1)} %bitcast.20, f32[1,8,1024]{2,1,0:T(8,128)S(1)} %bitcast.16, ...), custom_call_target="tpu_custom_call" | custom-call | flops 4294967296 | bytes 1048576 | tf_op jit(solution)/shard_map/far_half/pallas_call | solution.py:335
  53.3 1.3 %collective-permute-start.12 = (f32[8,128]{1,0:T(8,128)S(1)}, f32[8,128]{1,0:T(8,128)S(1)}, u32[]{:S(2)}, u32[]{:S(2)}) collective-permute-start(f32[8,128]{1,0:T(8,128)S(1)} %get-tuple-element.44), channel_id=1, source_target_pairs={{0,12},{1,13},{2,14},{3,15},{4,0},{5,1},{6,2},{7,3},{8,4},{9,5},{1... | collective-permute-start | bytes 12296 | tf_op jit(solution)/shard_map/ppermute | solution.py:59
  54.6 0.3 collective-permute-start.13
  54.8 1.6 %collective-permute-start.14 = (f32[8,128]{1,0:T(8,128)S(1)}, f32[8,128]{1,0:T(8,128)S(1)}, u32[]{:S(2)}, u32[]{:S(2)}) collective-permute-start(f32[8,128]{1,0:T(8,128)S(1)} %get-tuple-element.44), channel_id=1, source_target_pairs={{0,4},{1,5},{2,6},{3,7},{4,8},{5,9},{6,10},{7,11},{8,12},{9,13},{1... | collective-permute-start | bytes 12296 | tf_op jit(solution)/shard_map/ppermute | solution.py:59
  56.4 3.1 %across_rest.1.refs_1_ = f32[8,1024]{1,0:T(8,128)S(1)} custom-call(s32[2]{0:T(128)S(1)} %fusion.refs_0_, f32[8,1024]{1,0:T(8,128)S(1)} %get-tuple-element.45.refs_1_, bf16[64,1024]{1,0:T(8,128)(2,1)S(1)} %get-tuple-element.28.refs_0_.refs_1_.refs_3_.refs_2_, bf16[4,1024,64]{2,1,0:T(8,128)(2,1)S(1)} %get-tuple-element.36.refs_2_.refs_3_, ...), custom_call_target="tpu_custom_call" | custom-call | flops 4294967296 | bytes 1048576 | tf_op jit(solution)/shard_map/across_rest/pallas_call | solution.py:335
  59.5 2.3 %beside_rest.1.refs_1_ = f32[8,1024]{1,0:T(8,128)S(1)} custom-call(s32[2]{0:T(128)S(1)} %fusion.1.refs_0_, f32[8,1024]{1,0:T(8,128)S(1)} %across_rest.1.refs_1_, bf16[2,4,2048,256]{3,2,1,0:T(8,128)(2,1)S(1)} %get-tuple-element.39.refs_2_, bf16[64,1024]{1,0:T(8,128)(2,1)S(1)} %get-tuple-element.28.refs_0_.refs_1_.refs_3_.refs_2_, ...), custom_call_target="tpu_custom_call" | custom-call | flops 4294967296 | bytes 1048576 | tf_op jit(solution)/shard_map/beside_rest/pallas_call | solution.py:335
  61.9 0.3 scalars.1.scalars_ref
  62.2 0.0 collective-permute-done.12
  62.2 0.0 collective-permute-done.13
  62.2 0.0 collective-permute-done.14
  62.3 0.1 collective-permute-start.15
  62.3 1.3 %collective-permute-start.16 = (f32[8,128]{1,0:T(8,128)S(1)}, f32[8,128]{1,0:T(8,128)S(1)}, u32[]{:S(2)}, u32[]{:S(2)}) collective-permute-start(f32[8,128]{1,0:T(8,128)S(1)} %add_add_fusion.1), channel_id=1, source_target_pairs={{0,2},{1,3},{2,0},{3,1},{4,6},{5,7},{6,4},{7,5},{8,10},{9,11},{10,... | collective-permute-start | bytes 12296 | tf_op jit(solution)/shard_map/ppermute | solution.py:52
  63.6 0.6 collective-permute-start.17
  64.2 1.7 %far_rest.1.total_ref = f32[8,1024]{1,0:T(8,128)S(1)} custom-call(s32[2]{0:T(128)S(1)} %fusion.refs_0_, f32[8,1024]{1,0:T(8,128)S(1)} %beside_rest.1.refs_1_, bf16[4,4,2048,256]{3,2,1,0:T(8,128)(2,1)S(1)} %get-tuple-element.43.refs_5_.refs_2_, f32[4,8,1024]{2,1,0:T(8,128)S(1)} %collective-permute-done.11.refs_13_.refs_6_.refs_3_), custom_call_target="tpu_custom_call" | custom-call | flops 4294967296 | bytes 1048576 | tf_op jit(solution)/shard_map/far_rest/pallas_call | solution.py:335
  65.9 0.0 collective-permute-done.15
  65.9 0.1 collective-permute-done.16
  66.0 0.6 collective-permute-done.17
  66.6 0.7 %last_update.1 = (f32[8,1024]{1,0:T(8,128)}, f32[8,1024]{1,0:T(8,128)}) custom-call(f32[4,8,128]{2,1,0:T(8,128)S(1)} %scalars.1.scalars_ref, f32[8,128]{1,0:T(8,128)S(1)} %add_add_fusion.form_ref, f32[8,1024]{1,0:T(8,128)S(1)} %far_rest.1.total_ref, f32[1,1024]{1,0:T(1,128)S(1)} %bitcast.21, f32[1,16,1024]{2,1,0:T(8,128)S(1)} %bitcast.10, ...), custom_call_target="tpu_custom_call" | custom-call | tf_op jit(solution)/shard_map/last_update/pallas_call | solution.py:444
  (8 shorter events, 0.1 us)
Async XLA Ops:
  0.6 0.8 %copy-start = (f32[8,1024]{1,0:T(8,128)S(1)}, f32[8,1024]{1,0:T(8,128)}, u32[]{:S(2)}) copy-start(f32[8,1024]{1,0:T(8,128)} %features_ref.1) | copy-start | bytes 98308
  1.4 0.8 %copy-start.1 = (f32[8,1024]{1,0:T(8,128)S(1)}, f32[8,1024]{1,0:T(8,128)}, u32[]{:S(2)}) copy-start(f32[8,1024]{1,0:T(8,128)} %rhs_ref.1) | copy-start | bytes 98308
  2.1 0.7 copy-start.3
  3.4 7.7 %collective-permute-start = (f32[1,16,1024]{2,1,0:T(8,128)S(1)}, f32[1,16,1024]{2,1,0:T(8,128)S(1)}, u32[]{:S(2)}, u32[]{:S(2)}) collective-permute-start(f32[1,16,1024]{2,1,0:T(8,128)S(1)} %bitcast.3), channel_id=1, source_target_pairs={{0,12},{1,13},{2,14},{3,15},{4,0},{5,1},{6,2},{7,3},{8,4},{9,5},{1... | collective-permute-start | bytes 196616 | tf_op jit(solution)/shard_map/ppermute | solution.py:59
  8.5 6.5 %collective-permute-start.1 = (f32[1,16,1024]{2,1,0:T(8,128)S(1)}, f32[1,16,1024]{2,1,0:T(8,128)S(1)}, u32[]{:S(2)}, u32[]{:S(2)}) collective-permute-start(f32[1,16,1024]{2,1,0:T(8,128)S(1)} %bitcast.4), channel_id=1, source_target_pairs={{0,8},{1,9},{2,10},{3,11},{4,12},{5,13},{6,14},{7,15},{8,0},{9,1},... | collective-permute-start | bytes 196616 | tf_op jit(solution)/shard_map/ppermute | solution.py:59
  8.5 6.5 %collective-permute-start.2 = (f32[1,16,1024]{2,1,0:T(8,128)S(1)}, f32[1,16,1024]{2,1,0:T(8,128)S(1)}, u32[]{:S(2)}, u32[]{:S(2)}) collective-permute-start(f32[1,16,1024]{2,1,0:T(8,128)S(1)} %bitcast.5), channel_id=1, source_target_pairs={{0,4},{1,5},{2,6},{3,7},{4,8},{5,9},{6,10},{7,11},{8,12},{9,13},{1... | collective-permute-start | bytes 196616 | tf_op jit(solution)/shard_map/ppermute | solution.py:59
  15.0 5.4 %collective-permute-start.3 = (f32[4,16,1024]{2,1,0:T(8,128)S(1)}, f32[4,16,1024]{2,1,0:T(8,128)S(1)}, u32[]{:S(2)}, u32[]{:S(2)}) collective-permute-start(f32[4,16,1024]{2,1,0:T(8,128)S(1)} %pad_maximum_fusion), channel_id=1, source_target_pairs={{0,1},{1,0},{2,3},{3,2},{4,5},{5,4},{6,7},{7,6},{8,9},{9,8},{10,11... | collective-permute-start | bytes 786440 | tf_op jit(solution)/shard_map/ppermute | solution.py:52
  15.0 10.3 %collective-permute-start.4 = (f32[4,16,1024]{2,1,0:T(8,128)S(1)}, f32[4,16,1024]{2,1,0:T(8,128)S(1)}, u32[]{:S(2)}, u32[]{:S(2)}) collective-permute-start(f32[4,16,1024]{2,1,0:T(8,128)S(1)} %pad_maximum_fusion), channel_id=1, source_target_pairs={{0,2},{1,3},{2,0},{3,1},{4,6},{5,7},{6,4},{7,5},{8,10},{9,11},{10,... | collective-permute-start | bytes 786440 | tf_op jit(solution)/shard_map/ppermute | solution.py:52
  25.3 5.3 %copy-start.2 = (f32[1024]{0:T(1024)S(1)}, f32[1024]{0:T(1024)}, u32[]{:S(2)}) copy-start(f32[1024]{0:T(1024)} %param.6) | copy-start | bytes 12292
  25.3 5.3 %collective-permute-start.5 = (f32[4,16,1024]{2,1,0:T(8,128)S(1)}, f32[4,16,1024]{2,1,0:T(8,128)S(1)}, u32[]{:S(2)}, u32[]{:S(2)}) collective-permute-start(f32[4,16,1024]{2,1,0:T(8,128)S(1)} %collective-permute-done.4.refs_2_.refs_5_), channel_id=1, source_target_pairs={{0,1},{1,0},{2,3},{3,2},{4,5},{5,4},{6,7},{7,6},{8,9},{9,8},{10,11... | collective-permute-start | bytes 786440 | tf_op jit(solution)/shard_map/ppermute | solution.py:52
  35.5 5.3 %collective-permute-start.6 = (f32[1,8,1024]{2,1,0:T(8,128)S(1)}, f32[1,8,1024]{2,1,0:T(8,128)S(1)}, u32[]{:S(2)}, u32[]{:S(2)}) collective-permute-start(f32[1,8,1024]{2,1,0:T(8,128)S(1)} %bitcast.11), channel_id=1, source_target_pairs={{0,12},{1,13},{2,14},{3,15},{4,0},{5,1},{6,2},{7,3},{8,4},{9,5},{1... | collective-permute-start | bytes 98312 | tf_op jit(solution)/shard_map/ppermute | solution.py:59
  37.4 5.2 %collective-permute-start.7 = (f32[1,8,1024]{2,1,0:T(8,128)S(1)}, f32[1,8,1024]{2,1,0:T(8,128)S(1)}, u32[]{:S(2)}, u32[]{:S(2)}) collective-permute-start(f32[1,8,1024]{2,1,0:T(8,128)S(1)} %bitcast.12), channel_id=1, source_target_pairs={{0,8},{1,9},{2,10},{3,11},{4,12},{5,13},{6,14},{7,15},{8,0},{9,1},... | collective-permute-start | bytes 98312 | tf_op jit(solution)/shard_map/ppermute | solution.py:59
  37.4 5.7 %collective-permute-start.8 = (f32[1,8,1024]{2,1,0:T(8,128)S(1)}, f32[1,8,1024]{2,1,0:T(8,128)S(1)}, u32[]{:S(2)}, u32[]{:S(2)}) collective-permute-start(f32[1,8,1024]{2,1,0:T(8,128)S(1)} %bitcast.13), channel_id=1, source_target_pairs={{0,4},{1,5},{2,6},{3,7},{4,8},{5,9},{6,10},{7,11},{8,12},{9,13},{1... | collective-permute-start | bytes 98312 | tf_op jit(solution)/shard_map/ppermute | solution.py:59
  43.1 2.4 %collective-permute-start.9 = (f32[4,8,1024]{2,1,0:T(8,128)S(1)}, f32[4,8,1024]{2,1,0:T(8,128)S(1)}, u32[]{:S(2)}, u32[]{:S(2)}) collective-permute-start(f32[4,8,1024]{2,1,0:T(8,128)S(1)} %pad_maximum_fusion.1), channel_id=1, source_target_pairs={{0,1},{1,0},{2,3},{3,2},{4,5},{5,4},{6,7},{7,6},{8,9},{9,8},{10,11... | collective-permute-start | bytes 393224 | tf_op jit(solution)/shard_map/ppermute | solution.py:52
  43.2 5.9 %collective-permute-start.10 = (f32[4,8,1024]{2,1,0:T(8,128)S(1)}, f32[4,8,1024]{2,1,0:T(8,128)S(1)}, u32[]{:S(2)}, u32[]{:S(2)}) collective-permute-start(f32[4,8,1024]{2,1,0:T(8,128)S(1)} %pad_maximum_fusion.1), channel_id=1, source_target_pairs={{0,2},{1,3},{2,0},{3,1},{4,6},{5,7},{6,4},{7,5},{8,10},{9,11},{10,... | collective-permute-start | bytes 393224 | tf_op jit(solution)/shard_map/ppermute | solution.py:52
  49.1 2.3 %collective-permute-start.11 = (f32[4,8,1024]{2,1,0:T(8,128)S(1)}, f32[4,8,1024]{2,1,0:T(8,128)S(1)}, u32[]{:S(2)}, u32[]{:S(2)}) collective-permute-start(f32[4,8,1024]{2,1,0:T(8,128)S(1)} %collective-permute-done.10.refs_12_.refs_5_), channel_id=1, source_target_pairs={{0,1},{1,0},{2,3},{3,2},{4,5},{5,4},{6,7},{7,6},{8,9},{9,8},{10,11... | collective-permute-start | bytes 393224 | tf_op jit(solution)/shard_map/ppermute | solution.py:52
  53.3 9.0 %collective-permute-start.12 = (f32[8,128]{1,0:T(8,128)S(1)}, f32[8,128]{1,0:T(8,128)S(1)}, u32[]{:S(2)}, u32[]{:S(2)}) collective-permute-start(f32[8,128]{1,0:T(8,128)S(1)} %get-tuple-element.44), channel_id=1, source_target_pairs={{0,12},{1,13},{2,14},{3,15},{4,0},{5,1},{6,2},{7,3},{8,4},{9,5},{1... | collective-permute-start | bytes 12296 | tf_op jit(solution)/shard_map/ppermute | solution.py:59
  54.6 7.7 %collective-permute-start.13 = (f32[8,128]{1,0:T(8,128)S(1)}, f32[8,128]{1,0:T(8,128)S(1)}, u32[]{:S(2)}, u32[]{:S(2)}) collective-permute-start(f32[8,128]{1,0:T(8,128)S(1)} %get-tuple-element.44), channel_id=1, source_target_pairs={{0,8},{1,9},{2,10},{3,11},{4,12},{5,13},{6,14},{7,15},{8,0},{9,1},... | collective-permute-start | bytes 12296 | tf_op jit(solution)/shard_map/ppermute | solution.py:59
  54.8 7.4 %collective-permute-start.14 = (f32[8,128]{1,0:T(8,128)S(1)}, f32[8,128]{1,0:T(8,128)S(1)}, u32[]{:S(2)}, u32[]{:S(2)}) collective-permute-start(f32[8,128]{1,0:T(8,128)S(1)} %get-tuple-element.44), channel_id=1, source_target_pairs={{0,4},{1,5},{2,6},{3,7},{4,8},{5,9},{6,10},{7,11},{8,12},{9,13},{1... | collective-permute-start | bytes 12296 | tf_op jit(solution)/shard_map/ppermute | solution.py:59
  62.3 3.7 %collective-permute-start.15 = (f32[8,128]{1,0:T(8,128)S(1)}, f32[8,128]{1,0:T(8,128)S(1)}, u32[]{:S(2)}, u32[]{:S(2)}) collective-permute-start(f32[8,128]{1,0:T(8,128)S(1)} %add_add_fusion.1), channel_id=1, source_target_pairs={{0,1},{1,0},{2,3},{3,2},{4,5},{5,4},{6,7},{7,6},{8,9},{9,8},{10,11... | collective-permute-start | bytes 12296 | tf_op jit(solution)/shard_map/ppermute | solution.py:52
  62.3 3.7 %collective-permute-start.16 = (f32[8,128]{1,0:T(8,128)S(1)}, f32[8,128]{1,0:T(8,128)S(1)}, u32[]{:S(2)}, u32[]{:S(2)}) collective-permute-start(f32[8,128]{1,0:T(8,128)S(1)} %add_add_fusion.1), channel_id=1, source_target_pairs={{0,2},{1,3},{2,0},{3,1},{4,6},{5,7},{6,4},{7,5},{8,10},{9,11},{10,... | collective-permute-start | bytes 12296 | tf_op jit(solution)/shard_map/ppermute | solution.py:52
  63.6 3.0 %collective-permute-start.17 = (f32[8,128]{1,0:T(8,128)S(1)}, f32[8,128]{1,0:T(8,128)S(1)}, u32[]{:S(2)}, u32[]{:S(2)}) collective-permute-start(f32[8,128]{1,0:T(8,128)S(1)} %add_add_fusion.1), channel_id=1, source_target_pairs={{0,3},{1,2},{2,1},{3,0},{4,7},{5,6},{6,5},{7,4},{8,11},{9,10},{10,... | collective-permute-start | bytes 12296 | tf_op jit(solution)/shard_map/ppermute | solution.py:52

commit v15 on v11

--- a/solution.py
+++ b/solution.py
@@ -12,8 +12,8 @@
 DEPTH = 64
 TILE = 256
 MIB = 1024 * 1024
-KEPT_ORDER = (0, 1, 4, 3, 2)
-KEPT_ROOM = 52 * MIB
+KEPT_ORDER = (2, 5, 4)
+KEPT_ROOM = 44 * MIB
 F32 = jnp.float32
 BF16 = jnp.bfloat16
 
@@ -67,19 +67,25 @@
     return chips // near, near
 
 
-def gathered(value):
-    far, near = digits()
+def neighbours(value):
+    far, _ = digits()
     own = value[None]
-    line = [turned(own, by) for by in range(1, far)]
-    group = jnp.concatenate([own] + line, axis=0)
-    across = swapped(group, 0, 0, 1)
+    return [[own], [swapped(own, 0, 0, 1)], [turned(own, by) for by in range(1, far)]]
+
+
+def with_groups(groups, value):
+    _, near = digits()
+    *line, value = lax.optimization_barrier((*groups[2], value))
+    stack = jnp.concatenate(line, axis=0)
+    group = jnp.concatenate(groups[0] + line, axis=0)
+    across = swapped(stack, 0, 0, 1)
     beside = [swapped(group, 0, by, 0) for by in range(1, near)]
-    return [[own], line, [across], beside]
+    return groups[:2] + [line, [across], beside], value
 
 
 def held_back(groups, value):
-    *beside, value = lax.optimization_barrier((*groups[3], value))
-    return groups[:3] + [beside, [swapped(g, 0, 0, 1) for g in beside]], value
+    *beside, value = lax.optimization_barrier((*groups[4], value))
+    return groups[:4] + [beside, [swapped(g, 0, 0, 1) for g in beside]], value
 
 
 def along_line(value):
@@ -104,7 +110,6 @@
             return k * far + picks + (side + flip) % 2
 
         return [
-            one(0, core),
             jnp.concatenate([one(k, side) for k, side in enumerate(sides)]),
             jnp.concatenate([one(k, core) for k in range(near - 1)]),
         ]
@@ -338,12 +343,12 @@
     def amount(stacks):
         return sum(s.shape[0] for s in stacks)
 
-    groups = gathered(jnp.concatenate([features, rhs], axis=0))
+    groups = neighbours(jnp.concatenate([features, rhs], axis=0))
     mine = groups[0][0]
     own_shape = jax.ShapeDtypeStruct((DEPTH, width), BF16)
     room = KEPT_ROOM - lax.axis_size("row") * 512 * width
-    sizes = [amount(g) for g in groups]
-    sizes.append(sizes[3])
+    far, near = digits()
+    sizes = [1, 1, far - 1, far - 1, far * (near - 1), far * (near - 1)]
     keep = [0] * len(sizes)
     for k in KEPT_ORDER:
         fit = max(room, 0) // (4 * width * width)
@@ -352,7 +357,9 @@
         room -= 4 * keep[k] * width * width
     own, total, prepared = None, None, []
     for k, blocks in enumerate(sizes):
-        if k == 3:
+        if k == 2:
+            groups, total = with_groups(groups, total)
+        if k == 4:
             groups, total = held_back(groups, total)
         stacks = groups[k]
         final = k == len(sizes) - 1
@@ -374,12 +381,12 @@
             own, *made = made
         total, *sources = made
         prepared.append(sources)
-    images = gathered(total)
+    images = neighbours(total)
     image = images[0][0]
 
     def again(group, out, name, sofar=(), table=None, form=()):
         stacks = images[group]
-        blocks = amount(stacks)
+        blocks = sizes[group]
         listed = () if table is None else (table,)
         work = blocks if table is None else table.shape[0]
         sources = list(prepared[group])
@@ -398,21 +405,26 @@
         )
 
     halves, rests = tables()
+    shifts = jnp.arange(far - 1, dtype=jnp.int32)
+    middle = far // 2 - 1
     once = again(0, field, "own_again")
-    once = again(1, field, "line_again", sofar=(once,))
-    half = again(2, field, "across_half", table=halves[0])
+    once = again(1, field, "pair_again", sofar=(once,))
+    images, once = with_groups(images, once)
+    once = again(2, field, "line_again", sofar=(once,))
+    once = again(3, field, "across_once", sofar=(once,), table=shifts[middle : middle + 1])
+    half = again(3, field, "across_half", table=shifts[:middle])
     images, half = held_back(images, half)
-    half = again(3, field, "beside_half", sofar=(half,), table=halves[1])
+    half = again(4, field, "beside_half", sofar=(half,), table=halves[0])
     total, form = again(
-        4, (field, small), "far_half", sofar=(half,), table=halves[2], form=(once, noise, image)
+        5, (field, small), "far_half", sofar=(half,), table=halves[1], form=(once, noise, image)
     )
     parts = along_line(form)
-    total = again(2, field, "across_rest", sofar=(total,), table=rests[0])
-    total = again(3, field, "beside_rest", sofar=(total,), table=rests[1])
+    total = again(3, field, "across_rest", sofar=(total,), table=shifts[middle + 1 :])
+    total = again(4, field, "beside_rest", sofar=(total,), table=rests[0])
     *parts, total = lax.optimization_barrier((*parts, total))
     form = sum(parts, form)
     parts = over_quad(form)
-    total = again(4, field, "far_rest", sofar=(total,), table=rests[2])
+    total = again(5, field, "far_rest", sofar=(total,), table=rests[1])
     *parts, total = lax.optimization_barrier((*parts, total))
     form = sum(parts, form)
     flat = [s for g in groups for s in g]

time: 65.9 us -> 69.7 us (1.058)
  starting transfers between devices: 16.5 us -> 19 us
  Pallas kernels: 38.4 us -> 40.8 us
  local copies, waits for them, and re-layouts: 2.71 us -> 1.94 us
    ppermute x9, waiting for transfers between devices: 5.24 us -> 2.71 us  [turned(): lax.ppermute(value, 'row', [(i, (i - by * step) % length) for i in range(...]
    pallas_call x13 -> x16, Pallas kernels: 37.3 us -> 39.8 us  [call(): pl.pallas_call(kernel, out_shape=out_shape, in_specs=[smem if table and k...]
    ppermute x9 -> x11, waiting for transfers between devices: 1.22 us -> 3.4 us  [swapped(): return lax.ppermute(value, 'row', [(i, i ^ by) for i in range(length)])]
    unnamed x6 -> x2, local copies, waits for them, and re-layouts: 1.98 us -> 0.02 us
    ppermute x9 -> x11, starting transfers between devices: 4.46 us -> 6.41 us  [swapped(): return lax.ppermute(value, 'row', [(i, i ^ by) for i in range(length)])]
    slice x0 -> x2, local copies, waits for them, and re-layouts: none -> 1.18 us  [the longest x1 0.6 us: shards(): shifts[middle:middle + 1]]
  transfers between devices with their start and end apart: 18 -> 20, of which waited for: 6 -> 4; matrix products, arithmetic and copies ran while one was open for 1% -> 3% of each run, Pallas kernels for 47% -> 48%
where the time goes in v15:
time: 69.7 us; the launch traced here: 69.5 us
  Pallas kernels  40.8 us (59%)
  starting transfers between devices  19 us (27%)
  waiting for transfers between devices  6.1 us (9%)
  local copies, waits for them, and re-layouts  1.94 us (3%)
  other arithmetic  0.87 us (1%)
  between operations  0.75 us (1%)
    pallas_call x16, Pallas kernels, call(): pl.pallas_call(kernel, out_shape=out_shape, in_specs=[smem if table and k...  39.8 us
    ppermute x9, starting transfers between devices, turned(): lax.ppermute(value, 'row', [(i, (i - by * step) % length) for i in range(...  12.6 us
    ppermute x11, starting transfers between devices, swapped(): return lax.ppermute(value, 'row', [(i, i ^ by) for i in range(length)])  6.41 us
    ppermute x11, waiting for transfers between devices, swapped(): return lax.ppermute(value, 'row', [(i, i ^ by) for i in range(length)])  3.4 us
    ppermute x9, waiting for transfers between devices, turned(): lax.ppermute(value, 'row', [(i, (i - by * step) % length) for i in range(...  2.71 us
  transfers between devices with their start and end apart: 20, of which 4 were waited for; matrix products, arithmetic and copies ran while one was open for 3% of the time, Pallas kernels for 48%

profile of v15, /device:TPU:0, one launch (start us, length us, event | category | flops | bytes accessed | tf_op | source)
XLA Modules:
  0.0 69.5 jit_solution(10967883900574145684)
XLA Ops:
  0.6 0.8 %maximum_bitcast_fusion.refs_1_.refs_4_.refs_0_.mine_ref = f32[1,16,1024]{2,1,0:T(8,128)S(1)} fusion(f32[8,1024]{1,0:T(8,128)} %param.7, f32[8,1024]{1,0:T(8,128)} %param.4), kind=kLoop, calls=%fused_computation.4 | loop fusion | flops 16384 | bytes 131072 | tf_op jit(solution)/shard_map/broadcast_in_dim | solution.py:72
  1.4 0.5 collective-permute-start
  1.9 4.7 %collective-permute-start.1 = (f32[1,16,1024]{2,1,0:T(8,128)S(1)}, f32[1,16,1024]{2,1,0:T(8,128)S(1)}, u32[]{:S(2)}, u32[]{:S(2)}) collective-permute-start(f32[1,16,1024]{2,1,0:T(8,128)S(1)} %maximum_bitcast_fusion.refs_1_.refs_4_.refs_0_.mine_ref), channel_id=1, source_target_pairs={{0,12},{1,13},{2,14},{3,15},{4,0},{5,1},{6,2},{7,3},{8,4},{9,5},{1... | collective-permute-start | bytes 196616 | tf_op jit(solution)/shard_map/ppermute | solution.py:59
  6.5 0.0 collective-permute-start.2
  6.5 1.0 %collective-permute-start.3 = (f32[1,16,1024]{2,1,0:T(8,128)S(1)}, f32[1,16,1024]{2,1,0:T(8,128)S(1)}, u32[]{:S(2)}, u32[]{:S(2)}) collective-permute-start(f32[1,16,1024]{2,1,0:T(8,128)S(1)} %maximum_bitcast_fusion.refs_1_.refs_4_.refs_0_.mine_ref), channel_id=1, source_target_pairs={{0,4},{1,5},{2,6},{3,7},{4,8},{5,9},{6,10},{7,11},{8,12},{9,13},{1... | collective-permute-start | bytes 196616 | tf_op jit(solution)/shard_map/ppermute | solution.py:59
  7.5 0.7 %copy.7.refs_0_ = f32[8,1]{1,0:T(8,128)S(1)} copy(f32[8,1]{0,1:T(1,128)} %bitcast.19) | data formatting | bytes 64 | tf_op jit(solution)/shard_map/broadcast_in_dim | solution.py:315
  8.3 1.6 %blocks_0.1 = (bf16[64,1024]{1,0:T(8,128)(2,1)S(1)}, f32[8,1024]{1,0:T(8,128)S(1)}, bf16[1,1024,64]{2,1,0:T(8,128)(2,1)S(1)}) custom-call(f32[8,1]{1,0:T(8,128)S(1)} %copy.7.refs_0_, f32[1,16,1024]{2,1,0:T(8,128)S(1)} %maximum_bitcast_fusion.refs_1_.refs_4_.refs_0_.mine_ref), custom_call_target="tpu_custom_call" | custom-call | flops 2147483648 | bytes 1048576 | tf_op jit(solution)/shard_map/blocks_0/pallas_call | solution.py:331
  9.9 0.6 slice.10.refs_0_
  10.5 0.6 slice.11.refs_0_
  11.1 0.0 collective-permute-done.refs_3_.refs_1_
  11.1 1.6 %blocks_1.1 = (f32[8,1024]{1,0:T(8,128)S(1)}, bf16[1,1024,64]{2,1,0:T(8,128)(2,1)S(1)}) custom-call(f32[8,1]{1,0:T(8,128)S(1)} %copy.7.refs_0_, bf16[64,1024]{1,0:T(8,128)(2,1)S(1)} %get-tuple-element.38.refs_1_.refs_0_.refs_3_.refs_2_, f32[8,1024]{1,0:T(8,128)S(1)} %get-tuple-element.39.refs_2_, f32[1,16,1024]{2,1,0:T(8,128)S(1)} %collective-permute-done.refs_3_.refs_1_), custom_call_target="tpu_custom_call" | custom-call | flops 2147483648 | bytes 1048576 | tf_op jit(solution)/shard_map/blocks_1/pallas_call | solution.py:331
  12.8 0.0 collective-permute-done.1.refs_3_.refs_2_
  12.8 0.9 %collective-permute-done.2.refs_4_.refs_3_ = f32[1,16,1024]{2,1,0:T(8,128)S(1)} collective-permute-done((f32[1,16,1024]{2,1,0:T(8,128)S(1)}, f32[1,16,1024]{2,1,0:T(8,128)S(1)}, u32[]{:S(2)}, u32[]{:S(2)}) %collective-permute-start.2) | collective-permute-done | bytes 65568 | tf_op jit(solution)/shard_map/ppermute | solution.py:59
  13.6 0.0 collective-permute-done.3.refs_5_.refs_4_
  13.6 0.1 collective-permute-start.4
  13.7 3.8 %blocks_2.1 = (f32[8,1024]{1,0:T(8,128)S(1)}, bf16[3,4,2048,256]{3,2,1,0:T(8,128)(2,1)S(1)}) custom-call(f32[8,1]{1,0:T(8,128)S(1)} %copy.7.refs_0_, bf16[64,1024]{1,0:T(8,128)(2,1)S(1)} %get-tuple-element.38.refs_1_.refs_0_.refs_3_.refs_2_, f32[8,1024]{1,0:T(8,128)S(1)} %get-tuple-element.44.refs_2_, ...), custom_call_target="tpu_custom_call" | custom-call | flops 6442450944 | bytes 1048576 | tf_op jit(solution)/shard_map/blocks_2/pallas_call | solution.py:331
  17.6 1.6 %collective-permute-start.5 = (f32[4,16,1024]{2,1,0:T(8,128)S(1)}, f32[4,16,1024]{2,1,0:T(8,128)S(1)}, u32[]{:S(2)}, u32[]{:S(2)}) collective-permute-start(f32[4,16,1024]{2,1,0:T(8,128)S(1)} %pad_maximum_fusion), channel_id=1, source_target_pairs={{0,2},{1,3},{2,0},{3,1},{4,6},{5,7},{6,4},{7,5},{8,10},{9,11},{10,... | collective-permute-start | bytes 786440 | tf_op jit(solution)/shard_map/ppermute | solution.py:52
  19.2 0.0 collective-permute-done.4.refs_3_.refs_5_
  19.2 3.9 %blocks_3.1 = (f32[8,1024]{1,0:T(8,128)S(1)}, bf16[3,1024,64]{2,1,0:T(8,128)(2,1)S(1)}) custom-call(f32[8,1]{1,0:T(8,128)S(1)} %copy.7.refs_0_, bf16[64,1024]{1,0:T(8,128)(2,1)S(1)} %get-tuple-element.38.refs_1_.refs_0_.refs_3_.refs_2_, f32[8,1024]{1,0:T(8,128)S(1)} %get-tuple-element.45.refs_2_, f32[3,16,1024]{2,1,0:T(8,128)S(1)} %collective-permute-done.4.refs_3_.refs_5_), custom_call_target="tpu_custom_call" | custom-call | flops 6442450944 | bytes 1048576 | tf_op jit(solution)/shard_map/blocks_3/pallas_call | solution.py:331
  23.1 3.3 %collective-permute-done.5.refs_3_.refs_6_ = f32[4,16,1024]{2,1,0:T(8,128)S(1)} collective-permute-done((f32[4,16,1024]{2,1,0:T(8,128)S(1)}, f32[4,16,1024]{2,1,0:T(8,128)S(1)}, u32[]{:S(2)}, u32[]{:S(2)}) %collective-permute-start.5) | collective-permute-done | bytes 262176 | tf_op jit(solution)/shard_map/ppermute | solution.py:52
  26.4 0.0 copy-start
  26.4 0.0 collective-permute-start.6
  26.4 5.1 %blocks_4.1 = (f32[8,1024]{1,0:T(8,128)S(1)}, bf16[2,4,2048,256]{3,2,1,0:T(8,128)(2,1)S(1)}, bf16[2,1024,64]{2,1,0:T(8,128)(2,1)S(1)}) custom-call(f32[8,1]{1,0:T(8,128)S(1)} %copy.7.refs_0_, bf16[64,1024]{1,0:T(8,128)(2,1)S(1)} %get-tuple-element.38.refs_1_.refs_0_.refs_3_.refs_2_, f32[8,1024]{1,0:T(8,128)S(1)} %get-tuple-element.48.refs_2_, ...), custom_call_target="tpu_custom_call" | custom-call | flops 8589934592 | bytes 1048576 | tf_op jit(solution)/shard_map/blocks_4/pallas_call | solution.py:331
  31.5 0.0 collective-permute-done.6.refs_5_.refs_7_
  31.5 0.0 copy-done
  31.5 4.9 %blocks_5.1 = (f32[8,1024]{1,0:T(8,128)S(1)}, bf16[4,4,2048,256]{3,2,1,0:T(8,128)(2,1)S(1)}) custom-call(f32[8,1]{1,0:T(8,128)S(1)} %copy.7.refs_0_, bf16[64,1024]{1,0:T(8,128)(2,1)S(1)} %get-tuple-element.38.refs_1_.refs_0_.refs_3_.refs_2_, f32[8,1024]{1,0:T(8,128)S(1)} %get-tuple-element.49.refs_2_, f32[1,1024]{1,0:T(1,128)S(1)} %bitcast.15, ...), custom_call_target="tpu_custom_call" | custom-call | flops 8589934592 | bytes 1048576 | tf_op jit(solution)/shard_map/blocks_5/pallas_call | solution.py:331
  36.5 0.5 collective-permute-start.7
  37.0 1.7 %collective-permute-start.10 = (f32[1,8,1024]{2,1,0:T(8,128)S(1)}, f32[1,8,1024]{2,1,0:T(8,128)S(1)}, u32[]{:S(2)}, u32[]{:S(2)}) collective-permute-start(f32[1,8,1024]{2,1,0:T(8,128)S(1)} %bitcast.7), channel_id=1, source_target_pairs={{0,4},{1,5},{2,6},{3,7},{4,8},{5,9},{6,10},{7,11},{8,12},{9,13},{1... | collective-permute-start | bytes 98312 | tf_op jit(solution)/shard_map/ppermute | solution.py:59
  38.7 2.2 %collective-permute-start.8 = (f32[1,8,1024]{2,1,0:T(8,128)S(1)}, f32[1,8,1024]{2,1,0:T(8,128)S(1)}, u32[]{:S(2)}, u32[]{:S(2)}) collective-permute-start(f32[1,8,1024]{2,1,0:T(8,128)S(1)} %bitcast.8), channel_id=1, source_target_pairs={{0,12},{1,13},{2,14},{3,15},{4,0},{5,1},{6,2},{7,3},{8,4},{9,5},{1... | collective-permute-start | bytes 98312 | tf_op jit(solution)/shard_map/ppermute | solution.py:59
  40.8 0.0 collective-permute-start.9
  40.8 1.5 %own_again.1.refs_0_ = f32[8,1024]{1,0:T(8,128)S(1)} custom-call(bf16[64,1024]{1,0:T(8,128)(2,1)S(1)} %get-tuple-element.38.refs_1_.refs_0_.refs_3_.refs_2_, bf16[1,1024,64]{2,1,0:T(8,128)(2,1)S(1)} %get-tuple-element.51.refs_1_, f32[1,8,1024]{2,1,0:T(8,128)S(1)} %bitcast.10), custom_call_target="tpu_custom_call" | custom-call | flops 2147483648 | bytes 1048576 | tf_op jit(solution)/shard_map/own_again/pallas_call | solution.py:331
  42.3 0.0 collective-permute-done.7.refs_3_.refs_9_
  42.3 1.5 %pair_again.1.refs_0_ = f32[8,1024]{1,0:T(8,128)S(1)} custom-call(f32[8,1024]{1,0:T(8,128)S(1)} %own_again.1.refs_0_, bf16[64,1024]{1,0:T(8,128)(2,1)S(1)} %get-tuple-element.38.refs_1_.refs_0_.refs_3_.refs_2_, bf16[1,1024,64]{2,1,0:T(8,128)(2,1)S(1)} %get-tuple-element.52.refs_2_, f32[1,8,1024]{2,1,0:T(8,128)S(1)} %collective-permute-done.7.refs_3_.refs_9_), custom_call_target="tpu_custom_call" | custom-call | flops 2147483648 | bytes 1048576 | tf_op jit(solution)/shard_map/pair_again/pallas_call | solution.py:331
  43.8 0.0 collective-permute-done.10.refs_12_.refs_4_
  43.8 0.0 collective-permute-done.8.refs_10_.refs_2_
  43.8 1.8 %collective-permute-done.9.refs_11_.refs_3_ = f32[1,8,1024]{2,1,0:T(8,128)S(1)} collective-permute-done((f32[1,8,1024]{2,1,0:T(8,128)S(1)}, f32[1,8,1024]{2,1,0:T(8,128)S(1)}, u32[]{:S(2)}, u32[]{:S(2)}) %collective-permute-start.9) | collective-permute-done | bytes 32800 | tf_op jit(solution)/shard_map/ppermute | solution.py:59
  45.7 0.1 collective-permute-start.11
  45.8 1.6 %collective-permute-start.12 = (f32[4,8,1024]{2,1,0:T(8,128)S(1)}, f32[4,8,1024]{2,1,0:T(8,128)S(1)}, u32[]{:S(2)}, u32[]{:S(2)}) collective-permute-start(f32[4,8,1024]{2,1,0:T(8,128)S(1)} %pad_maximum_fusion.2), channel_id=1, source_target_pairs={{0,2},{1,3},{2,0},{3,1},{4,6},{5,7},{6,4},{7,5},{8,10},{9,11},{10,... | collective-permute-start | bytes 393224 | tf_op jit(solution)/shard_map/ppermute | solution.py:52
  47.3 1.7 %line_again.1.refs_1_ = f32[8,1024]{1,0:T(8,128)S(1)} custom-call(f32[8,1024]{1,0:T(8,128)S(1)} %pair_again.1.refs_0_, bf16[3,4,2048,256]{3,2,1,0:T(8,128)(2,1)S(1)} %get-tuple-element.62.refs_1_, f32[1,8,1024]{2,1,0:T(8,128)S(1)} %collective-permute-done.8.refs_10_.refs_2_, f32[1,8,1024]{2,1,0:T(8,128)S(1)} %collective-permute-done.9.refs_11_.refs_3_, ...), custom_call_target="tpu_custom_call" | custom-call | flops 6442450944 | bytes 1048576 | tf_op jit(solution)/shard_map/line_again/pallas_call | solution.py:331
  49.1 0.0 collective-permute-done.11.refs_3_.refs_13_.refs_4_
  49.1 1.5 %across_half.1.refs_1_ = f32[8,1024]{1,0:T(8,128)S(1)} custom-call(s32[1]{0:T(128)S(1)} %bitcast.18, bf16[64,1024]{1,0:T(8,128)(2,1)S(1)} %get-tuple-element.38.refs_1_.refs_0_.refs_3_.refs_2_, bf16[3,1024,64]{2,1,0:T(8,128)(2,1)S(1)} %get-tuple-element.56.refs_2_.refs_3_, f32[3,8,1024]{2,1,0:T(8,128)S(1)} %collective-permute-done.11.refs_3_.refs_13_.refs_4_), custom_call_target="tpu_custom_call" | custom-call | flops 2147483648 | bytes 1048576 | tf_op jit(solution)/shard_map/across_half/pallas_call | solution.py:331
  50.6 2.1 %across_once.1.refs_2_ = f32[8,1024]{1,0:T(8,128)S(1)} custom-call(s32[1]{0:T(128)} %slice.10.refs_0_, f32[8,1024]{1,0:T(8,128)S(1)} %line_again.1.refs_1_, bf16[64,1024]{1,0:T(8,128)(2,1)S(1)} %get-tuple-element.38.refs_1_.refs_0_.refs_3_.refs_2_, bf16[3,1024,64]{2,1,0:T(8,128)(2,1)S(1)} %get-tuple-element.56.refs_2_.refs_3_, ...), custom_call_target="tpu_custom_call" | custom-call | flops 2147483648 | bytes 1048576 | tf_op jit(solution)/shard_map/across_once/pallas_call | solution.py:331
  52.7 0.0 collective-permute-done.12.refs_14_.refs_5_
  52.7 0.2 collective-permute-start.13
  52.9 2.3 %beside_half.1.refs_1_ = f32[8,1024]{1,0:T(8,128)S(1)} custom-call(s32[2]{0:T(128)S(1)} %fusion.2.refs_0_, f32[8,1024]{1,0:T(8,128)S(1)} %across_half.1.refs_1_, bf16[2,4,2048,256]{3,2,1,0:T(8,128)(2,1)S(1)} %get-tuple-element.59.refs_2_, bf16[64,1024]{1,0:T(8,128)(2,1)S(1)} %get-tuple-element.38.refs_1_.refs_0_.refs_3_.refs_2_, ...), custom_call_target="tpu_custom_call" | custom-call | flops 4294967296 | bytes 1048576 | tf_op jit(solution)/shard_map/beside_half/pallas_call | solution.py:331
  55.2 0.0 collective-permute-done.13.refs_15_.refs_6_.refs_3_
  55.2 1.8 %far_half.1 = (f32[8,1024]{1,0:T(8,128)S(1)}, f32[8,128]{1,0:T(8,128)S(1)}) custom-call(s32[2]{0:T(128)S(1)} %fusion.3.refs_0_, f32[8,1024]{1,0:T(8,128)S(1)} %beside_half.1.refs_1_, f32[8,1024]{1,0:T(8,128)S(1)} %across_once.1.refs_2_, f32[1,1024]{1,0:T(1,128)S(1)} %bitcast.16, f32[1,8,1024]{2,1,0:T(8,128)S(1)} %bitcast.12, ...), custom_call_target="tpu_custom_call" | custom-call | flops 4294967296 | bytes 1048576 | tf_op jit(solution)/shard_map/far_half/pallas_call | solution.py:331
  57.1 0.9 %collective-permute-start.14 = (f32[8,128]{1,0:T(8,128)S(1)}, f32[8,128]{1,0:T(8,128)S(1)}, u32[]{:S(2)}, u32[]{:S(2)}) collective-permute-start(f32[8,128]{1,0:T(8,128)S(1)} %get-tuple-element.64), channel_id=1, source_target_pairs={{0,12},{1,13},{2,14},{3,15},{4,0},{5,1},{6,2},{7,3},{8,4},{9,5},{1... | collective-permute-start | bytes 12296 | tf_op jit(solution)/shard_map/ppermute | solution.py:59
  58.0 0.4 collective-permute-start.15
  58.4 1.8 %collective-permute-start.16 = (f32[8,128]{1,0:T(8,128)S(1)}, f32[8,128]{1,0:T(8,128)S(1)}, u32[]{:S(2)}, u32[]{:S(2)}) collective-permute-start(f32[8,128]{1,0:T(8,128)S(1)} %get-tuple-element.64), channel_id=1, source_target_pairs={{0,4},{1,5},{2,6},{3,7},{4,8},{5,9},{6,10},{7,11},{8,12},{9,13},{1... | collective-permute-start | bytes 12296 | tf_op jit(solution)/shard_map/ppermute | solution.py:59
  60.2 2.1 %across_rest.1.refs_1_ = f32[8,1024]{1,0:T(8,128)S(1)} custom-call(s32[1]{0:T(128)} %slice.11.refs_0_, f32[8,1024]{1,0:T(8,128)S(1)} %get-tuple-element.65.refs_1_, bf16[64,1024]{1,0:T(8,128)(2,1)S(1)} %get-tuple-element.38.refs_1_.refs_0_.refs_3_.refs_2_, bf16[3,1024,64]{2,1,0:T(8,128)(2,1)S(1)} %get-tuple-element.56.refs_2_.refs_3_, ...), custom_call_target="tpu_custom_call" | custom-call | flops 2147483648 | bytes 1048576 | tf_op jit(solution)/shard_map/across_rest/pallas_call | solution.py:331
  62.3 2.3 %beside_rest.1.refs_1_ = f32[8,1024]{1,0:T(8,128)S(1)} custom-call(s32[2]{0:T(128)S(1)} %fusion.1.refs_0_, f32[8,1024]{1,0:T(8,128)S(1)} %across_rest.1.refs_1_, bf16[2,4,2048,256]{3,2,1,0:T(8,128)(2,1)S(1)} %get-tuple-element.59.refs_2_, bf16[64,1024]{1,0:T(8,128)(2,1)S(1)} %get-tuple-element.38.refs_1_.refs_0_.refs_3_.refs_2_, ...), custom_call_target="tpu_custom_call" | custom-call | flops 4294967296 | bytes 1048576 | tf_op jit(solution)/shard_map/beside_rest/pallas_call | solution.py:331
  64.7 0.3 scalars.1.scalars_ref
  65.0 0.0 collective-permute-done.14
  65.0 0.0 collective-permute-done.15
  65.0 0.0 collective-permute-done.16
  65.0 0.1 collective-permute-start.17
  65.1 0.6 collective-permute-start.18
  65.7 1.3 %collective-permute-start.19 = (f32[8,128]{1,0:T(8,128)S(1)}, f32[8,128]{1,0:T(8,128)S(1)}, u32[]{:S(2)}, u32[]{:S(2)}) collective-permute-start(f32[8,128]{1,0:T(8,128)S(1)} %add_add_fusion.1), channel_id=1, source_target_pairs={{0,3},{1,2},{2,1},{3,0},{4,7},{5,6},{6,5},{7,4},{8,11},{9,10},{10,... | collective-permute-start | bytes 12296 | tf_op jit(solution)/shard_map/ppermute | solution.py:52
  67.0 1.7 %far_rest.1.total_ref = f32[8,1024]{1,0:T(8,128)S(1)} custom-call(s32[2]{0:T(128)S(1)} %fusion.refs_0_, f32[8,1024]{1,0:T(8,128)S(1)} %beside_rest.1.refs_1_, bf16[4,4,2048,256]{3,2,1,0:T(8,128)(2,1)S(1)} %get-tuple-element.63.refs_5_.refs_2_, f32[4,8,1024]{2,1,0:T(8,128)S(1)} %collective-permute-done.13.refs_15_.refs_6_.refs_3_), custom_call_target="tpu_custom_call" | custom-call | flops 4294967296 | bytes 1048576 | tf_op jit(solution)/shard_map/far_rest/pallas_call | solution.py:331
  68.7 0.0 collective-permute-done.17
  68.7 0.1 collective-permute-done.18
  68.8 0.0 collective-permute-done.19
  68.8 0.7 %last_update.1 = (f32[8,1024]{1,0:T(8,128)}, f32[8,1024]{1,0:T(8,128)}) custom-call(f32[4,8,128]{2,1,0:T(8,128)S(1)} %scalars.1.scalars_ref, f32[8,128]{1,0:T(8,128)S(1)} %add_add_fusion.form_ref, f32[8,1024]{1,0:T(8,128)S(1)} %far_rest.1.total_ref, f32[1,1024]{1,0:T(1,128)S(1)} %bitcast.17, ...), custom_call_target="tpu_custom_call" | custom-call | tf_op jit(solution)/shard_map/last_update/pallas_call | solution.py:440
  (13 shorter events, 0.1 us)
Async XLA Ops:
  1.4 9.7 %collective-permute-start = (f32[1,16,1024]{2,1,0:T(8,128)S(1)}, f32[1,16,1024]{2,1,0:T(8,128)S(1)}, u32[]{:S(2)}, u32[]{:S(2)}) collective-permute-start(f32[1,16,1024]{2,1,0:T(8,128)S(1)} %maximum_bitcast_fusion.refs_1_.refs_4_.refs_0_.mine_ref), channel_id=1, source_target_pairs={{0,1},{1,0},{2,3},{3,2},{4,5},{5,4},{6,7},{7,6},{8,9},{9,8},{10,11... | collective-permute-start | bytes 196616 | tf_op jit(solution)/shard_map/ppermute | solution.py:52
  1.9 10.9 %collective-permute-start.1 = (f32[1,16,1024]{2,1,0:T(8,128)S(1)}, f32[1,16,1024]{2,1,0:T(8,128)S(1)}, u32[]{:S(2)}, u32[]{:S(2)}) collective-permute-start(f32[1,16,1024]{2,1,0:T(8,128)S(1)} %maximum_bitcast_fusion.refs_1_.refs_4_.refs_0_.mine_ref), channel_id=1, source_target_pairs={{0,12},{1,13},{2,14},{3,15},{4,0},{5,1},{6,2},{7,3},{8,4},{9,5},{1... | collective-permute-start | bytes 196616 | tf_op jit(solution)/shard_map/ppermute | solution.py:59
  6.5 7.1 %collective-permute-start.2 = (f32[1,16,1024]{2,1,0:T(8,128)S(1)}, f32[1,16,1024]{2,1,0:T(8,128)S(1)}, u32[]{:S(2)}, u32[]{:S(2)}) collective-permute-start(f32[1,16,1024]{2,1,0:T(8,128)S(1)} %maximum_bitcast_fusion.refs_1_.refs_4_.refs_0_.mine_ref), channel_id=1, source_target_pairs={{0,8},{1,9},{2,10},{3,11},{4,12},{5,13},{6,14},{7,15},{8,0},{9,1},... | collective-permute-start | bytes 196616 | tf_op jit(solution)/shard_map/ppermute | solution.py:59
  6.5 7.1 %collective-permute-start.3 = (f32[1,16,1024]{2,1,0:T(8,128)S(1)}, f32[1,16,1024]{2,1,0:T(8,128)S(1)}, u32[]{:S(2)}, u32[]{:S(2)}) collective-permute-start(f32[1,16,1024]{2,1,0:T(8,128)S(1)} %maximum_bitcast_fusion.refs_1_.refs_4_.refs_0_.mine_ref), channel_id=1, source_target_pairs={{0,4},{1,5},{2,6},{3,7},{4,8},{5,9},{6,10},{7,11},{8,12},{9,13},{1... | collective-permute-start | bytes 196616 | tf_op jit(solution)/shard_map/ppermute | solution.py:59
  13.6 5.6 %collective-permute-start.4 = (f32[3,16,1024]{2,1,0:T(8,128)S(1)}, f32[3,16,1024]{2,1,0:T(8,128)S(1)}, u32[]{:S(2)}, u32[]{:S(2)}) collective-permute-start(f32[3,16,1024]{2,1,0:T(8,128)S(1)} %pad_maximum_fusion.1), channel_id=1, source_target_pairs={{0,1},{1,0},{2,3},{3,2},{4,5},{5,4},{6,7},{7,6},{8,9},{9,8},{10,11... | collective-permute-start | bytes 589832 | tf_op jit(solution)/shard_map/ppermute | solution.py:52
  17.6 8.8 %collective-permute-start.5 = (f32[4,16,1024]{2,1,0:T(8,128)S(1)}, f32[4,16,1024]{2,1,0:T(8,128)S(1)}, u32[]{:S(2)}, u32[]{:S(2)}) collective-permute-start(f32[4,16,1024]{2,1,0:T(8,128)S(1)} %pad_maximum_fusion), channel_id=1, source_target_pairs={{0,2},{1,3},{2,0},{3,1},{4,6},{5,7},{6,4},{7,5},{8,10},{9,11},{10,... | collective-permute-start | bytes 786440 | tf_op jit(solution)/shard_map/ppermute | solution.py:52
  26.4 5.2 %copy-start = (f32[1024]{0:T(1024)S(1)}, f32[1024]{0:T(1024)}, u32[]{:S(2)}) copy-start(f32[1024]{0:T(1024)} %param.6) | copy-start | bytes 12292
  26.4 5.1 %collective-permute-start.6 = (f32[4,16,1024]{2,1,0:T(8,128)S(1)}, f32[4,16,1024]{2,1,0:T(8,128)S(1)}, u32[]{:S(2)}, u32[]{:S(2)}) collective-permute-start(f32[4,16,1024]{2,1,0:T(8,128)S(1)} %collective-permute-done.5.refs_3_.refs_6_), channel_id=1, source_target_pairs={{0,1},{1,0},{2,3},{3,2},{4,5},{5,4},{6,7},{7,6},{8,9},{9,8},{10,11... | collective-permute-start | bytes 786440 | tf_op jit(solution)/shard_map/ppermute | solution.py:52
  36.5 5.8 %collective-permute-start.7 = (f32[1,8,1024]{2,1,0:T(8,128)S(1)}, f32[1,8,1024]{2,1,0:T(8,128)S(1)}, u32[]{:S(2)}, u32[]{:S(2)}) collective-permute-start(f32[1,8,1024]{2,1,0:T(8,128)S(1)} %bitcast.6), channel_id=1, source_target_pairs={{0,1},{1,0},{2,3},{3,2},{4,5},{5,4},{6,7},{7,6},{8,9},{9,8},{10,11... | collective-permute-start | bytes 98312 | tf_op jit(solution)/shard_map/ppermute | solution.py:52
  37.0 6.8 %collective-permute-start.10 = (f32[1,8,1024]{2,1,0:T(8,128)S(1)}, f32[1,8,1024]{2,1,0:T(8,128)S(1)}, u32[]{:S(2)}, u32[]{:S(2)}) collective-permute-start(f32[1,8,1024]{2,1,0:T(8,128)S(1)} %bitcast.7), channel_id=1, source_target_pairs={{0,4},{1,5},{2,6},{3,7},{4,8},{5,9},{6,10},{7,11},{8,12},{9,13},{1... | collective-permute-start | bytes 98312 | tf_op jit(solution)/shard_map/ppermute | solution.py:59
  38.7 5.1 %collective-permute-start.8 = (f32[1,8,1024]{2,1,0:T(8,128)S(1)}, f32[1,8,1024]{2,1,0:T(8,128)S(1)}, u32[]{:S(2)}, u32[]{:S(2)}) collective-permute-start(f32[1,8,1024]{2,1,0:T(8,128)S(1)} %bitcast.8), channel_id=1, source_target_pairs={{0,12},{1,13},{2,14},{3,15},{4,0},{5,1},{6,2},{7,3},{8,4},{9,5},{1... | collective-permute-start | bytes 98312 | tf_op jit(solution)/shard_map/ppermute | solution.py:59
  40.8 4.8 %collective-permute-start.9 = (f32[1,8,1024]{2,1,0:T(8,128)S(1)}, f32[1,8,1024]{2,1,0:T(8,128)S(1)}, u32[]{:S(2)}, u32[]{:S(2)}) collective-permute-start(f32[1,8,1024]{2,1,0:T(8,128)S(1)} %bitcast.9), channel_id=1, source_target_pairs={{0,8},{1,9},{2,10},{3,11},{4,12},{5,13},{6,14},{7,15},{8,0},{9,1},... | collective-permute-start | bytes 98312 | tf_op jit(solution)/shard_map/ppermute | solution.py:59
  45.7 3.4 %collective-permute-start.11 = (f32[3,8,1024]{2,1,0:T(8,128)S(1)}, f32[3,8,1024]{2,1,0:T(8,128)S(1)}, u32[]{:S(2)}, u32[]{:S(2)}) collective-permute-start(f32[3,8,1024]{2,1,0:T(8,128)S(1)} %pad_maximum_fusion.3), channel_id=1, source_target_pairs={{0,1},{1,0},{2,3},{3,2},{4,5},{5,4},{6,7},{7,6},{8,9},{9,8},{10,11... | collective-permute-start | bytes 294920 | tf_op jit(solution)/shard_map/ppermute | solution.py:52
  45.8 7.0 %collective-permute-start.12 = (f32[4,8,1024]{2,1,0:T(8,128)S(1)}, f32[4,8,1024]{2,1,0:T(8,128)S(1)}, u32[]{:S(2)}, u32[]{:S(2)}) collective-permute-start(f32[4,8,1024]{2,1,0:T(8,128)S(1)} %pad_maximum_fusion.2), channel_id=1, source_target_pairs={{0,2},{1,3},{2,0},{3,1},{4,6},{5,7},{6,4},{7,5},{8,10},{9,11},{10,... | collective-permute-start | bytes 393224 | tf_op jit(solution)/shard_map/ppermute | solution.py:52
  52.7 2.5 %collective-permute-start.13 = (f32[4,8,1024]{2,1,0:T(8,128)S(1)}, f32[4,8,1024]{2,1,0:T(8,128)S(1)}, u32[]{:S(2)}, u32[]{:S(2)}) collective-permute-start(f32[4,8,1024]{2,1,0:T(8,128)S(1)} %collective-permute-done.12.refs_14_.refs_5_), channel_id=1, source_target_pairs={{0,1},{1,0},{2,3},{3,2},{4,5},{5,4},{6,7},{7,6},{8,9},{9,8},{10,11... | collective-permute-start | bytes 393224 | tf_op jit(solution)/shard_map/ppermute | solution.py:52
  57.1 7.9 %collective-permute-start.14 = (f32[8,128]{1,0:T(8,128)S(1)}, f32[8,128]{1,0:T(8,128)S(1)}, u32[]{:S(2)}, u32[]{:S(2)}) collective-permute-start(f32[8,128]{1,0:T(8,128)S(1)} %get-tuple-element.64), channel_id=1, source_target_pairs={{0,12},{1,13},{2,14},{3,15},{4,0},{5,1},{6,2},{7,3},{8,4},{9,5},{1... | collective-permute-start | bytes 12296 | tf_op jit(solution)/shard_map/ppermute | solution.py:59
  58.0 7.0 %collective-permute-start.15 = (f32[8,128]{1,0:T(8,128)S(1)}, f32[8,128]{1,0:T(8,128)S(1)}, u32[]{:S(2)}, u32[]{:S(2)}) collective-permute-start(f32[8,128]{1,0:T(8,128)S(1)} %get-tuple-element.64), channel_id=1, source_target_pairs={{0,8},{1,9},{2,10},{3,11},{4,12},{5,13},{6,14},{7,15},{8,0},{9,1},... | collective-permute-start | bytes 12296 | tf_op jit(solution)/shard_map/ppermute | solution.py:59
  58.4 6.6 %collective-permute-start.16 = (f32[8,128]{1,0:T(8,128)S(1)}, f32[8,128]{1,0:T(8,128)S(1)}, u32[]{:S(2)}, u32[]{:S(2)}) collective-permute-start(f32[8,128]{1,0:T(8,128)S(1)} %get-tuple-element.64), channel_id=1, source_target_pairs={{0,4},{1,5},{2,6},{3,7},{4,8},{5,9},{6,10},{7,11},{8,12},{9,13},{1... | collective-permute-start | bytes 12296 | tf_op jit(solution)/shard_map/ppermute | solution.py:59
  65.0 3.7 %collective-permute-start.17 = (f32[8,128]{1,0:T(8,128)S(1)}, f32[8,128]{1,0:T(8,128)S(1)}, u32[]{:S(2)}, u32[]{:S(2)}) collective-permute-start(f32[8,128]{1,0:T(8,128)S(1)} %add_add_fusion.1), channel_id=1, source_target_pairs={{0,1},{1,0},{2,3},{3,2},{4,5},{5,4},{6,7},{7,6},{8,9},{9,8},{10,11... | collective-permute-start | bytes 12296 | tf_op jit(solution)/shard_map/ppermute | solution.py:52
  65.1 3.7 %collective-permute-start.18 = (f32[8,128]{1,0:T(8,128)S(1)}, f32[8,128]{1,0:T(8,128)S(1)}, u32[]{:S(2)}, u32[]{:S(2)}) collective-permute-start(f32[8,128]{1,0:T(8,128)S(1)} %add_add_fusion.1), channel_id=1, source_target_pairs={{0,2},{1,3},{2,0},{3,1},{4,6},{5,7},{6,4},{7,5},{8,10},{9,11},{10,... | collective-permute-start | bytes 12296 | tf_op jit(solution)/shard_map/ppermute | solution.py:52
  65.7 3.1 %collective-permute-start.19 = (f32[8,128]{1,0:T(8,128)S(1)}, f32[8,128]{1,0:T(8,128)S(1)}, u32[]{:S(2)}, u32[]{:S(2)}) collective-permute-start(f32[8,128]{1,0:T(8,128)S(1)} %add_add_fusion.1), channel_id=1, source_target_pairs={{0,3},{1,2},{2,1},{3,0},{4,7},{5,6},{6,5},{7,4},{8,11},{9,10},{10,... | collective-permute-start | bytes 12296 | tf_op jit(solution)/shard_map/ppermute | solution.py:52

commit v16 on v15

--- a/solution.py
+++ b/solution.py
@@ -83,9 +83,22 @@
     return groups[:2] + [line, [across], beside], value
 
 
-def held_back(groups, value):
-    *beside, value = lax.optimization_barrier((*groups[4], value))
-    return groups[:4] + [beside, [swapped(g, 0, 0, 1) for g in beside]], value
+def gathered(value, done):
+    far, near = digits()
+    own = value[None]
+    line = [turned(own, by) for by in range(1, far)]
+    *line, done = lax.optimization_barrier((*line, done))
+    group = jnp.concatenate([own] + line, axis=0)
+    across = swapped(group, 0, 0, 1)
+    beside = [swapped(group, 0, by, 0) for by in range(1, near)]
+    return [[own], line, [across], beside], done
+
+
+def held_back(groups, *values):
+    near = len(groups[-1])
+    tied = lax.optimization_barrier((*groups[-1], *values))
+    beside = list(tied[:near])
+    return (groups[:-1] + [beside, [swapped(g, 0, 0, 1) for g in beside]], *tied[near:])
 
 
 def along_line(value):
@@ -110,6 +123,7 @@
             return k * far + picks + (side + flip) % 2
 
         return [
+            one(0, core),
             jnp.concatenate([one(k, side) for k, side in enumerate(sides)]),
             jnp.concatenate([one(k, core) for k in range(near - 1)]),
         ]
@@ -335,7 +349,7 @@
             scratch_shapes=scratch,
             compiler_params=pltpu.CompilerParams(vmem_limit_bytes=min(limit, 60 * MIB)),
             cost_estimate=pl.CostEstimate(
-                flops=2 * entries * 4 * TILE, bytes_accessed=1024 * width, transcendentals=entries
+                flops=2 * entries * TILE, bytes_accessed=1024 * width, transcendentals=0
             ),
             name=name,
         )(*operands)
@@ -381,7 +395,11 @@
             own, *made = made
         total, *sources = made
         prepared.append(sources)
-    images = neighbours(total)
+    images = [[total[None]]]
+    across_points = jnp.concatenate([prepared[1][0], prepared[3][0]], axis=0)
+    prepared = [prepared[0], prepared[2], [across_points]] + prepared[4:]
+    keep = [keep[0], keep[2], 0] + keep[4:]
+    sizes = [sizes[0], sizes[2], far] + sizes[4:]
     image = images[0][0]
 
     def again(group, out, name, sofar=(), table=None, form=()):
@@ -405,30 +423,28 @@
         )
 
     halves, rests = tables()
-    shifts = jnp.arange(far - 1, dtype=jnp.int32)
-    middle = far // 2 - 1
     once = again(0, field, "own_again")
-    once = again(1, field, "pair_again", sofar=(once,))
-    images, once = with_groups(images, once)
-    once = again(2, field, "line_again", sofar=(once,))
-    once = again(3, field, "across_once", sofar=(once,), table=shifts[middle : middle + 1])
-    half = again(3, field, "across_half", table=shifts[:middle])
-    images, half = held_back(images, half)
-    half = again(4, field, "beside_half", sofar=(half,), table=halves[0])
+    images, once = gathered(total, once)
+    once = again(1, field, "line_again", sofar=(once,))
+    half = again(2, field, "across_half", table=halves[0])
+    images, half, once = held_back(images, half, once)
+    half = again(3, field, "beside_half", sofar=(half,), table=halves[1])
     total, form = again(
-        5, (field, small), "far_half", sofar=(half,), table=halves[1], form=(once, noise, image)
+        4, (field, small), "far_half", sofar=(half,), table=halves[2], form=(once, noise, image)
     )
     parts = along_line(form)
-    total = again(3, field, "across_rest", sofar=(total,), table=shifts[middle + 1 :])
-    total = again(4, field, "beside_rest", sofar=(total,), table=rests[0])
+    total = again(2, field, "across_rest", sofar=(total,), table=rests[0])
+    total = again(3, field, "beside_rest", sofar=(total,), table=rests[1])
     *parts, total = lax.optimization_barrier((*parts, total))
     form = sum(parts, form)
     parts = over_quad(form)
-    total = again(5, field, "far_rest", sofar=(total,), table=rests[1])
+    total = again(4, field, "far_rest", sofar=(total,), table=rests[2])
     *parts, total = lax.optimization_barrier((*parts, total))
     form = sum(parts, form)
     flat = [s for g in groups for s in g]
-    flat_images = [s for g in images for s in g]
+    own_images, line_images, (core_image,), beside_images, far_images = images
+    flat_images = own_images + [core_image[:1]] + line_images + [core_image[1:]]
+    flat_images += beside_images + far_images
     scalars = pl.pallas_call(
         functools.partial(scalars_kernel, nfeat, len(flat)),
         out_shape=jax.ShapeDtypeStruct((4, nrhs, 128), F32),

time: 69.7 us -> 65.6 us (0.941)
  starting transfers between devices: 19 us -> 17.6 us
  local copies, waits for them, and re-layouts: 1.94 us -> 0.89 us
  Pallas kernels: 40.8 us -> 39.8 us
    ppermute x11 -> x10, waiting for transfers between devices: 3.4 us -> 1.01 us  [swapped(): return lax.ppermute(value, 'row', [(i, i ^ by) for i in range(length)])]
    ppermute x9, waiting for transfers between devices: 2.71 us -> 4.43 us  [turned(): lax.ppermute(value, 'row', [(i, (i - by * step) % length) for i in range(...]
    ppermute x11 -> x10, starting transfers between devices: 6.41 us -> 5.08 us  [swapped(): return lax.ppermute(value, 'row', [(i, i ^ by) for i in range(length)])]
    slice x2, local copies, waits for them, and re-layouts: 1.18 us -> 0.01 us  [shards(): flat_images = own_images + [core_image[:1]] + line_images + [core_image[1:]]]
    pallas_call x16 -> x14, Pallas kernels: 39.8 us -> 38.8 us  [call(): pl.pallas_call(kernel, out_shape=out_shape, in_specs=[smem if table and k...]
  transfers between devices with their start and end apart: 20 -> 19, of which waited for: 4 -> 6; matrix products, arithmetic and copies ran while one was open for 3% -> 1% of each run, Pallas kernels for 48% -> 49%
where the time goes in v16:
time: 65.6 us; the launch traced here: 65.4 us
  Pallas kernels  39.8 us (61%)
  starting transfers between devices  17.6 us (27%)
  waiting for transfers between devices  5.44 us (8%)
  local copies, waits for them, and re-layouts  0.89 us (1%)
  other arithmetic  0.85 us (1%)
  between operations  0.75 us (1%)
    pallas_call x14, Pallas kernels, call(): pl.pallas_call(kernel, out_shape=out_shape, in_specs=[smem if table and k...  38.8 us
    ppermute x9, starting transfers between devices, turned(): lax.ppermute(value, 'row', [(i, (i - by * step) % length) for i in range(...  12.5 us
    ppermute x10, starting transfers between devices, swapped(): return lax.ppermute(value, 'row', [(i, i ^ by) for i in range(length)])  5.08 us
    ppermute x9, waiting for transfers between devices, turned(): lax.ppermute(value, 'row', [(i, (i - by * step) % length) for i in range(...  4.43 us
  transfers between devices with their start and end apart: 19, of which 6 were waited for; matrix products, arithmetic and copies ran while one was open for 1% of the time, Pallas kernels for 49%

profile of v16, /device:TPU:0, one launch (start us, length us, event | category | flops | bytes accessed | tf_op | source)
XLA Modules:
  0.0 65.4 jit_solution(17828090813548890908)
XLA Ops:
  0.6 0.8 %maximum_bitcast_fusion.refs_1_.refs_4_.refs_0_.mine_ref = f32[1,16,1024]{2,1,0:T(8,128)S(1)} fusion(f32[8,1024]{1,0:T(8,128)} %param.7, f32[8,1024]{1,0:T(8,128)} %param.4), kind=kLoop, calls=%fused_computation.3 | loop fusion | flops 16384 | bytes 131072 | tf_op jit(solution)/shard_map/broadcast_in_dim | solution.py:72
  1.4 0.5 collective-permute-start
  1.9 4.7 %collective-permute-start.1 = (f32[1,16,1024]{2,1,0:T(8,128)S(1)}, f32[1,16,1024]{2,1,0:T(8,128)S(1)}, u32[]{:S(2)}, u32[]{:S(2)}) collective-permute-start(f32[1,16,1024]{2,1,0:T(8,128)S(1)} %maximum_bitcast_fusion.refs_1_.refs_4_.refs_0_.mine_ref), channel_id=1, source_target_pairs={{0,12},{1,13},{2,14},{3,15},{4,0},{5,1},{6,2},{7,3},{8,4},{9,5},{1... | collective-permute-start | bytes 196616 | tf_op jit(solution)/shard_map/ppermute | solution.py:59
  6.5 0.0 collective-permute-start.2
  6.5 1.0 %collective-permute-start.3 = (f32[1,16,1024]{2,1,0:T(8,128)S(1)}, f32[1,16,1024]{2,1,0:T(8,128)S(1)}, u32[]{:S(2)}, u32[]{:S(2)}) collective-permute-start(f32[1,16,1024]{2,1,0:T(8,128)S(1)} %maximum_bitcast_fusion.refs_1_.refs_4_.refs_0_.mine_ref), channel_id=1, source_target_pairs={{0,4},{1,5},{2,6},{3,7},{4,8},{5,9},{6,10},{7,11},{8,12},{9,13},{1... | collective-permute-start | bytes 196616 | tf_op jit(solution)/shard_map/ppermute | solution.py:59
  7.5 0.7 %copy.7.refs_0_ = f32[8,1]{1,0:T(8,128)S(1)} copy(f32[8,1]{0,1:T(1,128)} %bitcast.16) | data formatting | bytes 64 | tf_op jit(solution)/shard_map/broadcast_in_dim | solution.py:329
  8.3 1.6 %blocks_0.1 = (bf16[64,1024]{1,0:T(8,128)(2,1)S(1)}, f32[8,1024]{1,0:T(8,128)S(1)}, bf16[1,1024,64]{2,1,0:T(8,128)(2,1)S(1)}) custom-call(f32[8,1]{1,0:T(8,128)S(1)} %copy.7.refs_0_, f32[1,16,1024]{2,1,0:T(8,128)S(1)} %maximum_bitcast_fusion.refs_1_.refs_4_.refs_0_.mine_ref), custom_call_target="tpu_custom_call" | custom-call | flops 536870912 | bytes 1048576 | tf_op jit(solution)/shard_map/blocks_0/pallas_call | solution.py:345
  9.9 0.0 copy-start
  9.9 0.0 collective-permute-done.refs_3_.refs_1_
  9.9 1.7 %blocks_1.1 = (f32[8,1024]{1,0:T(8,128)S(1)}, bf16[1,1024,64]{2,1,0:T(8,128)(2,1)S(1)}) custom-call(f32[8,1]{1,0:T(8,128)S(1)} %copy.7.refs_0_, bf16[64,1024]{1,0:T(8,128)(2,1)S(1)} %get-tuple-element.39.refs_1_.refs_0_.refs_3_.refs_2_, f32[8,1024]{1,0:T(8,128)S(1)} %get-tuple-element.40.refs_2_, f32[1,16,1024]{2,1,0:T(8,128)S(1)} %collective-permute-done.refs_3_.refs_1_), custom_call_target="tpu_custom_call" | custom-call | flops 536870912 | bytes 1048576 | tf_op jit(solution)/shard_map/blocks_1/pallas_call | solution.py:345
  11.6 0.0 collective-permute-done.1.refs_3_.refs_2_
  11.6 2.0 %collective-permute-done.2.refs_4_.refs_3_ = f32[1,16,1024]{2,1,0:T(8,128)S(1)} collective-permute-done((f32[1,16,1024]{2,1,0:T(8,128)S(1)}, f32[1,16,1024]{2,1,0:T(8,128)S(1)}, u32[]{:S(2)}, u32[]{:S(2)}) %collective-permute-start.2) | collective-permute-done | bytes 65568 | tf_op jit(solution)/shard_map/ppermute | solution.py:59
  13.6 0.0 collective-permute-done.3.refs_5_.refs_4_
  13.7 0.1 collective-permute-start.4
  13.7 1.6 %collective-permute-start.5 = (f32[4,16,1024]{2,1,0:T(8,128)S(1)}, f32[4,16,1024]{2,1,0:T(8,128)S(1)}, u32[]{:S(2)}, u32[]{:S(2)}) collective-permute-start(f32[4,16,1024]{2,1,0:T(8,128)S(1)} %pad_maximum_fusion), channel_id=1, source_target_pairs={{0,2},{1,3},{2,0},{3,1},{4,6},{5,7},{6,4},{7,5},{8,10},{9,11},{10,... | collective-permute-start | bytes 786440 | tf_op jit(solution)/shard_map/ppermute | solution.py:52
  15.3 3.8 %blocks_2.1 = (f32[8,1024]{1,0:T(8,128)S(1)}, bf16[3,4,2048,256]{3,2,1,0:T(8,128)(2,1)S(1)}) custom-call(f32[8,1]{1,0:T(8,128)S(1)} %copy.7.refs_0_, bf16[64,1024]{1,0:T(8,128)(2,1)S(1)} %get-tuple-element.39.refs_1_.refs_0_.refs_3_.refs_2_, f32[8,1024]{1,0:T(8,128)S(1)} %get-tuple-element.45.refs_2_, ...), custom_call_target="tpu_custom_call" | custom-call | flops 1610612736 | bytes 1048576 | tf_op jit(solution)/shard_map/blocks_2/pallas_call | solution.py:345
  19.2 0.0 collective-permute-done.4.refs_3_.refs_5_
  19.2 3.9 %blocks_3.1 = (f32[8,1024]{1,0:T(8,128)S(1)}, bf16[3,1024,64]{2,1,0:T(8,128)(2,1)S(1)}) custom-call(f32[8,1]{1,0:T(8,128)S(1)} %copy.7.refs_0_, bf16[64,1024]{1,0:T(8,128)(2,1)S(1)} %get-tuple-element.39.refs_1_.refs_0_.refs_3_.refs_2_, f32[8,1024]{1,0:T(8,128)S(1)} %get-tuple-element.46.refs_2_, f32[3,16,1024]{2,1,0:T(8,128)S(1)} %collective-permute-done.4.refs_3_.refs_5_), custom_call_target="tpu_custom_call" | custom-call | flops 1610612736 | bytes 1048576 | tf_op jit(solution)/shard_map/blocks_3/pallas_call | solution.py:345
  23.1 0.0 collective-permute-done.5.refs_3_.refs_6_
  23.1 0.2 collective-permute-start.6
  23.3 0.1 constant_dynamic-update-slice_fusion.refs_2_.refs_3_
  23.4 5.1 %blocks_4.1 = (f32[8,1024]{1,0:T(8,128)S(1)}, bf16[2,4,2048,256]{3,2,1,0:T(8,128)(2,1)S(1)}, bf16[2,1024,64]{2,1,0:T(8,128)(2,1)S(1)}) custom-call(f32[8,1]{1,0:T(8,128)S(1)} %copy.7.refs_0_, bf16[64,1024]{1,0:T(8,128)(2,1)S(1)} %get-tuple-element.39.refs_1_.refs_0_.refs_3_.refs_2_, f32[8,1024]{1,0:T(8,128)S(1)} %get-tuple-element.49.refs_2_, ...), custom_call_target="tpu_custom_call" | custom-call | flops 2147483648 | bytes 1048576 | tf_op jit(solution)/shard_map/blocks_4/pallas_call | solution.py:345
  28.5 0.0 collective-permute-done.6.refs_5_.refs_7_
  28.5 0.0 copy-done
  28.6 4.9 %blocks_5.1 = (f32[8,1024]{1,0:T(8,128)S(1)}, bf16[4,4,2048,256]{3,2,1,0:T(8,128)(2,1)S(1)}) custom-call(f32[8,1]{1,0:T(8,128)S(1)} %copy.7.refs_0_, bf16[64,1024]{1,0:T(8,128)(2,1)S(1)} %get-tuple-element.39.refs_1_.refs_0_.refs_3_.refs_2_, f32[8,1024]{1,0:T(8,128)S(1)} %get-tuple-element.50.refs_2_, f32[1,1024]{1,0:T(1,128)S(1)} %bitcast.13, ...), custom_call_target="tpu_custom_call" | custom-call | flops 2147483648 | bytes 1048576 | tf_op jit(solution)/shard_map/blocks_5/pallas_call | solution.py:345
  33.5 1.9 %collective-permute-start.7 = (f32[1,8,1024]{2,1,0:T(8,128)S(1)}, f32[1,8,1024]{2,1,0:T(8,128)S(1)}, u32[]{:S(2)}, u32[]{:S(2)}) collective-permute-start(f32[1,8,1024]{2,1,0:T(8,128)S(1)} %bitcast.5), channel_id=1, source_target_pairs={{0,12},{1,13},{2,14},{3,15},{4,0},{5,1},{6,2},{7,3},{8,4},{9,5},{1... | collective-permute-start | bytes 98312 | tf_op jit(solution)/shard_map/ppermute | solution.py:59
  35.4 0.1 collective-permute-start.8
  35.5 1.8 %collective-permute-start.9 = (f32[1,8,1024]{2,1,0:T(8,128)S(1)}, f32[1,8,1024]{2,1,0:T(8,128)S(1)}, u32[]{:S(2)}, u32[]{:S(2)}) collective-permute-start(f32[1,8,1024]{2,1,0:T(8,128)S(1)} %bitcast.7), channel_id=1, source_target_pairs={{0,4},{1,5},{2,6},{3,7},{4,8},{5,9},{6,10},{7,11},{8,12},{9,13},{1... | collective-permute-start | bytes 98312 | tf_op jit(solution)/shard_map/ppermute | solution.py:59
  37.3 1.5 %own_again.1.refs_0_ = f32[8,1024]{1,0:T(8,128)S(1)} custom-call(bf16[64,1024]{1,0:T(8,128)(2,1)S(1)} %get-tuple-element.39.refs_1_.refs_0_.refs_3_.refs_2_, bf16[1,1024,64]{2,1,0:T(8,128)(2,1)S(1)} %get-tuple-element.52.refs_1_, f32[1,8,1024]{2,1,0:T(8,128)S(1)} %bitcast.8), custom_call_target="tpu_custom_call" | custom-call | flops 536870912 | bytes 1048576 | tf_op jit(solution)/shard_map/own_again/pallas_call | solution.py:345
  38.8 0.0 collective-permute-done.7.refs_2_.refs_10_
  38.8 1.8 %collective-permute-done.8.refs_3_.refs_11_ = f32[1,8,1024]{2,1,0:T(8,128)S(1)} collective-permute-done((f32[1,8,1024]{2,1,0:T(8,128)S(1)}, f32[1,8,1024]{2,1,0:T(8,128)S(1)}, u32[]{:S(2)}, u32[]{:S(2)}) %collective-permute-start.8) | collective-permute-done | bytes 32800 | tf_op jit(solution)/shard_map/ppermute | solution.py:59
  40.6 0.6 collective-permute-done.9.refs_4_.refs_12_
  41.2 0.1 collective-permute-start.10
  41.3 0.8 %collective-permute-start.11 = (f32[4,8,1024]{2,1,0:T(8,128)S(1)}, f32[4,8,1024]{2,1,0:T(8,128)S(1)}, u32[]{:S(2)}, u32[]{:S(2)}) collective-permute-start(f32[4,8,1024]{2,1,0:T(8,128)S(1)} %pad_maximum_fusion.2), channel_id=1, source_target_pairs={{0,2},{1,3},{2,0},{3,1},{4,6},{5,7},{6,4},{7,5},{8,10},{9,11},{10,... | collective-permute-start | bytes 393224 | tf_op jit(solution)/shard_map/ppermute | solution.py:52
  42.1 1.7 %line_again.1.refs_2_ = f32[8,1024]{1,0:T(8,128)S(1)} custom-call(f32[8,1024]{1,0:T(8,128)S(1)} %own_again.1.refs_0_, bf16[3,4,2048,256]{3,2,1,0:T(8,128)(2,1)S(1)} %get-tuple-element.59.refs_1_, f32[1,8,1024]{2,1,0:T(8,128)S(1)} %collective-permute-done.7.refs_2_.refs_10_, f32[1,8,1024]{2,1,0:T(8,128)S(1)} %collective-permute-done.8.refs_3_.refs_11_, ...), custom_call_target="tpu_custom_call" | custom-call | flops 1610612736 | bytes 1048576 | tf_op jit(solution)/shard_map/line_again/pallas_call | solution.py:345
  43.8 0.0 collective-permute-done.10.refs_3_.refs_4_
  43.8 3.1 %across_half.1.refs_1_ = f32[8,1024]{1,0:T(8,128)S(1)} custom-call(s32[2]{0:T(128)S(1)} %fusion.3.refs_0_, bf16[64,1024]{1,0:T(8,128)(2,1)S(1)} %get-tuple-element.39.refs_1_.refs_0_.refs_3_.refs_2_, bf16[4,1024,64]{2,1,0:T(8,128)(2,1)S(1)} %constant_dynamic-update-slice_fusion.refs_2_.refs_3_, f32[4,8,1024]{2,1,0:T(8,128)S(1)} %collective-permute-done.10.refs_3_.refs_4_), custom_call_target="tpu_custom_call" | custom-call | flops 1073741824 | bytes 1048576 | tf_op jit(solution)/shard_map/across_half/pallas_call | solution.py:345
  46.9 0.3 collective-permute-done.11.refs_14_.refs_5_
  47.2 0.0 collective-permute-start.12
  47.2 2.3 %beside_half.1.refs_1_ = f32[8,1024]{1,0:T(8,128)S(1)} custom-call(s32[2]{0:T(128)S(1)} %fusion.2.refs_0_, f32[8,1024]{1,0:T(8,128)S(1)} %across_half.1.refs_1_, bf16[2,4,2048,256]{3,2,1,0:T(8,128)(2,1)S(1)} %get-tuple-element.62.refs_2_, bf16[64,1024]{1,0:T(8,128)(2,1)S(1)} %get-tuple-element.39.refs_1_.refs_0_.refs_3_.refs_2_, ...), custom_call_target="tpu_custom_call" | custom-call | flops 1073741824 | bytes 1048576 | tf_op jit(solution)/shard_map/beside_half/pallas_call | solution.py:345
  49.6 0.0 collective-permute-done.12.refs_15_.refs_6_.refs_3_
  49.6 1.8 %far_half.1 = (f32[8,1024]{1,0:T(8,128)S(1)}, f32[8,128]{1,0:T(8,128)S(1)}) custom-call(s32[2]{0:T(128)S(1)} %fusion.3.refs_0_, f32[8,1024]{1,0:T(8,128)S(1)} %beside_half.1.refs_1_, f32[8,1024]{1,0:T(8,128)S(1)} %line_again.1.refs_2_, f32[1,1024]{1,0:T(1,128)S(1)} %bitcast.14, f32[1,8,1024]{2,1,0:T(8,128)S(1)} %bitcast.10, ...), custom_call_target="tpu_custom_call" | custom-call | flops 1073741824 | bytes 1048576 | tf_op jit(solution)/shard_map/far_half/pallas_call | solution.py:345
  51.4 1.2 %collective-permute-start.13 = (f32[8,128]{1,0:T(8,128)S(1)}, f32[8,128]{1,0:T(8,128)S(1)}, u32[]{:S(2)}, u32[]{:S(2)}) collective-permute-start(f32[8,128]{1,0:T(8,128)S(1)} %get-tuple-element.66), channel_id=1, source_target_pairs={{0,12},{1,13},{2,14},{3,15},{4,0},{5,1},{6,2},{7,3},{8,4},{9,5},{1... | collective-permute-start | bytes 12296 | tf_op jit(solution)/shard_map/ppermute | solution.py:59
  52.6 0.3 collective-permute-start.14
  52.9 1.6 %collective-permute-start.15 = (f32[8,128]{1,0:T(8,128)S(1)}, f32[8,128]{1,0:T(8,128)S(1)}, u32[]{:S(2)}, u32[]{:S(2)}) collective-permute-start(f32[8,128]{1,0:T(8,128)S(1)} %get-tuple-element.66), channel_id=1, source_target_pairs={{0,4},{1,5},{2,6},{3,7},{4,8},{5,9},{6,10},{7,11},{8,12},{9,13},{1... | collective-permute-start | bytes 12296 | tf_op jit(solution)/shard_map/ppermute | solution.py:59
  54.5 3.1 %across_rest.1.refs_1_ = f32[8,1024]{1,0:T(8,128)S(1)} custom-call(s32[2]{0:T(128)S(1)} %fusion.refs_0_, f32[8,1024]{1,0:T(8,128)S(1)} %get-tuple-element.67.refs_1_, bf16[64,1024]{1,0:T(8,128)(2,1)S(1)} %get-tuple-element.39.refs_1_.refs_0_.refs_3_.refs_2_, bf16[4,1024,64]{2,1,0:T(8,128)(2,1)S(1)} %constant_dynamic-update-slice_fusion.refs_2_.refs_3_, ...), custom_call_target="tpu_custom_call" | custom-call | flops 1073741824 | bytes 1048576 | tf_op jit(solution)/shard_map/across_rest/pallas_call | solution.py:345
  57.6 2.3 %beside_rest.1.refs_1_ = f32[8,1024]{1,0:T(8,128)S(1)} custom-call(s32[2]{0:T(128)S(1)} %fusion.1.refs_0_, f32[8,1024]{1,0:T(8,128)S(1)} %across_rest.1.refs_1_, bf16[2,4,2048,256]{3,2,1,0:T(8,128)(2,1)S(1)} %get-tuple-element.62.refs_2_, bf16[64,1024]{1,0:T(8,128)(2,1)S(1)} %get-tuple-element.39.refs_1_.refs_0_.refs_3_.refs_2_, ...), custom_call_target="tpu_custom_call" | custom-call | flops 1073741824 | bytes 1048576 | tf_op jit(solution)/shard_map/beside_rest/pallas_call | solution.py:345
  59.9 0.4 scalars.1.scalars_ref
  60.3 0.0 collective-permute-done.13
  60.3 0.0 collective-permute-done.14
  60.3 0.0 collective-permute-done.15
  60.3 0.1 collective-permute-start.16
  60.4 1.3 %collective-permute-start.17 = (f32[8,128]{1,0:T(8,128)S(1)}, f32[8,128]{1,0:T(8,128)S(1)}, u32[]{:S(2)}, u32[]{:S(2)}) collective-permute-start(f32[8,128]{1,0:T(8,128)S(1)} %add_add_fusion.1), channel_id=1, source_target_pairs={{0,2},{1,3},{2,0},{3,1},{4,6},{5,7},{6,4},{7,5},{8,10},{9,11},{10,... | collective-permute-start | bytes 12296 | tf_op jit(solution)/shard_map/ppermute | solution.py:52
  61.7 0.6 collective-permute-start.18
  62.2 1.7 %far_rest.1.total_ref = f32[8,1024]{1,0:T(8,128)S(1)} custom-call(s32[2]{0:T(128)S(1)} %fusion.refs_0_, f32[8,1024]{1,0:T(8,128)S(1)} %beside_rest.1.refs_1_, bf16[4,4,2048,256]{3,2,1,0:T(8,128)(2,1)S(1)} %get-tuple-element.65.refs_5_.refs_2_, f32[4,8,1024]{2,1,0:T(8,128)S(1)} %collective-permute-done.12.refs_15_.refs_6_.refs_3_), custom_call_target="tpu_custom_call" | custom-call | flops 1073741824 | bytes 1048576 | tf_op jit(solution)/shard_map/far_rest/pallas_call | solution.py:345
  64.0 0.0 collective-permute-done.16
  64.0 0.1 collective-permute-done.17
  64.1 0.6 collective-permute-done.18
  64.7 0.7 %last_update.1 = (f32[8,1024]{1,0:T(8,128)}, f32[8,1024]{1,0:T(8,128)}) custom-call(f32[4,8,128]{2,1,0:T(8,128)S(1)} %scalars.1.scalars_ref, f32[8,128]{1,0:T(8,128)S(1)} %add_add_fusion.form_ref, f32[8,1024]{1,0:T(8,128)S(1)} %far_rest.1.total_ref, f32[1,1024]{1,0:T(1,128)S(1)} %bitcast.15, ...), custom_call_target="tpu_custom_call" | custom-call | tf_op jit(solution)/shard_map/last_update/pallas_call | solution.py:456
  (12 shorter events, 0.1 us)
Async XLA Ops:
  1.4 8.5 %collective-permute-start = (f32[1,16,1024]{2,1,0:T(8,128)S(1)}, f32[1,16,1024]{2,1,0:T(8,128)S(1)}, u32[]{:S(2)}, u32[]{:S(2)}) collective-permute-start(f32[1,16,1024]{2,1,0:T(8,128)S(1)} %maximum_bitcast_fusion.refs_1_.refs_4_.refs_0_.mine_ref), channel_id=1, source_target_pairs={{0,1},{1,0},{2,3},{3,2},{4,5},{5,4},{6,7},{7,6},{8,9},{9,8},{10,11... | collective-permute-start | bytes 196616 | tf_op jit(solution)/shard_map/ppermute | solution.py:52
  1.9 9.7 %collective-permute-start.1 = (f32[1,16,1024]{2,1,0:T(8,128)S(1)}, f32[1,16,1024]{2,1,0:T(8,128)S(1)}, u32[]{:S(2)}, u32[]{:S(2)}) collective-permute-start(f32[1,16,1024]{2,1,0:T(8,128)S(1)} %maximum_bitcast_fusion.refs_1_.refs_4_.refs_0_.mine_ref), channel_id=1, source_target_pairs={{0,12},{1,13},{2,14},{3,15},{4,0},{5,1},{6,2},{7,3},{8,4},{9,5},{1... | collective-permute-start | bytes 196616 | tf_op jit(solution)/shard_map/ppermute | solution.py:59
  6.5 7.1 %collective-permute-start.2 = (f32[1,16,1024]{2,1,0:T(8,128)S(1)}, f32[1,16,1024]{2,1,0:T(8,128)S(1)}, u32[]{:S(2)}, u32[]{:S(2)}) collective-permute-start(f32[1,16,1024]{2,1,0:T(8,128)S(1)} %maximum_bitcast_fusion.refs_1_.refs_4_.refs_0_.mine_ref), channel_id=1, source_target_pairs={{0,8},{1,9},{2,10},{3,11},{4,12},{5,13},{6,14},{7,15},{8,0},{9,1},... | collective-permute-start | bytes 196616 | tf_op jit(solution)/shard_map/ppermute | solution.py:59
  6.5 7.1 %collective-permute-start.3 = (f32[1,16,1024]{2,1,0:T(8,128)S(1)}, f32[1,16,1024]{2,1,0:T(8,128)S(1)}, u32[]{:S(2)}, u32[]{:S(2)}) collective-permute-start(f32[1,16,1024]{2,1,0:T(8,128)S(1)} %maximum_bitcast_fusion.refs_1_.refs_4_.refs_0_.mine_ref), channel_id=1, source_target_pairs={{0,4},{1,5},{2,6},{3,7},{4,8},{5,9},{6,10},{7,11},{8,12},{9,13},{1... | collective-permute-start | bytes 196616 | tf_op jit(solution)/shard_map/ppermute | solution.py:59
  9.9 18.6 %copy-start = (f32[1024]{0:T(1024)S(1)}, f32[1024]{0:T(1024)}, u32[]{:S(2)}) copy-start(f32[1024]{0:T(1024)} %param.6) | copy-start | bytes 12292
  13.7 5.6 %collective-permute-start.4 = (f32[3,16,1024]{2,1,0:T(8,128)S(1)}, f32[3,16,1024]{2,1,0:T(8,128)S(1)}, u32[]{:S(2)}, u32[]{:S(2)}) collective-permute-start(f32[3,16,1024]{2,1,0:T(8,128)S(1)} %pad_maximum_fusion.1), channel_id=1, source_target_pairs={{0,1},{1,0},{2,3},{3,2},{4,5},{5,4},{6,7},{7,6},{8,9},{9,8},{10,11... | collective-permute-start | bytes 589832 | tf_op jit(solution)/shard_map/ppermute | solution.py:52
  13.7 9.4 %collective-permute-start.5 = (f32[4,16,1024]{2,1,0:T(8,128)S(1)}, f32[4,16,1024]{2,1,0:T(8,128)S(1)}, u32[]{:S(2)}, u32[]{:S(2)}) collective-permute-start(f32[4,16,1024]{2,1,0:T(8,128)S(1)} %pad_maximum_fusion), channel_id=1, source_target_pairs={{0,2},{1,3},{2,0},{3,1},{4,6},{5,7},{6,4},{7,5},{8,10},{9,11},{10,... | collective-permute-start | bytes 786440 | tf_op jit(solution)/shard_map/ppermute | solution.py:52
  23.1 5.4 %collective-permute-start.6 = (f32[4,16,1024]{2,1,0:T(8,128)S(1)}, f32[4,16,1024]{2,1,0:T(8,128)S(1)}, u32[]{:S(2)}, u32[]{:S(2)}) collective-permute-start(f32[4,16,1024]{2,1,0:T(8,128)S(1)} %collective-permute-done.5.refs_3_.refs_6_), channel_id=1, source_target_pairs={{0,1},{1,0},{2,3},{3,2},{4,5},{5,4},{6,7},{7,6},{8,9},{9,8},{10,11... | collective-permute-start | bytes 786440 | tf_op jit(solution)/shard_map/ppermute | solution.py:52
  33.5 5.3 %collective-permute-start.7 = (f32[1,8,1024]{2,1,0:T(8,128)S(1)}, f32[1,8,1024]{2,1,0:T(8,128)S(1)}, u32[]{:S(2)}, u32[]{:S(2)}) collective-permute-start(f32[1,8,1024]{2,1,0:T(8,128)S(1)} %bitcast.5), channel_id=1, source_target_pairs={{0,12},{1,13},{2,14},{3,15},{4,0},{5,1},{6,2},{7,3},{8,4},{9,5},{1... | collective-permute-start | bytes 98312 | tf_op jit(solution)/shard_map/ppermute | solution.py:59
  35.4 5.2 %collective-permute-start.8 = (f32[1,8,1024]{2,1,0:T(8,128)S(1)}, f32[1,8,1024]{2,1,0:T(8,128)S(1)}, u32[]{:S(2)}, u32[]{:S(2)}) collective-permute-start(f32[1,8,1024]{2,1,0:T(8,128)S(1)} %bitcast.6), channel_id=1, source_target_pairs={{0,8},{1,9},{2,10},{3,11},{4,12},{5,13},{6,14},{7,15},{8,0},{9,1},... | collective-permute-start | bytes 98312 | tf_op jit(solution)/shard_map/ppermute | solution.py:59
  35.5 5.7 %collective-permute-start.9 = (f32[1,8,1024]{2,1,0:T(8,128)S(1)}, f32[1,8,1024]{2,1,0:T(8,128)S(1)}, u32[]{:S(2)}, u32[]{:S(2)}) collective-permute-start(f32[1,8,1024]{2,1,0:T(8,128)S(1)} %bitcast.7), channel_id=1, source_target_pairs={{0,4},{1,5},{2,6},{3,7},{4,8},{5,9},{6,10},{7,11},{8,12},{9,13},{1... | collective-permute-start | bytes 98312 | tf_op jit(solution)/shard_map/ppermute | solution.py:59
  41.2 2.6 %collective-permute-start.10 = (f32[4,8,1024]{2,1,0:T(8,128)S(1)}, f32[4,8,1024]{2,1,0:T(8,128)S(1)}, u32[]{:S(2)}, u32[]{:S(2)}) collective-permute-start(f32[4,8,1024]{2,1,0:T(8,128)S(1)} %pad_maximum_fusion.2), channel_id=1, source_target_pairs={{0,1},{1,0},{2,3},{3,2},{4,5},{5,4},{6,7},{7,6},{8,9},{9,8},{10,11... | collective-permute-start | bytes 393224 | tf_op jit(solution)/shard_map/ppermute | solution.py:52
  41.3 5.9 %collective-permute-start.11 = (f32[4,8,1024]{2,1,0:T(8,128)S(1)}, f32[4,8,1024]{2,1,0:T(8,128)S(1)}, u32[]{:S(2)}, u32[]{:S(2)}) collective-permute-start(f32[4,8,1024]{2,1,0:T(8,128)S(1)} %pad_maximum_fusion.2), channel_id=1, source_target_pairs={{0,2},{1,3},{2,0},{3,1},{4,6},{5,7},{6,4},{7,5},{8,10},{9,11},{10,... | collective-permute-start | bytes 393224 | tf_op jit(solution)/shard_map/ppermute | solution.py:52
  47.2 2.4 %collective-permute-start.12 = (f32[4,8,1024]{2,1,0:T(8,128)S(1)}, f32[4,8,1024]{2,1,0:T(8,128)S(1)}, u32[]{:S(2)}, u32[]{:S(2)}) collective-permute-start(f32[4,8,1024]{2,1,0:T(8,128)S(1)} %collective-permute-done.11.refs_14_.refs_5_), channel_id=1, source_target_pairs={{0,1},{1,0},{2,3},{3,2},{4,5},{5,4},{6,7},{7,6},{8,9},{9,8},{10,11... | collective-permute-start | bytes 393224 | tf_op jit(solution)/shard_map/ppermute | solution.py:52
  51.4 8.9 %collective-permute-start.13 = (f32[8,128]{1,0:T(8,128)S(1)}, f32[8,128]{1,0:T(8,128)S(1)}, u32[]{:S(2)}, u32[]{:S(2)}) collective-permute-start(f32[8,128]{1,0:T(8,128)S(1)} %get-tuple-element.66), channel_id=1, source_target_pairs={{0,12},{1,13},{2,14},{3,15},{4,0},{5,1},{6,2},{7,3},{8,4},{9,5},{1... | collective-permute-start | bytes 12296 | tf_op jit(solution)/shard_map/ppermute | solution.py:59
  52.6 7.6 %collective-permute-start.14 = (f32[8,128]{1,0:T(8,128)S(1)}, f32[8,128]{1,0:T(8,128)S(1)}, u32[]{:S(2)}, u32[]{:S(2)}) collective-permute-start(f32[8,128]{1,0:T(8,128)S(1)} %get-tuple-element.66), channel_id=1, source_target_pairs={{0,8},{1,9},{2,10},{3,11},{4,12},{5,13},{6,14},{7,15},{8,0},{9,1},... | collective-permute-start | bytes 12296 | tf_op jit(solution)/shard_map/ppermute | solution.py:59
  52.9 7.4 %collective-permute-start.15 = (f32[8,128]{1,0:T(8,128)S(1)}, f32[8,128]{1,0:T(8,128)S(1)}, u32[]{:S(2)}, u32[]{:S(2)}) collective-permute-start(f32[8,128]{1,0:T(8,128)S(1)} %get-tuple-element.66), channel_id=1, source_target_pairs={{0,4},{1,5},{2,6},{3,7},{4,8},{5,9},{6,10},{7,11},{8,12},{9,13},{1... | collective-permute-start | bytes 12296 | tf_op jit(solution)/shard_map/ppermute | solution.py:59
  60.3 3.7 %collective-permute-start.16 = (f32[8,128]{1,0:T(8,128)S(1)}, f32[8,128]{1,0:T(8,128)S(1)}, u32[]{:S(2)}, u32[]{:S(2)}) collective-permute-start(f32[8,128]{1,0:T(8,128)S(1)} %add_add_fusion.1), channel_id=1, source_target_pairs={{0,1},{1,0},{2,3},{3,2},{4,5},{5,4},{6,7},{7,6},{8,9},{9,8},{10,11... | collective-permute-start | bytes 12296 | tf_op jit(solution)/shard_map/ppermute | solution.py:52
  60.4 3.7 %collective-permute-start.17 = (f32[8,128]{1,0:T(8,128)S(1)}, f32[8,128]{1,0:T(8,128)S(1)}, u32[]{:S(2)}, u32[]{:S(2)}) collective-permute-start(f32[8,128]{1,0:T(8,128)S(1)} %add_add_fusion.1), channel_id=1, source_target_pairs={{0,2},{1,3},{2,0},{3,1},{4,6},{5,7},{6,4},{7,5},{8,10},{9,11},{10,... | collective-permute-start | bytes 12296 | tf_op jit(solution)/shard_map/ppermute | solution.py:52
  61.7 3.0 %collective-permute-start.18 = (f32[8,128]{1,0:T(8,128)S(1)}, f32[8,128]{1,0:T(8,128)S(1)}, u32[]{:S(2)}, u32[]{:S(2)}) collective-permute-start(f32[8,128]{1,0:T(8,128)S(1)} %add_add_fusion.1), channel_id=1, source_target_pairs={{0,3},{1,2},{2,1},{3,0},{4,7},{5,6},{6,5},{7,4},{8,11},{9,10},{10,... | collective-permute-start | bytes 12296 | tf_op jit(solution)/shard_map/ppermute | solution.py:52

commit v17 on v11

--- a/solution.py
+++ b/solution.py
@@ -12,8 +12,8 @@
 DEPTH = 64
 TILE = 256
 MIB = 1024 * 1024
-KEPT_ORDER = (0, 1, 4, 3, 2)
-KEPT_ROOM = 52 * MIB
+KEPT_ORDER = (2, 4, 3)
+KEPT_ROOM = 48 * MIB
 F32 = jnp.float32
 BF16 = jnp.bfloat16
 

time: 65.9 us -> 66.7 us (1.012)
  starting transfers between devices: 16.5 us -> 17.7 us
    ppermute x9, starting transfers between devices: 12.1 us -> 13 us  [turned(): lax.ppermute(value, 'row', [(i, (i - by * step) % length) for i in range(...]
    unnamed x6 -> x8, local copies, waits for them, and re-layouts: 1.98 us -> 1.55 us
  transfers between devices with their start and end apart: 18 -> 18, of which waited for: 6 -> 5; matrix products, arithmetic and copies ran while one was open for 1% -> 1% of each run, Pallas kernels for 47% -> 47%
where the time goes in v17:
time: 66.7 us; the launch traced here: 66.5 us
  Pallas kernels  38.5 us (58%)
  starting transfers between devices  17.7 us (27%)
  waiting for transfers between devices  6.44 us (10%)
  local copies, waits for them, and re-layouts  2.27 us (3%)
  other arithmetic  0.85 us (1%)
  between operations  0.8 us (1%)
    pallas_call x13, Pallas kernels, call(): pl.pallas_call(kernel, out_shape=out_shape, in_specs=[smem if table and k...  37.4 us
    ppermute x9, starting transfers between devices, turned(): lax.ppermute(value, 'row', [(i, (i - by * step) % length) for i in range(...  13 us
    ppermute x9, waiting for transfers between devices, turned(): lax.ppermute(value, 'row', [(i, (i - by * step) % length) for i in range(...  5.37 us
    ppermute x9, starting transfers between devices, swapped(): return lax.ppermute(value, 'row', [(i, i ^ by) for i in range(length)])  4.64 us
    unnamed x8, local copies, waits for them, and re-layouts  1.55 us
  transfers between devices with their start and end apart: 18, of which 5 were waited for; matrix products, arithmetic and copies ran while one was open for 1% of the time, Pallas kernels for 47%

profile of v17, /device:TPU:0, one launch (start us, length us, event | category | flops | bytes accessed | tf_op | source)
XLA Modules:
  0.0 66.5 jit_solution(1572588177137999335)
XLA Ops:
  0.6 0.8 %maximum_bitcast_fusion.refs_1_.refs_4_.refs_0_.mine_ref = f32[1,16,1024]{2,1,0:T(8,128)S(1)} fusion(f32[8,1024]{1,0:T(8,128)} %param.7, f32[8,1024]{1,0:T(8,128)} %param.4), kind=kLoop, calls=%fused_computation.2 | loop fusion | flops 16384 | bytes 131072 | tf_op jit(solution)/shard_map/broadcast_in_dim | solution.py:72
  1.4 5.0 %collective-permute-start = (f32[1,16,1024]{2,1,0:T(8,128)S(1)}, f32[1,16,1024]{2,1,0:T(8,128)S(1)}, u32[]{:S(2)}, u32[]{:S(2)}) collective-permute-start(f32[1,16,1024]{2,1,0:T(8,128)S(1)} %maximum_bitcast_fusion.refs_1_.refs_4_.refs_0_.mine_ref), channel_id=1, source_target_pairs={{0,12},{1,13},{2,14},{3,15},{4,0},{5,1},{6,2},{7,3},{8,4},{9,5},{1... | collective-permute-start | bytes 196616 | tf_op jit(solution)/shard_map/ppermute | solution.py:59
  6.5 0.0 collective-permute-start.1
  6.5 1.0 %collective-permute-start.2 = (f32[1,16,1024]{2,1,0:T(8,128)S(1)}, f32[1,16,1024]{2,1,0:T(8,128)S(1)}, u32[]{:S(2)}, u32[]{:S(2)}) collective-permute-start(f32[1,16,1024]{2,1,0:T(8,128)S(1)} %maximum_bitcast_fusion.refs_1_.refs_4_.refs_0_.mine_ref), channel_id=1, source_target_pairs={{0,4},{1,5},{2,6},{3,7},{4,8},{5,9},{6,10},{7,11},{8,12},{9,13},{1... | collective-permute-start | bytes 196616 | tf_op jit(solution)/shard_map/ppermute | solution.py:59
  7.5 0.7 %copy.8.refs_0_ = f32[8,1]{1,0:T(8,128)S(1)} copy(f32[8,1]{0,1:T(1,128)} %bitcast.18) | data formatting | bytes 64 | tf_op jit(solution)/shard_map/broadcast_in_dim | solution.py:310
  8.2 1.6 %blocks_0.1 = (bf16[64,1024]{1,0:T(8,128)(2,1)S(1)}, f32[8,1024]{1,0:T(8,128)S(1)}, bf16[1,1024,64]{2,1,0:T(8,128)(2,1)S(1)}) custom-call(f32[8,1]{1,0:T(8,128)S(1)} %copy.8.refs_0_, f32[1,16,1024]{2,1,0:T(8,128)S(1)} %maximum_bitcast_fusion.refs_1_.refs_4_.refs_0_.mine_ref), custom_call_target="tpu_custom_call" | custom-call | flops 2147483648 | bytes 1048576 | tf_op jit(solution)/shard_map/blocks_0/pallas_call | solution.py:326
  9.9 0.0 collective-permute-done.refs_3_.refs_1_
  9.9 3.0 %collective-permute-done.1.refs_4_.refs_2_ = f32[1,16,1024]{2,1,0:T(8,128)S(1)} collective-permute-done((f32[1,16,1024]{2,1,0:T(8,128)S(1)}, f32[1,16,1024]{2,1,0:T(8,128)S(1)}, u32[]{:S(2)}, u32[]{:S(2)}) %collective-permute-start.1) | collective-permute-done | bytes 65568 | tf_op jit(solution)/shard_map/ppermute | solution.py:59
  12.9 0.0 collective-permute-done.2.refs_5_.refs_3_
  13.0 0.1 collective-permute-start.3
  13.0 1.6 %collective-permute-start.4 = (f32[4,16,1024]{2,1,0:T(8,128)S(1)}, f32[4,16,1024]{2,1,0:T(8,128)S(1)}, u32[]{:S(2)}, u32[]{:S(2)}) collective-permute-start(f32[4,16,1024]{2,1,0:T(8,128)S(1)} %pad_maximum_fusion), channel_id=1, source_target_pairs={{0,2},{1,3},{2,0},{3,1},{4,6},{5,7},{6,4},{7,5},{8,10},{9,11},{10,... | collective-permute-start | bytes 786440 | tf_op jit(solution)/shard_map/ppermute | solution.py:52
  14.6 3.9 %blocks_1.1 = (f32[8,1024]{1,0:T(8,128)S(1)}, bf16[3,1024,64]{2,1,0:T(8,128)(2,1)S(1)}) custom-call(f32[8,1]{1,0:T(8,128)S(1)} %copy.8.refs_0_, bf16[64,1024]{1,0:T(8,128)(2,1)S(1)} %get-tuple-element.28.refs_1_.refs_3_.refs_0_, f32[8,1024]{1,0:T(8,128)S(1)} %get-tuple-element.29.refs_2_, f32[1,16,1024]{2,1,0:T(8,128)S(1)} %collective-permute-done.refs_3_.refs_1_, ...), custom_call_target="tpu_custom_call" | custom-call | flops 6442450944 | bytes 1048576 | tf_op jit(solution)/shard_map/blocks_1/pallas_call | solution.py:326
  18.5 0.0 collective-permute-done.3.refs_3_.refs_4_
  18.5 5.0 %blocks_2.1 = (f32[8,1024]{1,0:T(8,128)S(1)}, bf16[4,4,2048,256]{3,2,1,0:T(8,128)(2,1)S(1)}) custom-call(f32[8,1]{1,0:T(8,128)S(1)} %copy.8.refs_0_, bf16[64,1024]{1,0:T(8,128)(2,1)S(1)} %get-tuple-element.28.refs_1_.refs_3_.refs_0_, f32[8,1024]{1,0:T(8,128)S(1)} %get-tuple-element.30.refs_2_, f32[4,16,1024]{2,1,0:T(8,128)S(1)} %collective-permute-done.3.refs_3_.refs_4_), custom_call_target="tpu_custom_call" | custom-call | flops 8589934592 | bytes 1048576 | tf_op jit(solution)/shard_map/blocks_2/pallas_call | solution.py:326
  23.5 0.0 copy-start
  23.5 0.0 collective-permute-done.4.refs_3_.refs_5_
  23.5 0.2 collective-permute-start.5
  23.7 5.1 %blocks_3.1 = (f32[8,1024]{1,0:T(8,128)S(1)}, bf16[2,4,2048,256]{3,2,1,0:T(8,128)(2,1)S(1)}, bf16[2,1024,64]{2,1,0:T(8,128)(2,1)S(1)}) custom-call(f32[8,1]{1,0:T(8,128)S(1)} %copy.8.refs_0_, bf16[64,1024]{1,0:T(8,128)(2,1)S(1)} %get-tuple-element.28.refs_1_.refs_3_.refs_0_, f32[8,1024]{1,0:T(8,128)S(1)} %get-tuple-element.33.refs_2_, ...), custom_call_target="tpu_custom_call" | custom-call | flops 8589934592 | bytes 1048576 | tf_op jit(solution)/shard_map/blocks_3/pallas_call | solution.py:326
  28.9 0.0 copy-start.1
  28.9 0.0 collective-permute-done.5.refs_5_.refs_6_
  28.9 0.0 copy-done
  28.9 4.9 %blocks_4.1 = (f32[8,1024]{1,0:T(8,128)S(1)}, bf16[4,4,2048,256]{3,2,1,0:T(8,128)(2,1)S(1)}) custom-call(f32[8,1]{1,0:T(8,128)S(1)} %copy.8.refs_0_, bf16[64,1024]{1,0:T(8,128)(2,1)S(1)} %get-tuple-element.28.refs_1_.refs_3_.refs_0_, f32[8,1024]{1,0:T(8,128)S(1)} %get-tuple-element.34.refs_2_, f32[1,1024]{1,0:T(1,128)S(1)} %bitcast.13, ...), custom_call_target="tpu_custom_call" | custom-call | flops 8589934592 | bytes 1048576 | tf_op jit(solution)/shard_map/blocks_4/pallas_call | solution.py:326
  33.9 1.9 %collective-permute-start.6 = (f32[1,8,1024]{2,1,0:T(8,128)S(1)}, f32[1,8,1024]{2,1,0:T(8,128)S(1)}, u32[]{:S(2)}, u32[]{:S(2)}) collective-permute-start(f32[1,8,1024]{2,1,0:T(8,128)S(1)} %bitcast.5), channel_id=1, source_target_pairs={{0,12},{1,13},{2,14},{3,15},{4,0},{5,1},{6,2},{7,3},{8,4},{9,5},{1... | collective-permute-start | bytes 98312 | tf_op jit(solution)/shard_map/ppermute | solution.py:59
  35.8 0.0 collective-permute-start.7
  35.8 1.9 %collective-permute-start.8 = (f32[1,8,1024]{2,1,0:T(8,128)S(1)}, f32[1,8,1024]{2,1,0:T(8,128)S(1)}, u32[]{:S(2)}, u32[]{:S(2)}) collective-permute-start(f32[1,8,1024]{2,1,0:T(8,128)S(1)} %bitcast.7), channel_id=1, source_target_pairs={{0,4},{1,5},{2,6},{3,7},{4,8},{5,9},{6,10},{7,11},{8,12},{9,13},{1... | collective-permute-start | bytes 98312 | tf_op jit(solution)/shard_map/ppermute | solution.py:59
  37.7 1.5 %own_again.1.refs_0_ = f32[8,1024]{1,0:T(8,128)S(1)} custom-call(bf16[64,1024]{1,0:T(8,128)(2,1)S(1)} %get-tuple-element.28.refs_1_.refs_3_.refs_0_, bf16[1,1024,64]{2,1,0:T(8,128)(2,1)S(1)} %get-tuple-element.41.refs_1_, f32[1,8,1024]{2,1,0:T(8,128)S(1)} %bitcast.8), custom_call_target="tpu_custom_call" | custom-call | flops 2147483648 | bytes 1048576 | tf_op jit(solution)/shard_map/own_again/pallas_call | solution.py:326
  39.1 0.0 copy-done.1
  39.1 0.0 collective-permute-done.6.refs_8_.refs_3_
  39.1 1.8 %collective-permute-done.7.refs_9_.refs_4_ = f32[1,8,1024]{2,1,0:T(8,128)S(1)} collective-permute-done((f32[1,8,1024]{2,1,0:T(8,128)S(1)}, f32[1,8,1024]{2,1,0:T(8,128)S(1)}, u32[]{:S(2)}, u32[]{:S(2)}) %collective-permute-start.7) | collective-permute-done | bytes 32800 | tf_op jit(solution)/shard_map/ppermute | solution.py:59
  40.9 0.6 collective-permute-done.8.refs_10_.refs_5_
  41.5 0.1 collective-permute-start.9
  41.6 0.6 collective-permute-start.10
  42.1 3.7 %line_again.1.refs_2_ = f32[8,1024]{1,0:T(8,128)S(1)} custom-call(f32[8,1024]{1,0:T(8,128)S(1)} %own_again.1.refs_0_, bf16[64,1024]{1,0:T(8,128)(2,1)S(1)} %get-tuple-element.28.refs_1_.refs_3_.refs_0_, bf16[3,1024,64]{2,1,0:T(8,128)(2,1)S(1)} %get-tuple-element.42.refs_2_, f32[1,8,1024]{2,1,0:T(8,128)S(1)} %collective-permute-done.6.refs_8_.refs_3_, ...), custom_call_target="tpu_custom_call" | custom-call | flops 6442450944 | bytes 1048576 | tf_op jit(solution)/shard_map/line_again/pallas_call | solution.py:326
  45.8 0.0 slice-start
  45.8 0.0 collective-permute-done.9.refs_2_.refs_11_.refs_3_
  45.8 0.0 slice-start.1
  45.9 1.7 %across_half.1.refs_1_ = f32[8,1024]{1,0:T(8,128)S(1)} custom-call(s32[2]{0:T(128)S(1)} %fusion.3.refs_0_, bf16[4,4,2048,256]{3,2,1,0:T(8,128)(2,1)S(1)} %get-tuple-element.36.refs_1_.refs_2_, f32[4,8,1024]{2,1,0:T(8,128)S(1)} %collective-permute-done.9.refs_2_.refs_11_.refs_3_), custom_call_target="tpu_custom_call" | custom-call | flops 4294967296 | bytes 1048576 | tf_op jit(solution)/shard_map/across_half/pallas_call | solution.py:326
  47.6 0.0 collective-permute-done.10.refs_12_.refs_5_
  47.6 0.2 collective-permute-start.11
  47.8 0.3 slice-done
  48.0 1.3 %slice-done.1 = s8[4194304]{0:T(1024)(128)(4,1)S(1)} async-done(((s8[8388608]{0:T(1024)(128)(4,1)}), s8[4194304]{0:T(1024)(128)(4,1)S(1)}, s32[]{:S(2)}) %slice-start.1) | async-done | bytes 4194328
  49.3 2.3 %beside_half.1.refs_1_ = f32[8,1024]{1,0:T(8,128)S(1)} custom-call(s32[2]{0:T(128)S(1)} %fusion.2.refs_0_, f32[8,1024]{1,0:T(8,128)S(1)} %across_half.1.refs_1_, bf16[2,4,2048,256]{3,2,1,0:T(8,128)(2,1)S(1)} %bitcast.17, bf16[64,1024]{1,0:T(8,128)(2,1)S(1)} %get-tuple-element.28.refs_1_.refs_3_.refs_0_, bf16[2,1024,64]{2,1,0:T(8,128)(2,1)S(1)} %get-tuple-element.40.refs_4_, ...), custom_call_target="tpu_custom_call" | custom-call | flops 4294967296 | bytes 1048576 | tf_op jit(solution)/shard_map/beside_half/pallas_call | solution.py:326
  51.6 0.0 collective-permute-done.11.refs_13_.refs_6_.refs_3_
  51.6 1.8 %far_half.1 = (f32[8,1024]{1,0:T(8,128)S(1)}, f32[8,128]{1,0:T(8,128)S(1)}) custom-call(s32[2]{0:T(128)S(1)} %fusion.3.refs_0_, f32[8,1024]{1,0:T(8,128)S(1)} %beside_half.1.refs_1_, f32[8,1024]{1,0:T(8,128)S(1)} %line_again.1.refs_2_, f32[1,1024]{1,0:T(1,128)S(1)} %bitcast.14, f32[1,8,1024]{2,1,0:T(8,128)S(1)} %bitcast.10, ...), custom_call_target="tpu_custom_call" | custom-call | flops 4294967296 | bytes 1048576 | tf_op jit(solution)/shard_map/far_half/pallas_call | solution.py:326
  53.5 1.3 %collective-permute-start.12 = (f32[8,128]{1,0:T(8,128)S(1)}, f32[8,128]{1,0:T(8,128)S(1)}, u32[]{:S(2)}, u32[]{:S(2)}) collective-permute-start(f32[8,128]{1,0:T(8,128)S(1)} %get-tuple-element.44), channel_id=1, source_target_pairs={{0,12},{1,13},{2,14},{3,15},{4,0},{5,1},{6,2},{7,3},{8,4},{9,5},{1... | collective-permute-start | bytes 12296 | tf_op jit(solution)/shard_map/ppermute | solution.py:59
  54.8 0.3 collective-permute-start.13
  55.0 1.6 %collective-permute-start.14 = (f32[8,128]{1,0:T(8,128)S(1)}, f32[8,128]{1,0:T(8,128)S(1)}, u32[]{:S(2)}, u32[]{:S(2)}) collective-permute-start(f32[8,128]{1,0:T(8,128)S(1)} %get-tuple-element.44), channel_id=1, source_target_pairs={{0,4},{1,5},{2,6},{3,7},{4,8},{5,9},{6,10},{7,11},{8,12},{9,13},{1... | collective-permute-start | bytes 12296 | tf_op jit(solution)/shard_map/ppermute | solution.py:59
  56.6 1.7 %across_rest.1.refs_1_ = f32[8,1024]{1,0:T(8,128)S(1)} custom-call(s32[2]{0:T(128)S(1)} %fusion.refs_0_, f32[8,1024]{1,0:T(8,128)S(1)} %get-tuple-element.45.refs_1_, bf16[4,4,2048,256]{3,2,1,0:T(8,128)(2,1)S(1)} %get-tuple-element.36.refs_1_.refs_2_, f32[4,8,1024]{2,1,0:T(8,128)S(1)} %collective-permute-done.9.refs_2_.refs_11_.refs_3_), custom_call_target="tpu_custom_call" | custom-call | flops 4294967296 | bytes 1048576 | tf_op jit(solution)/shard_map/across_rest/pallas_call | solution.py:326
  58.4 2.3 %beside_rest.1.refs_1_ = f32[8,1024]{1,0:T(8,128)S(1)} custom-call(s32[2]{0:T(128)S(1)} %fusion.1.refs_0_, f32[8,1024]{1,0:T(8,128)S(1)} %across_rest.1.refs_1_, bf16[2,4,2048,256]{3,2,1,0:T(8,128)(2,1)S(1)} %bitcast.17, bf16[64,1024]{1,0:T(8,128)(2,1)S(1)} %get-tuple-element.28.refs_1_.refs_3_.refs_0_, bf16[2,1024,64]{2,1,0:T(8,128)(2,1)S(1)} %get-tuple-element.40.refs_4_, ...), custom_call_target="tpu_custom_call" | custom-call | flops 4294967296 | bytes 1048576 | tf_op jit(solution)/shard_map/beside_rest/pallas_call | solution.py:326
  60.7 0.4 scalars.1.scalars_ref
  61.0 0.0 collective-permute-done.12
  61.0 0.0 collective-permute-done.13
  61.0 0.0 collective-permute-done.14
  61.1 0.1 collective-permute-start.15
  61.2 1.6 %collective-permute-start.16 = (f32[8,128]{1,0:T(8,128)S(1)}, f32[8,128]{1,0:T(8,128)S(1)}, u32[]{:S(2)}, u32[]{:S(2)}) collective-permute-start(f32[8,128]{1,0:T(8,128)S(1)} %add_add_fusion.1), channel_id=1, source_target_pairs={{0,2},{1,3},{2,0},{3,1},{4,6},{5,7},{6,4},{7,5},{8,10},{9,11},{10,... | collective-permute-start | bytes 12296 | tf_op jit(solution)/shard_map/ppermute | solution.py:52
  62.7 0.3 collective-permute-start.17
  63.0 1.7 %far_rest.1.total_ref = f32[8,1024]{1,0:T(8,128)S(1)} custom-call(s32[2]{0:T(128)S(1)} %fusion.refs_0_, f32[8,1024]{1,0:T(8,128)S(1)} %beside_rest.1.refs_1_, bf16[4,4,2048,256]{3,2,1,0:T(8,128)(2,1)S(1)} %get-tuple-element.43.refs_5_.refs_2_, f32[4,8,1024]{2,1,0:T(8,128)S(1)} %collective-permute-done.11.refs_13_.refs_6_.refs_3_), custom_call_target="tpu_custom_call" | custom-call | flops 4294967296 | bytes 1048576 | tf_op jit(solution)/shard_map/far_rest/pallas_call | solution.py:326
  64.7 0.0 collective-permute-done.15
  64.8 0.1 collective-permute-done.16
  64.8 0.9 %collective-permute-done.17 = f32[8,128]{1,0:T(8,128)S(1)} collective-permute-done((f32[8,128]{1,0:T(8,128)S(1)}, f32[8,128]{1,0:T(8,128)S(1)}, u32[]{:S(2)}, u32[]{:S(2)}) %collective-permute-start.17) | collective-permute-done | bytes 4128 | tf_op jit(solution)/shard_map/ppermute | solution.py:52
  65.8 0.7 %last_update.1 = (f32[8,1024]{1,0:T(8,128)}, f32[8,1024]{1,0:T(8,128)}) custom-call(f32[4,8,128]{2,1,0:T(8,128)S(1)} %scalars.1.scalars_ref, f32[8,128]{1,0:T(8,128)S(1)} %add_add_fusion.form_ref, f32[8,1024]{1,0:T(8,128)S(1)} %far_rest.1.total_ref, f32[1,1024]{1,0:T(1,128)S(1)} %bitcast.15, ...), custom_call_target="tpu_custom_call" | custom-call | tf_op jit(solution)/shard_map/last_update/pallas_call | solution.py:428
  (9 shorter events, 0.1 us)
Async XLA Ops:
  1.4 8.5 %collective-permute-start = (f32[1,16,1024]{2,1,0:T(8,128)S(1)}, f32[1,16,1024]{2,1,0:T(8,128)S(1)}, u32[]{:S(2)}, u32[]{:S(2)}) collective-permute-start(f32[1,16,1024]{2,1,0:T(8,128)S(1)} %maximum_bitcast_fusion.refs_1_.refs_4_.refs_0_.mine_ref), channel_id=1, source_target_pairs={{0,12},{1,13},{2,14},{3,15},{4,0},{5,1},{6,2},{7,3},{8,4},{9,5},{1... | collective-permute-start | bytes 196616 | tf_op jit(solution)/shard_map/ppermute | solution.py:59
  6.5 6.5 %collective-permute-start.1 = (f32[1,16,1024]{2,1,0:T(8,128)S(1)}, f32[1,16,1024]{2,1,0:T(8,128)S(1)}, u32[]{:S(2)}, u32[]{:S(2)}) collective-permute-start(f32[1,16,1024]{2,1,0:T(8,128)S(1)} %maximum_bitcast_fusion.refs_1_.refs_4_.refs_0_.mine_ref), channel_id=1, source_target_pairs={{0,8},{1,9},{2,10},{3,11},{4,12},{5,13},{6,14},{7,15},{8,0},{9,1},... | collective-permute-start | bytes 196616 | tf_op jit(solution)/shard_map/ppermute | solution.py:59
  6.5 6.5 %collective-permute-start.2 = (f32[1,16,1024]{2,1,0:T(8,128)S(1)}, f32[1,16,1024]{2,1,0:T(8,128)S(1)}, u32[]{:S(2)}, u32[]{:S(2)}) collective-permute-start(f32[1,16,1024]{2,1,0:T(8,128)S(1)} %maximum_bitcast_fusion.refs_1_.refs_4_.refs_0_.mine_ref), channel_id=1, source_target_pairs={{0,4},{1,5},{2,6},{3,7},{4,8},{5,9},{6,10},{7,11},{8,12},{9,13},{1... | collective-permute-start | bytes 196616 | tf_op jit(solution)/shard_map/ppermute | solution.py:59
  13.0 5.6 %collective-permute-start.3 = (f32[4,16,1024]{2,1,0:T(8,128)S(1)}, f32[4,16,1024]{2,1,0:T(8,128)S(1)}, u32[]{:S(2)}, u32[]{:S(2)}) collective-permute-start(f32[4,16,1024]{2,1,0:T(8,128)S(1)} %pad_maximum_fusion), channel_id=1, source_target_pairs={{0,1},{1,0},{2,3},{3,2},{4,5},{5,4},{6,7},{7,6},{8,9},{9,8},{10,11... | collective-permute-start | bytes 786440 | tf_op jit(solution)/shard_map/ppermute | solution.py:52
  13.0 10.5 %collective-permute-start.4 = (f32[4,16,1024]{2,1,0:T(8,128)S(1)}, f32[4,16,1024]{2,1,0:T(8,128)S(1)}, u32[]{:S(2)}, u32[]{:S(2)}) collective-permute-start(f32[4,16,1024]{2,1,0:T(8,128)S(1)} %pad_maximum_fusion), channel_id=1, source_target_pairs={{0,2},{1,3},{2,0},{3,1},{4,6},{5,7},{6,4},{7,5},{8,10},{9,11},{10,... | collective-permute-start | bytes 786440 | tf_op jit(solution)/shard_map/ppermute | solution.py:52
  23.5 5.4 %copy-start = (f32[1024]{0:T(1024)S(1)}, f32[1024]{0:T(1024)}, u32[]{:S(2)}) copy-start(f32[1024]{0:T(1024)} %param.6) | copy-start | bytes 12292
  23.5 5.4 %collective-permute-start.5 = (f32[4,16,1024]{2,1,0:T(8,128)S(1)}, f32[4,16,1024]{2,1,0:T(8,128)S(1)}, u32[]{:S(2)}, u32[]{:S(2)}) collective-permute-start(f32[4,16,1024]{2,1,0:T(8,128)S(1)} %collective-permute-done.4.refs_3_.refs_5_), channel_id=1, source_target_pairs={{0,1},{1,0},{2,3},{3,2},{4,5},{5,4},{6,7},{7,6},{8,9},{9,8},{10,11... | collective-permute-start | bytes 786440 | tf_op jit(solution)/shard_map/ppermute | solution.py:52
  28.9 10.3 %copy-start.1 = (bf16[2,4,2048,256]{3,2,1,0:T(8,128)(2,1)}, bf16[2,4,2048,256]{3,2,1,0:T(8,128)(2,1)S(1)}, u32[]{:S(2)}) copy-start(bf16[2,4,2048,256]{3,2,1,0:T(8,128)(2,1)S(1)} %get-tuple-element.39.refs_2_) | copy-start | bytes 25165828
  33.9 5.3 %collective-permute-start.6 = (f32[1,8,1024]{2,1,0:T(8,128)S(1)}, f32[1,8,1024]{2,1,0:T(8,128)S(1)}, u32[]{:S(2)}, u32[]{:S(2)}) collective-permute-start(f32[1,8,1024]{2,1,0:T(8,128)S(1)} %bitcast.5), channel_id=1, source_target_pairs={{0,12},{1,13},{2,14},{3,15},{4,0},{5,1},{6,2},{7,3},{8,4},{9,5},{1... | collective-permute-start | bytes 98312 | tf_op jit(solution)/shard_map/ppermute | solution.py:59
  35.8 5.2 %collective-permute-start.7 = (f32[1,8,1024]{2,1,0:T(8,128)S(1)}, f32[1,8,1024]{2,1,0:T(8,128)S(1)}, u32[]{:S(2)}, u32[]{:S(2)}) collective-permute-start(f32[1,8,1024]{2,1,0:T(8,128)S(1)} %bitcast.6), channel_id=1, source_target_pairs={{0,8},{1,9},{2,10},{3,11},{4,12},{5,13},{6,14},{7,15},{8,0},{9,1},... | collective-permute-start | bytes 98312 | tf_op jit(solution)/shard_map/ppermute | solution.py:59
  35.8 5.7 %collective-permute-start.8 = (f32[1,8,1024]{2,1,0:T(8,128)S(1)}, f32[1,8,1024]{2,1,0:T(8,128)S(1)}, u32[]{:S(2)}, u32[]{:S(2)}) collective-permute-start(f32[1,8,1024]{2,1,0:T(8,128)S(1)} %bitcast.7), channel_id=1, source_target_pairs={{0,4},{1,5},{2,6},{3,7},{4,8},{5,9},{6,10},{7,11},{8,12},{9,13},{1... | collective-permute-start | bytes 98312 | tf_op jit(solution)/shard_map/ppermute | solution.py:59
  41.5 4.3 %collective-permute-start.9 = (f32[4,8,1024]{2,1,0:T(8,128)S(1)}, f32[4,8,1024]{2,1,0:T(8,128)S(1)}, u32[]{:S(2)}, u32[]{:S(2)}) collective-permute-start(f32[4,8,1024]{2,1,0:T(8,128)S(1)} %pad_maximum_fusion.1), channel_id=1, source_target_pairs={{0,1},{1,0},{2,3},{3,2},{4,5},{5,4},{6,7},{7,6},{8,9},{9,8},{10,11... | collective-permute-start | bytes 393224 | tf_op jit(solution)/shard_map/ppermute | solution.py:52
  41.6 6.0 %collective-permute-start.10 = (f32[4,8,1024]{2,1,0:T(8,128)S(1)}, f32[4,8,1024]{2,1,0:T(8,128)S(1)}, u32[]{:S(2)}, u32[]{:S(2)}) collective-permute-start(f32[4,8,1024]{2,1,0:T(8,128)S(1)} %pad_maximum_fusion.1), channel_id=1, source_target_pairs={{0,2},{1,3},{2,0},{3,1},{4,6},{5,7},{6,4},{7,5},{8,10},{9,11},{10,... | collective-permute-start | bytes 393224 | tf_op jit(solution)/shard_map/ppermute | solution.py:52
  45.8 2.2 %slice-start = ((s8[8388608]{0:T(1024)(128)(4,1)}), s8[4194304]{0:T(1024)(128)(4,1)S(1)}, s32[]{:S(2)}) async-start(s8[8388608]{0:T(1024)(128)(4,1)} %bitcast.16), calls=%async_computation | async-start | bytes 8388608
  45.8 3.5 %slice-start.1 = ((s8[8388608]{0:T(1024)(128)(4,1)}), s8[4194304]{0:T(1024)(128)(4,1)S(1)}, s32[]{:S(2)}) async-start(s8[8388608]{0:T(1024)(128)(4,1)} %bitcast.16), calls=%async_computation.1 | async-start | bytes 8388608
  47.6 4.0 %collective-permute-start.11 = (f32[4,8,1024]{2,1,0:T(8,128)S(1)}, f32[4,8,1024]{2,1,0:T(8,128)S(1)}, u32[]{:S(2)}, u32[]{:S(2)}) collective-permute-start(f32[4,8,1024]{2,1,0:T(8,128)S(1)} %collective-permute-done.10.refs_12_.refs_5_), channel_id=1, source_target_pairs={{0,1},{1,0},{2,3},{3,2},{4,5},{5,4},{6,7},{7,6},{8,9},{9,8},{10,11... | collective-permute-start | bytes 393224 | tf_op jit(solution)/shard_map/ppermute | solution.py:52
  53.5 7.6 %collective-permute-start.12 = (f32[8,128]{1,0:T(8,128)S(1)}, f32[8,128]{1,0:T(8,128)S(1)}, u32[]{:S(2)}, u32[]{:S(2)}) collective-permute-start(f32[8,128]{1,0:T(8,128)S(1)} %get-tuple-element.44), channel_id=1, source_target_pairs={{0,12},{1,13},{2,14},{3,15},{4,0},{5,1},{6,2},{7,3},{8,4},{9,5},{1... | collective-permute-start | bytes 12296 | tf_op jit(solution)/shard_map/ppermute | solution.py:59
  54.8 6.3 %collective-permute-start.13 = (f32[8,128]{1,0:T(8,128)S(1)}, f32[8,128]{1,0:T(8,128)S(1)}, u32[]{:S(2)}, u32[]{:S(2)}) collective-permute-start(f32[8,128]{1,0:T(8,128)S(1)} %get-tuple-element.44), channel_id=1, source_target_pairs={{0,8},{1,9},{2,10},{3,11},{4,12},{5,13},{6,14},{7,15},{8,0},{9,1},... | collective-permute-start | bytes 12296 | tf_op jit(solution)/shard_map/ppermute | solution.py:59
  55.0 6.0 %collective-permute-start.14 = (f32[8,128]{1,0:T(8,128)S(1)}, f32[8,128]{1,0:T(8,128)S(1)}, u32[]{:S(2)}, u32[]{:S(2)}) collective-permute-start(f32[8,128]{1,0:T(8,128)S(1)} %get-tuple-element.44), channel_id=1, source_target_pairs={{0,4},{1,5},{2,6},{3,7},{4,8},{5,9},{6,10},{7,11},{8,12},{9,13},{1... | collective-permute-start | bytes 12296 | tf_op jit(solution)/shard_map/ppermute | solution.py:59
  61.1 3.7 %collective-permute-start.15 = (f32[8,128]{1,0:T(8,128)S(1)}, f32[8,128]{1,0:T(8,128)S(1)}, u32[]{:S(2)}, u32[]{:S(2)}) collective-permute-start(f32[8,128]{1,0:T(8,128)S(1)} %add_add_fusion.1), channel_id=1, source_target_pairs={{0,1},{1,0},{2,3},{3,2},{4,5},{5,4},{6,7},{7,6},{8,9},{9,8},{10,11... | collective-permute-start | bytes 12296 | tf_op jit(solution)/shard_map/ppermute | solution.py:52
  61.2 3.7 %collective-permute-start.16 = (f32[8,128]{1,0:T(8,128)S(1)}, f32[8,128]{1,0:T(8,128)S(1)}, u32[]{:S(2)}, u32[]{:S(2)}) collective-permute-start(f32[8,128]{1,0:T(8,128)S(1)} %add_add_fusion.1), channel_id=1, source_target_pairs={{0,2},{1,3},{2,0},{3,1},{4,6},{5,7},{6,4},{7,5},{8,10},{9,11},{10,... | collective-permute-start | bytes 12296 | tf_op jit(solution)/shard_map/ppermute | solution.py:52
  62.7 3.0 %collective-permute-start.17 = (f32[8,128]{1,0:T(8,128)S(1)}, f32[8,128]{1,0:T(8,128)S(1)}, u32[]{:S(2)}, u32[]{:S(2)}) collective-permute-start(f32[8,128]{1,0:T(8,128)S(1)} %add_add_fusion.1), channel_id=1, source_target_pairs={{0,3},{1,2},{2,1},{3,0},{4,7},{5,6},{6,5},{7,4},{8,11},{9,10},{10,... | collective-permute-start | bytes 12296 | tf_op jit(solution)/shard_map/ppermute | solution.py:52
